TPU v7x, 32 devices: a whole 2x2x4 slice. The times are simulated.
32 devices in a mesh: group: 2 (over y), expert: 4 (over z), tensor: 4 (over x, core).
Axes of the slice: x: 2, y: 2, z: 4, core: 2. Of those that a mesh axis runs over, the one named last changes fastest.
Arguments:
- tokens: bfloat16 [768, 3584], P(('group', 'expert'), 'tensor'), parts along dimension 0, may hold values from -6 to 6
- expert_ids: int32 [768, 2], P(('group', 'expert')), parts along dimension 0, may hold values from 0 to 3, all different within a row
- weight_codes: int32 [768, 2], P(('group', 'expert')), parts along dimension 0, may hold values from 1 to 8
- up_weight: bfloat16 [4, 3584, 2432], P('expert', None, 'tensor'), may hold values from -0.09375 to 0.09375
- down_weight: bfloat16 [4, 2432, 3584], P('expert', 'tensor'), may hold values from -0.125 to 0.125
Outputs:
- mixed: bfloat16 [768, 3584], P(('group', 'expert'), 'tensor'), parts along dimension 0
There are 2 independent parts, one for each index of `group`. A program takes and returns all parts, laid end to end along the dimension named above; an argument that names none is the same for every part. Nothing has to cross between parts.
Inputs may be any that keep to these rules, and one draw needn't show every extreme that they name: `expert_ids`: the two experts of a token differ.
All inputs are finite; a program needn't handle non-finite values.
Results may differ from a plain program's by a relative error of at most 0.012.
Values may be sent and summed in bfloat16 or wider, within the bound.
No kernel may reach another device: no remote copies, remote signals or barrier semaphores. Data moves between devices by JAX's collectives and lax.ppermute only.
A program may use at most 64 MiB of HBM per device.

v0:
```python
import jax
import jax.numpy as jnp
from jax import lax
from jax.sharding import PartitionSpec as P


def body(tokens, expert_ids, weight_codes, up_weight, down_weight):
    rows = tokens.shape[0]
    share_width = tokens.shape[1]
    experts_n = lax.axis_size("expert")
    capacity = 4 * rows // experts_n
    slots_n = experts_n * capacity
    flat_ids = expert_ids.reshape(rows * 2)
    onehot = (flat_ids[:, None] == jnp.arange(experts_n, dtype=jnp.int32)[None, :]).astype(
        jnp.int32
    )
    prior = jnp.cumsum(onehot, axis=0) - onehot
    slot = jnp.sum(prior * onehot, axis=1)
    target = jnp.where(slot < capacity, flat_ids * capacity + slot, -1)
    select = (jnp.arange(slots_n, dtype=jnp.int32)[:, None] == target[None, :]).astype(jnp.bfloat16)
    select = select.reshape(slots_n, rows, 2)
    gather_mat = jnp.sum(select, axis=2)
    up_local = up_weight[0]
    down_local = down_weight[0]
    features = lax.all_gather(tokens, "tensor", axis=1, tiled=True)
    sending = jnp.dot(gather_mat, features, preferred_element_type=jnp.float32).astype(jnp.bfloat16)
    sending = sending.reshape(experts_n, capacity, features.shape[1])
    received = lax.all_to_all(sending, "expert", split_axis=0, concat_axis=0, tiled=True)
    received = received.reshape(slots_n, features.shape[1])
    lifted = jnp.dot(received, up_local, preferred_element_type=jnp.float32)
    hidden = jax.nn.silu(lifted).astype(jnp.bfloat16)
    partial_out = jnp.dot(hidden, down_local, preferred_element_type=jnp.float32)
    total = lax.psum(partial_out.astype(jnp.bfloat16), "tensor")
    total = total.reshape(experts_n, capacity, total.shape[1])
    returned = lax.all_to_all(total, "expert", split_axis=0, concat_axis=0, tiled=True)
    returned = returned.reshape(slots_n, returned.shape[2])
    returned = lax.dynamic_slice_in_dim(
        returned, lax.axis_index("tensor") * share_width, share_width, 1
    )
    picked = jnp.einsum("srk,sd->krd", select, returned, preferred_element_type=jnp.float32)
    codes = weight_codes.astype(jnp.float32)
    weight = codes / jnp.sum(codes, axis=1, keepdims=True)
    mixed = weight[:, 0:1] * picked[0] + weight[:, 1:2] * picked[1]
    return mixed.astype(jnp.bfloat16)


def solution(mesh):
    return jax.shard_map(
        body,
        mesh=mesh,
        in_specs=(
            P(("group", "expert"), "tensor"),
            P(("group", "expert"), None),
            P(("group", "expert"), None),
            P("expert", None, "tensor"),
            P("expert", "tensor", None),
        ),
        out_specs=P(("group", "expert"), "tensor"),
        check_vma=False,
    )
```

profile of v0, /device:TPU:0, one launch (start us, length us, event | category | flops | bytes accessed | tf_op | source)
XLA Modules:
  0.0 230.8 jit_solution(1799409090872710876)
XLA Ops:
  6.5 0.8 copy.14
  7.3 0.7 broadcast_multiply_fusion
  8.0 0.1 eq.38
  8.2 1.2 reduce-window.6
  9.4 0.1 slice.28
  9.5 0.1 copy.15
  9.6 0.1 copy.16
  9.7 0.1 add_bitcast_fusion
  9.8 0.1 reduce_sum.34
  10.0 0.1 copy.18
  10.1 0.1 copy.19
  10.1 0.1 fusion.12
  10.3 9.7 %all_gather.3 = bf16[96,3584]{1,0:T(8,128)(2,1)S(1)} all-gather(bf16[96,896]{1,0:T(8,128)(2,1)} %param.5), channel_id=1, replica_groups=mesh['group'=2,'expert'=4,'tensor'=4] {'tensor'}, dimensions={1}, use_global_device_ids=true | all-gather | bytes 860160 | tf_op jit(solution)/shard_map/all_gather | solution.py:25
  20.0 0.9 convolution_convert_fusion.1
  20.9 0.0 slice-start
  20.9 67.7 %all_to_all.10 = bf16[4,96,3584]{2,1,0:T(8,128)(2,1)S(1)} all-to-all(bf16[4,96,3584]{2,1,0:T(8,128)(2,1)S(1)} %bitcast.51), channel_id=1, replica_groups=mesh['group'=2,'expert'=4,'tensor'=4] {'expert'}, dimensions={0} | all-to-all | bytes 5505024 | tf_op jit(solution)/shard_map/all_to_all | solution.py:28
  88.6 2.5 %multiply_convert_fusion = bf16[384,608]{0,1:T(8,128)(2,1)S(1)} fusion(bf16[384,3584]{1,0:T(8,128)(2,1)S(1)} %bitcast.53, bf16[1,3584,608]{1,2,0:T(8,128)(2,1)S(1)} %copy-done.1), kind=kOutput, calls=%fused_computation.6 | convolution fusion | flops 1674694656 | bytes 7577600 | tf_op jit(solution)/shard_map/dot_general | solution.py:30
  91.1 3.9 %convolution_convert_fusion = bf16[384,3584]{1,0:T(8,128)(2,1)} fusion(bf16[384,608]{0,1:T(8,128)(2,1)S(1)} %multiply_convert_fusion, bf16[1,608,3584]{2,1,0:T(8,128)(2,1)S(1)} %bitcast.49), kind=kOutput, calls=%fused_computation | convolution fusion | flops 1674903552 | bytes 7577600 | tf_op jit(solution)/shard_map/dot_general | solution.py:32
  95.1 0.0 all-reduce.3.cloned.1.call-update
  95.1 60.9 %all-reduce.3.cloned.1.call-done = bf16[4,96,3584]{2,1,0:T(8,128)(2,1)} async-done(((bf16[4,96,3584]{2,1,0:T(8,128)(2,1)}), bf16[4,96,3584]{2,1,0:T(8,128)(2,1)}) %all-reduce.3.cloned.1.call-update) | async-done | bytes 2752528 | tf_op jit(solution)/shard_map/psum | solution.py:33
  156.0 4.6 %all-to-all-start.1 = ((bf16[4,96,3584]{2,1,0:T(8,128)(2,1)}), bf16[4,96,3584]{2,1,0:T(8,128)(2,1)S(1)}, u32[]{:S(2)}, u32[]{:S(2)}) async-start(bf16[4,96,3584]{2,1,0:T(8,128)(2,1)} %all-reduce.3.cloned.1.call-done), calls=%async_computation.1 | async-start | bytes 5505024 | tf_op jit(solution)/shard_map/all_to_all | solution.py:35
  160.7 62.1 %all-to-all-done.1 = bf16[4,96,3584]{2,1,0:T(8,128)(2,1)S(1)} async-done(((bf16[4,96,3584]{2,1,0:T(8,128)(2,1)}), bf16[4,96,3584]{2,1,0:T(8,128)(2,1)S(1)}, u32[]{:S(2)}, u32[]{:S(2)}) %all-to-all-start.1) | async-done | bytes 2752544 | tf_op jit(solution)/shard_map/all_to_all | solution.py:35
  222.8 0.4 convolution_bitcast_fusion
  223.2 0.8 fusion.9
  (20 shorter events, 0.2 us)
Async XLA Ops:
  6.5 149.5 %all-reduce.3.cloned.1.call-start = ((), (), s32[]{:S(2)}) async-start(), calls=%async_computation.2 | async-start | bytes 5505024 | tf_op jit(solution)/shard_map/psum | solution.py:33
  20.0 68.6 %copy-start.1 = (bf16[1,3584,608]{1,2,0:T(8,128)(2,1)S(1)}, bf16[1,3584,608]{1,2,0:T(8,128)(2,1)}, u32[]{:S(2)}) copy-start(bf16[1,3584,608]{1,2,0:T(8,128)(2,1)} %param.8) | copy-start | bytes 13074436
  20.9 70.2 %slice-start = ((s8[4358144]{0:T(1024)(128)(4,1)}), s8[4194304]{0:T(1024)(128)(4,1)S(1)}, s32[]{:S(2)}) async-start(s8[4358144]{0:T(1024)(128)(4,1)} %bitcast.48), calls=%async_computation.3 | async-start | bytes 8388608
  88.6 2.5 %slice-start.1 = ((s8[4358144]{0:T(1024)(128)(4,1)}), s8[163840]{0:T(1024)(128)(4,1)S(1)}, s32[]{:S(2)}) async-start(s8[4358144]{0:T(1024)(128)(4,1)} %bitcast.48), calls=%async_computation.4 | async-start | bytes 327680
  95.1 65.5 %copy-start = (s32[96,2]{0,1:T(2,128)S(1)}, s32[96,2]{0,1:T(2,128)}, u32[]{:S(2)}) copy-start(s32[96,2]{0,1:T(2,128)} %param.7) | copy-start | bytes 2308
  156.0 66.7 %all-to-all-start.1 = ((bf16[4,96,3584]{2,1,0:T(8,128)(2,1)}), bf16[4,96,3584]{2,1,0:T(8,128)(2,1)S(1)}, u32[]{:S(2)}, u32[]{:S(2)}) async-start(bf16[4,96,3584]{2,1,0:T(8,128)(2,1)} %all-reduce.3.cloned.1.call-done), calls=%async_computation.1 | async-start | bytes 5505024 | tf_op jit(solution)/shard_map/all_to_all | solution.py:35
Sparse Core Ops, SparseCore 0:
  95.2 60.7 all-reduce.2
where the time goes:
time: 231 us
  waiting for transfers between devices  123 us (53%)
  blocking collectives  77.4 us (34%)
  between operations  13.5 us (6%)
  matrix products  7.75 us (3%)
  starting transfers between devices  4.6 us (2%)
  other arithmetic  2.98 us (1%)
    all_to_all x1, blocking collectives, body(): lax.all_to_all(sending, 'expert', split_axis=0, concat_axis=0, tiled=True)  67.7 us
    all_to_all x1, waiting for transfers between devices, body(): lax.all_to_all(total, 'expert', split_axis=0, concat_axis=0, tiled=True)  62.1 us
    psum x1, waiting for transfers between devices, body(): total = lax.psum(partial_out.astype(jnp.bfloat16), 'tensor')  60.9 us
    all_gather x1, blocking collectives, body(): features = lax.all_gather(tokens, 'tensor', axis=1, tiled=True)  9.72 us
  transfers between devices with their start and end apart: 2, of which 2 were waited for; matrix products, arithmetic and copies ran while one was open for 0% of the time, Pallas kernels for 0%

commit v1 on v0

v1 whole, which is shorter than its diff:
```python
import jax
import jax.numpy as jnp
from jax import lax
from jax.sharding import PartitionSpec as P


def kept_weights(expert_ids, weight_codes, experts_n, capacity):
    rows = expert_ids.shape[0]
    experts = jnp.arange(experts_n, dtype=jnp.int32)
    chosen = expert_ids[:, :, None] == experts[None, None, :]
    counts = jnp.sum(chosen.astype(jnp.float32), axis=1)
    earlier = (
        jnp.arange(rows, dtype=jnp.int32)[:, None] > jnp.arange(rows, dtype=jnp.int32)[None, :]
    ).astype(jnp.float32)
    before = jnp.dot(earlier, counts, preferred_element_type=jnp.float32)
    codes = weight_codes.astype(jnp.float32)
    weight = codes / jnp.sum(codes, axis=1, keepdims=True)
    first = jnp.where(chosen[:, 0] & (before < capacity), weight[:, 0:1], 0.0)
    slot = before + chosen[:, 0].astype(jnp.float32)
    second = jnp.where(chosen[:, 1] & (slot < capacity), weight[:, 1:2], 0.0)
    return first + second


def whole_blocks(tokens, expert_ids, weight_codes, up_local, down_local, capacity):
    rows = tokens.shape[0]
    experts_n = lax.axis_size("expert")
    weight = kept_weights(expert_ids, weight_codes, experts_n, capacity)
    weight = lax.all_gather(weight, "expert", axis=0, tiled=True)
    column = lax.dynamic_slice_in_dim(weight, lax.axis_index("expert"), 1, 1)
    features = lax.all_gather(tokens, "expert", axis=0, tiled=True)
    features = lax.all_gather(features, "tensor", axis=1, tiled=True)
    lifted = jnp.dot(features, up_local, preferred_element_type=jnp.float32)
    hidden = jax.nn.silu(lifted).astype(jnp.bfloat16)
    partial_out = jnp.dot(hidden, down_local, preferred_element_type=jnp.float32)
    partial_out = (partial_out * column).astype(jnp.bfloat16)
    total = lax.psum_scatter(partial_out, "tensor", scatter_dimension=1, tiled=True)
    return lax.psum_scatter(total, "expert", scatter_dimension=0, tiled=True)


def slotted(tokens, expert_ids, weight_codes, up_local, down_local, capacity):
    rows, share_width = tokens.shape
    experts_n = lax.axis_size("expert")
    slots_n = experts_n * capacity
    flat_ids = expert_ids.reshape(rows * 2)
    onehot = (flat_ids[:, None] == jnp.arange(experts_n, dtype=jnp.int32)[None, :]).astype(
        jnp.int32
    )
    prior = jnp.cumsum(onehot, axis=0) - onehot
    slot = jnp.sum(prior * onehot, axis=1)
    target = jnp.where(slot < capacity, flat_ids * capacity + slot, -1)
    select = (jnp.arange(slots_n, dtype=jnp.int32)[:, None] == target[None, :]).astype(jnp.bfloat16)
    select = select.reshape(slots_n, rows, 2)
    gather_mat = jnp.sum(select, axis=2)
    sending = jnp.dot(gather_mat, tokens, preferred_element_type=jnp.float32).astype(jnp.bfloat16)
    sending = sending.reshape(experts_n, capacity, share_width)
    received = lax.all_to_all(sending, "expert", split_axis=0, concat_axis=0, tiled=True)
    received = received.reshape(slots_n, share_width)
    received = lax.all_gather(received, "tensor", axis=1, tiled=True)
    lifted = jnp.dot(received, up_local, preferred_element_type=jnp.float32)
    hidden = jax.nn.silu(lifted).astype(jnp.bfloat16)
    partial_out = jnp.dot(hidden, down_local, preferred_element_type=jnp.float32)
    total = lax.psum_scatter(
        partial_out.astype(jnp.bfloat16), "tensor", scatter_dimension=1, tiled=True
    )
    total = total.reshape(experts_n, capacity, share_width)
    returned = lax.all_to_all(total, "expert", split_axis=0, concat_axis=0, tiled=True)
    returned = returned.reshape(slots_n, share_width)
    picked = jnp.einsum("srk,sd->krd", select, returned, preferred_element_type=jnp.float32)
    codes = weight_codes.astype(jnp.float32)
    weight = codes / jnp.sum(codes, axis=1, keepdims=True)
    mixed = weight[:, 0:1] * picked[0] + weight[:, 1:2] * picked[1]
    return mixed.astype(jnp.bfloat16)


def body(tokens, expert_ids, weight_codes, up_weight, down_weight):
    rows = tokens.shape[0]
    capacity = 4 * rows // lax.axis_size("expert")
    plan = whole_blocks if capacity >= rows else slotted
    return plan(tokens, expert_ids, weight_codes, up_weight[0], down_weight[0], capacity)


def solution(mesh):
    return jax.shard_map(
        body,
        mesh=mesh,
        in_specs=(
            P(("group", "expert"), "tensor"),
            P(("group", "expert"), None),
            P(("group", "expert"), None),
            P("expert", None, "tensor"),
            P("expert", "tensor", None),
        ),
        out_specs=P(("group", "expert"), "tensor"),
        check_vma=False,
    )
```

time: 231 us -> 134 us (0.58)
  waiting for transfers between devices: 123 us -> 69.4 us
  blocking collectives: 77.4 us -> 32.7 us
  starting transfers between devices: 4.6 us -> 0.09 us
  local copies, waits for them, and re-layouts: 1.54 us -> 5.07 us
  matrix products: 7.75 us -> 10.3 us
    all_to_all x1 -> x0, blocking collectives: 67.7 us -> none  [body(): lax.all_to_all(sending, 'expert', split_axis=0, concat_axis=0, tiled=True)]
    all_to_all x1 -> x0, waiting for transfers between devices: 62.1 us -> none  [body(): lax.all_to_all(total, 'expert', split_axis=0, concat_axis=0, tiled=True)]
    psum x1 -> x0, waiting for transfers between devices: 60.9 us -> none  [body(): total = lax.psum(partial_out.astype(jnp.bfloat16), 'tensor')]
    unnamed x1 -> x4, waiting for transfers between devices: 0.02 us -> 35.7 us
    all_gather x1 -> x2, blocking collectives: 9.72 us -> 32.7 us  [the longest x1 20.9 us: whole_blocks(): features = lax.all_gather(tokens, 'expert', axis=0, tiled=True)]
    reduce_scatter x0 -> x1, waiting for transfers between devices: none -> 22.7 us  [whole_blocks(): return lax.psum_scatter(total, 'expert', scatter_dimension=0, tiled=True)]
    all_gather x0 -> x1, waiting for transfers between devices: none -> 11.1 us  [whole_blocks(): features = lax.all_gather(features, 'tensor', axis=1, tiled=True)]
    all_to_all x1 -> x0, starting transfers between devices: 4.6 us -> none  [body(): lax.all_to_all(total, 'expert', split_axis=0, concat_axis=0, tiled=True)]
  transfers between devices with their start and end apart: 2 -> 3, of which waited for: 2 -> 3; matrix products, arithmetic and copies ran while one was open for 0% -> 2% of each run, Pallas kernels for 0% -> 0%
where the time goes in v1:
time: 134 us; the launch traced here: 133 us
  waiting for transfers between devices  69.4 us (52%)
  blocking collectives  32.7 us (24%)
  between operations  13.1 us (10%)
  matrix products  10.3 us (8%)
  local copies, waits for them, and re-layouts  5.07 us (4%)
  other arithmetic  2.76 us (2%)
    unnamed x4, waiting for transfers between devices  35.7 us
    reduce_scatter x1, waiting for transfers between devices, whole_blocks(): return lax.psum_scatter(total, 'expert', scatter_dimension=0, tiled=True)  22.7 us
    all_gather x1, blocking collectives, whole_blocks(): features = lax.all_gather(tokens, 'expert', axis=0, tiled=True)  20.9 us
    all_gather x1, blocking collectives, whole_blocks(): weight = lax.all_gather(weight, 'expert', axis=0, tiled=True)  11.9 us
    all_gather x1, waiting for transfers between devices, whole_blocks(): features = lax.all_gather(features, 'tensor', axis=1, tiled=True)  11.1 us
    dot_general x1, matrix products, whole_blocks(): lifted = jnp.dot(features, up_local, preferred_element_type=jnp.float32)  5.57 us
    unnamed x3, local copies, waits for them, and re-layouts  5.03 us
    dot_general x1, matrix products, whole_blocks(): jnp.dot(hidden, down_local, preferred_element_type=jnp.float32)  4.58 us
  transfers between devices with their start and end apart: 3, of which 3 were waited for; matrix products, arithmetic and copies ran while one was open for 2% of the time, Pallas kernels for 0%

profile of v1, /device:TPU:0, one launch (start us, length us, event | category | flops | bytes accessed | tf_op | source)
XLA Modules:
  0.0 133.5 jit_solution(13669354182793644768)
XLA Ops:
  6.5 0.0 all-gather.3.cloned.1.call-start
  6.5 20.9 %all_gather.9 = bf16[384,896]{1,0:T(8,128)(2,1)} all-gather(bf16[96,896]{1,0:T(8,128)(2,1)} %param.5), channel_id=1, replica_groups=mesh['group'=2,'expert'=4,'tensor'=4] {'expert'}, dimensions={0}, use_global_device_ids=true | all-gather | bytes 860160 | tf_op jit(solution)/shard_map/all_gather | solution.py:30
  27.4 0.0 all-gather.3.cloned.1.call-update
  27.4 0.0 reduce-scatter.7.cloned.1.call-start
  27.5 0.7 convert_reduce_fusion.1
  28.2 0.7 convert_reduce_fusion
  28.9 0.7 iota_compare_fusion.2
  29.5 0.7 convert_divide_fusion
  30.2 0.1 add_bitcast_fusion
  30.4 11.9 %all-gather = f32[4,96,4]{1,2,0:T(4,128)S(1)} all-gather(f32[1,96,4]{1,2,0:T(4,128)S(1)} %add_bitcast_fusion), channel_id=1, replica_groups=mesh['group'=2,'expert'=4,'tensor'=4] {'expert'}, dimensions={0}, use_global_device_ids=true | all-gather | bytes 7680 | tf_op jit(solution)/shard_map/all_gather | solution.py:28
  42.3 0.1 reshape.3
  42.4 11.1 %all-gather.3.cloned.1.call-done = bf16[384,3584]{1,0:T(8,128)(2,1)} async-done(((bf16[384,896]{1,0:T(8,128)(2,1)}), bf16[384,3584]{1,0:T(8,128)(2,1)}) %all-gather.3.cloned.1.call-update) | async-done | bytes 2752528 | tf_op jit(solution)/shard_map/all_gather | solution.py:31
  53.4 5.6 %multiply_convert_fusion = bf16[384,608]{0,1:T(8,128)(2,1)S(1)} fusion(bf16[384,3584]{1,0:T(8,128)(2,1)} %all-gather.3.cloned.1.call-done, bf16[1,3584,608]{1,2,0:T(8,128)(2,1)} %param.8), kind=kOutput, calls=%fused_computation.5 | convolution fusion | flops 1674694656 | bytes 7577600 | tf_op jit(solution)/shard_map/dot_general | solution.py:32
  59.0 4.6 %fusion = bf16[384,3584]{1,0:T(8,128)(2,1)S(1)} fusion(bf16[384,608]{0,1:T(8,128)(2,1)S(1)} %multiply_convert_fusion, bf16[1,608,3584]{2,1,0:T(8,128)(2,1)} %param.9, f32[384]{0:T(512)S(1)} %dynamic-slice_reduce_fusion), kind=kOutput, calls=%fused_computation.1 | convolution fusion | flops 1676279808 | bytes 7579136 | tf_op jit(solution)/shard_map/dot_general | solution.py:34
  63.6 2.7 %copy.8 = bf16[384,3584]{0,1:T(8,128)(2,1)} copy(bf16[384,3584]{1,0:T(8,128)(2,1)S(1)} %fusion) | data formatting | bytes 5505024
  66.3 0.0 reduce-scatter.7.cloned.1.call-update
  66.3 0.0 reduce-scatter.5.cloned.1.call-start
  66.4 35.6 %reduce-scatter.7.cloned.1.call-done = bf16[896,384]{1,0:T(8,128)(2,1)} async-done(((bf16[3584,384]{1,0:T(8,128)(2,1)}), bf16[896,384]{1,0:T(8,128)(2,1)}) %reduce-scatter.7.cloned.1.call-update) | async-done | bytes 688144
  102.0 2.2 %copy.9 = bf16[384,896]{1,0:T(8,128)(2,1)} copy(bf16[384,896]{0,1:T(8,128)(2,1)} %bitcast.30) | data formatting | bytes 1376256
  104.2 0.0 reduce-scatter.5.cloned.1.call-update
  104.2 22.7 %reduce-scatter.5.cloned.1.call-done = bf16[96,896]{1,0:T(8,128)(2,1)} async-done(((bf16[384,896]{1,0:T(8,128)(2,1)}), bf16[96,896]{1,0:T(8,128)(2,1)}) %reduce-scatter.5.cloned.1.call-update) | async-done | bytes 172048 | tf_op jit(solution)/shard_map/reduce_scatter | solution.py:37
  (3 shorter events, 0.0 us)
Async XLA Ops:
  6.5 46.9 %all-gather.3.cloned.1.call-start = ((), (), s32[]{:S(2)}) async-start(), calls=%async_computation.2 | async-start | bytes 3440640 | tf_op jit(solution)/shard_map/all_gather | solution.py:31
  27.4 74.6 %reduce-scatter.7.cloned.1.call-start = ((), (), s32[]{:S(2)}) async-start(), calls=%async_computation.4 | async-start | bytes 3440640
  66.3 60.6 %reduce-scatter.5.cloned.1.call-start = ((), (), s32[]{:S(2)}) async-start(), calls=%async_computation.3 | async-start | bytes 860160 | tf_op jit(solution)/shard_map/reduce_scatter | solution.py:37
Sparse Core Ops, SparseCore 0:
  27.5 25.8 all-gather.2
  66.5 35.4 reduce-scatter.6
  104.4 22.5 reduce-scatter.4

commit v2 on v1

--- a/solution.py
+++ b/solution.py
@@ -21,20 +21,53 @@
     return first + second
 
 
+def swap(array, bit):
+    return lax.ppermute(array, "tensor", [(i, i ^ bit) for i in range(4)])
+
+
 def whole_blocks(tokens, expert_ids, weight_codes, up_local, down_local, capacity):
-    rows = tokens.shape[0]
+    width = tokens.shape[1]
     experts_n = lax.axis_size("expert")
-    weight = kept_weights(expert_ids, weight_codes, experts_n, capacity)
-    weight = lax.all_gather(weight, "expert", axis=0, tiled=True)
-    column = lax.dynamic_slice_in_dim(weight, lax.axis_index("expert"), 1, 1)
-    features = lax.all_gather(tokens, "expert", axis=0, tiled=True)
-    features = lax.all_gather(features, "tensor", axis=1, tiled=True)
-    lifted = jnp.dot(features, up_local, preferred_element_type=jnp.float32)
-    hidden = jax.nn.silu(lifted).astype(jnp.bfloat16)
-    partial_out = jnp.dot(hidden, down_local, preferred_element_type=jnp.float32)
-    partial_out = (partial_out * column).astype(jnp.bfloat16)
-    total = lax.psum_scatter(partial_out, "tensor", scatter_dimension=1, tiled=True)
-    return lax.psum_scatter(total, "expert", scatter_dimension=0, tiled=True)
+    me = lax.axis_index("expert")
+    place = lax.axis_index("tensor")
+    weight = kept_weights(expert_ids, weight_codes, experts_n, capacity).T
+
+    def ring(array, by):
+        return lax.ppermute(
+            array, "expert", [(i, (i + by) % experts_n) for i in range(experts_n)]
+        )
+
+    order = (0, 2, 1, 3)
+    ups = [lax.dynamic_slice_in_dim(up_local, (place ^ j) * width, width, 0) for j in order]
+    downs = [lax.dynamic_slice_in_dim(down_local, (place ^ j) * width, width, 1) for j in order]
+    up_mine = jnp.concatenate(ups, axis=0)
+    down_mine = jnp.concatenate(downs, axis=1)
+
+    blocks = [tokens]
+    scales = [lax.dynamic_index_in_dim(weight, me, 0, keepdims=False)]
+    for step in range(1, experts_n):
+        blocks.append(ring(blocks[-1], 1))
+        to = lax.rem(me + step, experts_n)
+        scales.append(ring(lax.dynamic_index_in_dim(weight, to, 0, keepdims=False), step))
+
+    sums = []
+    for block, scale in zip(blocks, scales):
+        chip = jnp.concatenate([block, swap(block, 2)], axis=1)
+        features = jnp.concatenate([chip, swap(chip, 1)], axis=1)
+        lifted = jnp.dot(features, up_mine, preferred_element_type=jnp.float32)
+        hidden = (jax.nn.silu(lifted) * scale[:, None]).astype(jnp.bfloat16)
+        out = jnp.dot(hidden, down_mine, preferred_element_type=jnp.float32)
+        got = swap(out[:, 2 * width :].astype(jnp.bfloat16), 1)
+        out = out[:, : 2 * width] + got.astype(jnp.float32)
+        got = swap(out[:, width:].astype(jnp.bfloat16), 2)
+        sums.append(out[:, :width] + got.astype(jnp.float32))
+
+    total = None
+    for part in sums[1:]:
+        total = part if total is None else total.astype(jnp.float32) + part
+        total = ring(total.astype(jnp.bfloat16), 1)
+    mixed = sums[0] if total is None else total.astype(jnp.float32) + sums[0]
+    return mixed.astype(jnp.bfloat16)
 
 
 def slotted(tokens, expert_ids, weight_codes, up_local, down_local, capacity):
@@ -75,7 +108,8 @@
 def body(tokens, expert_ids, weight_codes, up_weight, down_weight):
     rows = tokens.shape[0]
     capacity = 4 * rows // lax.axis_size("expert")
-    plan = whole_blocks if capacity >= rows else slotted
+    whole = capacity >= rows and lax.axis_size("tensor") == 4
+    plan = whole_blocks if whole else slotted
     return plan(tokens, expert_ids, weight_codes, up_weight[0], down_weight[0], capacity)
 
 

time: 134 us -> 106 us (0.79)
  waiting for transfers between devices: 69.4 us -> 35.7 us
  blocking collectives: 32.7 us -> 0 us
  starting transfers between devices: 0.09 us -> 17.6 us
  matrix products: 10.3 us -> 27.2 us
  between operations: 13.1 us -> 0.22 us
  local copies, waits for them, and re-layouts: 5.07 us -> 14.7 us
  other arithmetic: 2.76 us -> 9.84 us
    ppermute x0 -> x25, waiting for transfers between devices: none -> 35.7 us  [the longest x9 26.4 us: ring(): lax.ppermute(array, 'expert', [(i, (i + by) % experts_n) for i in range(e...]
    unnamed x4 -> x0, waiting for transfers between devices: 35.7 us -> none
    all_gather x2 -> x0, blocking collectives: 32.7 us -> none  [the longest x1 20.9 us: whole_blocks(): features = lax.all_gather(tokens, 'expert', axis=0, tiled=True)]
    reduce_scatter x1 -> x0, waiting for transfers between devices: 22.7 us -> none  [whole_blocks(): return lax.psum_scatter(total, 'expert', scatter_dimension=0, tiled=True)]
    ppermute x0 -> x25, starting transfers between devices: none -> 17.6 us  [the longest x16 8.91 us: swap(): return lax.ppermute(array, 'tensor', [(i, i ^ bit) for i in range(4)])]
    dot_general x2 -> x4, matrix products: 10.2 us -> 27.1 us  [whole_blocks(): out = jnp.dot(hidden, down_mine, preferred_element_type=jnp.float32)]
    all_gather x1 -> x0, waiting for transfers between devices: 11.1 us -> none  [whole_blocks(): features = lax.all_gather(features, 'tensor', axis=1, tiled=True)]
    slice x0 -> x8, local copies, waits for them, and re-layouts: none -> 7.67 us  [the longest x4 6.23 us: whole_blocks(): got = swap(out[:, 2 * width:].astype(jnp.bfloat16), 1)]
  transfers between devices with their start and end apart: 3 -> 25, of which waited for: 3 -> 7; matrix products, arithmetic and copies ran while one was open for 2% -> 48% of each run, Pallas kernels for 0% -> 0%
where the time goes in v2:
time: 106 us; the launch traced here: 105 us
  waiting for transfers between devices  35.7 us (34%)
  matrix products  27.2 us (26%)
  starting transfers between devices  17.6 us (17%)
  local copies, waits for them, and re-layouts  14.7 us (14%)
  other arithmetic  9.84 us (9%)
    dot_general x4, matrix products, whole_blocks(): out = jnp.dot(hidden, down_mine, preferred_element_type=jnp.float32)  27.1 us
    ppermute x9, waiting for transfers between devices, ring(): lax.ppermute(array, 'expert', [(i, (i + by) % experts_n) for i in range(e...  26.4 us
    ppermute x16, waiting for transfers between devices, swap(): return lax.ppermute(array, 'tensor', [(i, i ^ bit) for i in range(4)])  9.29 us
    ppermute x16, starting transfers between devices, swap(): return lax.ppermute(array, 'tensor', [(i, i ^ bit) for i in range(4)])  8.91 us
    ppermute x9, starting transfers between devices, ring(): lax.ppermute(array, 'expert', [(i, (i + by) % experts_n) for i in range(e...  8.66 us
    slice x4, local copies, waits for them, and re-layouts, whole_blocks(): got = swap(out[:, 2 * width:].astype(jnp.bfloat16), 1)  6.23 us
    dynamic_slice x1, local copies, waits for them, and re-layouts, whole_blocks(): lax.dynamic_slice_in_dim(down_local, (place ^ j) * width, width, 1)  4.12 us
    convert_element_type x3, other arithmetic, whole_blocks(): total = ring(total.astype(jnp.bfloat16), 1)  2.84 us
  transfers between devices with their start and end apart: 25, of which 7 were waited for; matrix products, arithmetic and copies ran while one was open for 48% of the time, Pallas kernels for 0%

profile of v2, /device:TPU:0, one launch (start us, length us, event | category | flops | bytes accessed | tf_op | source)
XLA Modules:
  0.0 105.3 jit_solution(4403064308846072599)
XLA Ops:
  0.0 3.0 %collective-permute-start = (bf16[96,896]{1,0:T(8,128)(2,1)}, bf16[96,896]{1,0:T(8,128)(2,1)S(1)}, u32[]{:S(2)}, u32[]{:S(2)}) collective-permute-start(bf16[96,896]{1,0:T(8,128)(2,1)} %param.5), channel_id=1, source_target_pairs={{0,4},{4,8},{8,12},{12,0},{1,5},{5,9},{9,13},{13,1},{2,6},{6,10},{... | collective-permute-start | bytes 516104 | tf_op jit(solution)/shard_map/ppermute | solution.py:36
  3.0 1.5 %collective-permute-start.21 = (bf16[96,896]{1,0:T(8,128)(2,1)}, bf16[96,896]{1,0:T(8,128)(2,1)S(1)}, u32[]{:S(2)}, u32[]{:S(2)}) collective-permute-start(bf16[96,896]{1,0:T(8,128)(2,1)} %param.5), channel_id=1, source_target_pairs={{0,2},{1,3},{2,0},{3,1},{4,6},{5,7},{6,4},{7,5},{8,10},{9,11},{10,... | collective-permute-start | bytes 516104 | tf_op jit(solution)/shard_map/ppermute | solution.py:25
  8.0 1.6 %collective-permute-start.3 = (f32[96]{0:T(128)}, f32[96]{0:T(128)}, u32[]{:S(2)}, u32[]{:S(2)}) collective-permute-start(f32[96]{0:T(128)} %get-tuple-element.13), channel_id=1, source_target_pairs={{0,4},{4,8},{8,12},{12,0},{1,5},{5,9},{9,13},{13,1},{2,6},{6,10},{... | collective-permute-start | bytes 1160 | tf_op jit(solution)/shard_map/ppermute | solution.py:36
  9.6 1.2 %collective-permute-start.10 = (f32[96]{0:T(128)}, f32[96]{0:T(128)}, u32[]{:S(2)}, u32[]{:S(2)}) collective-permute-start(f32[96]{0:T(128)} %get-tuple-element.16), channel_id=1, source_target_pairs={{0,8},{4,12},{8,0},{12,4},{1,9},{5,13},{9,1},{13,5},{2,10},{6,14},... | collective-permute-start | bytes 1160 | tf_op jit(solution)/shard_map/ppermute | solution.py:36
  10.8 2.7 %collective-permute-start.17 = (f32[96]{0:T(128)}, f32[96]{0:T(128)}, u32[]{:S(2)}, u32[]{:S(2)}) collective-permute-start(f32[96]{0:T(128)} %get-tuple-element.15), channel_id=1, source_target_pairs={{0,12},{4,0},{8,4},{12,8},{1,13},{5,1},{9,5},{13,9},{2,14},{6,2},{... | collective-permute-start | bytes 1160 | tf_op jit(solution)/shard_map/ppermute | solution.py:36
  13.5 4.1 %dynamic-slice_bitcast_fusion.3 = (bf16[608,896]{1,0:T(8,128)(2,1)S(1)}, bf16[608,896]{1,0:T(8,128)(2,1)S(1)}, bf16[608,896]{1,0:T(8,128)(2,1)}, bf16[608,896]{1,0:T(8,128)(2,1)}) fusion(bf16[1,608,3584]{2,1,0:T(8,128)(2,1)} %param.9, s32[]{:T(128)S(6)} %select_n.36, s32[]{:T(128)S(6)} %select_n.37, s32[]{:T(128)S(6)} %select_n.39, s32[]{:T(128)S(6)} %select_n.38), kind=kLoop, calls=%fused_computation.5 | loop fusion | bytes 8716304 | tf_op jit(solution)/shard_map/dynamic_slice | solution.py:42
  18.2 2.2 %dynamic-slice_bitcast_fusion.7 = (bf16[896,608]{0,1:T(8,128)(2,1)}, bf16[896,608]{0,1:T(8,128)(2,1)}, bf16[896,608]{0,1:T(8,128)(2,1)}, bf16[896,608]{0,1:T(8,128)(2,1)}) fusion(bf16[1,3584,608]{1,2,0:T(8,128)(2,1)S(1)} %bitcast.38, s32[]{:T(128)S(6)} %select_n.36, s32[]{:T(128)S(6)} %select_n.37, s32[]{:T(128)S(6)} %select_n.39, s32[]{:T(128)S(6)} %select_n.38), kind=kLoop, calls=%fused_computation.9 | loop fusion | bytes 8716304 | tf_op jit(solution)/shard_map/dynamic_slice | solution.py:41
  20.4 2.7 %collective-permute-done.1 = bf16[96,896]{1,0:T(8,128)(2,1)S(1)} collective-permute-done((bf16[96,896]{1,0:T(8,128)(2,1)S(1)}, bf16[96,896]{1,0:T(8,128)(2,1)S(1)}, u32[]{:S(2)}, u32[]{:S(2)}) %collective-permute-start.1) | collective-permute-done | bytes 172064 | tf_op jit(solution)/shard_map/ppermute | solution.py:25
  23.2 7.1 %collective-permute-done.7 = bf16[96,896]{1,0:T(8,128)(2,1)S(1)} collective-permute-done((bf16[96,896]{1,0:T(8,128)(2,1)S(1)}, bf16[96,896]{1,0:T(8,128)(2,1)S(1)}, u32[]{:S(2)}, u32[]{:S(2)}) %collective-permute-start.7) | collective-permute-done | bytes 172064 | tf_op jit(solution)/shard_map/ppermute | solution.py:36
  30.9 4.8 %collective-permute-done.8 = bf16[96,896]{1,0:T(8,128)(2,1)S(1)} collective-permute-done((bf16[96,896]{1,0:T(8,128)(2,1)S(1)}, bf16[96,896]{1,0:T(8,128)(2,1)S(1)}, u32[]{:S(2)}, u32[]{:S(2)}) %collective-permute-start.8) | collective-permute-done | bytes 172064 | tf_op jit(solution)/shard_map/ppermute | solution.py:25
  35.8 7.2 %collective-permute-done.14 = bf16[96,896]{1,0:T(8,128)(2,1)} collective-permute-done((bf16[96,896]{1,0:T(8,128)(2,1)S(1)}, bf16[96,896]{1,0:T(8,128)(2,1)}, u32[]{:S(2)}, u32[]{:S(2)}) %collective-permute-start.14) | collective-permute-done | bytes 172064 | tf_op jit(solution)/shard_map/ppermute | solution.py:36
  43.8 6.7 %fusion.49 = f32[96,3584]{1,0:T(8,128)} fusion(bf16[96,1792]{1,0:T(8,128)(2,1)} %copy-done.8, bf16[96,896]{1,0:T(8,128)(2,1)} %copy-done.6, bf16[96,896]{1,0:T(8,128)(2,1)S(1)} %collective-permute-done, f32[96]{0:T(128)} %collective-permute-done.3, bf16[608,896]{1,0:T(8,128)(2,1)} %get-tuple-element.11, bf16[608,896]{1,0:T(8,128)(2,1)} %get-tuple-element.12, ...), kind=kOutput, calls=%fused_computation.68 | convolution fusion | flops 874043392 | bytes 10781056 | tf_op jit(solution)/shard_map/dot_general | solution.py:59
  53.3 6.8 %fusion.44 = f32[96,3584]{1,0:T(8,128)} fusion(bf16[96,1792]{1,0:T(8,128)(2,1)} %collective-permute-done.9, bf16[96,896]{1,0:T(8,128)(2,1)} %copy-done.7, bf16[96,896]{1,0:T(8,128)(2,1)} %copy-done.5, f32[96]{0:T(128)} %collective-permute-done.10, bf16[608,896]{1,0:T(8,128)(2,1)} %get-tuple-element.11, bf16[608,896]{1,0:T(8,128)(2,1)} %get-tuple-element.12, ...), kind=kOutput, calls=%fused_computation.66 | convolution fusion | flops 874043392 | bytes 10781056 | tf_op jit(solution)/shard_map/dot_general | solution.py:59
  60.1 1.9 %slice.147 = bf16[96,1792]{1,0:T(8,128)(2,1)} slice(f32[96,3584]{1,0:T(8,128)} %fusion.44), slice={[0:96], [1792:3584]} | slice | bytes 688128 | tf_op jit(solution)/shard_map/slice | solution.py:60
  62.5 1.2 %slice_add_fusion.3 = f32[96,1792]{1,0:T(8,128)S(1)} fusion(f32[96,3584]{1,0:T(8,128)} %fusion.49, bf16[96,1792]{1,0:T(8,128)(2,1)} %collective-permute-done.4), kind=kLoop, calls=%fused_computation.17 | loop fusion | flops 344064 | bytes 1720320 | tf_op jit(solution)/shard_map/add | solution.py:61
  65.5 6.8 %fusion.39 = f32[96,3584]{1,0:T(8,128)} fusion(bf16[96,1792]{1,0:T(8,128)(2,1)} %collective-permute-done.16, bf16[96,896]{1,0:T(8,128)(2,1)} %collective-permute-done.15, bf16[96,896]{1,0:T(8,128)(2,1)} %collective-permute-done.14, f32[96]{0:T(128)} %collective-permute-done.17, bf16[608,896]{1,0:T(8,128)(2,1)} %get-tuple-element.11, ...), kind=kOutput, calls=%fused_computation.64 | convolution fusion | flops 874043392 | bytes 10781056 | tf_op jit(solution)/shard_map/dot_general | solution.py:59
  72.3 2.0 %slice.146 = bf16[96,1792]{1,0:T(8,128)(2,1)} slice(f32[96,3584]{1,0:T(8,128)} %fusion.39), slice={[0:96], [1792:3584]} | slice | bytes 688128 | tf_op jit(solution)/shard_map/slice | solution.py:60
  74.3 1.6 %fusion.30 = bf16[96,896]{1,0:T(8,128)(2,1)} fusion(f32[96,1792]{1,0:T(8,128)S(1)} %slice_add_fusion.3, bf16[96,896]{1,0:T(8,128)(2,1)} %collective-permute-done.5), kind=kLoop, calls=%fused_computation.56 | loop fusion | flops 258048 | bytes 688128 | tf_op jit(solution)/shard_map/convert_element_type | solution.py:68
  78.6 6.8 %fusion.34 = f32[96,3584]{1,0:T(8,128)} fusion(bf16[96,1792]{1,0:T(8,128)(2,1)} %collective-permute-done.22, bf16[96,896]{1,0:T(8,128)(2,1)} %copy-done.4, bf16[96,896]{1,0:T(8,128)(2,1)} %param.5, f32[96]{0:T(128)} %get-tuple-element.14, bf16[608,896]{1,0:T(8,128)(2,1)} %get-tuple-element.11, bf16[608,896]{1,0:T(8,128)(2,1)} %get-tuple-element.12, ...), kind=kOutput, calls=%fused_computation.62 | convolution fusion | flops 874043392 | bytes 10781056 | tf_op jit(solution)/shard_map/dot_general | solution.py:59
  85.4 1.2 %slice.145 = bf16[96,1792]{1,0:T(8,128)(2,1)S(1)} slice(f32[96,3584]{1,0:T(8,128)} %fusion.34), slice={[0:96], [1792:3584]} | slice | bytes 688128 | tf_op jit(solution)/shard_map/slice | solution.py:60
  88.3 1.2 %collective-permute-start.19 = (bf16[96,896]{1,0:T(8,128)(2,1)S(1)}, bf16[96,896]{1,0:T(8,128)(2,1)S(1)}, u32[]{:S(2)}, u32[]{:S(2)}) collective-permute-start(bf16[96,896]{1,0:T(8,128)(2,1)S(1)} %slice.150), channel_id=1, source_target_pairs={{0,2},{1,3},{2,0},{3,1},{4,6},{5,7},{6,4},{7,5},{8,10},{9,11},{10,... | collective-permute-start | bytes 516104 | tf_op jit(solution)/shard_map/ppermute | solution.py:25
  90.6 6.1 %collective-permute-done.13 = bf16[96,896]{1,0:T(8,128)(2,1)S(1)} collective-permute-done((bf16[96,896]{1,0:T(8,128)(2,1)S(1)}, bf16[96,896]{1,0:T(8,128)(2,1)S(1)}, u32[]{:S(2)}, u32[]{:S(2)}) %collective-permute-start.13) | collective-permute-done | bytes 172064 | tf_op jit(solution)/shard_map/ppermute | solution.py:36
  96.9 1.7 %collective-permute-done.24 = bf16[96,896]{1,0:T(8,128)(2,1)S(1)} collective-permute-done((bf16[96,896]{1,0:T(8,128)(2,1)S(1)}, bf16[96,896]{1,0:T(8,128)(2,1)S(1)}, u32[]{:S(2)}, u32[]{:S(2)}) %collective-permute-start.24) | collective-permute-done | bytes 172064 | tf_op jit(solution)/shard_map/ppermute | solution.py:25
  98.6 6.0 %collective-permute-done.20 = bf16[96,896]{1,0:T(8,128)(2,1)S(1)} collective-permute-done((bf16[96,896]{1,0:T(8,128)(2,1)S(1)}, bf16[96,896]{1,0:T(8,128)(2,1)S(1)}, u32[]{:S(2)}, u32[]{:S(2)}) %collective-permute-start.20) | collective-permute-done | bytes 172064 | tf_op jit(solution)/shard_map/ppermute | solution.py:36
  (82 shorter events, 16.9 us)
Async XLA Ops:
  0.0 17.7 %collective-permute-start = (bf16[96,896]{1,0:T(8,128)(2,1)}, bf16[96,896]{1,0:T(8,128)(2,1)S(1)}, u32[]{:S(2)}, u32[]{:S(2)}) collective-permute-start(bf16[96,896]{1,0:T(8,128)(2,1)} %param.5), channel_id=1, source_target_pairs={{0,4},{4,8},{8,12},{12,0},{1,5},{5,9},{9,13},{13,1},{2,6},{6,10},{... | collective-permute-start | bytes 516104 | tf_op jit(solution)/shard_map/ppermute | solution.py:36
  3.0 20.1 %collective-permute-start.21 = (bf16[96,896]{1,0:T(8,128)(2,1)}, bf16[96,896]{1,0:T(8,128)(2,1)S(1)}, u32[]{:S(2)}, u32[]{:S(2)}) collective-permute-start(bf16[96,896]{1,0:T(8,128)(2,1)} %param.5), channel_id=1, source_target_pairs={{0,2},{1,3},{2,0},{3,1},{4,6},{5,7},{6,4},{7,5},{8,10},{9,11},{10,... | collective-permute-start | bytes 516104 | tf_op jit(solution)/shard_map/ppermute | solution.py:25
  8.0 27.7 %collective-permute-start.3 = (f32[96]{0:T(128)}, f32[96]{0:T(128)}, u32[]{:S(2)}, u32[]{:S(2)}) collective-permute-start(f32[96]{0:T(128)} %get-tuple-element.13), channel_id=1, source_target_pairs={{0,4},{4,8},{8,12},{12,0},{1,5},{5,9},{9,13},{13,1},{2,6},{6,10},{... | collective-permute-start | bytes 1160 | tf_op jit(solution)/shard_map/ppermute | solution.py:36
  9.6 43.6 %collective-permute-start.10 = (f32[96]{0:T(128)}, f32[96]{0:T(128)}, u32[]{:S(2)}, u32[]{:S(2)}) collective-permute-start(f32[96]{0:T(128)} %get-tuple-element.16), channel_id=1, source_target_pairs={{0,8},{4,12},{8,0},{12,4},{1,9},{5,13},{9,1},{13,5},{2,10},{6,14},... | collective-permute-start | bytes 1160 | tf_op jit(solution)/shard_map/ppermute | solution.py:36
  10.8 54.7 %collective-permute-start.17 = (f32[96]{0:T(128)}, f32[96]{0:T(128)}, u32[]{:S(2)}, u32[]{:S(2)}) collective-permute-start(f32[96]{0:T(128)} %get-tuple-element.15), channel_id=1, source_target_pairs={{0,12},{4,0},{8,4},{12,8},{1,13},{5,1},{9,5},{13,9},{2,14},{6,2},{... | collective-permute-start | bytes 1160 | tf_op jit(solution)/shard_map/ppermute | solution.py:36
  17.7 5.4 %collective-permute-start.1 = (bf16[96,896]{1,0:T(8,128)(2,1)S(1)}, bf16[96,896]{1,0:T(8,128)(2,1)S(1)}, u32[]{:S(2)}, u32[]{:S(2)}) collective-permute-start(bf16[96,896]{1,0:T(8,128)(2,1)S(1)} %collective-permute-done), channel_id=1, source_target_pairs={{0,2},{1,3},{2,0},{3,1},{4,6},{5,7},{6,4},{7,5},{8,10},{9,11},{10,... | collective-permute-start | bytes 516104 | tf_op jit(solution)/shard_map/ppermute | solution.py:25
  23.1 7.2 %collective-permute-start.7 = (bf16[96,896]{1,0:T(8,128)(2,1)S(1)}, bf16[96,896]{1,0:T(8,128)(2,1)S(1)}, u32[]{:S(2)}, u32[]{:S(2)}) collective-permute-start(bf16[96,896]{1,0:T(8,128)(2,1)S(1)} %collective-permute-done), channel_id=1, source_target_pairs={{0,4},{4,8},{8,12},{12,0},{1,5},{5,9},{9,13},{13,1},{2,6},{6,10},{... | collective-permute-start | bytes 516104 | tf_op jit(solution)/shard_map/ppermute | solution.py:36
  23.1 19.9 %collective-permute-start.2 = (bf16[96,1792]{1,0:T(8,128)(2,1)S(1)}, bf16[96,1792]{1,0:T(8,128)(2,1)S(1)}, u32[]{:S(2)}, u32[]{:S(2)}) collective-permute-start(bf16[96,1792]{1,0:T(8,128)(2,1)S(1)} %pad_maximum_fusion.2), channel_id=1, source_target_pairs={{0,1},{1,0},{2,3},{3,2},{4,5},{5,4},{6,7},{7,6},{8,9},{9,8},{10,11... | collective-permute-start | bytes 1032200 | tf_op jit(solution)/shard_map/ppermute | solution.py:25
  30.3 5.4 %collective-permute-start.8 = (bf16[96,896]{1,0:T(8,128)(2,1)S(1)}, bf16[96,896]{1,0:T(8,128)(2,1)S(1)}, u32[]{:S(2)}, u32[]{:S(2)}) collective-permute-start(bf16[96,896]{1,0:T(8,128)(2,1)S(1)} %collective-permute-done.7), channel_id=1, source_target_pairs={{0,2},{1,3},{2,0},{3,1},{4,6},{5,7},{6,4},{7,5},{8,10},{9,11},{10,... | collective-permute-start | bytes 516104 | tf_op jit(solution)/shard_map/ppermute | solution.py:25
  35.7 7.3 %collective-permute-start.14 = (bf16[96,896]{1,0:T(8,128)(2,1)S(1)}, bf16[96,896]{1,0:T(8,128)(2,1)}, u32[]{:S(2)}, u32[]{:S(2)}) collective-permute-start(bf16[96,896]{1,0:T(8,128)(2,1)S(1)} %collective-permute-done.7), channel_id=1, source_target_pairs={{0,4},{4,8},{8,12},{12,0},{1,5},{5,9},{9,13},{13,1},{2,6},{6,10},{... | collective-permute-start | bytes 516104 | tf_op jit(solution)/shard_map/ppermute | solution.py:36
  35.7 42.9 %collective-permute-start.22 = (bf16[96,1792]{1,0:T(8,128)(2,1)S(1)}, bf16[96,1792]{1,0:T(8,128)(2,1)}, u32[]{:S(2)}, u32[]{:S(2)}) collective-permute-start(bf16[96,1792]{1,0:T(8,128)(2,1)S(1)} %pad_maximum_fusion.5), channel_id=1, source_target_pairs={{0,1},{1,0},{2,3},{3,2},{4,5},{5,4},{6,7},{7,6},{8,9},{9,8},{10,11... | collective-permute-start | bytes 1032200 | tf_op jit(solution)/shard_map/ppermute | solution.py:25
  43.0 10.3 %collective-permute-start.9 = (bf16[96,1792]{1,0:T(8,128)(2,1)S(1)}, bf16[96,1792]{1,0:T(8,128)(2,1)}, u32[]{:S(2)}, u32[]{:S(2)}) collective-permute-start(bf16[96,1792]{1,0:T(8,128)(2,1)S(1)} %pad_maximum_fusion.3), channel_id=1, source_target_pairs={{0,1},{1,0},{2,3},{3,2},{4,5},{5,4},{6,7},{7,6},{8,9},{9,8},{10,11... | collective-permute-start | bytes 1032200 | tf_op jit(solution)/shard_map/ppermute | solution.py:25
  43.0 8.6 %collective-permute-start.15 = (bf16[96,896]{1,0:T(8,128)(2,1)}, bf16[96,896]{1,0:T(8,128)(2,1)}, u32[]{:S(2)}, u32[]{:S(2)}) collective-permute-start(bf16[96,896]{1,0:T(8,128)(2,1)} %collective-permute-done.14), channel_id=1, source_target_pairs={{0,2},{1,3},{2,0},{3,1},{4,6},{5,7},{6,4},{7,5},{8,10},{9,11},{10,... | collective-permute-start | bytes 516104 | tf_op jit(solution)/shard_map/ppermute | solution.py:25
  51.6 10.9 %collective-permute-start.4 = (bf16[96,1792]{1,0:T(8,128)(2,1)S(1)}, bf16[96,1792]{1,0:T(8,128)(2,1)}, u32[]{:S(2)}, u32[]{:S(2)}) collective-permute-start(bf16[96,1792]{1,0:T(8,128)(2,1)S(1)} %slice.148), channel_id=1, source_target_pairs={{0,1},{1,0},{2,3},{3,2},{4,5},{5,4},{6,7},{7,6},{8,9},{9,8},{10,11... | collective-permute-start | bytes 1032200 | tf_op jit(solution)/shard_map/ppermute | solution.py:25
  53.2 12.3 %collective-permute-start.16 = (bf16[96,1792]{1,0:T(8,128)(2,1)S(1)}, bf16[96,1792]{1,0:T(8,128)(2,1)}, u32[]{:S(2)}, u32[]{:S(2)}) collective-permute-start(bf16[96,1792]{1,0:T(8,128)(2,1)S(1)} %pad_maximum_fusion.4), channel_id=1, source_target_pairs={{0,1},{1,0},{2,3},{3,2},{4,5},{5,4},{6,7},{7,6},{8,9},{9,8},{10,11... | collective-permute-start | bytes 1032200 | tf_op jit(solution)/shard_map/ppermute | solution.py:25
  62.0 14.0 %collective-permute-start.11 = (bf16[96,1792]{1,0:T(8,128)(2,1)}, bf16[96,1792]{1,0:T(8,128)(2,1)}, u32[]{:S(2)}, u32[]{:S(2)}) collective-permute-start(bf16[96,1792]{1,0:T(8,128)(2,1)} %slice.147), channel_id=1, source_target_pairs={{0,1},{1,0},{2,3},{3,2},{4,5},{5,4},{6,7},{7,6},{8,9},{9,8},{10,11... | collective-permute-start | bytes 1032200 | tf_op jit(solution)/shard_map/ppermute | solution.py:25
  64.4 9.9 %collective-permute-start.5 = (bf16[96,896]{1,0:T(8,128)(2,1)}, bf16[96,896]{1,0:T(8,128)(2,1)}, u32[]{:S(2)}, u32[]{:S(2)}) collective-permute-start(bf16[96,896]{1,0:T(8,128)(2,1)} %slice.152), channel_id=1, source_target_pairs={{0,2},{1,3},{2,0},{3,1},{4,6},{5,7},{6,4},{7,5},{8,10},{9,11},{10,... | collective-permute-start | bytes 516104 | tf_op jit(solution)/shard_map/ppermute | solution.py:25
  74.3 13.9 %collective-permute-start.18 = (bf16[96,1792]{1,0:T(8,128)(2,1)}, bf16[96,1792]{1,0:T(8,128)(2,1)S(1)}, u32[]{:S(2)}, u32[]{:S(2)}) collective-permute-start(bf16[96,1792]{1,0:T(8,128)(2,1)} %slice.146), channel_id=1, source_target_pairs={{0,1},{1,0},{2,3},{3,2},{4,5},{5,4},{6,7},{7,6},{8,9},{9,8},{10,11... | collective-permute-start | bytes 1032200 | tf_op jit(solution)/shard_map/ppermute | solution.py:25
  76.0 11.0 %collective-permute-start.6 = (bf16[96,896]{1,0:T(8,128)(2,1)}, bf16[96,896]{1,0:T(8,128)(2,1)}, u32[]{:S(2)}, u32[]{:S(2)}) collective-permute-start(bf16[96,896]{1,0:T(8,128)(2,1)} %fusion.30), channel_id=1, source_target_pairs={{0,4},{4,8},{8,12},{12,0},{1,5},{5,9},{9,13},{13,1},{2,6},{6,10},{... | collective-permute-start | bytes 516104 | tf_op jit(solution)/shard_map/ppermute | solution.py:36
  77.7 9.3 %collective-permute-start.12 = (bf16[96,896]{1,0:T(8,128)(2,1)}, bf16[96,896]{1,0:T(8,128)(2,1)}, u32[]{:S(2)}, u32[]{:S(2)}) collective-permute-start(bf16[96,896]{1,0:T(8,128)(2,1)} %slice.151), channel_id=1, source_target_pairs={{0,2},{1,3},{2,0},{3,1},{4,6},{5,7},{6,4},{7,5},{8,10},{9,11},{10,... | collective-permute-start | bytes 516104 | tf_op jit(solution)/shard_map/ppermute | solution.py:25
  88.1 8.6 %collective-permute-start.13 = (bf16[96,896]{1,0:T(8,128)(2,1)S(1)}, bf16[96,896]{1,0:T(8,128)(2,1)S(1)}, u32[]{:S(2)}, u32[]{:S(2)}) collective-permute-start(bf16[96,896]{1,0:T(8,128)(2,1)S(1)} %fusion.29), channel_id=1, source_target_pairs={{0,4},{4,8},{8,12},{12,0},{1,5},{5,9},{9,13},{13,1},{2,6},{6,10},{... | collective-permute-start | bytes 516104 | tf_op jit(solution)/shard_map/ppermute | solution.py:36
  88.3 8.4 %collective-permute-start.19 = (bf16[96,896]{1,0:T(8,128)(2,1)S(1)}, bf16[96,896]{1,0:T(8,128)(2,1)S(1)}, u32[]{:S(2)}, u32[]{:S(2)}) collective-permute-start(bf16[96,896]{1,0:T(8,128)(2,1)S(1)} %slice.150), channel_id=1, source_target_pairs={{0,2},{1,3},{2,0},{3,1},{4,6},{5,7},{6,4},{7,5},{8,10},{9,11},{10,... | collective-permute-start | bytes 516104 | tf_op jit(solution)/shard_map/ppermute | solution.py:25
  89.6 9.0 %collective-permute-start.24 = (bf16[96,896]{1,0:T(8,128)(2,1)S(1)}, bf16[96,896]{1,0:T(8,128)(2,1)S(1)}, u32[]{:S(2)}, u32[]{:S(2)}) collective-permute-start(bf16[96,896]{1,0:T(8,128)(2,1)S(1)} %slice.149), channel_id=1, source_target_pairs={{0,2},{1,3},{2,0},{3,1},{4,6},{5,7},{6,4},{7,5},{8,10},{9,11},{10,... | collective-permute-start | bytes 516104 | tf_op jit(solution)/shard_map/ppermute | solution.py:25
  96.8 7.8 %collective-permute-start.20 = (bf16[96,896]{1,0:T(8,128)(2,1)S(1)}, bf16[96,896]{1,0:T(8,128)(2,1)S(1)}, u32[]{:S(2)}, u32[]{:S(2)}) collective-permute-start(bf16[96,896]{1,0:T(8,128)(2,1)S(1)} %fusion.27), channel_id=1, source_target_pairs={{0,4},{4,8},{8,12},{12,0},{1,5},{5,9},{9,13},{13,1},{2,6},{6,10},{... | collective-permute-start | bytes 516104 | tf_op jit(solution)/shard_map/ppermute | solution.py:36
  (12 other events, 90.6 us)

commit v3 on v1

--- a/solution.py
+++ b/solution.py
@@ -1,40 +1,156 @@
+import functools
+
 import jax
 import jax.numpy as jnp
 from jax import lax
+from jax.experimental import pallas as pl
+from jax.experimental.pallas import tpu as pltpu
 from jax.sharding import PartitionSpec as P
 
 
-def kept_weights(expert_ids, weight_codes, experts_n, capacity):
-    rows = expert_ids.shape[0]
-    experts = jnp.arange(experts_n, dtype=jnp.int32)
-    chosen = expert_ids[:, :, None] == experts[None, None, :]
-    counts = jnp.sum(chosen.astype(jnp.float32), axis=1)
-    earlier = (
-        jnp.arange(rows, dtype=jnp.int32)[:, None] > jnp.arange(rows, dtype=jnp.int32)[None, :]
-    ).astype(jnp.float32)
-    before = jnp.dot(earlier, counts, preferred_element_type=jnp.float32)
-    codes = weight_codes.astype(jnp.float32)
-    weight = codes / jnp.sum(codes, axis=1, keepdims=True)
-    first = jnp.where(chosen[:, 0] & (before < capacity), weight[:, 0:1], 0.0)
-    slot = before + chosen[:, 0].astype(jnp.float32)
-    second = jnp.where(chosen[:, 1] & (slot < capacity), weight[:, 1:2], 0.0)
-    return first + second
+MIB = 1 << 20
+HBM = pl.BlockSpec(memory_space=pl.ANY)
+VMEM = pl.BlockSpec(memory_space=pltpu.VMEM)
+
+
+def kept_weights(ids, codes, experts_n, capacity):
+    rows = ids.shape[1]
+    experts = lax.broadcasted_iota(jnp.int32, (experts_n, rows), 0)
+    first = ids[0:1, :] == experts
+    second = ids[1:2, :] == experts
+    counts = first.astype(jnp.float32) + second.astype(jnp.float32)
+    earlier = lax.broadcasted_iota(jnp.int32, (rows, rows), 0) < lax.broadcasted_iota(
+        jnp.int32, (rows, rows), 1
+    )
+    before = jnp.dot(
+        counts.astype(jnp.bfloat16),
+        earlier.astype(jnp.float32).astype(jnp.bfloat16),
+        preferred_element_type=jnp.float32,
+    )
+    codes = codes.astype(jnp.float32)
+    weight = codes / (codes[0:1, :] + codes[1:2, :])
+    keep_first = first & (before < capacity)
+    keep_second = second & (before + first.astype(jnp.float32) < capacity)
+    return jnp.where(keep_first, weight[0:1, :], 0.0) + jnp.where(
+        keep_second, weight[1:2, :], 0.0
+    )
+
+
+def prepare_kernel(capacity, experts_n, ids, codes, up, down, up_out, down_out, *rest):
+    scales, (up_sem, down_sem) = rest[:experts_n], rest[experts_n:]
+    up_copy = pltpu.make_async_copy(up, up_out, up_sem)
+    down_copy = pltpu.make_async_copy(down, down_out, down_sem)
+    up_copy.start()
+    down_copy.start()
+    me = lax.axis_index("expert")
+    weight = kept_weights(ids[...], codes[...], experts_n, capacity)
+    index = lax.broadcasted_iota(jnp.int32, weight.shape, 0)
+    for step, scale in enumerate(scales):
+        mine = index == lax.rem(me + step, experts_n)
+        scale[...] = jnp.sum(jnp.where(mine, weight, 0.0), axis=0, keepdims=True)
+    up_copy.wait()
+    down_copy.wait()
+
+
+def prepare(ids, codes, up_t, down, experts_n, capacity):
+    rows = ids.shape[1]
+    return pl.pallas_call(
+        functools.partial(prepare_kernel, capacity, experts_n),
+        out_shape=[pltpu.VMEM(up_t.shape, up_t.dtype), pltpu.VMEM(down.shape, down.dtype)]
+        + [jax.ShapeDtypeStruct((1, rows), jnp.float32)] * experts_n,
+        in_specs=[VMEM, VMEM, HBM, HBM],
+        out_specs=[VMEM] * (2 + experts_n),
+        scratch_shapes=[pltpu.SemaphoreType.DMA, pltpu.SemaphoreType.DMA],
+        compiler_params=pltpu.CompilerParams(vmem_limit_bytes=20 * MIB),
+        cost_estimate=pl.CostEstimate(
+            flops=0, bytes_accessed=4 * up_t.size + 4 * down.size, transcendentals=0
+        ),
+    )(ids, codes, up_t, down)
+
+
+def expert_kernel(own, other, own_core, other_core, scale, up_t, down, keep, send, features, out):
+    rows, width = own.shape
+    place = lax.axis_index("tensor")
+
+    def columns(bits):
+        return pl.ds(pl.multiple_of((place ^ bits) * width, width), width)
+
+    features[:, columns(0)] = own[...]
+    features[:, columns(2)] = other[...]
+    features[:, columns(1)] = own_core[...]
+    features[:, columns(3)] = other_core[...]
+    lifted = lax.dot_general(
+        features[...], up_t[...], (((1,), (1,)), ((), ())), preferred_element_type=jnp.float32
+    )
+    diagonal = lax.broadcasted_iota(jnp.int32, (rows, rows), 0) == lax.broadcasted_iota(
+        jnp.int32, (rows, rows), 1
+    )
+    column = jnp.sum(jnp.where(diagonal, scale[...], 0.0), axis=1, keepdims=True)
+    hidden = (lifted / (1.0 + jnp.exp(-lifted)) * column).astype(jnp.bfloat16)
+    out[...] = jnp.dot(hidden, down[...], preferred_element_type=jnp.float32)
+    keep[:, :width] = out[:, columns(0)]
+    keep[:, width:] = out[:, columns(2)]
+    send[:, :width] = out[:, columns(1)].astype(jnp.bfloat16)
+    send[:, width:] = out[:, columns(3)].astype(jnp.bfloat16)
+
+
+def expert_block(own, other, own_core, other_core, scale, up_t, down):
+    rows, width = own.shape
+    hidden_n, model = up_t.shape
+    return pl.pallas_call(
+        expert_kernel,
+        out_shape=[
+            jax.ShapeDtypeStruct((rows, 2 * width), jnp.float32),
+            jax.ShapeDtypeStruct((rows, 2 * width), jnp.bfloat16),
+        ],
+        in_specs=[VMEM] * 7,
+        out_specs=[VMEM] * 2,
+        scratch_shapes=[
+            pltpu.VMEM((rows, model), jnp.bfloat16),
+            pltpu.VMEM((rows, model), jnp.float32),
+        ],
+        compiler_params=pltpu.CompilerParams(vmem_limit_bytes=20 * MIB),
+        cost_estimate=pl.CostEstimate(
+            flops=4 * rows * model * hidden_n,
+            bytes_accessed=4 * rows * model,
+            transcendentals=rows * hidden_n,
+        ),
+    )(own, other, own_core, other_core, scale, up_t, down)
+
+
+def swap(array, bit):
+    return lax.ppermute(array, "tensor", [(i, i ^ bit) for i in range(4)])
 
 
 def whole_blocks(tokens, expert_ids, weight_codes, up_local, down_local, capacity):
-    rows = tokens.shape[0]
+    width = tokens.shape[1]
     experts_n = lax.axis_size("expert")
-    weight = kept_weights(expert_ids, weight_codes, experts_n, capacity)
-    weight = lax.all_gather(weight, "expert", axis=0, tiled=True)
-    column = lax.dynamic_slice_in_dim(weight, lax.axis_index("expert"), 1, 1)
-    features = lax.all_gather(tokens, "expert", axis=0, tiled=True)
-    features = lax.all_gather(features, "tensor", axis=1, tiled=True)
-    lifted = jnp.dot(features, up_local, preferred_element_type=jnp.float32)
-    hidden = jax.nn.silu(lifted).astype(jnp.bfloat16)
-    partial_out = jnp.dot(hidden, down_local, preferred_element_type=jnp.float32)
-    partial_out = (partial_out * column).astype(jnp.bfloat16)
-    total = lax.psum_scatter(partial_out, "tensor", scatter_dimension=1, tiled=True)
-    return lax.psum_scatter(total, "expert", scatter_dimension=0, tiled=True)
+
+    def shift(array, by):
+        if by % experts_n == 0:
+            return array
+        return lax.ppermute(
+            array, "expert", [(i, (i + by) % experts_n) for i in range(experts_n)]
+        )
+
+    blocks = [shift(tokens, step) for step in range(experts_n)]
+    up_t, down, *scales = prepare(
+        expert_ids.T, weight_codes.T, up_local.T, down_local, experts_n, capacity
+    )
+    scales = [shift(scale, step) for step, scale in enumerate(scales)]
+
+    mixed = None
+    for step, (block, scale) in enumerate(zip(blocks, scales)):
+        other = swap(block, 2)
+        keep, send = expert_block(
+            block, other, swap(block, 1), swap(other, 1), scale, up_t, down
+        )
+        keep = keep + swap(send, 1).astype(jnp.float32)
+        part = keep[:, :width] + swap(keep[:, width:].astype(jnp.bfloat16), 2).astype(jnp.float32)
+        if step:
+            part = shift(part.astype(jnp.bfloat16), -step).astype(jnp.float32)
+        mixed = part if mixed is None else mixed + part
+    return mixed.astype(jnp.bfloat16)
 
 
 def slotted(tokens, expert_ids, weight_codes, up_local, down_local, capacity):
@@ -75,7 +191,8 @@
 def body(tokens, expert_ids, weight_codes, up_weight, down_weight):
     rows = tokens.shape[0]
     capacity = 4 * rows // lax.axis_size("expert")
-    plan = whole_blocks if capacity >= rows else slotted
+    whole = capacity >= rows and lax.axis_size("tensor") == 4
+    plan = whole_blocks if whole else slotted
     return plan(tokens, expert_ids, weight_codes, up_weight[0], down_weight[0], capacity)
 
 

time: 134 us -> 74.4 us (0.56)
  waiting for transfers between devices: 69.4 us -> 31.5 us
  blocking collectives: 32.7 us -> 0 us
  starting transfers between devices: 0.09 us -> 23.7 us
  between operations: 13.1 us -> 0.18 us
  Pallas kernels: 0 us -> 11.7 us
  matrix products: 10.3 us -> 0 us
  other arithmetic: 2.76 us -> 1.16 us
    unnamed x4 -> x0, waiting for transfers between devices: 35.7 us -> none
    all_gather x2 -> x0, blocking collectives: 32.7 us -> none  [the longest x1 20.9 us: whole_blocks(): features = lax.all_gather(tokens, 'expert', axis=0, tiled=True)]
    ppermute x0 -> x29, waiting for transfers between devices: none -> 31.5 us  [the longest x20 17 us: swap(): return lax.ppermute(array, 'tensor', [(i, i ^ bit) for i in range(4)])]
    ppermute x0 -> x29, starting transfers between devices: none -> 23.7 us  [the longest x9 12.6 us: shift(): lax.ppermute(array, 'expert', [(i, (i + by) % experts_n) for i in range(e...]
    reduce_scatter x1 -> x0, waiting for transfers between devices: 22.7 us -> none  [whole_blocks(): return lax.psum_scatter(total, 'expert', scatter_dimension=0, tiled=True)]
    pallas_call x0 -> x5, Pallas kernels: none -> 11.7 us  [the longest x4 10.6 us: expert_block(): pl.pallas_call(expert_kernel, out_shape=[jax.ShapeDtypeStruct((rows, 2 *...]
    all_gather x1 -> x0, waiting for transfers between devices: 11.1 us -> none  [whole_blocks(): features = lax.all_gather(features, 'tensor', axis=1, tiled=True)]
    dot_general x3 -> x0, matrix products: 10.3 us -> none  [the longest x1 5.57 us: whole_blocks(): lifted = jnp.dot(features, up_local, preferred_element_type=jnp.float32)]
  transfers between devices with their start and end apart: 3 -> 29, of which waited for: 3 -> 8; matrix products, arithmetic and copies ran while one was open for 2% -> 1% of each run, Pallas kernels for 0% -> 16%
where the time goes in v3:
time: 74.4 us; the launch traced here: 74.2 us
  waiting for transfers between devices  31.5 us (42%)
  starting transfers between devices  23.7 us (32%)
  Pallas kernels  11.7 us (16%)
  local copies, waits for them, and re-layouts  5.91 us (8%)
  other arithmetic  1.16 us (2%)
    ppermute x20, waiting for transfers between devices, swap(): return lax.ppermute(array, 'tensor', [(i, i ^ bit) for i in range(4)])  17 us
    ppermute x9, waiting for transfers between devices, shift(): lax.ppermute(array, 'expert', [(i, (i + by) % experts_n) for i in range(e...  14.6 us
    ppermute x9, starting transfers between devices, shift(): lax.ppermute(array, 'expert', [(i, (i + by) % experts_n) for i in range(e...  12.6 us
    ppermute x20, starting transfers between devices, swap(): return lax.ppermute(array, 'tensor', [(i, i ^ bit) for i in range(4)])  11.2 us
    pallas_call x4, Pallas kernels, expert_block(): pl.pallas_call(expert_kernel, out_shape=[jax.ShapeDtypeStruct((rows, 2 *...  10.6 us
    unnamed x10, local copies, waits for them, and re-layouts  5.83 us
  transfers between devices with their start and end apart: 29, of which 8 were waited for; matrix products, arithmetic and copies ran while one was open for 1% of the time, Pallas kernels for 16%

profile of v3, /device:TPU:0, one launch (start us, length us, event | category | flops | bytes accessed | tf_op | source)
XLA Modules:
  0.0 74.2 jit_solution(578131271282363340)
XLA Ops:
  0.0 3.0 %collective-permute-start.5 = (bf16[96,896]{1,0:T(8,128)(2,1)}, bf16[96,896]{1,0:T(8,128)(2,1)S(1)}, u32[]{:S(2)}, u32[]{:S(2)}) collective-permute-start(bf16[96,896]{1,0:T(8,128)(2,1)} %own.1), channel_id=1, source_target_pairs={{0,4},{4,8},{8,12},{12,0},{1,5},{5,9},{9,13},{13,1},{2,6},{6,10},{... | collective-permute-start | bytes 516104 | tf_op jit(solution)/shard_map/ppermute | solution.py:132
  3.0 1.5 %collective-permute-start = (bf16[96,896]{1,0:T(8,128)(2,1)}, bf16[96,896]{1,0:T(8,128)(2,1)S(1)}, u32[]{:S(2)}, u32[]{:S(2)}) collective-permute-start(bf16[96,896]{1,0:T(8,128)(2,1)} %own.1), channel_id=1, source_target_pairs={{0,2},{1,3},{2,0},{3,1},{4,6},{5,7},{6,4},{7,5},{8,10},{9,11},{10,... | collective-permute-start | bytes 516104 | tf_op jit(solution)/shard_map/ppermute | solution.py:122
  4.5 2.6 %collective-permute-start.13 = (bf16[96,896]{1,0:T(8,128)(2,1)}, bf16[96,896]{1,0:T(8,128)(2,1)S(1)}, u32[]{:S(2)}, u32[]{:S(2)}) collective-permute-start(bf16[96,896]{1,0:T(8,128)(2,1)} %own.1), channel_id=1, source_target_pairs={{0,8},{4,12},{8,0},{12,4},{1,9},{5,13},{9,1},{13,5},{2,10},{6,14},... | collective-permute-start | bytes 516104 | tf_op jit(solution)/shard_map/ppermute | solution.py:132
  7.1 1.3 %collective-permute-start.21 = (bf16[96,896]{1,0:T(8,128)(2,1)}, bf16[96,896]{1,0:T(8,128)(2,1)S(1)}, u32[]{:S(2)}, u32[]{:S(2)}) collective-permute-start(bf16[96,896]{1,0:T(8,128)(2,1)} %own.1), channel_id=1, source_target_pairs={{0,12},{4,0},{8,4},{12,8},{1,13},{5,1},{9,5},{13,9},{2,14},{6,2},{... | collective-permute-start | bytes 516104 | tf_op jit(solution)/shard_map/ppermute | solution.py:132
  8.5 2.2 %copy-done = bf16[1,3584,608]{1,2,0:T(8,128)(2,1)S(1)} copy-done((bf16[1,3584,608]{1,2,0:T(8,128)(2,1)S(1)}, bf16[1,3584,608]{1,2,0:T(8,128)(2,1)}, u32[]{:S(2)}) %copy-start) | copy-done | bytes 4358168
  10.7 2.2 %copy-done.1 = bf16[1,608,3584]{2,1,0:T(8,128)(2,1)S(1)} copy-done((bf16[1,608,3584]{2,1,0:T(8,128)(2,1)S(1)}, bf16[1,608,3584]{2,1,0:T(8,128)(2,1)}, u32[]{:S(2)}) %copy-start.1) | copy-done | bytes 4358168
  14.3 1.2 %shard_map.55 = (bf16[608,3584]{1,0:T(8,128)(2,1)S(1)}, bf16[608,3584]{1,0:T(8,128)(2,1)S(1)}, f32[1,96]{1,0:T(1,128)S(1)}, f32[1,96]{1,0:T(1,128)S(1)}, f32[1,96]{1,0:T(1,128)S(1)}, /*index=5*/f32[1,96]{1,0:T(1,128)S(1)}) custom-call(s32[2,96]{1,0:T(2,128)S(1)} %bitcast.8, s32[2,96]{1,0:T(2,128)S(1)} %bitcast.9, bf16[608,3584]{1,0:T(8,128)(2,1)S(1)} %bitcast.6, ...), custom_call_target="tpu_custom_call" | custom-call | bytes 17432576 | tf_op jit(solution)/shard_map/pallas_call | solution.py:57
  16.2 4.7 %collective-permute-done.9.scale = f32[1,96]{1,0:T(1,128)S(1)} collective-permute-done((f32[1,96]{1,0:T(1,128)S(1)}, f32[1,96]{1,0:T(1,128)S(1)}, u32[]{:S(2)}, u32[]{:S(2)}) %collective-permute-start.9) | collective-permute-done | bytes 416 | tf_op jit(solution)/shard_map/ppermute | solution.py:132
  22.0 1.5 %collective-permute-start.14 = (bf16[96,896]{1,0:T(8,128)(2,1)S(1)}, bf16[96,896]{1,0:T(8,128)(2,1)S(1)}, u32[]{:S(2)}, u32[]{:S(2)}) collective-permute-start(bf16[96,896]{1,0:T(8,128)(2,1)S(1)} %collective-permute-done.13.own), channel_id=1, source_target_pairs={{0,2},{1,3},{2,0},{3,1},{4,6},{5,7},{6,4},{7,5},{8,10},{9,11},{10,... | collective-permute-start | bytes 516104 | tf_op jit(solution)/shard_map/ppermute | solution.py:122
  24.0 4.1 %collective-permute-done.6.other = bf16[96,896]{1,0:T(8,128)(2,1)S(1)} collective-permute-done((bf16[96,896]{1,0:T(8,128)(2,1)S(1)}, bf16[96,896]{1,0:T(8,128)(2,1)S(1)}, u32[]{:S(2)}, u32[]{:S(2)}) %collective-permute-start.6) | collective-permute-done | bytes 172064 | tf_op jit(solution)/shard_map/ppermute | solution.py:122
  28.6 2.6 %shard_map.56 = (f32[96,1792]{1,0:T(8,128)S(1)}, bf16[96,1792]{1,0:T(8,128)(2,1)S(1)}) custom-call(bf16[96,896]{1,0:T(8,128)(2,1)S(1)} %copy-done.2, bf16[96,896]{1,0:T(8,128)(2,1)S(1)} %collective-permute-done.other, bf16[96,896]{1,0:T(8,128)(2,1)S(1)} %collective-permute-done.1.own_core, bf16[96,896]{1,0:T(8,128)(2,1)S(1)} %collective-permute-done.2.other_core, ...), custom_call_target="tpu_custom_call" | custom-call | flops 836763648 | bytes 1376256 | tf_op jit(solution)/shard_map/pallas_call | solution.py:100
  32.4 2.6 %collective-permute-done.22.other = bf16[96,896]{1,0:T(8,128)(2,1)S(1)} collective-permute-done((bf16[96,896]{1,0:T(8,128)(2,1)S(1)}, bf16[96,896]{1,0:T(8,128)(2,1)S(1)}, u32[]{:S(2)}, u32[]{:S(2)}) %collective-permute-start.22) | collective-permute-done | bytes 172064 | tf_op jit(solution)/shard_map/ppermute | solution.py:122
  35.5 2.6 %shard_map.57 = (f32[96,1792]{1,0:T(8,128)S(1)}, bf16[96,1792]{1,0:T(8,128)(2,1)S(1)}) custom-call(bf16[96,896]{1,0:T(8,128)(2,1)S(1)} %collective-permute-done.5.own, bf16[96,896]{1,0:T(8,128)(2,1)S(1)} %collective-permute-done.6.other, bf16[96,896]{1,0:T(8,128)(2,1)S(1)} %collective-permute-done.7.own_core, ...), custom_call_target="tpu_custom_call" | custom-call | flops 836763648 | bytes 1376256 | tf_op jit(solution)/shard_map/pallas_call | solution.py:100
  38.3 2.6 %shard_map.58 = (f32[96,1792]{1,0:T(8,128)S(1)}, bf16[96,1792]{1,0:T(8,128)(2,1)S(1)}) custom-call(bf16[96,896]{1,0:T(8,128)(2,1)S(1)} %collective-permute-done.13.own, bf16[96,896]{1,0:T(8,128)(2,1)S(1)} %collective-permute-done.14.other, bf16[96,896]{1,0:T(8,128)(2,1)S(1)} %collective-permute-done.15.own_core, ...), custom_call_target="tpu_custom_call" | custom-call | flops 836763648 | bytes 1376256 | tf_op jit(solution)/shard_map/pallas_call | solution.py:100
  41.0 0.8 %collective-permute-done.25.scale = f32[1,96]{1,0:T(1,128)S(1)} collective-permute-done((f32[1,96]{1,0:T(1,128)S(1)}, f32[1,96]{1,0:T(1,128)S(1)}, u32[]{:S(2)}, u32[]{:S(2)}) %collective-permute-start.25) | collective-permute-done | bytes 416 | tf_op jit(solution)/shard_map/ppermute | solution.py:132
  41.8 2.6 %shard_map.59 = (f32[96,1792]{1,0:T(8,128)S(1)}, bf16[96,1792]{1,0:T(8,128)(2,1)S(1)}) custom-call(bf16[96,896]{1,0:T(8,128)(2,1)S(1)} %collective-permute-done.21.own, bf16[96,896]{1,0:T(8,128)(2,1)S(1)} %collective-permute-done.22.other, bf16[96,896]{1,0:T(8,128)(2,1)S(1)} %collective-permute-done.23.own_core, ...), custom_call_target="tpu_custom_call" | custom-call | flops 836763648 | bytes 1376256 | tf_op jit(solution)/shard_map/pallas_call | solution.py:100
  45.8 1.5 %collective-permute-start.11 = (bf16[96,896]{1,0:T(8,128)(2,1)S(1)}, bf16[96,896]{1,0:T(8,128)(2,1)S(1)}, u32[]{:S(2)}, u32[]{:S(2)}) collective-permute-start(bf16[96,896]{1,0:T(8,128)(2,1)S(1)} %slice.68), channel_id=1, source_target_pairs={{0,2},{1,3},{2,0},{3,1},{4,6},{5,7},{6,4},{7,5},{8,10},{9,11},{10,... | collective-permute-start | bytes 516104 | tf_op jit(solution)/shard_map/ppermute | solution.py:122
  48.2 1.5 %collective-permute-start.27 = (bf16[96,896]{1,0:T(8,128)(2,1)S(1)}, bf16[96,896]{1,0:T(8,128)(2,1)S(1)}, u32[]{:S(2)}, u32[]{:S(2)}) collective-permute-start(bf16[96,896]{1,0:T(8,128)(2,1)S(1)} %slice.66), channel_id=1, source_target_pairs={{0,2},{1,3},{2,0},{3,1},{4,6},{5,7},{6,4},{7,5},{8,10},{9,11},{10,... | collective-permute-start | bytes 516104 | tf_op jit(solution)/shard_map/ppermute | solution.py:122
  49.7 6.4 %collective-permute-done.11 = bf16[96,896]{1,0:T(8,128)(2,1)S(1)} collective-permute-done((bf16[96,896]{1,0:T(8,128)(2,1)S(1)}, bf16[96,896]{1,0:T(8,128)(2,1)S(1)}, u32[]{:S(2)}, u32[]{:S(2)}) %collective-permute-start.11) | collective-permute-done | bytes 172064 | tf_op jit(solution)/shard_map/ppermute | solution.py:122
  56.1 1.9 %collective-permute-start.12 = (bf16[96,896]{1,0:T(8,128)(2,1)S(1)}, bf16[96,896]{1,0:T(8,128)(2,1)S(1)}, u32[]{:S(2)}, u32[]{:S(2)}) collective-permute-start(bf16[96,896]{1,0:T(8,128)(2,1)S(1)} %fusion.2), channel_id=1, source_target_pairs={{0,12},{4,0},{8,4},{12,8},{1,13},{5,1},{9,5},{13,9},{2,14},{6,2},{... | collective-permute-start | bytes 516104 | tf_op jit(solution)/shard_map/ppermute | solution.py:132
  58.0 1.8 %collective-permute-done.19 = bf16[96,896]{1,0:T(8,128)(2,1)S(1)} collective-permute-done((bf16[96,896]{1,0:T(8,128)(2,1)S(1)}, bf16[96,896]{1,0:T(8,128)(2,1)S(1)}, u32[]{:S(2)}, u32[]{:S(2)}) %collective-permute-start.19) | collective-permute-done | bytes 172064 | tf_op jit(solution)/shard_map/ppermute | solution.py:122
  60.4 2.1 %collective-permute-done.27 = bf16[96,896]{1,0:T(8,128)(2,1)S(1)} collective-permute-done((bf16[96,896]{1,0:T(8,128)(2,1)S(1)}, bf16[96,896]{1,0:T(8,128)(2,1)S(1)}, u32[]{:S(2)}, u32[]{:S(2)}) %collective-permute-start.27) | collective-permute-done | bytes 172064 | tf_op jit(solution)/shard_map/ppermute | solution.py:122
  62.6 1.8 %collective-permute-start.28 = (bf16[96,896]{1,0:T(8,128)(2,1)S(1)}, bf16[96,896]{1,0:T(8,128)(2,1)S(1)}, u32[]{:S(2)}, u32[]{:S(2)}) collective-permute-start(bf16[96,896]{1,0:T(8,128)(2,1)S(1)} %fusion), channel_id=1, source_target_pairs={{0,4},{4,8},{8,12},{12,0},{1,5},{5,9},{9,13},{13,1},{2,6},{6,10},{... | collective-permute-start | bytes 516104 | tf_op jit(solution)/shard_map/ppermute | solution.py:132
  64.3 9.1 %collective-permute-done.20 = bf16[96,896]{1,0:T(8,128)(2,1)S(1)} collective-permute-done((bf16[96,896]{1,0:T(8,128)(2,1)S(1)}, bf16[96,896]{1,0:T(8,128)(2,1)S(1)}, u32[]{:S(2)}, u32[]{:S(2)}) %collective-permute-start.20) | collective-permute-done | bytes 172064 | tf_op jit(solution)/shard_map/ppermute | solution.py:132
  (61 shorter events, 9.8 us)
Async XLA Ops:
  0.0 20.8 %collective-permute-start.5 = (bf16[96,896]{1,0:T(8,128)(2,1)}, bf16[96,896]{1,0:T(8,128)(2,1)S(1)}, u32[]{:S(2)}, u32[]{:S(2)}) collective-permute-start(bf16[96,896]{1,0:T(8,128)(2,1)} %own.1), channel_id=1, source_target_pairs={{0,4},{4,8},{8,12},{12,0},{1,5},{5,9},{9,13},{13,1},{2,6},{6,10},{... | collective-permute-start | bytes 516104 | tf_op jit(solution)/shard_map/ppermute | solution.py:132
  3.0 18.4 %collective-permute-start = (bf16[96,896]{1,0:T(8,128)(2,1)}, bf16[96,896]{1,0:T(8,128)(2,1)S(1)}, u32[]{:S(2)}, u32[]{:S(2)}) collective-permute-start(bf16[96,896]{1,0:T(8,128)(2,1)} %own.1), channel_id=1, source_target_pairs={{0,2},{1,3},{2,0},{3,1},{4,6},{5,7},{6,4},{7,5},{8,10},{9,11},{10,... | collective-permute-start | bytes 516104 | tf_op jit(solution)/shard_map/ppermute | solution.py:122
  4.5 17.1 %collective-permute-start.13 = (bf16[96,896]{1,0:T(8,128)(2,1)}, bf16[96,896]{1,0:T(8,128)(2,1)S(1)}, u32[]{:S(2)}, u32[]{:S(2)}) collective-permute-start(bf16[96,896]{1,0:T(8,128)(2,1)} %own.1), channel_id=1, source_target_pairs={{0,8},{4,12},{8,0},{12,4},{1,9},{5,13},{9,1},{13,5},{2,10},{6,14},... | collective-permute-start | bytes 516104 | tf_op jit(solution)/shard_map/ppermute | solution.py:132
  7.1 14.9 %collective-permute-start.21 = (bf16[96,896]{1,0:T(8,128)(2,1)}, bf16[96,896]{1,0:T(8,128)(2,1)S(1)}, u32[]{:S(2)}, u32[]{:S(2)}) collective-permute-start(bf16[96,896]{1,0:T(8,128)(2,1)} %own.1), channel_id=1, source_target_pairs={{0,12},{4,0},{8,4},{12,8},{1,13},{5,1},{9,5},{13,9},{2,14},{6,2},{... | collective-permute-start | bytes 516104 | tf_op jit(solution)/shard_map/ppermute | solution.py:132
  20.8 7.2 %collective-permute-start.6 = (bf16[96,896]{1,0:T(8,128)(2,1)S(1)}, bf16[96,896]{1,0:T(8,128)(2,1)S(1)}, u32[]{:S(2)}, u32[]{:S(2)}) collective-permute-start(bf16[96,896]{1,0:T(8,128)(2,1)S(1)} %collective-permute-done.5.own), channel_id=1, source_target_pairs={{0,2},{1,3},{2,0},{3,1},{4,6},{5,7},{6,4},{7,5},{8,10},{9,11},{10,... | collective-permute-start | bytes 516104 | tf_op jit(solution)/shard_map/ppermute | solution.py:122
  21.5 7.2 %collective-permute-start.2 = (bf16[96,896]{1,0:T(8,128)(2,1)S(1)}, bf16[96,896]{1,0:T(8,128)(2,1)S(1)}, u32[]{:S(2)}, u32[]{:S(2)}) collective-permute-start(bf16[96,896]{1,0:T(8,128)(2,1)S(1)} %collective-permute-done.other), channel_id=1, source_target_pairs={{0,1},{1,0},{2,3},{3,2},{4,5},{5,4},{6,7},{7,6},{8,9},{9,8},{10,11... | collective-permute-start | bytes 516104 | tf_op jit(solution)/shard_map/ppermute | solution.py:122
  21.6 10.3 %collective-permute-start.7 = (bf16[96,896]{1,0:T(8,128)(2,1)S(1)}, bf16[96,896]{1,0:T(8,128)(2,1)S(1)}, u32[]{:S(2)}, u32[]{:S(2)}) collective-permute-start(bf16[96,896]{1,0:T(8,128)(2,1)S(1)} %collective-permute-done.5.own), channel_id=1, source_target_pairs={{0,1},{1,0},{2,3},{3,2},{4,5},{5,4},{6,7},{7,6},{8,9},{9,8},{10,11... | collective-permute-start | bytes 516104 | tf_op jit(solution)/shard_map/ppermute | solution.py:122
  22.0 10.0 %collective-permute-start.14 = (bf16[96,896]{1,0:T(8,128)(2,1)S(1)}, bf16[96,896]{1,0:T(8,128)(2,1)S(1)}, u32[]{:S(2)}, u32[]{:S(2)}) collective-permute-start(bf16[96,896]{1,0:T(8,128)(2,1)S(1)} %collective-permute-done.13.own), channel_id=1, source_target_pairs={{0,2},{1,3},{2,0},{3,1},{4,6},{5,7},{6,4},{7,5},{8,10},{9,11},{10,... | collective-permute-start | bytes 516104 | tf_op jit(solution)/shard_map/ppermute | solution.py:122
  23.5 7.8 %collective-permute-start.17 = (f32[1,96]{1,0:T(1,128)S(1)}, f32[1,96]{1,0:T(1,128)S(1)}, u32[]{:S(2)}, u32[]{:S(2)}) collective-permute-start(f32[1,96]{1,0:T(1,128)S(1)} %get-tuple-element.27), channel_id=1, source_target_pairs={{0,8},{4,12},{8,0},{12,4},{1,9},{5,13},{9,1},{13,5},{2,10},{6,14},... | collective-permute-start | bytes 1160 | tf_op jit(solution)/shard_map/ppermute | solution.py:132
  28.1 6.9 %collective-permute-start.22 = (bf16[96,896]{1,0:T(8,128)(2,1)S(1)}, bf16[96,896]{1,0:T(8,128)(2,1)S(1)}, u32[]{:S(2)}, u32[]{:S(2)}) collective-permute-start(bf16[96,896]{1,0:T(8,128)(2,1)S(1)} %collective-permute-done.21.own), channel_id=1, source_target_pairs={{0,2},{1,3},{2,0},{3,1},{4,6},{5,7},{6,4},{7,5},{8,10},{9,11},{10,... | collective-permute-start | bytes 516104 | tf_op jit(solution)/shard_map/ppermute | solution.py:122
  28.6 6.4 %collective-permute-start.8 = (bf16[96,896]{1,0:T(8,128)(2,1)S(1)}, bf16[96,896]{1,0:T(8,128)(2,1)S(1)}, u32[]{:S(2)}, u32[]{:S(2)}) collective-permute-start(bf16[96,896]{1,0:T(8,128)(2,1)S(1)} %collective-permute-done.6.other), channel_id=1, source_target_pairs={{0,1},{1,0},{2,3},{3,2},{4,5},{5,4},{6,7},{7,6},{8,9},{9,8},{10,11... | collective-permute-start | bytes 516104 | tf_op jit(solution)/shard_map/ppermute | solution.py:122
  31.3 13.7 %collective-permute-start.3 = (bf16[96,1792]{1,0:T(8,128)(2,1)S(1)}, bf16[96,1792]{1,0:T(8,128)(2,1)S(1)}, u32[]{:S(2)}, u32[]{:S(2)}) collective-permute-start(bf16[96,1792]{1,0:T(8,128)(2,1)S(1)} %get-tuple-element.23), channel_id=1, source_target_pairs={{0,1},{1,0},{2,3},{3,2},{4,5},{5,4},{6,7},{7,6},{8,9},{9,8},{10,11... | collective-permute-start | bytes 1032200 | tf_op jit(solution)/shard_map/ppermute | solution.py:122
  31.9 6.3 %collective-permute-start.15 = (bf16[96,896]{1,0:T(8,128)(2,1)S(1)}, bf16[96,896]{1,0:T(8,128)(2,1)S(1)}, u32[]{:S(2)}, u32[]{:S(2)}) collective-permute-start(bf16[96,896]{1,0:T(8,128)(2,1)S(1)} %collective-permute-done.13.own), channel_id=1, source_target_pairs={{0,1},{1,0},{2,3},{3,2},{4,5},{5,4},{6,7},{7,6},{8,9},{9,8},{10,11... | collective-permute-start | bytes 516104 | tf_op jit(solution)/shard_map/ppermute | solution.py:122
  32.0 6.3 %collective-permute-start.16 = (bf16[96,896]{1,0:T(8,128)(2,1)S(1)}, bf16[96,896]{1,0:T(8,128)(2,1)S(1)}, u32[]{:S(2)}, u32[]{:S(2)}) collective-permute-start(bf16[96,896]{1,0:T(8,128)(2,1)S(1)} %collective-permute-done.14.other), channel_id=1, source_target_pairs={{0,1},{1,0},{2,3},{3,2},{4,5},{5,4},{6,7},{7,6},{8,9},{9,8},{10,11... | collective-permute-start | bytes 516104 | tf_op jit(solution)/shard_map/ppermute | solution.py:122
  35.0 6.8 %collective-permute-start.23 = (bf16[96,896]{1,0:T(8,128)(2,1)S(1)}, bf16[96,896]{1,0:T(8,128)(2,1)S(1)}, u32[]{:S(2)}, u32[]{:S(2)}) collective-permute-start(bf16[96,896]{1,0:T(8,128)(2,1)S(1)} %collective-permute-done.21.own), channel_id=1, source_target_pairs={{0,1},{1,0},{2,3},{3,2},{4,5},{5,4},{6,7},{7,6},{8,9},{9,8},{10,11... | collective-permute-start | bytes 516104 | tf_op jit(solution)/shard_map/ppermute | solution.py:122
  35.0 6.8 %collective-permute-start.24 = (bf16[96,896]{1,0:T(8,128)(2,1)S(1)}, bf16[96,896]{1,0:T(8,128)(2,1)S(1)}, u32[]{:S(2)}, u32[]{:S(2)}) collective-permute-start(bf16[96,896]{1,0:T(8,128)(2,1)S(1)} %collective-permute-done.22.other), channel_id=1, source_target_pairs={{0,1},{1,0},{2,3},{3,2},{4,5},{5,4},{6,7},{7,6},{8,9},{9,8},{10,11... | collective-permute-start | bytes 516104 | tf_op jit(solution)/shard_map/ppermute | solution.py:122
  38.3 7.5 %collective-permute-start.10 = (bf16[96,1792]{1,0:T(8,128)(2,1)S(1)}, bf16[96,1792]{1,0:T(8,128)(2,1)S(1)}, u32[]{:S(2)}, u32[]{:S(2)}) collective-permute-start(bf16[96,1792]{1,0:T(8,128)(2,1)S(1)} %get-tuple-element.26), channel_id=1, source_target_pairs={{0,1},{1,0},{2,3},{3,2},{4,5},{5,4},{6,7},{7,6},{8,9},{9,8},{10,11... | collective-permute-start | bytes 1032200 | tf_op jit(solution)/shard_map/ppermute | solution.py:122
  45.1 19.2 %collective-permute-start.4 = (bf16[96,896]{1,0:T(8,128)(2,1)S(1)}, bf16[96,896]{1,0:T(8,128)(2,1)S(1)}, u32[]{:S(2)}, u32[]{:S(2)}) collective-permute-start(bf16[96,896]{1,0:T(8,128)(2,1)S(1)} %slice.69), channel_id=1, source_target_pairs={{0,2},{1,3},{2,0},{3,1},{4,6},{5,7},{6,4},{7,5},{8,10},{9,11},{10,... | collective-permute-start | bytes 516104 | tf_op jit(solution)/shard_map/ppermute | solution.py:122
  45.8 10.3 %collective-permute-start.11 = (bf16[96,896]{1,0:T(8,128)(2,1)S(1)}, bf16[96,896]{1,0:T(8,128)(2,1)S(1)}, u32[]{:S(2)}, u32[]{:S(2)}) collective-permute-start(bf16[96,896]{1,0:T(8,128)(2,1)S(1)} %slice.68), channel_id=1, source_target_pairs={{0,2},{1,3},{2,0},{3,1},{4,6},{5,7},{6,4},{7,5},{8,10},{9,11},{10,... | collective-permute-start | bytes 516104 | tf_op jit(solution)/shard_map/ppermute | solution.py:122
  47.5 12.3 %collective-permute-start.19 = (bf16[96,896]{1,0:T(8,128)(2,1)S(1)}, bf16[96,896]{1,0:T(8,128)(2,1)S(1)}, u32[]{:S(2)}, u32[]{:S(2)}) collective-permute-start(bf16[96,896]{1,0:T(8,128)(2,1)S(1)} %slice.67), channel_id=1, source_target_pairs={{0,2},{1,3},{2,0},{3,1},{4,6},{5,7},{6,4},{7,5},{8,10},{9,11},{10,... | collective-permute-start | bytes 516104 | tf_op jit(solution)/shard_map/ppermute | solution.py:122
  48.2 14.3 %collective-permute-start.27 = (bf16[96,896]{1,0:T(8,128)(2,1)S(1)}, bf16[96,896]{1,0:T(8,128)(2,1)S(1)}, u32[]{:S(2)}, u32[]{:S(2)}) collective-permute-start(bf16[96,896]{1,0:T(8,128)(2,1)S(1)} %slice.66), channel_id=1, source_target_pairs={{0,2},{1,3},{2,0},{3,1},{4,6},{5,7},{6,4},{7,5},{8,10},{9,11},{10,... | collective-permute-start | bytes 516104 | tf_op jit(solution)/shard_map/ppermute | solution.py:122
  56.1 8.2 %collective-permute-start.12 = (bf16[96,896]{1,0:T(8,128)(2,1)S(1)}, bf16[96,896]{1,0:T(8,128)(2,1)S(1)}, u32[]{:S(2)}, u32[]{:S(2)}) collective-permute-start(bf16[96,896]{1,0:T(8,128)(2,1)S(1)} %fusion.2), channel_id=1, source_target_pairs={{0,12},{4,0},{8,4},{12,8},{1,13},{5,1},{9,5},{13,9},{2,14},{6,2},{... | collective-permute-start | bytes 516104 | tf_op jit(solution)/shard_map/ppermute | solution.py:132
  59.8 13.6 %collective-permute-start.20 = (bf16[96,896]{1,0:T(8,128)(2,1)S(1)}, bf16[96,896]{1,0:T(8,128)(2,1)S(1)}, u32[]{:S(2)}, u32[]{:S(2)}) collective-permute-start(bf16[96,896]{1,0:T(8,128)(2,1)S(1)} %fusion.1), channel_id=1, source_target_pairs={{0,8},{4,12},{8,0},{12,4},{1,9},{5,13},{9,1},{13,5},{2,10},{6,14},... | collective-permute-start | bytes 516104 | tf_op jit(solution)/shard_map/ppermute | solution.py:132
  62.6 10.9 %collective-permute-start.28 = (bf16[96,896]{1,0:T(8,128)(2,1)S(1)}, bf16[96,896]{1,0:T(8,128)(2,1)S(1)}, u32[]{:S(2)}, u32[]{:S(2)}) collective-permute-start(bf16[96,896]{1,0:T(8,128)(2,1)S(1)} %fusion), channel_id=1, source_target_pairs={{0,4},{4,8},{8,12},{12,0},{1,5},{5,9},{9,13},{13,1},{2,6},{6,10},{... | collective-permute-start | bytes 516104 | tf_op jit(solution)/shard_map/ppermute | solution.py:132
  (10 other events, 33.3 us)

commit v4 on v3

--- a/solution.py
+++ b/solution.py
@@ -9,7 +9,7 @@
 
 
 MIB = 1 << 20
-HBM = pl.BlockSpec(memory_space=pl.ANY)
+HBM = pl.BlockSpec(memory_space=pltpu.HBM)
 VMEM = pl.BlockSpec(memory_space=pltpu.VMEM)
 
 
@@ -36,40 +36,65 @@
     )
 
 
-def prepare_kernel(capacity, experts_n, ids, codes, up, down, up_out, down_out, *rest):
-    scales, (up_sem, down_sem) = rest[:experts_n], rest[experts_n:]
-    up_copy = pltpu.make_async_copy(up, up_out, up_sem)
-    down_copy = pltpu.make_async_copy(down, down_out, down_sem)
-    up_copy.start()
-    down_copy.start()
+def prepare_kernel(capacity, experts_n, ids, codes, up, down, columns, up_out, down_out, sems):
+    copies = [
+        pltpu.make_async_copy(up, up_out, sems.at[0]),
+        pltpu.make_async_copy(down, down_out, sems.at[1]),
+    ]
+    for copy in copies:
+        copy.start()
     me = lax.axis_index("expert")
     weight = kept_weights(ids[...], codes[...], experts_n, capacity)
+    rows = weight.shape[1]
     index = lax.broadcasted_iota(jnp.int32, weight.shape, 0)
-    for step, scale in enumerate(scales):
+    diagonal = lax.broadcasted_iota(jnp.int32, (rows, rows), 0) == lax.broadcasted_iota(
+        jnp.int32, (rows, rows), 1
+    )
+    for step in range(experts_n):
         mine = index == lax.rem(me + step, experts_n)
-        scale[...] = jnp.sum(jnp.where(mine, weight, 0.0), axis=0, keepdims=True)
-    up_copy.wait()
-    down_copy.wait()
+        row = jnp.sum(jnp.where(mine, weight, 0.0), axis=0, keepdims=True)
+        column = jnp.sum(jnp.where(diagonal, row, 0.0), axis=1, keepdims=True)
+        columns[step] = jnp.broadcast_to(column, columns.shape[1:])
+    for copy in copies:
+        copy.wait()
+
+
+def local_call(kernel, out_shape, operands, others=(), in_specs=None, **kwargs):
+    count = len(operands)
+
+    def body_of(*refs):
+        kernel(*refs[:count], *refs[count + len(others) :])
+
+    return pl.pallas_call(
+        body_of,
+        out_shape=out_shape,
+        in_specs=list(in_specs or [VMEM] * count) + [pl.BlockSpec(memory_space=pl.ANY)] * len(others),
+        out_specs=jax.tree.map(lambda _: VMEM, out_shape),
+        **kwargs,
+    )(*operands, *others)
 
 
 def prepare(ids, codes, up_t, down, experts_n, capacity):
     rows = ids.shape[1]
-    return pl.pallas_call(
+    return local_call(
         functools.partial(prepare_kernel, capacity, experts_n),
-        out_shape=[pltpu.VMEM(up_t.shape, up_t.dtype), pltpu.VMEM(down.shape, down.dtype)]
-        + [jax.ShapeDtypeStruct((1, rows), jnp.float32)] * experts_n,
+        [
+            jax.ShapeDtypeStruct((experts_n, rows, 128), jnp.float32),
+            pltpu.VMEM(up_t.shape, up_t.dtype),
+            pltpu.VMEM(down.shape, down.dtype),
+        ],
+        (ids, codes, up_t, down),
         in_specs=[VMEM, VMEM, HBM, HBM],
-        out_specs=[VMEM] * (2 + experts_n),
-        scratch_shapes=[pltpu.SemaphoreType.DMA, pltpu.SemaphoreType.DMA],
-        compiler_params=pltpu.CompilerParams(vmem_limit_bytes=20 * MIB),
+        scratch_shapes=[pltpu.SemaphoreType.DMA((2,))],
+        compiler_params=pltpu.CompilerParams(vmem_limit_bytes=52 * MIB),
         cost_estimate=pl.CostEstimate(
-            flops=0, bytes_accessed=4 * up_t.size + 4 * down.size, transcendentals=0
+            flops=0, bytes_accessed=2 * up_t.size + 2 * down.size, transcendentals=0
         ),
-    )(ids, codes, up_t, down)
-
-
-def expert_kernel(own, other, own_core, other_core, scale, up_t, down, keep, send, features, out):
-    rows, width = own.shape
+    )
+
+
+def expert_kernel(own, other, own_core, other_core, up_t, down, keep, send, features, out):
+    width = own.shape[1]
     place = lax.axis_index("tensor")
 
     def columns(bits):
@@ -82,11 +107,7 @@
     lifted = lax.dot_general(
         features[...], up_t[...], (((1,), (1,)), ((), ())), preferred_element_type=jnp.float32
     )
-    diagonal = lax.broadcasted_iota(jnp.int32, (rows, rows), 0) == lax.broadcasted_iota(
-        jnp.int32, (rows, rows), 1
-    )
-    column = jnp.sum(jnp.where(diagonal, scale[...], 0.0), axis=1, keepdims=True)
-    hidden = (lifted / (1.0 + jnp.exp(-lifted)) * column).astype(jnp.bfloat16)
+    hidden = (lifted / (1.0 + jnp.exp(-lifted))).astype(jnp.bfloat16)
     out[...] = jnp.dot(hidden, down[...], preferred_element_type=jnp.float32)
     keep[:, :width] = out[:, columns(0)]
     keep[:, width:] = out[:, columns(2)]
@@ -94,28 +115,70 @@
     send[:, width:] = out[:, columns(3)].astype(jnp.bfloat16)
 
 
-def expert_block(own, other, own_core, other_core, scale, up_t, down):
-    rows, width = own.shape
-    hidden_n, model = up_t.shape
-    return pl.pallas_call(
+def expert_block(block, up_t, down, others):
+    rows, width = block[0].shape
+    model = up_t.shape[1]
+    return local_call(
         expert_kernel,
-        out_shape=[
+        [
             jax.ShapeDtypeStruct((rows, 2 * width), jnp.float32),
             jax.ShapeDtypeStruct((rows, 2 * width), jnp.bfloat16),
         ],
-        in_specs=[VMEM] * 7,
-        out_specs=[VMEM] * 2,
+        (*block, up_t, down),
+        others,
         scratch_shapes=[
             pltpu.VMEM((rows, model), jnp.bfloat16),
             pltpu.VMEM((rows, model), jnp.float32),
         ],
         compiler_params=pltpu.CompilerParams(vmem_limit_bytes=20 * MIB),
-        cost_estimate=pl.CostEstimate(
-            flops=4 * rows * model * hidden_n,
-            bytes_accessed=4 * rows * model,
-            transcendentals=rows * hidden_n,
-        ),
-    )(own, other, own_core, other_core, scale, up_t, down)
+        cost_estimate=pl.CostEstimate(flops=1, bytes_accessed=1, transcendentals=0),
+    )
+
+
+def core_sum_kernel(keep, got, own, send):
+    width = own.shape[1]
+    own[...] = keep[:, :width] + got[:, :width].astype(jnp.float32)
+    send[...] = (keep[:, width:] + got[:, width:].astype(jnp.float32)).astype(send.dtype)
+
+
+def core_sum(keep, got, others):
+    rows, width = keep.shape[0], keep.shape[1] // 2
+    return local_call(
+        core_sum_kernel,
+        [
+            jax.ShapeDtypeStruct((rows, width), jnp.float32),
+            jax.ShapeDtypeStruct((rows, width), jnp.bfloat16),
+        ],
+        (keep, got),
+        others,
+    )
+
+
+def chip_sum_kernel(own, got, part):
+    part[...] = (own[...] + got[...].astype(jnp.float32)).astype(part.dtype)
+
+
+def chip_sum(own, got, others):
+    return local_call(
+        chip_sum_kernel, jax.ShapeDtypeStruct(own.shape, jnp.bfloat16), (own, got), others
+    )
+
+
+def combine_kernel(columns, own, got, *rest):
+    parts, mixed = rest[:-1], rest[-1]
+    total = columns[0, :, 0:1] * (own[...] + got[...].astype(jnp.float32))
+    for step, part in enumerate(parts, 1):
+        total += columns[step, :, 0:1] * part[...].astype(jnp.float32)
+    mixed[...] = total.astype(mixed.dtype)
+
+
+def combine(columns, own, got, parts, others):
+    return local_call(
+        combine_kernel,
+        jax.ShapeDtypeStruct(own.shape, jnp.bfloat16),
+        (columns, own, got, *parts),
+        others,
+    )
 
 
 def swap(array, bit):
@@ -123,34 +186,51 @@
 
 
 def whole_blocks(tokens, expert_ids, weight_codes, up_local, down_local, capacity):
-    width = tokens.shape[1]
     experts_n = lax.axis_size("expert")
 
     def shift(array, by):
-        if by % experts_n == 0:
-            return array
         return lax.ppermute(
             array, "expert", [(i, (i + by) % experts_n) for i in range(experts_n)]
         )
 
-    blocks = [shift(tokens, step) for step in range(experts_n)]
-    up_t, down, *scales = prepare(
+    steps = list(range(1, experts_n))
+    steps = steps[:1] + steps[:0:-1]
+    blocks = {0: tokens} | {step: shift(tokens, step) for step in steps}
+    others = {step: swap(block, 2) for step, block in blocks.items()}
+    columns, up_t, down = prepare(
         expert_ids.T, weight_codes.T, up_local.T, down_local, experts_n, capacity
     )
-    scales = [shift(scale, step) for step, scale in enumerate(scales)]
-
-    mixed = None
-    for step, (block, scale) in enumerate(zip(blocks, scales)):
-        other = swap(block, 2)
-        keep, send = expert_block(
-            block, other, swap(block, 1), swap(other, 1), scale, up_t, down
-        )
-        keep = keep + swap(send, 1).astype(jnp.float32)
-        part = keep[:, :width] + swap(keep[:, width:].astype(jnp.bfloat16), 2).astype(jnp.float32)
-        if step:
-            part = shift(part.astype(jnp.bfloat16), -step).astype(jnp.float32)
-        mixed = part if mixed is None else mixed + part
-    return mixed.astype(jnp.bfloat16)
+
+    order = [0] + steps
+    kept, sums, parts = {}, {}, {}
+    last = [columns]
+
+    def expert(step, *waits):
+        block = blocks[step], others[step], swap(blocks[step], 1), swap(others[step], 1)
+        kept[step] = expert_block(block, up_t, down, last + list(waits))
+        last[:] = kept[step][:1]
+
+    def cores(step):
+        keep, send = kept[step]
+        own, away = core_sum(keep, swap(send, 1), last)
+        sums[step] = own, swap(away, 2)
+        last[:] = [own]
+
+    def chips(step):
+        part = chip_sum(*sums[step], last)
+        parts[step] = shift(part, -step)
+        last[:] = [part]
+
+    for place, step in enumerate(order):
+        expert(step, *[blocks[following] for following in order[place + 1 : place + 3]])
+        if place >= 2:
+            cores(order[place - 1])
+    if steps:
+        cores(order[-1])
+    cores(0)
+    for step in steps:
+        chips(step)
+    return combine(columns, *sums[0], [parts[step] for step in range(1, experts_n)], last)
 
 
 def slotted(tokens, expert_ids, weight_codes, up_local, down_local, capacity):

time: 74.4 us -> 90.4 us (1.22)
  Pallas kernels: 11.7 us -> 30.9 us
  waiting for transfers between devices: 31.5 us -> 18.7 us
  local copies, waits for them, and re-layouts: 5.91 us -> 13.9 us
  starting transfers between devices: 23.7 us -> 26.2 us
  other arithmetic: 1.16 us -> 0 us
    pallas_call x5 -> x13, Pallas kernels: 11.7 us -> 30.9 us  [local_call(): pl.pallas_call(body_of, out_shape=out_shape, in_specs=list(in_specs or [V...]
    ppermute x20, waiting for transfers between devices: 17 us -> 5.13 us  [swap(): return lax.ppermute(array, 'tensor', [(i, i ^ bit) for i in range(4)])]
    unnamed x10 -> x46, local copies, waits for them, and re-layouts: 5.83 us -> 13.9 us
    ppermute x20, starting transfers between devices: 11.2 us -> 12.7 us  [swap(): return lax.ppermute(array, 'tensor', [(i, i ^ bit) for i in range(4)])]
    ppermute x9 -> x6, waiting for transfers between devices: 14.6 us -> 13.6 us  [shift(): lax.ppermute(array, 'expert', [(i, (i + by) % experts_n) for i in range(e...]
    ppermute x9 -> x6, starting transfers between devices: 12.6 us -> 13.5 us  [shift(): lax.ppermute(array, 'expert', [(i, (i + by) % experts_n) for i in range(e...]
  transfers between devices with their start and end apart: 29 -> 26, of which waited for: 8 -> 4; matrix products, arithmetic and copies ran while one was open for 1% -> 0% of each run, Pallas kernels for 16% -> 32%
where the time goes in v4:
time: 90.4 us; the launch traced here: 89.9 us
  Pallas kernels  30.9 us (34%)
  starting transfers between devices  26.2 us (29%)
  waiting for transfers between devices  18.7 us (21%)
  local copies, waits for them, and re-layouts  13.9 us (15%)
    pallas_call x13, Pallas kernels, local_call(): pl.pallas_call(body_of, out_shape=out_shape, in_specs=list(in_specs or [V...  30.9 us
    unnamed x46, local copies, waits for them, and re-layouts  13.9 us
    ppermute x6, waiting for transfers between devices, shift(): lax.ppermute(array, 'expert', [(i, (i + by) % experts_n) for i in range(e...  13.6 us
    ppermute x6, starting transfers between devices, shift(): lax.ppermute(array, 'expert', [(i, (i + by) % experts_n) for i in range(e...  13.5 us
    ppermute x20, starting transfers between devices, swap(): return lax.ppermute(array, 'tensor', [(i, i ^ bit) for i in range(4)])  12.7 us
    ppermute x20, waiting for transfers between devices, swap(): return lax.ppermute(array, 'tensor', [(i, i ^ bit) for i in range(4)])  5.13 us
  transfers between devices with their start and end apart: 26, of which 4 were waited for; matrix products, arithmetic and copies ran while one was open for 0% of the time, Pallas kernels for 32%

profile of v4, /device:TPU:0, one launch (start us, length us, event | category | flops | bytes accessed | tf_op | source)
XLA Modules:
  0.0 89.9 jit_solution(16878121575926558736)
XLA Ops:
  0.0 3.0 %collective-permute-start.3 = (bf16[96,896]{1,0:T(8,128)(2,1)}, bf16[96,896]{1,0:T(8,128)(2,1)S(1)}, u32[]{:S(2)}, u32[]{:S(2)}) collective-permute-start(bf16[96,896]{1,0:T(8,128)(2,1)} %refs_0_.1), channel_id=1, source_target_pairs={{0,4},{4,8},{8,12},{12,0},{1,5},{5,9},{9,13},{13,1},{2,6},{6,10},{... | collective-permute-start | bytes 516104 | tf_op jit(solution)/shard_map/ppermute | solution.py:192
  4.5 2.2 %collective-permute-start.4 = (bf16[96,896]{1,0:T(8,128)(2,1)}, bf16[96,896]{1,0:T(8,128)(2,1)S(1)}, u32[]{:S(2)}, u32[]{:S(2)}) collective-permute-start(bf16[96,896]{1,0:T(8,128)(2,1)} %refs_0_.1), channel_id=1, source_target_pairs={{0,12},{4,0},{8,4},{12,8},{1,13},{5,1},{9,5},{13,9},{2,14},{6,2},{... | collective-permute-start | bytes 516104 | tf_op jit(solution)/shard_map/ppermute | solution.py:192
  6.8 3.7 %collective-permute-done.3.refs_7_.refs_0_ = bf16[96,896]{1,0:T(8,128)(2,1)S(1)} collective-permute-done((bf16[96,896]{1,0:T(8,128)(2,1)}, bf16[96,896]{1,0:T(8,128)(2,1)S(1)}, u32[]{:S(2)}, u32[]{:S(2)}) %collective-permute-start.3) | collective-permute-done | bytes 172064 | tf_op jit(solution)/shard_map/ppermute | solution.py:192
  10.5 1.8 %collective-permute-start.10 = (bf16[96,896]{1,0:T(8,128)(2,1)S(1)}, bf16[96,896]{1,0:T(8,128)(2,1)S(1)}, u32[]{:S(2)}, u32[]{:S(2)}) collective-permute-start(bf16[96,896]{1,0:T(8,128)(2,1)S(1)} %collective-permute-done.3.refs_7_.refs_0_), channel_id=1, source_target_pairs={{0,2},{1,3},{2,0},{3,1},{4,6},{5,7},{6,4},{7,5},{8,10},{9,11},{10,... | collective-permute-start | bytes 516104 | tf_op jit(solution)/shard_map/ppermute | solution.py:185
  12.8 3.3 %collective-permute-start.6 = (bf16[96,896]{1,0:T(8,128)(2,1)}, bf16[96,896]{1,0:T(8,128)(2,1)S(1)}, u32[]{:S(2)}, u32[]{:S(2)}) collective-permute-start(bf16[96,896]{1,0:T(8,128)(2,1)} %refs_0_.1), channel_id=1, source_target_pairs={{0,8},{4,12},{8,0},{12,4},{1,9},{5,13},{9,1},{13,5},{2,10},{6,14},... | collective-permute-start | bytes 516104 | tf_op jit(solution)/shard_map/ppermute | solution.py:192
  16.6 5.0 %shard_map.55 = (f32[4,96,128]{2,1,0:T(8,128)}, bf16[608,3584]{1,0:T(8,128)(2,1)S(1)}, bf16[608,3584]{1,0:T(8,128)(2,1)S(1)}) custom-call(s32[2,96]{1,0:T(2,128)} %bitcast.8, s32[2,96]{1,0:T(2,128)} %bitcast.9, bf16[608,3584]{1,0:T(8,128)(2,1)} %bitcast.6, bf16[608,3584]{1,0:T(8,128)(2,1)} %bitcast.7), custom_call_target="tpu_custom_call" | custom-call | bytes 8716288 | tf_op jit(solution)/shard_map/pallas_call | solution.py:68
  23.9 2.6 %shard_map.56 = (f32[96,1792]{1,0:T(8,128)S(1)}, bf16[96,1792]{1,0:T(8,128)(2,1)S(1)}) custom-call(bf16[96,896]{1,0:T(8,128)(2,1)S(1)} %copy-done.10, bf16[96,896]{1,0:T(8,128)(2,1)S(1)} %collective-permute-done.refs_1_, bf16[96,896]{1,0:T(8,128)(2,1)S(1)} %collective-permute-done.1.refs_2_, bf16[96,896]{1,0:T(8,128)(2,1)S(1)} %collective-permute-done.2.refs_3_, ...), custom_call_target="tpu_custom_call" | custom-call | flops 1 | bytes 1 | tf_op jit(solution)/shard_map/pallas_call | solution.py:68
  26.6 2.6 %shard_map.57 = (f32[96,1792]{1,0:T(8,128)S(1)}, bf16[96,1792]{1,0:T(8,128)(2,1)S(1)}) custom-call(bf16[96,896]{1,0:T(8,128)(2,1)S(1)} %collective-permute-done.3.refs_7_.refs_0_, bf16[96,896]{1,0:T(8,128)(2,1)S(1)} %collective-permute-done.10.refs_1_, bf16[96,896]{1,0:T(8,128)(2,1)S(1)} %collective-permute-done.11.refs_2_, ...), custom_call_target="tpu_custom_call" | custom-call | flops 1 | bytes 1 | tf_op jit(solution)/shard_map/pallas_call | solution.py:68
  31.0 5.1 %collective-permute-done.7.refs_1_ = bf16[96,896]{1,0:T(8,128)(2,1)S(1)} collective-permute-done((bf16[96,896]{1,0:T(8,128)(2,1)S(1)}, bf16[96,896]{1,0:T(8,128)(2,1)S(1)}, u32[]{:S(2)}, u32[]{:S(2)}) %collective-permute-start.7) | collective-permute-done | bytes 172064 | tf_op jit(solution)/shard_map/ppermute | solution.py:185
  36.1 2.6 %shard_map.58 = (f32[96,1792]{1,0:T(8,128)S(1)}, bf16[96,1792]{1,0:T(8,128)(2,1)S(1)}) custom-call(bf16[96,896]{1,0:T(8,128)(2,1)S(1)} %collective-permute-done.4.refs_8_.refs_7_.refs_0_, bf16[96,896]{1,0:T(8,128)(2,1)S(1)} %collective-permute-done.14.refs_1_, bf16[96,896]{1,0:T(8,128)(2,1)S(1)} %collective-permute-done.15.refs_2_, ...), custom_call_target="tpu_custom_call" | custom-call | flops 1 | bytes 1 | tf_op jit(solution)/shard_map/pallas_call | solution.py:68
  40.9 2.0 %shard_map.59 = (f32[96,896]{1,0:T(8,128)}, bf16[96,896]{1,0:T(8,128)(2,1)}) custom-call(f32[96,1792]{1,0:T(8,128)} %copy-done.7, bf16[96,1792]{1,0:T(8,128)(2,1)} %copy-done.11, f32[96,1792]{1,0:T(8,128)} %copy-done.4), custom_call_target="tpu_custom_call" | custom-call | tf_op jit(solution)/shard_map/pallas_call | solution.py:68
  42.9 2.2 %copy-done.1 = bf16[608,3584]{1,0:T(8,128)(2,1)S(1)} copy-done((bf16[608,3584]{1,0:T(8,128)(2,1)S(1)}, bf16[608,3584]{1,0:T(8,128)(2,1)}, u32[]{:S(2)}) %copy-start.1) | copy-done | bytes 4358168
  45.1 2.2 %copy-done.3 = bf16[608,3584]{1,0:T(8,128)(2,1)S(1)} copy-done((bf16[608,3584]{1,0:T(8,128)(2,1)S(1)}, bf16[608,3584]{1,0:T(8,128)(2,1)}, u32[]{:S(2)}) %copy-start.3) | copy-done | bytes 4358168
  48.3 2.6 %shard_map.60 = (f32[96,1792]{1,0:T(8,128)S(1)}, bf16[96,1792]{1,0:T(8,128)(2,1)S(1)}) custom-call(bf16[96,896]{1,0:T(8,128)(2,1)S(1)} %collective-permute-done.6.refs_8_.refs_7_.refs_0_, bf16[96,896]{1,0:T(8,128)(2,1)S(1)} %collective-permute-done.7.refs_1_, bf16[96,896]{1,0:T(8,128)(2,1)S(1)} %collective-permute-done.8.refs_2_, ...), custom_call_target="tpu_custom_call" | custom-call | flops 1 | bytes 1 | tf_op jit(solution)/shard_map/pallas_call | solution.py:68
  54.0 2.0 %shard_map.61 = (f32[96,896]{1,0:T(8,128)}, bf16[96,896]{1,0:T(8,128)(2,1)}) custom-call(f32[96,1792]{1,0:T(8,128)} %copy-done.4, bf16[96,1792]{1,0:T(8,128)(2,1)} %copy-done.12, f32[96,1792]{1,0:T(8,128)} %copy-done.5), custom_call_target="tpu_custom_call" | custom-call | tf_op jit(solution)/shard_map/pallas_call | solution.py:68
  57.8 2.1 %shard_map.62 = (f32[96,896]{1,0:T(8,128)}, bf16[96,896]{1,0:T(8,128)(2,1)}) custom-call(f32[96,1792]{1,0:T(8,128)} %copy-done.5, bf16[96,1792]{1,0:T(8,128)(2,1)} %copy-done.14, f32[96,896]{1,0:T(8,128)} %get-tuple-element.36.refs_2_.refs_0_), custom_call_target="tpu_custom_call" | custom-call | tf_op jit(solution)/shard_map/pallas_call | solution.py:68
  61.6 2.0 %shard_map.63 = (f32[96,896]{1,0:T(8,128)}, bf16[96,896]{1,0:T(8,128)(2,1)}) custom-call(f32[96,1792]{1,0:T(8,128)} %copy-done.6, bf16[96,1792]{1,0:T(8,128)(2,1)} %copy-done.13, f32[96,896]{1,0:T(8,128)} %get-tuple-element.37.refs_2_.refs_0_), custom_call_target="tpu_custom_call" | custom-call | tf_op jit(solution)/shard_map/pallas_call | solution.py:68
  64.3 1.7 %shard_map.64.refs_2_ = bf16[96,896]{1,0:T(8,128)(2,1)} custom-call(f32[96,896]{1,0:T(8,128)} %get-tuple-element.32.refs_6_.refs_0_, bf16[96,896]{1,0:T(8,128)(2,1)} %copy-done.21, f32[96,896]{1,0:T(8,128)} %get-tuple-element.38.refs_2_.refs_1_), custom_call_target="tpu_custom_call" | custom-call | tf_op jit(solution)/shard_map/pallas_call | solution.py:68
  66.0 3.9 %collective-permute-start.21 = (bf16[96,896]{1,0:T(8,128)(2,1)}, bf16[96,896]{1,0:T(8,128)(2,1)S(1)}, u32[]{:S(2)}, u32[]{:S(2)}) collective-permute-start(bf16[96,896]{1,0:T(8,128)(2,1)} %shard_map.64.refs_2_), channel_id=1, source_target_pairs={{0,12},{4,0},{8,4},{12,8},{1,13},{5,1},{9,5},{13,9},{2,14},{6,2},{... | collective-permute-start | bytes 516104 | tf_op jit(solution)/shard_map/ppermute | solution.py:192
  70.6 1.7 %shard_map.65.refs_2_ = bf16[96,896]{1,0:T(8,128)(2,1)} custom-call(f32[96,896]{1,0:T(8,128)} %get-tuple-element.36.refs_2_.refs_0_, bf16[96,896]{1,0:T(8,128)(2,1)} %copy-done.20, bf16[96,896]{1,0:T(8,128)(2,1)} %shard_map.64.refs_2_), custom_call_target="tpu_custom_call" | custom-call | tf_op jit(solution)/shard_map/pallas_call | solution.py:68
  74.4 1.7 %shard_map.66.refs_6_ = bf16[96,896]{1,0:T(8,128)(2,1)} custom-call(f32[96,896]{1,0:T(8,128)} %get-tuple-element.37.refs_2_.refs_0_, bf16[96,896]{1,0:T(8,128)(2,1)} %copy-done.19, bf16[96,896]{1,0:T(8,128)(2,1)} %shard_map.65.refs_2_), custom_call_target="tpu_custom_call" | custom-call | tf_op jit(solution)/shard_map/pallas_call | solution.py:68
  77.2 2.9 %collective-permute-done.25.refs_5_ = bf16[96,896]{1,0:T(8,128)(2,1)S(1)} collective-permute-done((bf16[96,896]{1,0:T(8,128)(2,1)}, bf16[96,896]{1,0:T(8,128)(2,1)S(1)}, u32[]{:S(2)}, u32[]{:S(2)}) %collective-permute-start.25) | collective-permute-done | bytes 172064 | tf_op jit(solution)/shard_map/ppermute | solution.py:192
  80.1 7.0 %collective-permute-done.24.refs_4_ = bf16[96,896]{1,0:T(8,128)(2,1)S(1)} collective-permute-done((bf16[96,896]{1,0:T(8,128)(2,1)}, bf16[96,896]{1,0:T(8,128)(2,1)S(1)}, u32[]{:S(2)}, u32[]{:S(2)}) %collective-permute-start.24) | collective-permute-done | bytes 172064 | tf_op jit(solution)/shard_map/ppermute | solution.py:192
  87.8 2.2 %shard_map.67 = bf16[96,896]{1,0:T(8,128)(2,1)} custom-call(f32[4,96,128]{2,1,0:T(8,128)} %get-tuple-element.24.refs_6_.refs_0_, f32[96,896]{1,0:T(8,128)} %get-tuple-element.38.refs_2_.refs_1_, bf16[96,896]{1,0:T(8,128)(2,1)} %copy-done.17, bf16[96,896]{1,0:T(8,128)(2,1)} %copy-done.15, bf16[96,896]{1,0:T(8,128)(2,1)} %copy-done.18, ...), custom_call_target="tpu_custom_call" | custom-call | tf_op jit(solution)/shard_map/pallas_call | solution.py:68
  (87 shorter events, 21.5 us)
Async XLA Ops:
  0.0 10.5 %collective-permute-start.3 = (bf16[96,896]{1,0:T(8,128)(2,1)}, bf16[96,896]{1,0:T(8,128)(2,1)S(1)}, u32[]{:S(2)}, u32[]{:S(2)}) collective-permute-start(bf16[96,896]{1,0:T(8,128)(2,1)} %refs_0_.1), channel_id=1, source_target_pairs={{0,4},{4,8},{8,12},{12,0},{1,5},{5,9},{9,13},{13,1},{2,6},{6,10},{... | collective-permute-start | bytes 516104 | tf_op jit(solution)/shard_map/ppermute | solution.py:192
  3.0 9.2 %collective-permute-start = (bf16[96,896]{1,0:T(8,128)(2,1)}, bf16[96,896]{1,0:T(8,128)(2,1)S(1)}, u32[]{:S(2)}, u32[]{:S(2)}) collective-permute-start(bf16[96,896]{1,0:T(8,128)(2,1)} %refs_0_.1), channel_id=1, source_target_pairs={{0,2},{1,3},{2,0},{3,1},{4,6},{5,7},{6,4},{7,5},{8,10},{9,11},{10,... | collective-permute-start | bytes 516104 | tf_op jit(solution)/shard_map/ppermute | solution.py:185
  4.5 11.5 %collective-permute-start.4 = (bf16[96,896]{1,0:T(8,128)(2,1)}, bf16[96,896]{1,0:T(8,128)(2,1)S(1)}, u32[]{:S(2)}, u32[]{:S(2)}) collective-permute-start(bf16[96,896]{1,0:T(8,128)(2,1)} %refs_0_.1), channel_id=1, source_target_pairs={{0,12},{4,0},{8,4},{12,8},{1,13},{5,1},{9,5},{13,9},{2,14},{6,2},{... | collective-permute-start | bytes 516104 | tf_op jit(solution)/shard_map/ppermute | solution.py:192
  10.5 5.6 %collective-permute-start.10 = (bf16[96,896]{1,0:T(8,128)(2,1)S(1)}, bf16[96,896]{1,0:T(8,128)(2,1)S(1)}, u32[]{:S(2)}, u32[]{:S(2)}) collective-permute-start(bf16[96,896]{1,0:T(8,128)(2,1)S(1)} %collective-permute-done.3.refs_7_.refs_0_), channel_id=1, source_target_pairs={{0,2},{1,3},{2,0},{3,1},{4,6},{5,7},{6,4},{7,5},{8,10},{9,11},{10,... | collective-permute-start | bytes 516104 | tf_op jit(solution)/shard_map/ppermute | solution.py:185
  12.2 9.4 %collective-permute-start.1 = (bf16[96,896]{1,0:T(8,128)(2,1)}, bf16[96,896]{1,0:T(8,128)(2,1)S(1)}, u32[]{:S(2)}, u32[]{:S(2)}) collective-permute-start(bf16[96,896]{1,0:T(8,128)(2,1)} %refs_0_.1), channel_id=1, source_target_pairs={{0,1},{1,0},{2,3},{3,2},{4,5},{5,4},{6,7},{7,6},{8,9},{9,8},{10,11... | collective-permute-start | bytes 516104 | tf_op jit(solution)/shard_map/ppermute | solution.py:185
  12.2 10.5 %collective-permute-start.2 = (bf16[96,896]{1,0:T(8,128)(2,1)S(1)}, bf16[96,896]{1,0:T(8,128)(2,1)S(1)}, u32[]{:S(2)}, u32[]{:S(2)}) collective-permute-start(bf16[96,896]{1,0:T(8,128)(2,1)S(1)} %collective-permute-done.refs_1_), channel_id=1, source_target_pairs={{0,1},{1,0},{2,3},{3,2},{4,5},{5,4},{6,7},{7,6},{8,9},{9,8},{10,11... | collective-permute-start | bytes 516104 | tf_op jit(solution)/shard_map/ppermute | solution.py:185
  12.8 13.8 %collective-permute-start.6 = (bf16[96,896]{1,0:T(8,128)(2,1)}, bf16[96,896]{1,0:T(8,128)(2,1)S(1)}, u32[]{:S(2)}, u32[]{:S(2)}) collective-permute-start(bf16[96,896]{1,0:T(8,128)(2,1)} %refs_0_.1), channel_id=1, source_target_pairs={{0,8},{4,12},{8,0},{12,4},{1,9},{5,13},{9,1},{13,5},{2,10},{6,14},... | collective-permute-start | bytes 516104 | tf_op jit(solution)/shard_map/ppermute | solution.py:192
  16.1 10.5 %collective-permute-start.11 = (bf16[96,896]{1,0:T(8,128)(2,1)S(1)}, bf16[96,896]{1,0:T(8,128)(2,1)S(1)}, u32[]{:S(2)}, u32[]{:S(2)}) collective-permute-start(bf16[96,896]{1,0:T(8,128)(2,1)S(1)} %collective-permute-done.3.refs_7_.refs_0_), channel_id=1, source_target_pairs={{0,1},{1,0},{2,3},{3,2},{4,5},{5,4},{6,7},{7,6},{8,9},{9,8},{10,11... | collective-permute-start | bytes 516104 | tf_op jit(solution)/shard_map/ppermute | solution.py:185
  16.1 10.5 %collective-permute-start.12 = (bf16[96,896]{1,0:T(8,128)(2,1)S(1)}, bf16[96,896]{1,0:T(8,128)(2,1)S(1)}, u32[]{:S(2)}, u32[]{:S(2)}) collective-permute-start(bf16[96,896]{1,0:T(8,128)(2,1)S(1)} %collective-permute-done.10.refs_1_), channel_id=1, source_target_pairs={{0,1},{1,0},{2,3},{3,2},{4,5},{5,4},{6,7},{7,6},{8,9},{9,8},{10,11... | collective-permute-start | bytes 516104 | tf_op jit(solution)/shard_map/ppermute | solution.py:185
  21.6 8.9 %collective-permute-start.14 = (bf16[96,896]{1,0:T(8,128)(2,1)S(1)}, bf16[96,896]{1,0:T(8,128)(2,1)S(1)}, u32[]{:S(2)}, u32[]{:S(2)}) collective-permute-start(bf16[96,896]{1,0:T(8,128)(2,1)S(1)} %collective-permute-done.4.refs_8_.refs_7_.refs_0_), channel_id=1, source_target_pairs={{0,2},{1,3},{2,0},{3,1},{4,6},{5,7},{6,4},{7,5},{8,10},{9,11},{10,... | collective-permute-start | bytes 516104 | tf_op jit(solution)/shard_map/ppermute | solution.py:185
  29.2 10.9 %collective-permute-start.13 = (bf16[96,1792]{1,0:T(8,128)(2,1)S(1)}, bf16[96,1792]{1,0:T(8,128)(2,1)S(1)}, u32[]{:S(2)}, u32[]{:S(2)}) collective-permute-start(bf16[96,1792]{1,0:T(8,128)(2,1)S(1)} %get-tuple-element.30), channel_id=1, source_target_pairs={{0,1},{1,0},{2,3},{3,2},{4,5},{5,4},{6,7},{7,6},{8,9},{9,8},{10,11... | collective-permute-start | bytes 1032200 | tf_op jit(solution)/shard_map/ppermute | solution.py:185
  29.5 6.6 %collective-permute-start.7 = (bf16[96,896]{1,0:T(8,128)(2,1)S(1)}, bf16[96,896]{1,0:T(8,128)(2,1)S(1)}, u32[]{:S(2)}, u32[]{:S(2)}) collective-permute-start(bf16[96,896]{1,0:T(8,128)(2,1)S(1)} %collective-permute-done.6.refs_8_.refs_7_.refs_0_), channel_id=1, source_target_pairs={{0,2},{1,3},{2,0},{3,1},{4,6},{5,7},{6,4},{7,5},{8,10},{9,11},{10,... | collective-permute-start | bytes 516104 | tf_op jit(solution)/shard_map/ppermute | solution.py:185
  30.3 5.8 %collective-permute-start.15 = (bf16[96,896]{1,0:T(8,128)(2,1)S(1)}, bf16[96,896]{1,0:T(8,128)(2,1)S(1)}, u32[]{:S(2)}, u32[]{:S(2)}) collective-permute-start(bf16[96,896]{1,0:T(8,128)(2,1)S(1)} %collective-permute-done.4.refs_8_.refs_7_.refs_0_), channel_id=1, source_target_pairs={{0,1},{1,0},{2,3},{3,2},{4,5},{5,4},{6,7},{7,6},{8,9},{9,8},{10,11... | collective-permute-start | bytes 516104 | tf_op jit(solution)/shard_map/ppermute | solution.py:185
  30.8 12.0 %collective-permute-start.8 = (bf16[96,896]{1,0:T(8,128)(2,1)S(1)}, bf16[96,896]{1,0:T(8,128)(2,1)S(1)}, u32[]{:S(2)}, u32[]{:S(2)}) collective-permute-start(bf16[96,896]{1,0:T(8,128)(2,1)S(1)} %collective-permute-done.6.refs_8_.refs_7_.refs_0_), channel_id=1, source_target_pairs={{0,1},{1,0},{2,3},{3,2},{4,5},{5,4},{6,7},{7,6},{8,9},{9,8},{10,11... | collective-permute-start | bytes 516104 | tf_op jit(solution)/shard_map/ppermute | solution.py:185
  36.1 6.8 %collective-permute-start.9 = (bf16[96,896]{1,0:T(8,128)(2,1)S(1)}, bf16[96,896]{1,0:T(8,128)(2,1)S(1)}, u32[]{:S(2)}, u32[]{:S(2)}) collective-permute-start(bf16[96,896]{1,0:T(8,128)(2,1)S(1)} %collective-permute-done.7.refs_1_), channel_id=1, source_target_pairs={{0,1},{1,0},{2,3},{3,2},{4,5},{5,4},{6,7},{7,6},{8,9},{9,8},{10,11... | collective-permute-start | bytes 516104 | tf_op jit(solution)/shard_map/ppermute | solution.py:185
  39.6 13.7 %collective-permute-start.18 = (bf16[96,1792]{1,0:T(8,128)(2,1)S(1)}, bf16[96,1792]{1,0:T(8,128)(2,1)S(1)}, u32[]{:S(2)}, u32[]{:S(2)}) collective-permute-start(bf16[96,1792]{1,0:T(8,128)(2,1)S(1)} %get-tuple-element.35), channel_id=1, source_target_pairs={{0,1},{1,0},{2,3},{3,2},{4,5},{5,4},{6,7},{7,6},{8,9},{9,8},{10,11... | collective-permute-start | bytes 1032200 | tf_op jit(solution)/shard_map/ppermute | solution.py:185
  51.8 9.0 %collective-permute-start.5 = (bf16[96,1792]{1,0:T(8,128)(2,1)S(1)}, bf16[96,1792]{1,0:T(8,128)(2,1)S(1)}, u32[]{:S(2)}, u32[]{:S(2)}) collective-permute-start(bf16[96,1792]{1,0:T(8,128)(2,1)S(1)} %get-tuple-element.28), channel_id=1, source_target_pairs={{0,1},{1,0},{2,3},{3,2},{4,5},{5,4},{6,7},{7,6},{8,9},{9,8},{10,11... | collective-permute-start | bytes 1032200 | tf_op jit(solution)/shard_map/ppermute | solution.py:185
  52.3 11.3 %collective-permute-start.20 = (bf16[96,896]{1,0:T(8,128)(2,1)S(1)}, bf16[96,896]{1,0:T(8,128)(2,1)S(1)}, u32[]{:S(2)}, u32[]{:S(2)}) collective-permute-start(bf16[96,896]{1,0:T(8,128)(2,1)S(1)} %copy-done.22), channel_id=1, source_target_pairs={{0,2},{1,3},{2,0},{3,1},{4,6},{5,7},{6,4},{7,5},{8,10},{9,11},{10,... | collective-permute-start | bytes 516104 | tf_op jit(solution)/shard_map/ppermute | solution.py:185
  56.0 13.9 %collective-permute-start.23 = (bf16[96,896]{1,0:T(8,128)(2,1)}, bf16[96,896]{1,0:T(8,128)(2,1)S(1)}, u32[]{:S(2)}, u32[]{:S(2)}) collective-permute-start(bf16[96,896]{1,0:T(8,128)(2,1)} %get-tuple-element.42), channel_id=1, source_target_pairs={{0,2},{1,3},{2,0},{3,1},{4,6},{5,7},{6,4},{7,5},{8,10},{9,11},{10,... | collective-permute-start | bytes 516104 | tf_op jit(solution)/shard_map/ppermute | solution.py:185
  59.9 13.9 %collective-permute-start.22 = (bf16[96,896]{1,0:T(8,128)(2,1)}, bf16[96,896]{1,0:T(8,128)(2,1)S(1)}, u32[]{:S(2)}, u32[]{:S(2)}) collective-permute-start(bf16[96,896]{1,0:T(8,128)(2,1)} %get-tuple-element.41), channel_id=1, source_target_pairs={{0,2},{1,3},{2,0},{3,1},{4,6},{5,7},{6,4},{7,5},{8,10},{9,11},{10,... | collective-permute-start | bytes 516104 | tf_op jit(solution)/shard_map/ppermute | solution.py:185
  66.0 14.1 %collective-permute-start.21 = (bf16[96,896]{1,0:T(8,128)(2,1)}, bf16[96,896]{1,0:T(8,128)(2,1)S(1)}, u32[]{:S(2)}, u32[]{:S(2)}) collective-permute-start(bf16[96,896]{1,0:T(8,128)(2,1)} %shard_map.64.refs_2_), channel_id=1, source_target_pairs={{0,12},{4,0},{8,4},{12,8},{1,13},{5,1},{9,5},{13,9},{2,14},{6,2},{... | collective-permute-start | bytes 516104 | tf_op jit(solution)/shard_map/ppermute | solution.py:192
  72.3 7.8 %collective-permute-start.25 = (bf16[96,896]{1,0:T(8,128)(2,1)}, bf16[96,896]{1,0:T(8,128)(2,1)S(1)}, u32[]{:S(2)}, u32[]{:S(2)}) collective-permute-start(bf16[96,896]{1,0:T(8,128)(2,1)} %shard_map.65.refs_2_), channel_id=1, source_target_pairs={{0,4},{4,8},{8,12},{12,0},{1,5},{5,9},{9,13},{13,1},{2,6},{6,10},{... | collective-permute-start | bytes 516104 | tf_op jit(solution)/shard_map/ppermute | solution.py:192
  72.3 7.8 %collective-permute-start.19 = (bf16[96,896]{1,0:T(8,128)(2,1)}, bf16[96,896]{1,0:T(8,128)(2,1)S(1)}, u32[]{:S(2)}, u32[]{:S(2)}) collective-permute-start(bf16[96,896]{1,0:T(8,128)(2,1)} %get-tuple-element.39), channel_id=1, source_target_pairs={{0,2},{1,3},{2,0},{3,1},{4,6},{5,7},{6,4},{7,5},{8,10},{9,11},{10,... | collective-permute-start | bytes 516104 | tf_op jit(solution)/shard_map/ppermute | solution.py:185
  76.2 10.9 %collective-permute-start.24 = (bf16[96,896]{1,0:T(8,128)(2,1)}, bf16[96,896]{1,0:T(8,128)(2,1)S(1)}, u32[]{:S(2)}, u32[]{:S(2)}) collective-permute-start(bf16[96,896]{1,0:T(8,128)(2,1)} %shard_map.66.refs_6_), channel_id=1, source_target_pairs={{0,8},{4,12},{8,0},{12,4},{1,9},{5,13},{9,1},{13,5},{2,10},{6,14},... | collective-permute-start | bytes 516104 | tf_op jit(solution)/shard_map/ppermute | solution.py:192
  (25 other events, 97.3 us)

commit v5 on v4

--- a/solution.py
+++ b/solution.py
@@ -59,51 +59,85 @@
         copy.wait()
 
 
-def local_call(kernel, out_shape, operands, others=(), in_specs=None, **kwargs):
+def local_call(kernel, out_shape, operands, others=(), in_specs=None, limit=4 * MIB, **kwargs):
     count = len(operands)
+
+    name = getattr(kernel, "func", kernel).__name__
 
     def body_of(*refs):
         kernel(*refs[:count], *refs[count + len(others) :])
 
     return pl.pallas_call(
         body_of,
+        name=name,
         out_shape=out_shape,
         in_specs=list(in_specs or [VMEM] * count) + [pl.BlockSpec(memory_space=pl.ANY)] * len(others),
         out_specs=jax.tree.map(lambda _: VMEM, out_shape),
+        compiler_params=pltpu.CompilerParams(vmem_limit_bytes=limit),
         **kwargs,
     )(*operands, *others)
 
 
+def after(array, other):
+    anywhere = pl.BlockSpec(memory_space=pl.ANY)
+    return pl.pallas_call(
+        lambda *refs: None,
+        out_shape=jax.ShapeDtypeStruct(array.shape, array.dtype),
+        in_specs=[anywhere, anywhere],
+        out_specs=anywhere,
+        input_output_aliases={0: 0},
+        compiler_params=pltpu.CompilerParams(vmem_limit_bytes=MIB),
+    )(array, other)
+
+
 def prepare(ids, codes, up_t, down, experts_n, capacity):
     rows = ids.shape[1]
     return local_call(
         functools.partial(prepare_kernel, capacity, experts_n),
         [
-            jax.ShapeDtypeStruct((experts_n, rows, 128), jnp.float32),
+            pltpu.VMEM((experts_n, rows, 128), jnp.float32),
             pltpu.VMEM(up_t.shape, up_t.dtype),
             pltpu.VMEM(down.shape, down.dtype),
         ],
         (ids, codes, up_t, down),
         in_specs=[VMEM, VMEM, HBM, HBM],
         scratch_shapes=[pltpu.SemaphoreType.DMA((2,))],
-        compiler_params=pltpu.CompilerParams(vmem_limit_bytes=52 * MIB),
+        limit=50 * MIB,
         cost_estimate=pl.CostEstimate(
-            flops=0, bytes_accessed=2 * up_t.size + 2 * down.size, transcendentals=0
+            flops=0, bytes_accessed=4 * up_t.size, transcendentals=0
         ),
     )
 
 
-def expert_kernel(own, other, own_core, other_core, up_t, down, keep, send, features, out):
-    width = own.shape[1]
+def pack_kernel(*refs):
+    packed = refs[-1]
+    rows, width = refs[0].shape
+    for index, ref in enumerate(refs[:-1]):
+        at, column = index // 2 * rows, index % 2 * width
+        packed[at : at + rows, column : column + width] = ref[...]
+
+
+def pack(pairs, others):
+    rows, width = pairs[0][0].shape
+    return local_call(
+        pack_kernel,
+        jax.ShapeDtypeStruct((len(pairs) * rows, 2 * width), pairs[0][0].dtype),
+        [array for pair in pairs for array in pair],
+        others,
+    )
+
+
+def expert_kernel(chip, core, up_t, down, keep, send, features, out):
+    width = chip.shape[1] // 2
     place = lax.axis_index("tensor")
 
     def columns(bits):
         return pl.ds(pl.multiple_of((place ^ bits) * width, width), width)
 
-    features[:, columns(0)] = own[...]
-    features[:, columns(2)] = other[...]
-    features[:, columns(1)] = own_core[...]
-    features[:, columns(3)] = other_core[...]
+    features[:, columns(0)] = chip[:, :width]
+    features[:, columns(2)] = chip[:, width:]
+    features[:, columns(1)] = core[:, :width]
+    features[:, columns(3)] = core[:, width:]
     lifted = lax.dot_general(
         features[...], up_t[...], (((1,), (1,)), ((), ())), preferred_element_type=jnp.float32
     )
@@ -115,52 +149,57 @@
     send[:, width:] = out[:, columns(3)].astype(jnp.bfloat16)
 
 
-def expert_block(block, up_t, down, others):
-    rows, width = block[0].shape
-    model = up_t.shape[1]
+def expert_rows(chip, core, up_t, down, others):
+    rows, model = chip.shape[0], up_t.shape[1]
     return local_call(
         expert_kernel,
         [
-            jax.ShapeDtypeStruct((rows, 2 * width), jnp.float32),
-            jax.ShapeDtypeStruct((rows, 2 * width), jnp.bfloat16),
+            jax.ShapeDtypeStruct(chip.shape, jnp.float32),
+            jax.ShapeDtypeStruct(chip.shape, jnp.bfloat16),
         ],
-        (*block, up_t, down),
-        others,
+        (chip, core, up_t, down),
+        others,
+        limit=10 * MIB,
         scratch_shapes=[
             pltpu.VMEM((rows, model), jnp.bfloat16),
             pltpu.VMEM((rows, model), jnp.float32),
         ],
-        compiler_params=pltpu.CompilerParams(vmem_limit_bytes=20 * MIB),
-        cost_estimate=pl.CostEstimate(flops=1, bytes_accessed=1, transcendentals=0),
-    )
-
-
-def core_sum_kernel(keep, got, own, send):
+        cost_estimate=pl.CostEstimate(
+            flops=8 * chip.size * up_t.shape[0], bytes_accessed=0, transcendentals=0
+        ),
+    )
+
+
+def core_sum_kernel(keep, got, own, *sends):
     width = own.shape[1]
     own[...] = keep[:, :width] + got[:, :width].astype(jnp.float32)
-    send[...] = (keep[:, width:] + got[:, width:].astype(jnp.float32)).astype(send.dtype)
-
-
-def core_sum(keep, got, others):
+    for index, send in enumerate(sends):
+        rows = slice(index * send.shape[0], (index + 1) * send.shape[0])
+        send[...] = (keep[rows, width:] + got[rows, width:].astype(jnp.float32)).astype(send.dtype)
+
+
+def core_sum(keep, got, count, others):
     rows, width = keep.shape[0], keep.shape[1] // 2
     return local_call(
         core_sum_kernel,
-        [
-            jax.ShapeDtypeStruct((rows, width), jnp.float32),
-            jax.ShapeDtypeStruct((rows, width), jnp.bfloat16),
-        ],
+        [jax.ShapeDtypeStruct((rows, width), jnp.float32)]
+        + [jax.ShapeDtypeStruct((rows // count, width), jnp.bfloat16)] * count,
         (keep, got),
         others,
     )
 
 
-def chip_sum_kernel(own, got, part):
-    part[...] = (own[...] + got[...].astype(jnp.float32)).astype(part.dtype)
-
-
-def chip_sum(own, got, others):
-    return local_call(
-        chip_sum_kernel, jax.ShapeDtypeStruct(own.shape, jnp.bfloat16), (own, got), others
+def chip_sum_kernel(index, own, got, part):
+    rows = slice(index * got.shape[0], (index + 1) * got.shape[0])
+    part[...] = (own[rows, :] + got[...].astype(jnp.float32)).astype(part.dtype)
+
+
+def chip_sum(own, got, index, others):
+    return local_call(
+        functools.partial(chip_sum_kernel, index),
+        jax.ShapeDtypeStruct(got.shape, jnp.bfloat16),
+        (own, got),
+        others,
     )
 
 
@@ -193,44 +232,26 @@
             array, "expert", [(i, (i + by) % experts_n) for i in range(experts_n)]
         )
 
-    steps = list(range(1, experts_n))
-    steps = steps[:1] + steps[:0:-1]
-    blocks = {0: tokens} | {step: shift(tokens, step) for step in steps}
-    others = {step: swap(block, 2) for step, block in blocks.items()}
+    steps = (3, 2, 1)
+    order = [step for step in steps if step < experts_n] + [0]
+    blocks = {0: tokens} | {step: shift(tokens, step) for step in order[:-1]}
     columns, up_t, down = prepare(
         expert_ids.T, weight_codes.T, up_local.T, down_local, experts_n, capacity
     )
-
-    order = [0] + steps
-    kept, sums, parts = {}, {}, {}
-    last = [columns]
-
-    def expert(step, *waits):
-        block = blocks[step], others[step], swap(blocks[step], 1), swap(others[step], 1)
-        kept[step] = expert_block(block, up_t, down, last + list(waits))
-        last[:] = kept[step][:1]
-
-    def cores(step):
-        keep, send = kept[step]
-        own, away = core_sum(keep, swap(send, 1), last)
+    blocks[order[0]] = after(blocks[order[0]], columns)
+    others = {step: swap(block, 2) for step, block in blocks.items()}
+
+    chips, sums, parts = {}, {}, {}
+    for step in order:
+        waits = [] if chips else [others[0]]
+        chips[step] = pack([(blocks[step], others[step])], waits)
+    for step in order:
+        keep, send = expert_rows(chips[step], swap(chips[step], 1), up_t, down, ())
+        own, away = core_sum(keep, swap(send, 1), 1, ())
         sums[step] = own, swap(away, 2)
-        last[:] = [own]
-
-    def chips(step):
-        part = chip_sum(*sums[step], last)
-        parts[step] = shift(part, -step)
-        last[:] = [part]
-
-    for place, step in enumerate(order):
-        expert(step, *[blocks[following] for following in order[place + 1 : place + 3]])
-        if place >= 2:
-            cores(order[place - 1])
-    if steps:
-        cores(order[-1])
-    cores(0)
-    for step in steps:
-        chips(step)
-    return combine(columns, *sums[0], [parts[step] for step in range(1, experts_n)], last)
+    for step in order[:-1]:
+        parts[step] = shift(chip_sum(*sums[step], 0, ()), -step)
+    return combine(columns, *sums[0], [parts[step] for step in range(1, experts_n)], ())
 
 
 def slotted(tokens, expert_ids, weight_codes, up_local, down_local, capacity):

time: 90.4 us -> 66.1 us (0.73)
  Pallas kernels: 30.9 us -> 16.1 us
  waiting for transfers between devices: 18.7 us -> 32.9 us
  local copies, waits for them, and re-layouts: 13.9 us -> 0.01 us
  starting transfers between devices: 26.2 us -> 16.7 us
    ppermute x20 -> x16, waiting for transfers between devices: 5.13 us -> 20 us  [swap(): return lax.ppermute(array, 'tensor', [(i, i ^ bit) for i in range(4)])]
    pallas_call x13 -> x18, Pallas kernels: 30.9 us -> 16.1 us  [the longest x17 16.1 us: local_call(): pl.pallas_call(body_of, name=name, out_shape=out_shape, in_specs=list(in_...]
    unnamed x46 -> x2, local copies, waits for them, and re-layouts: 13.9 us -> 0.01 us
    ppermute x6, starting transfers between devices: 13.5 us -> 6.25 us  [shift(): lax.ppermute(array, 'expert', [(i, (i + by) % experts_n) for i in range(e...]
    ppermute x20 -> x16, starting transfers between devices: 12.7 us -> 10.5 us  [swap(): return lax.ppermute(array, 'tensor', [(i, i ^ bit) for i in range(4)])]
  transfers between devices with their start and end apart: 26 -> 22, of which waited for: 4 -> 9; matrix products, arithmetic and copies ran while one was open for 0% -> 0% of each run, Pallas kernels for 32% -> 23%
where the time goes in v5:
time: 66.1 us; the launch traced here: 65.9 us
  waiting for transfers between devices  32.9 us (50%)
  starting transfers between devices  16.7 us (25%)
  Pallas kernels  16.1 us (24%)
    ppermute x16, waiting for transfers between devices, swap(): return lax.ppermute(array, 'tensor', [(i, i ^ bit) for i in range(4)])  20 us
    pallas_call x17, Pallas kernels, local_call(): pl.pallas_call(body_of, name=name, out_shape=out_shape, in_specs=list(in_...  16.1 us
    ppermute x6, waiting for transfers between devices, shift(): lax.ppermute(array, 'expert', [(i, (i + by) % experts_n) for i in range(e...  12.8 us
    ppermute x16, starting transfers between devices, swap(): return lax.ppermute(array, 'tensor', [(i, i ^ bit) for i in range(4)])  10.5 us
    ppermute x6, starting transfers between devices, shift(): lax.ppermute(array, 'expert', [(i, (i + by) % experts_n) for i in range(e...  6.25 us
  transfers between devices with their start and end apart: 22, of which 9 were waited for; matrix products, arithmetic and copies ran while one was open for 0% of the time, Pallas kernels for 23%

profile of v5, /device:TPU:0, one launch (start us, length us, event | category | flops | bytes accessed | tf_op | source)
XLA Modules:
  0.0 65.9 jit_solution(10945238885695641394)
XLA Ops:
  0.0 5.0 %collective-permute-start.16 = (bf16[96,896]{1,0:T(8,128)(2,1)}, bf16[96,896]{1,0:T(8,128)(2,1)S(1)}, u32[]{:S(2)}, u32[]{:S(2)}) collective-permute-start(bf16[96,896]{1,0:T(8,128)(2,1)} %refs_0_.1), channel_id=1, source_target_pairs={{0,12},{4,0},{8,4},{12,8},{1,13},{5,1},{9,5},{13,9},{2,14},{6,2},{... | collective-permute-start | bytes 516104 | tf_op jit(solution)/shard_map/ppermute | solution.py:231
  5.1 1.0 %collective-permute-start.4 = (bf16[96,896]{1,0:T(8,128)(2,1)}, bf16[96,896]{1,0:T(8,128)(2,1)S(1)}, u32[]{:S(2)}, u32[]{:S(2)}) collective-permute-start(bf16[96,896]{1,0:T(8,128)(2,1)} %refs_0_.1), channel_id=1, source_target_pairs={{0,4},{4,8},{8,12},{12,0},{1,5},{5,9},{9,13},{13,1},{2,6},{6,10},{... | collective-permute-start | bytes 516104 | tf_op jit(solution)/shard_map/ppermute | solution.py:231
  6.1 1.5 %collective-permute-start = (bf16[96,896]{1,0:T(8,128)(2,1)}, bf16[96,896]{1,0:T(8,128)(2,1)S(1)}, u32[]{:S(2)}, u32[]{:S(2)}) collective-permute-start(bf16[96,896]{1,0:T(8,128)(2,1)} %refs_0_.1), channel_id=1, source_target_pairs={{0,2},{1,3},{2,0},{3,1},{4,6},{5,7},{6,4},{7,5},{8,10},{9,11},{10,... | collective-permute-start | bytes 516104 | tf_op jit(solution)/shard_map/ppermute | solution.py:224
  7.6 4.3 %prepare_kernel.1 = (f32[4,96,128]{2,1,0:T(8,128)S(1)}, bf16[608,3584]{1,0:T(8,128)(2,1)S(1)}, bf16[608,3584]{1,0:T(8,128)(2,1)S(1)}) custom-call(s32[2,96]{1,0:T(2,128)} %bitcast.8, s32[2,96]{1,0:T(2,128)} %bitcast.9, bf16[608,3584]{1,0:T(8,128)(2,1)} %bitcast.6, bf16[608,3584]{1,0:T(8,128)(2,1)} %bitcast.7), custom_call_target="tpu_custom_call" | custom-call | bytes 8716288 | tf_op jit(solution)/shard_map/prepare_kernel/pallas_call | solution.py:70
  11.9 0.6 collective-permute-start.17
  12.5 7.3 %collective-permute-done.10.refs_0_ = bf16[96,896]{1,0:T(8,128)(2,1)S(1)} collective-permute-done((bf16[96,896]{1,0:T(8,128)(2,1)}, bf16[96,896]{1,0:T(8,128)(2,1)S(1)}, u32[]{:S(2)}, u32[]{:S(2)}) %collective-permute-start.10) | collective-permute-done | bytes 172064 | tf_op jit(solution)/shard_map/ppermute | solution.py:231
  19.8 1.5 %collective-permute-start.11 = (bf16[96,896]{1,0:T(8,128)(2,1)S(1)}, bf16[96,896]{1,0:T(8,128)(2,1)S(1)}, u32[]{:S(2)}, u32[]{:S(2)}) collective-permute-start(bf16[96,896]{1,0:T(8,128)(2,1)S(1)} %collective-permute-done.10.refs_0_), channel_id=1, source_target_pairs={{0,2},{1,3},{2,0},{3,1},{4,6},{5,7},{6,4},{7,5},{8,10},{9,11},{10,... | collective-permute-start | bytes 516104 | tf_op jit(solution)/shard_map/ppermute | solution.py:224
  22.0 5.1 %collective-permute-done.11.refs_1_ = bf16[96,896]{1,0:T(8,128)(2,1)S(1)} collective-permute-done((bf16[96,896]{1,0:T(8,128)(2,1)S(1)}, bf16[96,896]{1,0:T(8,128)(2,1)S(1)}, u32[]{:S(2)}, u32[]{:S(2)}) %collective-permute-start.11) | collective-permute-done | bytes 172064 | tf_op jit(solution)/shard_map/ppermute | solution.py:224
  27.2 2.3 %collective-permute-done.5.refs_1_ = bf16[96,896]{1,0:T(8,128)(2,1)S(1)} collective-permute-done((bf16[96,896]{1,0:T(8,128)(2,1)S(1)}, bf16[96,896]{1,0:T(8,128)(2,1)S(1)}, u32[]{:S(2)}, u32[]{:S(2)}) %collective-permute-start.5) | collective-permute-done | bytes 172064 | tf_op jit(solution)/shard_map/ppermute | solution.py:224
  29.7 0.5 collective-permute-start.1
  30.2 2.6 %expert_kernel.7 = (f32[96,1792]{1,0:T(8,128)S(1)}, bf16[96,1792]{1,0:T(8,128)(2,1)S(1)}) custom-call(bf16[96,1792]{1,0:T(8,128)(2,1)S(1)} %pack_kernel.7.refs_0_, bf16[96,1792]{1,0:T(8,128)(2,1)S(1)} %collective-permute-done.18.refs_1_, bf16[608,3584]{1,0:T(8,128)(2,1)S(1)} %get-tuple-element.25.refs_2_, bf16[608,3584]{1,0:T(8,128)(2,1)S(1)} %get-tuple-element.26.refs_3_), custom_call_target="tpu_custom_call" | custom-call | flops 836763648 | tf_op jit(solution)/shard_map/expert_kernel/pallas_call | solution.py:70
  32.9 2.6 %expert_kernel.6 = (f32[96,1792]{1,0:T(8,128)S(1)}, bf16[96,1792]{1,0:T(8,128)(2,1)S(1)}) custom-call(bf16[96,1792]{1,0:T(8,128)(2,1)S(1)} %pack_kernel.6.refs_0_, bf16[96,1792]{1,0:T(8,128)(2,1)S(1)} %collective-permute-done.12.refs_1_, bf16[608,3584]{1,0:T(8,128)(2,1)S(1)} %get-tuple-element.25.refs_2_, bf16[608,3584]{1,0:T(8,128)(2,1)S(1)} %get-tuple-element.26.refs_3_), custom_call_target="tpu_custom_call" | custom-call | flops 836763648 | tf_op jit(solution)/shard_map/expert_kernel/pallas_call | solution.py:70
  35.6 0.5 collective-permute-start.13
  36.1 2.6 %expert_kernel.5 = (f32[96,1792]{1,0:T(8,128)S(1)}, bf16[96,1792]{1,0:T(8,128)(2,1)S(1)}) custom-call(bf16[96,1792]{1,0:T(8,128)(2,1)S(1)} %pack_kernel.5.refs_0_, bf16[96,1792]{1,0:T(8,128)(2,1)S(1)} %collective-permute-done.6.refs_1_, bf16[608,3584]{1,0:T(8,128)(2,1)S(1)} %get-tuple-element.25.refs_2_, bf16[608,3584]{1,0:T(8,128)(2,1)S(1)} %get-tuple-element.26.refs_3_), custom_call_target="tpu_custom_call" | custom-call | flops 836763648 | tf_op jit(solution)/shard_map/expert_kernel/pallas_call | solution.py:70
  38.8 2.6 %expert_kernel.4 = (f32[96,1792]{1,0:T(8,128)S(1)}, bf16[96,1792]{1,0:T(8,128)(2,1)S(1)}) custom-call(bf16[96,1792]{1,0:T(8,128)(2,1)S(1)} %pack_kernel.4.refs_0_, bf16[96,1792]{1,0:T(8,128)(2,1)S(1)} %collective-permute-done.1.refs_1_, bf16[608,3584]{1,0:T(8,128)(2,1)S(1)} %get-tuple-element.25.refs_2_, bf16[608,3584]{1,0:T(8,128)(2,1)S(1)} %get-tuple-element.26.refs_3_), custom_call_target="tpu_custom_call" | custom-call | flops 836763648 | tf_op jit(solution)/shard_map/expert_kernel/pallas_call | solution.py:70
  42.1 1.6 %collective-permute-start.20 = (bf16[96,896]{1,0:T(8,128)(2,1)S(1)}, bf16[96,896]{1,0:T(8,128)(2,1)S(1)}, u32[]{:S(2)}, u32[]{:S(2)}) collective-permute-start(bf16[96,896]{1,0:T(8,128)(2,1)S(1)} %get-tuple-element.42), channel_id=1, source_target_pairs={{0,2},{1,3},{2,0},{3,1},{4,6},{5,7},{6,4},{7,5},{8,10},{9,11},{10,... | collective-permute-start | bytes 516104 | tf_op jit(solution)/shard_map/ppermute | solution.py:224
  44.4 1.6 %collective-permute-start.8 = (bf16[96,896]{1,0:T(8,128)(2,1)S(1)}, bf16[96,896]{1,0:T(8,128)(2,1)S(1)}, u32[]{:S(2)}, u32[]{:S(2)}) collective-permute-start(bf16[96,896]{1,0:T(8,128)(2,1)S(1)} %get-tuple-element.34), channel_id=1, source_target_pairs={{0,2},{1,3},{2,0},{3,1},{4,6},{5,7},{6,4},{7,5},{8,10},{9,11},{10,... | collective-permute-start | bytes 516104 | tf_op jit(solution)/shard_map/ppermute | solution.py:224
  46.6 2.8 %collective-permute-done.20.refs_1_ = bf16[96,896]{1,0:T(8,128)(2,1)S(1)} collective-permute-done((bf16[96,896]{1,0:T(8,128)(2,1)S(1)}, bf16[96,896]{1,0:T(8,128)(2,1)S(1)}, u32[]{:S(2)}, u32[]{:S(2)}) %collective-permute-start.20) | collective-permute-done | bytes 172064 | tf_op jit(solution)/shard_map/ppermute | solution.py:224
  49.5 3.6 %collective-permute-done.14.refs_1_ = bf16[96,896]{1,0:T(8,128)(2,1)S(1)} collective-permute-done((bf16[96,896]{1,0:T(8,128)(2,1)S(1)}, bf16[96,896]{1,0:T(8,128)(2,1)S(1)}, u32[]{:S(2)}, u32[]{:S(2)}) %collective-permute-start.14) | collective-permute-done | bytes 172064 | tf_op jit(solution)/shard_map/ppermute | solution.py:224
  53.2 3.6 %collective-permute-done.8.refs_1_ = bf16[96,896]{1,0:T(8,128)(2,1)S(1)} collective-permute-done((bf16[96,896]{1,0:T(8,128)(2,1)S(1)}, bf16[96,896]{1,0:T(8,128)(2,1)S(1)}, u32[]{:S(2)}, u32[]{:S(2)}) %collective-permute-start.8) | collective-permute-done | bytes 172064 | tf_op jit(solution)/shard_map/ppermute | solution.py:224
  56.9 2.6 %collective-permute-done.3.refs_2_ = bf16[96,896]{1,0:T(8,128)(2,1)S(1)} collective-permute-done((bf16[96,896]{1,0:T(8,128)(2,1)S(1)}, bf16[96,896]{1,0:T(8,128)(2,1)S(1)}, u32[]{:S(2)}, u32[]{:S(2)}) %collective-permute-start.3) | collective-permute-done | bytes 172064 | tf_op jit(solution)/shard_map/ppermute | solution.py:224
  59.5 4.2 %collective-permute-done.15.refs_4_ = bf16[96,896]{1,0:T(8,128)(2,1)S(1)} collective-permute-done((bf16[96,896]{1,0:T(8,128)(2,1)S(1)}, bf16[96,896]{1,0:T(8,128)(2,1)S(1)}, u32[]{:S(2)}, u32[]{:S(2)}) %collective-permute-start.15) | collective-permute-done | bytes 172064 | tf_op jit(solution)/shard_map/ppermute | solution.py:231
  63.7 1.3 %collective-permute-done.9.refs_3_ = bf16[96,896]{1,0:T(8,128)(2,1)S(1)} collective-permute-done((bf16[96,896]{1,0:T(8,128)(2,1)S(1)}, bf16[96,896]{1,0:T(8,128)(2,1)S(1)}, u32[]{:S(2)}, u32[]{:S(2)}) %collective-permute-start.9) | collective-permute-done | bytes 172064 | tf_op jit(solution)/shard_map/ppermute | solution.py:231
  65.0 0.9 %combine_kernel.1 = bf16[96,896]{1,0:T(8,128)(2,1)} custom-call(f32[4,96,128]{2,1,0:T(8,128)S(1)} %get-tuple-element.24.refs_1_.refs_0_, f32[96,896]{1,0:T(8,128)S(1)} %get-tuple-element.29.refs_1_, bf16[96,896]{1,0:T(8,128)(2,1)S(1)} %collective-permute-done.3.refs_2_, bf16[96,896]{1,0:T(8,128)(2,1)S(1)} %collective-permute-done.9.refs_3_, ...), custom_call_target="tpu_custom_call" | custom-call | tf_op jit(solution)/shard_map/combine_kernel/pallas_call | solution.py:70
  (40 shorter events, 3.3 us)
Async XLA Ops:
  0.0 11.9 %collective-permute-start.16 = (bf16[96,896]{1,0:T(8,128)(2,1)}, bf16[96,896]{1,0:T(8,128)(2,1)S(1)}, u32[]{:S(2)}, u32[]{:S(2)}) collective-permute-start(bf16[96,896]{1,0:T(8,128)(2,1)} %refs_0_.1), channel_id=1, source_target_pairs={{0,12},{4,0},{8,4},{12,8},{1,13},{5,1},{9,5},{13,9},{2,14},{6,2},{... | collective-permute-start | bytes 516104 | tf_op jit(solution)/shard_map/ppermute | solution.py:231
  5.0 14.8 %collective-permute-start.10 = (bf16[96,896]{1,0:T(8,128)(2,1)}, bf16[96,896]{1,0:T(8,128)(2,1)S(1)}, u32[]{:S(2)}, u32[]{:S(2)}) collective-permute-start(bf16[96,896]{1,0:T(8,128)(2,1)} %refs_0_.1), channel_id=1, source_target_pairs={{0,8},{4,12},{8,0},{12,4},{1,9},{5,13},{9,1},{13,5},{2,10},{6,14},... | collective-permute-start | bytes 516104 | tf_op jit(solution)/shard_map/ppermute | solution.py:231
  5.1 16.3 %collective-permute-start.4 = (bf16[96,896]{1,0:T(8,128)(2,1)}, bf16[96,896]{1,0:T(8,128)(2,1)S(1)}, u32[]{:S(2)}, u32[]{:S(2)}) collective-permute-start(bf16[96,896]{1,0:T(8,128)(2,1)} %refs_0_.1), channel_id=1, source_target_pairs={{0,4},{4,8},{8,12},{12,0},{1,5},{5,9},{9,13},{13,1},{2,6},{6,10},{... | collective-permute-start | bytes 516104 | tf_op jit(solution)/shard_map/ppermute | solution.py:231
  6.1 15.8 %collective-permute-start = (bf16[96,896]{1,0:T(8,128)(2,1)}, bf16[96,896]{1,0:T(8,128)(2,1)S(1)}, u32[]{:S(2)}, u32[]{:S(2)}) collective-permute-start(bf16[96,896]{1,0:T(8,128)(2,1)} %refs_0_.1), channel_id=1, source_target_pairs={{0,2},{1,3},{2,0},{3,1},{4,6},{5,7},{6,4},{7,5},{8,10},{9,11},{10,... | collective-permute-start | bytes 516104 | tf_op jit(solution)/shard_map/ppermute | solution.py:224
  7.6 22.1 %copy-start = (bf16[96,896]{1,0:T(8,128)(2,1)S(1)}, bf16[96,896]{1,0:T(8,128)(2,1)}, u32[]{:S(2)}) copy-start(bf16[96,896]{1,0:T(8,128)(2,1)} %refs_0_.1) | copy-start | bytes 516100
  11.9 10.0 %collective-permute-start.17 = (bf16[96,896]{1,0:T(8,128)(2,1)S(1)}, bf16[96,896]{1,0:T(8,128)(2,1)S(1)}, u32[]{:S(2)}, u32[]{:S(2)}) collective-permute-start(bf16[96,896]{1,0:T(8,128)(2,1)S(1)} %shard_map.55.refs_0_), channel_id=1, source_target_pairs={{0,2},{1,3},{2,0},{3,1},{4,6},{5,7},{6,4},{7,5},{8,10},{9,11},{10,... | collective-permute-start | bytes 516104 | tf_op jit(solution)/shard_map/ppermute | solution.py:224
  19.8 7.3 %collective-permute-start.11 = (bf16[96,896]{1,0:T(8,128)(2,1)S(1)}, bf16[96,896]{1,0:T(8,128)(2,1)S(1)}, u32[]{:S(2)}, u32[]{:S(2)}) collective-permute-start(bf16[96,896]{1,0:T(8,128)(2,1)S(1)} %collective-permute-done.10.refs_0_), channel_id=1, source_target_pairs={{0,2},{1,3},{2,0},{3,1},{4,6},{5,7},{6,4},{7,5},{8,10},{9,11},{10,... | collective-permute-start | bytes 516104 | tf_op jit(solution)/shard_map/ppermute | solution.py:224
  21.3 8.2 %collective-permute-start.5 = (bf16[96,896]{1,0:T(8,128)(2,1)S(1)}, bf16[96,896]{1,0:T(8,128)(2,1)S(1)}, u32[]{:S(2)}, u32[]{:S(2)}) collective-permute-start(bf16[96,896]{1,0:T(8,128)(2,1)S(1)} %collective-permute-done.4.refs_0_), channel_id=1, source_target_pairs={{0,2},{1,3},{2,0},{3,1},{4,6},{5,7},{6,4},{7,5},{8,10},{9,11},{10,... | collective-permute-start | bytes 516104 | tf_op jit(solution)/shard_map/ppermute | solution.py:224
  21.9 8.3 %collective-permute-start.18 = (bf16[96,1792]{1,0:T(8,128)(2,1)S(1)}, bf16[96,1792]{1,0:T(8,128)(2,1)S(1)}, u32[]{:S(2)}, u32[]{:S(2)}) collective-permute-start(bf16[96,1792]{1,0:T(8,128)(2,1)S(1)} %pack_kernel.7.refs_0_), channel_id=1, source_target_pairs={{0,1},{1,0},{2,3},{3,2},{4,5},{5,4},{6,7},{7,6},{8,9},{9,8},{10,11... | collective-permute-start | bytes 1032200 | tf_op jit(solution)/shard_map/ppermute | solution.py:224
  27.2 5.8 %collective-permute-start.12 = (bf16[96,1792]{1,0:T(8,128)(2,1)S(1)}, bf16[96,1792]{1,0:T(8,128)(2,1)S(1)}, u32[]{:S(2)}, u32[]{:S(2)}) collective-permute-start(bf16[96,1792]{1,0:T(8,128)(2,1)S(1)} %pack_kernel.6.refs_0_), channel_id=1, source_target_pairs={{0,1},{1,0},{2,3},{3,2},{4,5},{5,4},{6,7},{7,6},{8,9},{9,8},{10,11... | collective-permute-start | bytes 1032200 | tf_op jit(solution)/shard_map/ppermute | solution.py:224
  29.5 6.6 %collective-permute-start.6 = (bf16[96,1792]{1,0:T(8,128)(2,1)S(1)}, bf16[96,1792]{1,0:T(8,128)(2,1)S(1)}, u32[]{:S(2)}, u32[]{:S(2)}) collective-permute-start(bf16[96,1792]{1,0:T(8,128)(2,1)S(1)} %pack_kernel.5.refs_0_), channel_id=1, source_target_pairs={{0,1},{1,0},{2,3},{3,2},{4,5},{5,4},{6,7},{7,6},{8,9},{9,8},{10,11... | collective-permute-start | bytes 1032200 | tf_op jit(solution)/shard_map/ppermute | solution.py:224
  29.7 9.2 %collective-permute-start.1 = (bf16[96,1792]{1,0:T(8,128)(2,1)S(1)}, bf16[96,1792]{1,0:T(8,128)(2,1)S(1)}, u32[]{:S(2)}, u32[]{:S(2)}) collective-permute-start(bf16[96,1792]{1,0:T(8,128)(2,1)S(1)} %pack_kernel.4.refs_0_), channel_id=1, source_target_pairs={{0,1},{1,0},{2,3},{3,2},{4,5},{5,4},{6,7},{7,6},{8,9},{9,8},{10,11... | collective-permute-start | bytes 1032200 | tf_op jit(solution)/shard_map/ppermute | solution.py:224
  32.8 9.2 %collective-permute-start.19 = (bf16[96,1792]{1,0:T(8,128)(2,1)S(1)}, bf16[96,1792]{1,0:T(8,128)(2,1)S(1)}, u32[]{:S(2)}, u32[]{:S(2)}) collective-permute-start(bf16[96,1792]{1,0:T(8,128)(2,1)S(1)} %get-tuple-element.40), channel_id=1, source_target_pairs={{0,1},{1,0},{2,3},{3,2},{4,5},{5,4},{6,7},{7,6},{8,9},{9,8},{10,11... | collective-permute-start | bytes 1032200 | tf_op jit(solution)/shard_map/ppermute | solution.py:224
  35.6 8.1 %collective-permute-start.13 = (bf16[96,1792]{1,0:T(8,128)(2,1)S(1)}, bf16[96,1792]{1,0:T(8,128)(2,1)S(1)}, u32[]{:S(2)}, u32[]{:S(2)}) collective-permute-start(bf16[96,1792]{1,0:T(8,128)(2,1)S(1)} %get-tuple-element.36), channel_id=1, source_target_pairs={{0,1},{1,0},{2,3},{3,2},{4,5},{5,4},{6,7},{7,6},{8,9},{9,8},{10,11... | collective-permute-start | bytes 1032200 | tf_op jit(solution)/shard_map/ppermute | solution.py:224
  38.7 5.6 %collective-permute-start.7 = (bf16[96,1792]{1,0:T(8,128)(2,1)S(1)}, bf16[96,1792]{1,0:T(8,128)(2,1)S(1)}, u32[]{:S(2)}, u32[]{:S(2)}) collective-permute-start(bf16[96,1792]{1,0:T(8,128)(2,1)S(1)} %get-tuple-element.32), channel_id=1, source_target_pairs={{0,1},{1,0},{2,3},{3,2},{4,5},{5,4},{6,7},{7,6},{8,9},{9,8},{10,11... | collective-permute-start | bytes 1032200 | tf_op jit(solution)/shard_map/ppermute | solution.py:224
  41.5 4.5 %collective-permute-start.2 = (bf16[96,1792]{1,0:T(8,128)(2,1)S(1)}, bf16[96,1792]{1,0:T(8,128)(2,1)S(1)}, u32[]{:S(2)}, u32[]{:S(2)}) collective-permute-start(bf16[96,1792]{1,0:T(8,128)(2,1)S(1)} %get-tuple-element.28), channel_id=1, source_target_pairs={{0,1},{1,0},{2,3},{3,2},{4,5},{5,4},{6,7},{7,6},{8,9},{9,8},{10,11... | collective-permute-start | bytes 1032200 | tf_op jit(solution)/shard_map/ppermute | solution.py:224
  42.1 7.3 %collective-permute-start.20 = (bf16[96,896]{1,0:T(8,128)(2,1)S(1)}, bf16[96,896]{1,0:T(8,128)(2,1)S(1)}, u32[]{:S(2)}, u32[]{:S(2)}) collective-permute-start(bf16[96,896]{1,0:T(8,128)(2,1)S(1)} %get-tuple-element.42), channel_id=1, source_target_pairs={{0,2},{1,3},{2,0},{3,1},{4,6},{5,7},{6,4},{7,5},{8,10},{9,11},{10,... | collective-permute-start | bytes 516104 | tf_op jit(solution)/shard_map/ppermute | solution.py:224
  43.8 9.3 %collective-permute-start.14 = (bf16[96,896]{1,0:T(8,128)(2,1)S(1)}, bf16[96,896]{1,0:T(8,128)(2,1)S(1)}, u32[]{:S(2)}, u32[]{:S(2)}) collective-permute-start(bf16[96,896]{1,0:T(8,128)(2,1)S(1)} %get-tuple-element.38), channel_id=1, source_target_pairs={{0,2},{1,3},{2,0},{3,1},{4,6},{5,7},{6,4},{7,5},{8,10},{9,11},{10,... | collective-permute-start | bytes 516104 | tf_op jit(solution)/shard_map/ppermute | solution.py:224
  44.4 12.4 %collective-permute-start.8 = (bf16[96,896]{1,0:T(8,128)(2,1)S(1)}, bf16[96,896]{1,0:T(8,128)(2,1)S(1)}, u32[]{:S(2)}, u32[]{:S(2)}) collective-permute-start(bf16[96,896]{1,0:T(8,128)(2,1)S(1)} %get-tuple-element.34), channel_id=1, source_target_pairs={{0,2},{1,3},{2,0},{3,1},{4,6},{5,7},{6,4},{7,5},{8,10},{9,11},{10,... | collective-permute-start | bytes 516104 | tf_op jit(solution)/shard_map/ppermute | solution.py:224
  46.1 13.5 %collective-permute-start.3 = (bf16[96,896]{1,0:T(8,128)(2,1)S(1)}, bf16[96,896]{1,0:T(8,128)(2,1)S(1)}, u32[]{:S(2)}, u32[]{:S(2)}) collective-permute-start(bf16[96,896]{1,0:T(8,128)(2,1)S(1)} %get-tuple-element.30), channel_id=1, source_target_pairs={{0,2},{1,3},{2,0},{3,1},{4,6},{5,7},{6,4},{7,5},{8,10},{9,11},{10,... | collective-permute-start | bytes 516104 | tf_op jit(solution)/shard_map/ppermute | solution.py:224
  49.4 10.1 %collective-permute-start.21 = (bf16[96,896]{1,0:T(8,128)(2,1)S(1)}, bf16[96,896]{1,0:T(8,128)(2,1)S(1)}, u32[]{:S(2)}, u32[]{:S(2)}) collective-permute-start(bf16[96,896]{1,0:T(8,128)(2,1)S(1)} %chip_sum_kernel.5), channel_id=1, source_target_pairs={{0,4},{4,8},{8,12},{12,0},{1,5},{5,9},{9,13},{13,1},{2,6},{6,10},{... | collective-permute-start | bytes 516104 | tf_op jit(solution)/shard_map/ppermute | solution.py:231
  53.1 10.6 %collective-permute-start.15 = (bf16[96,896]{1,0:T(8,128)(2,1)S(1)}, bf16[96,896]{1,0:T(8,128)(2,1)S(1)}, u32[]{:S(2)}, u32[]{:S(2)}) collective-permute-start(bf16[96,896]{1,0:T(8,128)(2,1)S(1)} %chip_sum_kernel.4), channel_id=1, source_target_pairs={{0,8},{4,12},{8,0},{12,4},{1,9},{5,13},{9,1},{13,5},{2,10},{6,14},... | collective-permute-start | bytes 516104 | tf_op jit(solution)/shard_map/ppermute | solution.py:231
  56.8 8.2 %collective-permute-start.9 = (bf16[96,896]{1,0:T(8,128)(2,1)S(1)}, bf16[96,896]{1,0:T(8,128)(2,1)S(1)}, u32[]{:S(2)}, u32[]{:S(2)}) collective-permute-start(bf16[96,896]{1,0:T(8,128)(2,1)S(1)} %chip_sum_kernel.3), channel_id=1, source_target_pairs={{0,12},{4,0},{8,4},{12,8},{1,13},{5,1},{9,5},{13,9},{2,14},{6,2},{... | collective-permute-start | bytes 516104 | tf_op jit(solution)/shard_map/ppermute | solution.py:231

commit v6 on v5

--- a/solution.py
+++ b/solution.py
@@ -232,25 +232,61 @@
             array, "expert", [(i, (i + by) % experts_n) for i in range(experts_n)]
         )
 
-    steps = (3, 2, 1)
-    order = [step for step in steps if step < experts_n] + [0]
-    blocks = {0: tokens} | {step: shift(tokens, step) for step in order[:-1]}
     columns, up_t, down = prepare(
         expert_ids.T, weight_codes.T, up_local.T, down_local, experts_n, capacity
     )
-    blocks[order[0]] = after(blocks[order[0]], columns)
-    others = {step: swap(block, 2) for step, block in blocks.items()}
-
-    chips, sums, parts = {}, {}, {}
-    for step in order:
-        waits = [] if chips else [others[0]]
+    blocks, others, chips, kept, sums, added, parts = {}, {}, {}, {}, {}, {}, {}
+
+    def arrive(step, waits):
+        blocks[step] = shift(blocks[step - 1], 1) if step else tokens
+        for wait in waits:
+            blocks[step] = after(blocks[step], wait)
+        others[step] = swap(blocks[step], 2)
+
+    def lay(step, waits):
         chips[step] = pack([(blocks[step], others[step])], waits)
-    for step in order:
-        keep, send = expert_rows(chips[step], swap(chips[step], 1), up_t, down, ())
-        own, away = core_sum(keep, swap(send, 1), 1, ())
+
+    def run(step, waits):
+        kept[step] = expert_rows(chips[step], swap(chips[step], 1), up_t, down, waits)
+
+    def leave(step, waits):
+        keep, send = kept[step]
+        own, away = core_sum(keep, swap(send, 1), 1, waits)
         sums[step] = own, swap(away, 2)
-    for step in order[:-1]:
-        parts[step] = shift(chip_sum(*sums[step], 0, ()), -step)
+
+    def give(step, waits):
+        added[step] = chip_sum(*sums[step], 0, waits)
+        parts[step] = shift(added[step], -step)
+
+    arrive(0, [])
+    if experts_n > 1:
+        arrive(1, [columns])
+    lay(0, [blocks[1]] if experts_n > 1 else [])
+    run(0, [])
+    waits = []
+    for step in range(1, experts_n):
+        if step + 1 < experts_n:
+            arrive(step + 1, [kept[step - 1][0]])
+            lay(step, [blocks[step + 1]])
+        else:
+            lay(step, [kept[step - 1][0]])
+            leave(0, [sums[1][0]] if 1 in sums else [])
+            waits = [sums[0][0]]
+        if step > 1:
+            leave(step - 1, waits)
+            waits = [sums[step - 1][0]]
+        if step > 2:
+            waits.append(sums[step - 2][1])
+        run(step, waits)
+        if step > 2:
+            give(step - 2, [kept[step][0]])
+    if not sums:
+        leave(0, [])
+    if experts_n > 1:
+        leave(experts_n - 1, list(added.values())[-1:])
+    for step in range(1, experts_n):
+        if step not in parts:
+            give(step, [sums[experts_n - 1][0]])
     return combine(columns, *sums[0], [parts[step] for step in range(1, experts_n)], ())
 
 

time: 66.1 us -> 65.3 us (0.988)
  waiting for transfers between devices: 32.9 us -> 29.8 us
  starting transfers between devices: 16.7 us -> 19 us
    ppermute x16, waiting for transfers between devices: 20 us -> 15.3 us  [swap(): return lax.ppermute(array, 'tensor', [(i, i ^ bit) for i in range(4)])]
    ppermute x16, starting transfers between devices: 10.5 us -> 12.2 us  [swap(): return lax.ppermute(array, 'tensor', [(i, i ^ bit) for i in range(4)])]
    ppermute x6, waiting for transfers between devices: 12.8 us -> 14.5 us  [shift(): lax.ppermute(array, 'expert', [(i, (i + by) % experts_n) for i in range(e...]
  transfers between devices with their start and end apart: 22 -> 22, of which waited for: 9 -> 9; matrix products, arithmetic and copies ran while one was open for 0% -> 0% of each run, Pallas kernels for 23% -> 19%
where the time goes in v6:
time: 65.3 us; the launch traced here: 65.1 us
  waiting for transfers between devices  29.8 us (46%)
  starting transfers between devices  19 us (29%)
  Pallas kernels  16.2 us (25%)
    pallas_call x17, Pallas kernels, local_call(): pl.pallas_call(body_of, name=name, out_shape=out_shape, in_specs=list(in_...  16.2 us
    ppermute x16, waiting for transfers between devices, swap(): return lax.ppermute(array, 'tensor', [(i, i ^ bit) for i in range(4)])  15.3 us
    ppermute x6, waiting for transfers between devices, shift(): lax.ppermute(array, 'expert', [(i, (i + by) % experts_n) for i in range(e...  14.5 us
    ppermute x16, starting transfers between devices, swap(): return lax.ppermute(array, 'tensor', [(i, i ^ bit) for i in range(4)])  12.2 us
    ppermute x6, starting transfers between devices, shift(): lax.ppermute(array, 'expert', [(i, (i + by) % experts_n) for i in range(e...  6.72 us
  transfers between devices with their start and end apart: 22, of which 9 were waited for; matrix products, arithmetic and copies ran while one was open for 0% of the time, Pallas kernels for 19%

profile of v6, /device:TPU:0, one launch (start us, length us, event | category | flops | bytes accessed | tf_op | source)
XLA Modules:
  0.0 65.1 jit_solution(14181725930750298180)
XLA Ops:
  0.0 3.0 %collective-permute-start.1 = (bf16[96,896]{1,0:T(8,128)(2,1)}, bf16[96,896]{1,0:T(8,128)(2,1)S(1)}, u32[]{:S(2)}, u32[]{:S(2)}) collective-permute-start(bf16[96,896]{1,0:T(8,128)(2,1)} %refs_0_.1), channel_id=1, source_target_pairs={{0,4},{4,8},{8,12},{12,0},{1,5},{5,9},{9,13},{13,1},{2,6},{6,10},{... | collective-permute-start | bytes 516104 | tf_op jit(solution)/shard_map/ppermute | solution.py:231
  3.0 1.5 %collective-permute-start = (bf16[96,896]{1,0:T(8,128)(2,1)}, bf16[96,896]{1,0:T(8,128)(2,1)S(1)}, u32[]{:S(2)}, u32[]{:S(2)}) collective-permute-start(bf16[96,896]{1,0:T(8,128)(2,1)} %refs_0_.1), channel_id=1, source_target_pairs={{0,2},{1,3},{2,0},{3,1},{4,6},{5,7},{6,4},{7,5},{8,10},{9,11},{10,... | collective-permute-start | bytes 516104 | tf_op jit(solution)/shard_map/ppermute | solution.py:224
  4.5 4.3 %prepare_kernel.1 = (f32[4,96,128]{2,1,0:T(8,128)S(1)}, bf16[608,3584]{1,0:T(8,128)(2,1)S(1)}, bf16[608,3584]{1,0:T(8,128)(2,1)S(1)}) custom-call(s32[2,96]{1,0:T(2,128)} %bitcast.8, s32[2,96]{1,0:T(2,128)} %bitcast.9, bf16[608,3584]{1,0:T(8,128)(2,1)} %bitcast.6, bf16[608,3584]{1,0:T(8,128)(2,1)} %bitcast.7), custom_call_target="tpu_custom_call" | custom-call | bytes 8716288 | tf_op jit(solution)/shard_map/prepare_kernel/pallas_call | solution.py:70
  9.7 1.1 %collective-permute-start.5 = (bf16[96,896]{1,0:T(8,128)(2,1)S(1)}, bf16[96,896]{1,0:T(8,128)(2,1)S(1)}, u32[]{:S(2)}, u32[]{:S(2)}) collective-permute-start(bf16[96,896]{1,0:T(8,128)(2,1)S(1)} %shard_map.55.refs_2_.refs_0_), channel_id=1, source_target_pairs={{0,4},{4,8},{8,12},{12,0},{1,5},{5,9},{9,13},{13,1},{2,6},{6,10},{... | collective-permute-start | bytes 516104 | tf_op jit(solution)/shard_map/ppermute | solution.py:231
  10.8 1.5 %collective-permute-start.4 = (bf16[96,896]{1,0:T(8,128)(2,1)S(1)}, bf16[96,896]{1,0:T(8,128)(2,1)S(1)}, u32[]{:S(2)}, u32[]{:S(2)}) collective-permute-start(bf16[96,896]{1,0:T(8,128)(2,1)S(1)} %shard_map.55.refs_2_.refs_0_), channel_id=1, source_target_pairs={{0,2},{1,3},{2,0},{3,1},{4,6},{5,7},{6,4},{7,5},{8,10},{9,11},{10,... | collective-permute-start | bytes 516104 | tf_op jit(solution)/shard_map/ppermute | solution.py:224
  12.3 2.6 %expert_kernel.4 = (f32[96,1792]{1,0:T(8,128)S(1)}, bf16[96,1792]{1,0:T(8,128)(2,1)S(1)}) custom-call(bf16[96,1792]{1,0:T(8,128)(2,1)S(1)} %pack_kernel.4.refs_0_, bf16[96,1792]{1,0:T(8,128)(2,1)S(1)} %collective-permute-done.2.refs_1_, bf16[608,3584]{1,0:T(8,128)(2,1)S(1)} %get-tuple-element.25.refs_2_, bf16[608,3584]{1,0:T(8,128)(2,1)S(1)} %get-tuple-element.26.refs_3_), custom_call_target="tpu_custom_call" | custom-call | flops 836763648 | tf_op jit(solution)/shard_map/expert_kernel/pallas_call | solution.py:70
  14.9 3.4 %collective-permute-done.5.refs_0_ = bf16[96,896]{1,0:T(8,128)(2,1)S(1)} collective-permute-done((bf16[96,896]{1,0:T(8,128)(2,1)S(1)}, bf16[96,896]{1,0:T(8,128)(2,1)S(1)}, u32[]{:S(2)}, u32[]{:S(2)}) %collective-permute-start.5) | collective-permute-done | bytes 172064 | tf_op jit(solution)/shard_map/ppermute | solution.py:231
  19.0 1.5 %collective-permute-start.12 = (bf16[96,896]{1,0:T(8,128)(2,1)S(1)}, bf16[96,896]{1,0:T(8,128)(2,1)S(1)}, u32[]{:S(2)}, u32[]{:S(2)}) collective-permute-start(bf16[96,896]{1,0:T(8,128)(2,1)S(1)} %shard_map.56.refs_2_.refs_0_), channel_id=1, source_target_pairs={{0,2},{1,3},{2,0},{3,1},{4,6},{5,7},{6,4},{7,5},{8,10},{9,11},{10,... | collective-permute-start | bytes 516104 | tf_op jit(solution)/shard_map/ppermute | solution.py:224
  20.5 2.6 %expert_kernel.5 = (f32[96,1792]{1,0:T(8,128)S(1)}, bf16[96,1792]{1,0:T(8,128)(2,1)S(1)}) custom-call(bf16[96,1792]{1,0:T(8,128)(2,1)S(1)} %pack_kernel.5.refs_0_, bf16[96,1792]{1,0:T(8,128)(2,1)S(1)} %collective-permute-done.6.refs_1_, bf16[608,3584]{1,0:T(8,128)(2,1)S(1)} %get-tuple-element.25.refs_2_, bf16[608,3584]{1,0:T(8,128)(2,1)S(1)} %get-tuple-element.26.refs_3_), custom_call_target="tpu_custom_call" | custom-call | flops 836763648 | tf_op jit(solution)/shard_map/expert_kernel/pallas_call | solution.py:70
  23.2 3.8 %collective-permute-done.10.refs_0_ = bf16[96,896]{1,0:T(8,128)(2,1)S(1)} collective-permute-done((bf16[96,896]{1,0:T(8,128)(2,1)S(1)}, bf16[96,896]{1,0:T(8,128)(2,1)S(1)}, u32[]{:S(2)}, u32[]{:S(2)}) %collective-permute-start.10) | collective-permute-done | bytes 172064 | tf_op jit(solution)/shard_map/ppermute | solution.py:231
  27.1 1.6 %collective-permute-start.11 = (bf16[96,896]{1,0:T(8,128)(2,1)S(1)}, bf16[96,896]{1,0:T(8,128)(2,1)S(1)}, u32[]{:S(2)}, u32[]{:S(2)}) collective-permute-start(bf16[96,896]{1,0:T(8,128)(2,1)S(1)} %shard_map.57.refs_2_.refs_0_), channel_id=1, source_target_pairs={{0,2},{1,3},{2,0},{3,1},{4,6},{5,7},{6,4},{7,5},{8,10},{9,11},{10,... | collective-permute-start | bytes 516104 | tf_op jit(solution)/shard_map/ppermute | solution.py:224
  28.9 2.6 %expert_kernel.6 = (f32[96,1792]{1,0:T(8,128)S(1)}, bf16[96,1792]{1,0:T(8,128)(2,1)S(1)}) custom-call(bf16[96,1792]{1,0:T(8,128)(2,1)S(1)} %pack_kernel.6.refs_0_, bf16[96,1792]{1,0:T(8,128)(2,1)S(1)} %collective-permute-done.13.refs_1_, bf16[608,3584]{1,0:T(8,128)(2,1)S(1)} %get-tuple-element.25.refs_2_, bf16[608,3584]{1,0:T(8,128)(2,1)S(1)} %get-tuple-element.26.refs_3_, ...), custom_call_target="tpu_custom_call" | custom-call | flops 836763648 | tf_op jit(solution)/shard_map/expert_kernel/pallas_call | solution.py:70
  32.0 1.9 %collective-permute-done.11.refs_1_ = bf16[96,896]{1,0:T(8,128)(2,1)S(1)} collective-permute-done((bf16[96,896]{1,0:T(8,128)(2,1)S(1)}, bf16[96,896]{1,0:T(8,128)(2,1)S(1)}, u32[]{:S(2)}, u32[]{:S(2)}) %collective-permute-start.11) | collective-permute-done | bytes 172064 | tf_op jit(solution)/shard_map/ppermute | solution.py:224
  34.0 1.6 %collective-permute-start.9 = (bf16[96,896]{1,0:T(8,128)(2,1)S(1)}, bf16[96,896]{1,0:T(8,128)(2,1)S(1)}, u32[]{:S(2)}, u32[]{:S(2)}) collective-permute-start(bf16[96,896]{1,0:T(8,128)(2,1)S(1)} %get-tuple-element.34), channel_id=1, source_target_pairs={{0,2},{1,3},{2,0},{3,1},{4,6},{5,7},{6,4},{7,5},{8,10},{9,11},{10,... | collective-permute-start | bytes 516104 | tf_op jit(solution)/shard_map/ppermute | solution.py:224
  35.8 5.1 %collective-permute-done.9.refs_5_.refs_1_ = bf16[96,896]{1,0:T(8,128)(2,1)S(1)} collective-permute-done((bf16[96,896]{1,0:T(8,128)(2,1)S(1)}, bf16[96,896]{1,0:T(8,128)(2,1)S(1)}, u32[]{:S(2)}, u32[]{:S(2)}) %collective-permute-start.9) | collective-permute-done | bytes 172064 | tf_op jit(solution)/shard_map/ppermute | solution.py:224
  40.8 2.6 %expert_kernel.7 = (f32[96,1792]{1,0:T(8,128)S(1)}, bf16[96,1792]{1,0:T(8,128)(2,1)S(1)}) custom-call(bf16[96,1792]{1,0:T(8,128)(2,1)S(1)} %pack_kernel.7.refs_0_, bf16[96,1792]{1,0:T(8,128)(2,1)S(1)} %collective-permute-done.14.refs_1_, bf16[608,3584]{1,0:T(8,128)(2,1)S(1)} %get-tuple-element.25.refs_2_, bf16[608,3584]{1,0:T(8,128)(2,1)S(1)} %get-tuple-element.26.refs_3_, ...), custom_call_target="tpu_custom_call" | custom-call | flops 836763648 | tf_op jit(solution)/shard_map/expert_kernel/pallas_call | solution.py:70
  43.5 1.6 %collective-permute-start.17 = (bf16[96,896]{1,0:T(8,128)(2,1)S(1)}, bf16[96,896]{1,0:T(8,128)(2,1)S(1)}, u32[]{:S(2)}, u32[]{:S(2)}) collective-permute-start(bf16[96,896]{1,0:T(8,128)(2,1)S(1)} %get-tuple-element.39), channel_id=1, source_target_pairs={{0,2},{1,3},{2,0},{3,1},{4,6},{5,7},{6,4},{7,5},{8,10},{9,11},{10,... | collective-permute-start | bytes 516104 | tf_op jit(solution)/shard_map/ppermute | solution.py:224
  45.2 1.6 %collective-permute-start.20 = (bf16[96,896]{1,0:T(8,128)(2,1)S(1)}, bf16[96,896]{1,0:T(8,128)(2,1)S(1)}, u32[]{:S(2)}, u32[]{:S(2)}) collective-permute-start(bf16[96,896]{1,0:T(8,128)(2,1)S(1)} %get-tuple-element.42), channel_id=1, source_target_pairs={{0,2},{1,3},{2,0},{3,1},{4,6},{5,7},{6,4},{7,5},{8,10},{9,11},{10,... | collective-permute-start | bytes 516104 | tf_op jit(solution)/shard_map/ppermute | solution.py:224
  47.3 1.7 %collective-permute-start.16 = (bf16[96,896]{1,0:T(8,128)(2,1)S(1)}, bf16[96,896]{1,0:T(8,128)(2,1)S(1)}, u32[]{:S(2)}, u32[]{:S(2)}) collective-permute-start(bf16[96,896]{1,0:T(8,128)(2,1)S(1)} %chip_sum_kernel.3.refs_2_), channel_id=1, source_target_pairs={{0,12},{4,0},{8,4},{12,8},{1,13},{5,1},{9,5},{13,9},{2,14},{6,2},{... | collective-permute-start | bytes 516104 | tf_op jit(solution)/shard_map/ppermute | solution.py:231
  49.1 1.7 %collective-permute-done.17.refs_1_ = bf16[96,896]{1,0:T(8,128)(2,1)S(1)} collective-permute-done((bf16[96,896]{1,0:T(8,128)(2,1)S(1)}, bf16[96,896]{1,0:T(8,128)(2,1)S(1)}, u32[]{:S(2)}, u32[]{:S(2)}) %collective-permute-start.17) | collective-permute-done | bytes 172064 | tf_op jit(solution)/shard_map/ppermute | solution.py:224
  51.1 3.4 %collective-permute-done.20.refs_1_ = bf16[96,896]{1,0:T(8,128)(2,1)S(1)} collective-permute-done((bf16[96,896]{1,0:T(8,128)(2,1)S(1)}, bf16[96,896]{1,0:T(8,128)(2,1)S(1)}, u32[]{:S(2)}, u32[]{:S(2)}) %collective-permute-start.20) | collective-permute-done | bytes 172064 | tf_op jit(solution)/shard_map/ppermute | solution.py:224
  54.6 3.1 %collective-permute-done.8.refs_2_ = bf16[96,896]{1,0:T(8,128)(2,1)S(1)} collective-permute-done((bf16[96,896]{1,0:T(8,128)(2,1)S(1)}, bf16[96,896]{1,0:T(8,128)(2,1)S(1)}, u32[]{:S(2)}, u32[]{:S(2)}) %collective-permute-start.8) | collective-permute-done | bytes 172064 | tf_op jit(solution)/shard_map/ppermute | solution.py:224
  57.7 6.5 %collective-permute-done.19.refs_4_ = bf16[96,896]{1,0:T(8,128)(2,1)S(1)} collective-permute-done((bf16[96,896]{1,0:T(8,128)(2,1)S(1)}, bf16[96,896]{1,0:T(8,128)(2,1)S(1)}, u32[]{:S(2)}, u32[]{:S(2)}) %collective-permute-start.19) | collective-permute-done | bytes 172064 | tf_op jit(solution)/shard_map/ppermute | solution.py:231
  64.2 0.9 %combine_kernel.1 = bf16[96,896]{1,0:T(8,128)(2,1)} custom-call(f32[4,96,128]{2,1,0:T(8,128)S(1)} %get-tuple-element.24.refs_1_.refs_0_, f32[96,896]{1,0:T(8,128)S(1)} %get-tuple-element.32.refs_2_.refs_1_, bf16[96,896]{1,0:T(8,128)(2,1)S(1)} %collective-permute-done.8.refs_2_, bf16[96,896]{1,0:T(8,128)(2,1)S(1)} %collective-permute-done.16.refs_3_, ...), custom_call_target="tpu_custom_call" | custom-call | tf_op jit(solution)/shard_map/combine_kernel/pallas_call | solution.py:70
  (42 shorter events, 3.8 us)
Async XLA Ops:
  0.0 9.6 %collective-permute-start.1 = (bf16[96,896]{1,0:T(8,128)(2,1)}, bf16[96,896]{1,0:T(8,128)(2,1)S(1)}, u32[]{:S(2)}, u32[]{:S(2)}) collective-permute-start(bf16[96,896]{1,0:T(8,128)(2,1)} %refs_0_.1), channel_id=1, source_target_pairs={{0,4},{4,8},{8,12},{12,0},{1,5},{5,9},{9,13},{13,1},{2,6},{6,10},{... | collective-permute-start | bytes 516104 | tf_op jit(solution)/shard_map/ppermute | solution.py:231
  3.0 6.6 %collective-permute-start = (bf16[96,896]{1,0:T(8,128)(2,1)}, bf16[96,896]{1,0:T(8,128)(2,1)S(1)}, u32[]{:S(2)}, u32[]{:S(2)}) collective-permute-start(bf16[96,896]{1,0:T(8,128)(2,1)} %refs_0_.1), channel_id=1, source_target_pairs={{0,2},{1,3},{2,0},{3,1},{4,6},{5,7},{6,4},{7,5},{8,10},{9,11},{10,... | collective-permute-start | bytes 516104 | tf_op jit(solution)/shard_map/ppermute | solution.py:224
  4.5 5.1 %copy-start = (bf16[96,896]{1,0:T(8,128)(2,1)S(1)}, bf16[96,896]{1,0:T(8,128)(2,1)}, u32[]{:S(2)}) copy-start(bf16[96,896]{1,0:T(8,128)(2,1)} %refs_0_.1) | copy-start | bytes 516100
  9.7 2.6 %collective-permute-start.2 = (bf16[96,1792]{1,0:T(8,128)(2,1)S(1)}, bf16[96,1792]{1,0:T(8,128)(2,1)S(1)}, u32[]{:S(2)}, u32[]{:S(2)}) collective-permute-start(bf16[96,1792]{1,0:T(8,128)(2,1)S(1)} %pack_kernel.4.refs_0_), channel_id=1, source_target_pairs={{0,1},{1,0},{2,3},{3,2},{4,5},{5,4},{6,7},{7,6},{8,9},{9,8},{10,11... | collective-permute-start | bytes 1032200 | tf_op jit(solution)/shard_map/ppermute | solution.py:224
  9.7 8.6 %collective-permute-start.5 = (bf16[96,896]{1,0:T(8,128)(2,1)S(1)}, bf16[96,896]{1,0:T(8,128)(2,1)S(1)}, u32[]{:S(2)}, u32[]{:S(2)}) collective-permute-start(bf16[96,896]{1,0:T(8,128)(2,1)S(1)} %shard_map.55.refs_2_.refs_0_), channel_id=1, source_target_pairs={{0,4},{4,8},{8,12},{12,0},{1,5},{5,9},{9,13},{13,1},{2,6},{6,10},{... | collective-permute-start | bytes 516104 | tf_op jit(solution)/shard_map/ppermute | solution.py:231
  10.8 7.5 %collective-permute-start.4 = (bf16[96,896]{1,0:T(8,128)(2,1)S(1)}, bf16[96,896]{1,0:T(8,128)(2,1)S(1)}, u32[]{:S(2)}, u32[]{:S(2)}) collective-permute-start(bf16[96,896]{1,0:T(8,128)(2,1)S(1)} %shard_map.55.refs_2_.refs_0_), channel_id=1, source_target_pairs={{0,2},{1,3},{2,0},{3,1},{4,6},{5,7},{6,4},{7,5},{8,10},{9,11},{10,... | collective-permute-start | bytes 516104 | tf_op jit(solution)/shard_map/ppermute | solution.py:224
  18.4 2.1 %collective-permute-start.6 = (bf16[96,1792]{1,0:T(8,128)(2,1)S(1)}, bf16[96,1792]{1,0:T(8,128)(2,1)S(1)}, u32[]{:S(2)}, u32[]{:S(2)}) collective-permute-start(bf16[96,1792]{1,0:T(8,128)(2,1)S(1)} %pack_kernel.5.refs_0_), channel_id=1, source_target_pairs={{0,1},{1,0},{2,3},{3,2},{4,5},{5,4},{6,7},{7,6},{8,9},{9,8},{10,11... | collective-permute-start | bytes 1032200 | tf_op jit(solution)/shard_map/ppermute | solution.py:224
  18.4 8.6 %collective-permute-start.10 = (bf16[96,896]{1,0:T(8,128)(2,1)S(1)}, bf16[96,896]{1,0:T(8,128)(2,1)S(1)}, u32[]{:S(2)}, u32[]{:S(2)}) collective-permute-start(bf16[96,896]{1,0:T(8,128)(2,1)S(1)} %shard_map.56.refs_2_.refs_0_), channel_id=1, source_target_pairs={{0,4},{4,8},{8,12},{12,0},{1,5},{5,9},{9,13},{13,1},{2,6},{6,10},{... | collective-permute-start | bytes 516104 | tf_op jit(solution)/shard_map/ppermute | solution.py:231
  19.0 8.0 %collective-permute-start.12 = (bf16[96,896]{1,0:T(8,128)(2,1)S(1)}, bf16[96,896]{1,0:T(8,128)(2,1)S(1)}, u32[]{:S(2)}, u32[]{:S(2)}) collective-permute-start(bf16[96,896]{1,0:T(8,128)(2,1)S(1)} %shard_map.56.refs_2_.refs_0_), channel_id=1, source_target_pairs={{0,2},{1,3},{2,0},{3,1},{4,6},{5,7},{6,4},{7,5},{8,10},{9,11},{10,... | collective-permute-start | bytes 516104 | tf_op jit(solution)/shard_map/ppermute | solution.py:224
  23.1 5.7 %collective-permute-start.7 = (bf16[96,1792]{1,0:T(8,128)(2,1)S(1)}, bf16[96,1792]{1,0:T(8,128)(2,1)S(1)}, u32[]{:S(2)}, u32[]{:S(2)}) collective-permute-start(bf16[96,1792]{1,0:T(8,128)(2,1)S(1)} %get-tuple-element.30), channel_id=1, source_target_pairs={{0,1},{1,0},{2,3},{3,2},{4,5},{5,4},{6,7},{7,6},{8,9},{9,8},{10,11... | collective-permute-start | bytes 1032200 | tf_op jit(solution)/shard_map/ppermute | solution.py:224
  27.0 1.9 %collective-permute-start.13 = (bf16[96,1792]{1,0:T(8,128)(2,1)S(1)}, bf16[96,1792]{1,0:T(8,128)(2,1)S(1)}, u32[]{:S(2)}, u32[]{:S(2)}) collective-permute-start(bf16[96,1792]{1,0:T(8,128)(2,1)S(1)} %pack_kernel.6.refs_0_), channel_id=1, source_target_pairs={{0,1},{1,0},{2,3},{3,2},{4,5},{5,4},{6,7},{7,6},{8,9},{9,8},{10,11... | collective-permute-start | bytes 1032200 | tf_op jit(solution)/shard_map/ppermute | solution.py:224
  27.1 6.8 %collective-permute-start.11 = (bf16[96,896]{1,0:T(8,128)(2,1)S(1)}, bf16[96,896]{1,0:T(8,128)(2,1)S(1)}, u32[]{:S(2)}, u32[]{:S(2)}) collective-permute-start(bf16[96,896]{1,0:T(8,128)(2,1)S(1)} %shard_map.57.refs_2_.refs_0_), channel_id=1, source_target_pairs={{0,2},{1,3},{2,0},{3,1},{4,6},{5,7},{6,4},{7,5},{8,10},{9,11},{10,... | collective-permute-start | bytes 516104 | tf_op jit(solution)/shard_map/ppermute | solution.py:224
  28.7 6.9 %collective-permute-start.3 = (bf16[96,1792]{1,0:T(8,128)(2,1)S(1)}, bf16[96,1792]{1,0:T(8,128)(2,1)S(1)}, u32[]{:S(2)}, u32[]{:S(2)}) collective-permute-start(bf16[96,1792]{1,0:T(8,128)(2,1)S(1)} %get-tuple-element.28), channel_id=1, source_target_pairs={{0,1},{1,0},{2,3},{3,2},{4,5},{5,4},{6,7},{7,6},{8,9},{9,8},{10,11... | collective-permute-start | bytes 1032200 | tf_op jit(solution)/shard_map/ppermute | solution.py:224
  31.6 4.1 %collective-permute-start.15 = (bf16[96,1792]{1,0:T(8,128)(2,1)S(1)}, bf16[96,1792]{1,0:T(8,128)(2,1)S(1)}, u32[]{:S(2)}, u32[]{:S(2)}) collective-permute-start(bf16[96,1792]{1,0:T(8,128)(2,1)S(1)} %get-tuple-element.36), channel_id=1, source_target_pairs={{0,1},{1,0},{2,3},{3,2},{4,5},{5,4},{6,7},{7,6},{8,9},{9,8},{10,11... | collective-permute-start | bytes 1032200 | tf_op jit(solution)/shard_map/ppermute | solution.py:224
  34.0 6.9 %collective-permute-start.14 = (bf16[96,1792]{1,0:T(8,128)(2,1)S(1)}, bf16[96,1792]{1,0:T(8,128)(2,1)S(1)}, u32[]{:S(2)}, u32[]{:S(2)}) collective-permute-start(bf16[96,1792]{1,0:T(8,128)(2,1)S(1)} %pack_kernel.7.refs_0_), channel_id=1, source_target_pairs={{0,1},{1,0},{2,3},{3,2},{4,5},{5,4},{6,7},{7,6},{8,9},{9,8},{10,11... | collective-permute-start | bytes 1032200 | tf_op jit(solution)/shard_map/ppermute | solution.py:224
  34.0 6.8 %collective-permute-start.9 = (bf16[96,896]{1,0:T(8,128)(2,1)S(1)}, bf16[96,896]{1,0:T(8,128)(2,1)S(1)}, u32[]{:S(2)}, u32[]{:S(2)}) collective-permute-start(bf16[96,896]{1,0:T(8,128)(2,1)S(1)} %get-tuple-element.34), channel_id=1, source_target_pairs={{0,2},{1,3},{2,0},{3,1},{4,6},{5,7},{6,4},{7,5},{8,10},{9,11},{10,... | collective-permute-start | bytes 516104 | tf_op jit(solution)/shard_map/ppermute | solution.py:224
  43.5 1.7 %collective-permute-start.18 = (bf16[96,1792]{1,0:T(8,128)(2,1)S(1)}, bf16[96,1792]{1,0:T(8,128)(2,1)S(1)}, u32[]{:S(2)}, u32[]{:S(2)}) collective-permute-start(bf16[96,1792]{1,0:T(8,128)(2,1)S(1)} %get-tuple-element.40), channel_id=1, source_target_pairs={{0,1},{1,0},{2,3},{3,2},{4,5},{5,4},{6,7},{7,6},{8,9},{9,8},{10,11... | collective-permute-start | bytes 1032200 | tf_op jit(solution)/shard_map/ppermute | solution.py:224
  43.5 7.2 %collective-permute-start.17 = (bf16[96,896]{1,0:T(8,128)(2,1)S(1)}, bf16[96,896]{1,0:T(8,128)(2,1)S(1)}, u32[]{:S(2)}, u32[]{:S(2)}) collective-permute-start(bf16[96,896]{1,0:T(8,128)(2,1)S(1)} %get-tuple-element.39), channel_id=1, source_target_pairs={{0,2},{1,3},{2,0},{3,1},{4,6},{5,7},{6,4},{7,5},{8,10},{9,11},{10,... | collective-permute-start | bytes 516104 | tf_op jit(solution)/shard_map/ppermute | solution.py:224
  45.2 9.2 %collective-permute-start.20 = (bf16[96,896]{1,0:T(8,128)(2,1)S(1)}, bf16[96,896]{1,0:T(8,128)(2,1)S(1)}, u32[]{:S(2)}, u32[]{:S(2)}) collective-permute-start(bf16[96,896]{1,0:T(8,128)(2,1)S(1)} %get-tuple-element.42), channel_id=1, source_target_pairs={{0,2},{1,3},{2,0},{3,1},{4,6},{5,7},{6,4},{7,5},{8,10},{9,11},{10,... | collective-permute-start | bytes 516104 | tf_op jit(solution)/shard_map/ppermute | solution.py:224
  46.8 10.9 %collective-permute-start.8 = (bf16[96,896]{1,0:T(8,128)(2,1)S(1)}, bf16[96,896]{1,0:T(8,128)(2,1)S(1)}, u32[]{:S(2)}, u32[]{:S(2)}) collective-permute-start(bf16[96,896]{1,0:T(8,128)(2,1)S(1)} %get-tuple-element.33), channel_id=1, source_target_pairs={{0,2},{1,3},{2,0},{3,1},{4,6},{5,7},{6,4},{7,5},{8,10},{9,11},{10,... | collective-permute-start | bytes 516104 | tf_op jit(solution)/shard_map/ppermute | solution.py:224
  47.3 10.4 %collective-permute-start.16 = (bf16[96,896]{1,0:T(8,128)(2,1)S(1)}, bf16[96,896]{1,0:T(8,128)(2,1)S(1)}, u32[]{:S(2)}, u32[]{:S(2)}) collective-permute-start(bf16[96,896]{1,0:T(8,128)(2,1)S(1)} %chip_sum_kernel.3.refs_2_), channel_id=1, source_target_pairs={{0,12},{4,0},{8,4},{12,8},{1,13},{5,1},{9,5},{13,9},{2,14},{6,2},{... | collective-permute-start | bytes 516104 | tf_op jit(solution)/shard_map/ppermute | solution.py:231
  50.8 13.4 %collective-permute-start.19 = (bf16[96,896]{1,0:T(8,128)(2,1)S(1)}, bf16[96,896]{1,0:T(8,128)(2,1)S(1)}, u32[]{:S(2)}, u32[]{:S(2)}) collective-permute-start(bf16[96,896]{1,0:T(8,128)(2,1)S(1)} %chip_sum_kernel.4), channel_id=1, source_target_pairs={{0,8},{4,12},{8,0},{12,4},{1,9},{5,13},{9,1},{13,5},{2,10},{6,14},... | collective-permute-start | bytes 516104 | tf_op jit(solution)/shard_map/ppermute | solution.py:231
  54.5 9.7 %collective-permute-start.21 = (bf16[96,896]{1,0:T(8,128)(2,1)S(1)}, bf16[96,896]{1,0:T(8,128)(2,1)S(1)}, u32[]{:S(2)}, u32[]{:S(2)}) collective-permute-start(bf16[96,896]{1,0:T(8,128)(2,1)S(1)} %chip_sum_kernel.5), channel_id=1, source_target_pairs={{0,4},{4,8},{8,12},{12,0},{1,5},{5,9},{9,13},{13,1},{2,6},{6,10},{... | collective-permute-start | bytes 516104 | tf_op jit(solution)/shard_map/ppermute | solution.py:231

commit v7 on v5

--- a/solution.py
+++ b/solution.py
@@ -59,7 +59,9 @@
         copy.wait()
 
 
-def local_call(kernel, out_shape, operands, others=(), in_specs=None, limit=4 * MIB, **kwargs):
+def local_call(
+    kernel, out_shape, operands, others=(), in_specs=None, limit=4 * MIB, cost=0.5, **kwargs
+):
     count = len(operands)
 
     name = getattr(kernel, "func", kernel).__name__
@@ -74,6 +76,9 @@
         in_specs=list(in_specs or [VMEM] * count) + [pl.BlockSpec(memory_space=pl.ANY)] * len(others),
         out_specs=jax.tree.map(lambda _: VMEM, out_shape),
         compiler_params=pltpu.CompilerParams(vmem_limit_bytes=limit),
+        cost_estimate=pl.CostEstimate(
+            flops=int(cost * 1.15e9), bytes_accessed=0, transcendentals=0
+        ),
         **kwargs,
     )(*operands, *others)
 
@@ -103,9 +108,7 @@
         in_specs=[VMEM, VMEM, HBM, HBM],
         scratch_shapes=[pltpu.SemaphoreType.DMA((2,))],
         limit=50 * MIB,
-        cost_estimate=pl.CostEstimate(
-            flops=0, bytes_accessed=4 * up_t.size, transcendentals=0
-        ),
+        cost=4,
     )
 
 
@@ -164,9 +167,7 @@
             pltpu.VMEM((rows, model), jnp.bfloat16),
             pltpu.VMEM((rows, model), jnp.float32),
         ],
-        cost_estimate=pl.CostEstimate(
-            flops=8 * chip.size * up_t.shape[0], bytes_accessed=0, transcendentals=0
-        ),
+        cost=2.6,
     )
 
 
@@ -186,6 +187,7 @@
         + [jax.ShapeDtypeStruct((rows // count, width), jnp.bfloat16)] * count,
         (keep, got),
         others,
+        cost=2,
     )
 
 
@@ -200,6 +202,7 @@
         jax.ShapeDtypeStruct(got.shape, jnp.bfloat16),
         (own, got),
         others,
+        cost=2,
     )
 
 
@@ -232,25 +235,51 @@
             array, "expert", [(i, (i + by) % experts_n) for i in range(experts_n)]
         )
 
-    steps = (3, 2, 1)
-    order = [step for step in steps if step < experts_n] + [0]
-    blocks = {0: tokens} | {step: shift(tokens, step) for step in order[:-1]}
     columns, up_t, down = prepare(
         expert_ids.T, weight_codes.T, up_local.T, down_local, experts_n, capacity
     )
-    blocks[order[0]] = after(blocks[order[0]], columns)
-    others = {step: swap(block, 2) for step, block in blocks.items()}
-
-    chips, sums, parts = {}, {}, {}
-    for step in order:
-        waits = [] if chips else [others[0]]
+    blocks, others, chips, kept, sums, added, parts = {}, {}, {}, {}, {}, {}, {}
+
+    def arrive(step, source, by, waits):
+        blocks[step] = shift(source, by) if step else tokens
+        for wait in waits:
+            blocks[step] = after(blocks[step], wait)
+        others[step] = swap(blocks[step], 2)
+
+    def lay(step, waits):
         chips[step] = pack([(blocks[step], others[step])], waits)
-    for step in order:
-        keep, send = expert_rows(chips[step], swap(chips[step], 1), up_t, down, ())
-        own, away = core_sum(keep, swap(send, 1), 1, ())
+
+    def run(step, waits):
+        kept[step] = expert_rows(chips[step], swap(chips[step], 1), up_t, down, waits)
+
+    def leave(step, waits):
+        keep, send = kept[step]
+        own, away = core_sum(keep, swap(send, 1), 1, waits)
         sums[step] = own, swap(away, 2)
-    for step in order[:-1]:
-        parts[step] = shift(chip_sum(*sums[step], 0, ()), -step)
+
+    def give(step, waits):
+        added[step] = chip_sum(*sums[step], 0, waits)
+        parts[step] = shift(added[step], -step)
+
+    arrive(0, tokens, 0, [])
+    arrive(1, tokens, 1, [columns])
+    arrive(3, tokens, -1, [columns])
+    lay(0, [blocks[1], blocks[3]])
+    run(0, [])
+    arrive(2, blocks[1], 1, [kept[0][0]])
+    lay(1, [kept[0][0], blocks[2], others[3]])
+    run(1, [])
+    lay(3, [chips[1]])
+    run(3, [kept[1][0]])
+    lay(2, [kept[3][0]])
+    leave(1, [])
+    run(2, [sums[1][0], chips[2]])
+    leave(3, [kept[2][0]])
+    give(1, [sums[3][0]])
+    leave(2, [added[1]])
+    leave(0, [sums[2][0]])
+    give(3, [sums[2][0]])
+    give(2, [added[3]])
     return combine(columns, *sums[0], [parts[step] for step in range(1, experts_n)], ())
 
 
@@ -292,7 +321,7 @@
 def body(tokens, expert_ids, weight_codes, up_weight, down_weight):
     rows = tokens.shape[0]
     capacity = 4 * rows // lax.axis_size("expert")
-    whole = capacity >= rows and lax.axis_size("tensor") == 4
+    whole = capacity >= rows and lax.axis_size("expert") == lax.axis_size("tensor") == 4
     plan = whole_blocks if whole else slotted
     return plan(tokens, expert_ids, weight_codes, up_weight[0], down_weight[0], capacity)
 

time: 66.1 us -> 59.4 us (0.90)
  waiting for transfers between devices: 32.9 us -> 22.3 us
  starting transfers between devices: 16.7 us -> 20.6 us
    ppermute x16, waiting for transfers between devices: 20 us -> 4.9 us  [swap(): return lax.ppermute(array, 'tensor', [(i, i ^ bit) for i in range(4)])]
    ppermute x6, waiting for transfers between devices: 12.8 us -> 17.4 us  [shift(): lax.ppermute(array, 'expert', [(i, (i + by) % experts_n) for i in range(e...]
    ppermute x6, starting transfers between devices: 6.25 us -> 9.51 us  [shift(): lax.ppermute(array, 'expert', [(i, (i + by) % experts_n) for i in range(e...]
  transfers between devices with their start and end apart: 22 -> 22, of which waited for: 9 -> 8; matrix products, arithmetic and copies ran while one was open for 0% -> 0% of each run, Pallas kernels for 23% -> 26%
where the time goes in v7:
time: 59.4 us; the launch traced here: 59.2 us
  waiting for transfers between devices  22.3 us (38%)
  starting transfers between devices  20.6 us (35%)
  Pallas kernels  16.2 us (27%)
    ppermute x6, waiting for transfers between devices, shift(): lax.ppermute(array, 'expert', [(i, (i + by) % experts_n) for i in range(e...  17.4 us
    pallas_call x17, Pallas kernels, local_call(): pl.pallas_call(body_of, name=name, out_shape=out_shape, in_specs=list(in_...  16.2 us
    ppermute x16, starting transfers between devices, swap(): return lax.ppermute(array, 'tensor', [(i, i ^ bit) for i in range(4)])  11.1 us
    ppermute x6, starting transfers between devices, shift(): lax.ppermute(array, 'expert', [(i, (i + by) % experts_n) for i in range(e...  9.51 us
    ppermute x16, waiting for transfers between devices, swap(): return lax.ppermute(array, 'tensor', [(i, i ^ bit) for i in range(4)])  4.9 us
  transfers between devices with their start and end apart: 22, of which 8 were waited for; matrix products, arithmetic and copies ran while one was open for 0% of the time, Pallas kernels for 26%

profile of v7, /device:TPU:0, one launch (start us, length us, event | category | flops | bytes accessed | tf_op | source)
XLA Modules:
  0.0 59.2 jit_solution(17265510534669116801)
XLA Ops:
  0.0 3.0 %collective-permute-start.1 = (bf16[96,896]{1,0:T(8,128)(2,1)}, bf16[96,896]{1,0:T(8,128)(2,1)S(1)}, u32[]{:S(2)}, u32[]{:S(2)}) collective-permute-start(bf16[96,896]{1,0:T(8,128)(2,1)} %refs_0_.1), channel_id=1, source_target_pairs={{0,4},{4,8},{8,12},{12,0},{1,5},{5,9},{9,13},{13,1},{2,6},{6,10},{... | collective-permute-start | bytes 516104 | tf_op jit(solution)/shard_map/ppermute | solution.py:234
  3.0 1.5 %collective-permute-start = (bf16[96,896]{1,0:T(8,128)(2,1)}, bf16[96,896]{1,0:T(8,128)(2,1)S(1)}, u32[]{:S(2)}, u32[]{:S(2)}) collective-permute-start(bf16[96,896]{1,0:T(8,128)(2,1)} %refs_0_.1), channel_id=1, source_target_pairs={{0,2},{1,3},{2,0},{3,1},{4,6},{5,7},{6,4},{7,5},{8,10},{9,11},{10,... | collective-permute-start | bytes 516104 | tf_op jit(solution)/shard_map/ppermute | solution.py:227
  4.5 2.2 %collective-permute-start.2 = (bf16[96,896]{1,0:T(8,128)(2,1)}, bf16[96,896]{1,0:T(8,128)(2,1)S(1)}, u32[]{:S(2)}, u32[]{:S(2)}) collective-permute-start(bf16[96,896]{1,0:T(8,128)(2,1)} %refs_0_.1), channel_id=1, source_target_pairs={{0,12},{4,0},{8,4},{12,8},{1,13},{5,1},{9,5},{13,9},{2,14},{6,2},{... | collective-permute-start | bytes 516104 | tf_op jit(solution)/shard_map/ppermute | solution.py:234
  6.8 4.3 %prepare_kernel.1 = (f32[4,96,128]{2,1,0:T(8,128)S(1)}, bf16[608,3584]{1,0:T(8,128)(2,1)S(1)}, bf16[608,3584]{1,0:T(8,128)(2,1)S(1)}) custom-call(s32[2,96]{1,0:T(2,128)} %bitcast.8, s32[2,96]{1,0:T(2,128)} %bitcast.9, bf16[608,3584]{1,0:T(8,128)(2,1)} %bitcast.6, bf16[608,3584]{1,0:T(8,128)(2,1)} %bitcast.7), custom_call_target="tpu_custom_call" | custom-call | flops 4600000000 | tf_op jit(solution)/shard_map/prepare_kernel/pallas_call | solution.py:72
  11.1 2.2 %collective-permute-done.2.refs_0_ = bf16[96,896]{1,0:T(8,128)(2,1)S(1)} collective-permute-done((bf16[96,896]{1,0:T(8,128)(2,1)}, bf16[96,896]{1,0:T(8,128)(2,1)S(1)}, u32[]{:S(2)}, u32[]{:S(2)}) %collective-permute-start.2) | collective-permute-done | bytes 172064 | tf_op jit(solution)/shard_map/ppermute | solution.py:234
  13.4 1.2 %collective-permute-start.7 = (bf16[96,896]{1,0:T(8,128)(2,1)S(1)}, bf16[96,896]{1,0:T(8,128)(2,1)S(1)}, u32[]{:S(2)}, u32[]{:S(2)}) collective-permute-start(bf16[96,896]{1,0:T(8,128)(2,1)S(1)} %shard_map.56.refs_3_.refs_0_), channel_id=1, source_target_pairs={{0,2},{1,3},{2,0},{3,1},{4,6},{5,7},{6,4},{7,5},{8,10},{9,11},{10,... | collective-permute-start | bytes 516104 | tf_op jit(solution)/shard_map/ppermute | solution.py:227
  16.1 2.6 %expert_kernel.4 = (f32[96,1792]{1,0:T(8,128)S(1)}, bf16[96,1792]{1,0:T(8,128)(2,1)S(1)}) custom-call(bf16[96,1792]{1,0:T(8,128)(2,1)S(1)} %pack_kernel.4.refs_0_, bf16[96,1792]{1,0:T(8,128)(2,1)S(1)} %collective-permute-done.3.refs_1_, bf16[608,3584]{1,0:T(8,128)(2,1)S(1)} %get-tuple-element.25.refs_2_, bf16[608,3584]{1,0:T(8,128)(2,1)S(1)} %get-tuple-element.26.refs_3_), custom_call_target="tpu_custom_call" | custom-call | flops 2990000128 | tf_op jit(solution)/shard_map/expert_kernel/pallas_call | solution.py:72
  18.7 4.8 %collective-permute-done.5.refs_0_ = bf16[96,896]{1,0:T(8,128)(2,1)S(1)} collective-permute-done((bf16[96,896]{1,0:T(8,128)(2,1)S(1)}, bf16[96,896]{1,0:T(8,128)(2,1)S(1)}, u32[]{:S(2)}, u32[]{:S(2)}) %collective-permute-start.5) | collective-permute-done | bytes 172064 | tf_op jit(solution)/shard_map/ppermute | solution.py:234
  24.6 1.2 %collective-permute-start.6 = (bf16[96,896]{1,0:T(8,128)(2,1)S(1)}, bf16[96,896]{1,0:T(8,128)(2,1)S(1)}, u32[]{:S(2)}, u32[]{:S(2)}) collective-permute-start(bf16[96,896]{1,0:T(8,128)(2,1)S(1)} %shard_map.57.refs_3_.refs_0_), channel_id=1, source_target_pairs={{0,2},{1,3},{2,0},{3,1},{4,6},{5,7},{6,4},{7,5},{8,10},{9,11},{10,... | collective-permute-start | bytes 516104 | tf_op jit(solution)/shard_map/ppermute | solution.py:227
  25.8 2.6 %expert_kernel.5 = (f32[96,1792]{1,0:T(8,128)S(1)}, bf16[96,1792]{1,0:T(8,128)(2,1)S(1)}) custom-call(bf16[96,1792]{1,0:T(8,128)(2,1)S(1)} %pack_kernel.5.refs_2_.refs_0_, bf16[96,1792]{1,0:T(8,128)(2,1)S(1)} %collective-permute-done.10.refs_1_, bf16[608,3584]{1,0:T(8,128)(2,1)S(1)} %get-tuple-element.25.refs_2_, bf16[608,3584]{1,0:T(8,128)(2,1)S(1)} %get-tuple-element.26.refs_3_), custom_call_target="tpu_custom_call" | custom-call | flops 2990000128 | tf_op jit(solution)/shard_map/expert_kernel/pallas_call | solution.py:72
  28.5 2.6 %expert_kernel.6 = (f32[96,1792]{1,0:T(8,128)S(1)}, bf16[96,1792]{1,0:T(8,128)(2,1)S(1)}) custom-call(bf16[96,1792]{1,0:T(8,128)(2,1)S(1)} %pack_kernel.6.refs_0_, bf16[96,1792]{1,0:T(8,128)(2,1)S(1)} %collective-permute-done.9.refs_1_, bf16[608,3584]{1,0:T(8,128)(2,1)S(1)} %get-tuple-element.25.refs_2_, bf16[608,3584]{1,0:T(8,128)(2,1)S(1)} %get-tuple-element.26.refs_3_, ...), custom_call_target="tpu_custom_call" | custom-call | flops 2990000128 | tf_op jit(solution)/shard_map/expert_kernel/pallas_call | solution.py:72
  32.3 1.1 %collective-permute-start.14 = (bf16[96,896]{1,0:T(8,128)(2,1)S(1)}, bf16[96,896]{1,0:T(8,128)(2,1)S(1)}, u32[]{:S(2)}, u32[]{:S(2)}) collective-permute-start(bf16[96,896]{1,0:T(8,128)(2,1)S(1)} %get-tuple-element.35), channel_id=1, source_target_pairs={{0,2},{1,3},{2,0},{3,1},{4,6},{5,7},{6,4},{7,5},{8,10},{9,11},{10,... | collective-permute-start | bytes 516104 | tf_op jit(solution)/shard_map/ppermute | solution.py:227
  33.5 2.6 %expert_kernel.7 = (f32[96,1792]{1,0:T(8,128)S(1)}, bf16[96,1792]{1,0:T(8,128)(2,1)S(1)}) custom-call(bf16[96,1792]{1,0:T(8,128)(2,1)S(1)} %pack_kernel.7.refs_0_.refs_5_, bf16[96,1792]{1,0:T(8,128)(2,1)S(1)} %collective-permute-done.11.refs_1_, bf16[608,3584]{1,0:T(8,128)(2,1)S(1)} %get-tuple-element.25.refs_2_, ...), custom_call_target="tpu_custom_call" | custom-call | flops 2990000128 | tf_op jit(solution)/shard_map/expert_kernel/pallas_call | solution.py:72
  36.3 1.1 %collective-permute-start.19 = (bf16[96,896]{1,0:T(8,128)(2,1)S(1)}, bf16[96,896]{1,0:T(8,128)(2,1)S(1)}, u32[]{:S(2)}, u32[]{:S(2)}) collective-permute-start(bf16[96,896]{1,0:T(8,128)(2,1)S(1)} %get-tuple-element.42), channel_id=1, source_target_pairs={{0,2},{1,3},{2,0},{3,1},{4,6},{5,7},{6,4},{7,5},{8,10},{9,11},{10,... | collective-permute-start | bytes 516104 | tf_op jit(solution)/shard_map/ppermute | solution.py:227
  37.3 1.4 %collective-permute-done.14.refs_1_ = bf16[96,896]{1,0:T(8,128)(2,1)S(1)} collective-permute-done((bf16[96,896]{1,0:T(8,128)(2,1)S(1)}, bf16[96,896]{1,0:T(8,128)(2,1)S(1)}, u32[]{:S(2)}, u32[]{:S(2)}) %collective-permute-start.14) | collective-permute-done | bytes 172064 | tf_op jit(solution)/shard_map/ppermute | solution.py:227
  38.8 2.1 %collective-permute-start.17 = (bf16[96,896]{1,0:T(8,128)(2,1)S(1)}, bf16[96,896]{1,0:T(8,128)(2,1)S(1)}, u32[]{:S(2)}, u32[]{:S(2)}) collective-permute-start(bf16[96,896]{1,0:T(8,128)(2,1)S(1)} %chip_sum_kernel.3.refs_2_), channel_id=1, source_target_pairs={{0,12},{4,0},{8,4},{12,8},{1,13},{5,1},{9,5},{13,9},{2,14},{6,2},{... | collective-permute-start | bytes 516104 | tf_op jit(solution)/shard_map/ppermute | solution.py:234
  41.0 1.2 %collective-permute-start.18 = (bf16[96,896]{1,0:T(8,128)(2,1)S(1)}, bf16[96,896]{1,0:T(8,128)(2,1)S(1)}, u32[]{:S(2)}, u32[]{:S(2)}) collective-permute-start(bf16[96,896]{1,0:T(8,128)(2,1)S(1)} %get-tuple-element.41), channel_id=1, source_target_pairs={{0,2},{1,3},{2,0},{3,1},{4,6},{5,7},{6,4},{7,5},{8,10},{9,11},{10,... | collective-permute-start | bytes 516104 | tf_op jit(solution)/shard_map/ppermute | solution.py:227
  42.2 1.3 %collective-permute-done.19.refs_1_ = bf16[96,896]{1,0:T(8,128)(2,1)S(1)} collective-permute-done((bf16[96,896]{1,0:T(8,128)(2,1)S(1)}, bf16[96,896]{1,0:T(8,128)(2,1)S(1)}, u32[]{:S(2)}, u32[]{:S(2)}) %collective-permute-start.19) | collective-permute-done | bytes 172064 | tf_op jit(solution)/shard_map/ppermute | solution.py:227
  43.5 0.9 %collective-permute-start.21 = (bf16[96,896]{1,0:T(8,128)(2,1)S(1)}, bf16[96,896]{1,0:T(8,128)(2,1)S(1)}, u32[]{:S(2)}, u32[]{:S(2)}) collective-permute-start(bf16[96,896]{1,0:T(8,128)(2,1)S(1)} %chip_sum_kernel.4.refs_2_), channel_id=1, source_target_pairs={{0,4},{4,8},{8,12},{12,0},{1,5},{5,9},{9,13},{13,1},{2,6},{6,10},{... | collective-permute-start | bytes 516104 | tf_op jit(solution)/shard_map/ppermute | solution.py:234
  44.5 1.1 %collective-permute-start.16 = (bf16[96,896]{1,0:T(8,128)(2,1)S(1)}, bf16[96,896]{1,0:T(8,128)(2,1)S(1)}, u32[]{:S(2)}, u32[]{:S(2)}) collective-permute-start(bf16[96,896]{1,0:T(8,128)(2,1)S(1)} %get-tuple-element.40), channel_id=1, source_target_pairs={{0,2},{1,3},{2,0},{3,1},{4,6},{5,7},{6,4},{7,5},{8,10},{9,11},{10,... | collective-permute-start | bytes 516104 | tf_op jit(solution)/shard_map/ppermute | solution.py:227
  45.6 1.7 %collective-permute-done.18.refs_1_ = bf16[96,896]{1,0:T(8,128)(2,1)S(1)} collective-permute-done((bf16[96,896]{1,0:T(8,128)(2,1)S(1)}, bf16[96,896]{1,0:T(8,128)(2,1)S(1)}, u32[]{:S(2)}, u32[]{:S(2)}) %collective-permute-start.18) | collective-permute-done | bytes 172064 | tf_op jit(solution)/shard_map/ppermute | solution.py:227
  47.9 4.0 %collective-permute-done.21.refs_5_ = bf16[96,896]{1,0:T(8,128)(2,1)S(1)} collective-permute-done((bf16[96,896]{1,0:T(8,128)(2,1)S(1)}, bf16[96,896]{1,0:T(8,128)(2,1)S(1)}, u32[]{:S(2)}, u32[]{:S(2)}) %collective-permute-start.21) | collective-permute-done | bytes 172064 | tf_op jit(solution)/shard_map/ppermute | solution.py:234
  51.9 6.4 %collective-permute-done.20.refs_4_ = bf16[96,896]{1,0:T(8,128)(2,1)S(1)} collective-permute-done((bf16[96,896]{1,0:T(8,128)(2,1)S(1)}, bf16[96,896]{1,0:T(8,128)(2,1)S(1)}, u32[]{:S(2)}, u32[]{:S(2)}) %collective-permute-start.20) | collective-permute-done | bytes 172064 | tf_op jit(solution)/shard_map/ppermute | solution.py:234
  58.4 0.9 %combine_kernel.1 = bf16[96,896]{1,0:T(8,128)(2,1)} custom-call(f32[4,96,128]{2,1,0:T(8,128)S(1)} %get-tuple-element.24.refs_1_.refs_0_, f32[96,896]{1,0:T(8,128)S(1)} %get-tuple-element.39.refs_1_, bf16[96,896]{1,0:T(8,128)(2,1)S(1)} %collective-permute-done.16.refs_2_, bf16[96,896]{1,0:T(8,128)(2,1)S(1)} %collective-permute-done.17.refs_3_, ...), custom_call_target="tpu_custom_call" | custom-call | flops 575000000 | tf_op jit(solution)/shard_map/combine_kernel/pallas_call | solution.py:72
  (42 shorter events, 4.9 us)
Async XLA Ops:
  0.0 11.1 %collective-permute-start.1 = (bf16[96,896]{1,0:T(8,128)(2,1)}, bf16[96,896]{1,0:T(8,128)(2,1)S(1)}, u32[]{:S(2)}, u32[]{:S(2)}) collective-permute-start(bf16[96,896]{1,0:T(8,128)(2,1)} %refs_0_.1), channel_id=1, source_target_pairs={{0,4},{4,8},{8,12},{12,0},{1,5},{5,9},{9,13},{13,1},{2,6},{6,10},{... | collective-permute-start | bytes 516104 | tf_op jit(solution)/shard_map/ppermute | solution.py:234
  3.0 10.3 %collective-permute-start = (bf16[96,896]{1,0:T(8,128)(2,1)}, bf16[96,896]{1,0:T(8,128)(2,1)S(1)}, u32[]{:S(2)}, u32[]{:S(2)}) collective-permute-start(bf16[96,896]{1,0:T(8,128)(2,1)} %refs_0_.1), channel_id=1, source_target_pairs={{0,2},{1,3},{2,0},{3,1},{4,6},{5,7},{6,4},{7,5},{8,10},{9,11},{10,... | collective-permute-start | bytes 516104 | tf_op jit(solution)/shard_map/ppermute | solution.py:227
  4.5 8.8 %collective-permute-start.2 = (bf16[96,896]{1,0:T(8,128)(2,1)}, bf16[96,896]{1,0:T(8,128)(2,1)S(1)}, u32[]{:S(2)}, u32[]{:S(2)}) collective-permute-start(bf16[96,896]{1,0:T(8,128)(2,1)} %refs_0_.1), channel_id=1, source_target_pairs={{0,12},{4,0},{8,4},{12,8},{1,13},{5,1},{9,5},{13,9},{2,14},{6,2},{... | collective-permute-start | bytes 516104 | tf_op jit(solution)/shard_map/ppermute | solution.py:234
  6.8 6.6 %copy-start = (bf16[96,896]{1,0:T(8,128)(2,1)S(1)}, bf16[96,896]{1,0:T(8,128)(2,1)}, u32[]{:S(2)}) copy-start(bf16[96,896]{1,0:T(8,128)(2,1)} %refs_0_.1) | copy-start | bytes 516100
  13.4 2.7 %collective-permute-start.3 = (bf16[96,1792]{1,0:T(8,128)(2,1)S(1)}, bf16[96,1792]{1,0:T(8,128)(2,1)S(1)}, u32[]{:S(2)}, u32[]{:S(2)}) collective-permute-start(bf16[96,1792]{1,0:T(8,128)(2,1)S(1)} %pack_kernel.4.refs_0_), channel_id=1, source_target_pairs={{0,1},{1,0},{2,3},{3,2},{4,5},{5,4},{6,7},{7,6},{8,9},{9,8},{10,11... | collective-permute-start | bytes 1032200 | tf_op jit(solution)/shard_map/ppermute | solution.py:227
  13.4 10.1 %collective-permute-start.7 = (bf16[96,896]{1,0:T(8,128)(2,1)S(1)}, bf16[96,896]{1,0:T(8,128)(2,1)S(1)}, u32[]{:S(2)}, u32[]{:S(2)}) collective-permute-start(bf16[96,896]{1,0:T(8,128)(2,1)S(1)} %shard_map.56.refs_3_.refs_0_), channel_id=1, source_target_pairs={{0,2},{1,3},{2,0},{3,1},{4,6},{5,7},{6,4},{7,5},{8,10},{9,11},{10,... | collective-permute-start | bytes 516104 | tf_op jit(solution)/shard_map/ppermute | solution.py:227
  14.7 9.2 %collective-permute-start.8 = (bf16[96,896]{1,0:T(8,128)(2,1)S(1)}, bf16[96,896]{1,0:T(8,128)(2,1)S(1)}, u32[]{:S(2)}, u32[]{:S(2)}) collective-permute-start(bf16[96,896]{1,0:T(8,128)(2,1)S(1)} %shard_map.55.refs_2_.refs_0_), channel_id=1, source_target_pairs={{0,2},{1,3},{2,0},{3,1},{4,6},{5,7},{6,4},{7,5},{8,10},{9,11},{10,... | collective-permute-start | bytes 516104 | tf_op jit(solution)/shard_map/ppermute | solution.py:227
  15.5 8.0 %collective-permute-start.5 = (bf16[96,896]{1,0:T(8,128)(2,1)S(1)}, bf16[96,896]{1,0:T(8,128)(2,1)S(1)}, u32[]{:S(2)}, u32[]{:S(2)}) collective-permute-start(bf16[96,896]{1,0:T(8,128)(2,1)S(1)} %shard_map.55.refs_2_.refs_0_), channel_id=1, source_target_pairs={{0,4},{4,8},{8,12},{12,0},{1,5},{5,9},{9,13},{13,1},{2,6},{6,10},{... | collective-permute-start | bytes 516104 | tf_op jit(solution)/shard_map/ppermute | solution.py:234
  23.9 1.9 %collective-permute-start.10 = (bf16[96,1792]{1,0:T(8,128)(2,1)S(1)}, bf16[96,1792]{1,0:T(8,128)(2,1)S(1)}, u32[]{:S(2)}, u32[]{:S(2)}) collective-permute-start(bf16[96,1792]{1,0:T(8,128)(2,1)S(1)} %pack_kernel.5.refs_2_.refs_0_), channel_id=1, source_target_pairs={{0,1},{1,0},{2,3},{3,2},{4,5},{5,4},{6,7},{7,6},{8,9},{9,8},{10,11... | collective-permute-start | bytes 1032200 | tf_op jit(solution)/shard_map/ppermute | solution.py:227
  24.1 4.5 %collective-permute-start.9 = (bf16[96,1792]{1,0:T(8,128)(2,1)S(1)}, bf16[96,1792]{1,0:T(8,128)(2,1)S(1)}, u32[]{:S(2)}, u32[]{:S(2)}) collective-permute-start(bf16[96,1792]{1,0:T(8,128)(2,1)S(1)} %pack_kernel.6.refs_0_), channel_id=1, source_target_pairs={{0,1},{1,0},{2,3},{3,2},{4,5},{5,4},{6,7},{7,6},{8,9},{9,8},{10,11... | collective-permute-start | bytes 1032200 | tf_op jit(solution)/shard_map/ppermute | solution.py:227
  24.6 6.5 %collective-permute-start.6 = (bf16[96,896]{1,0:T(8,128)(2,1)S(1)}, bf16[96,896]{1,0:T(8,128)(2,1)S(1)}, u32[]{:S(2)}, u32[]{:S(2)}) collective-permute-start(bf16[96,896]{1,0:T(8,128)(2,1)S(1)} %shard_map.57.refs_3_.refs_0_), channel_id=1, source_target_pairs={{0,2},{1,3},{2,0},{3,1},{4,6},{5,7},{6,4},{7,5},{8,10},{9,11},{10,... | collective-permute-start | bytes 516104 | tf_op jit(solution)/shard_map/ppermute | solution.py:227
  28.4 3.8 %collective-permute-start.12 = (bf16[96,1792]{1,0:T(8,128)(2,1)S(1)}, bf16[96,1792]{1,0:T(8,128)(2,1)S(1)}, u32[]{:S(2)}, u32[]{:S(2)}) collective-permute-start(bf16[96,1792]{1,0:T(8,128)(2,1)S(1)} %get-tuple-element.31), channel_id=1, source_target_pairs={{0,1},{1,0},{2,3},{3,2},{4,5},{5,4},{6,7},{7,6},{8,9},{9,8},{10,11... | collective-permute-start | bytes 1032200 | tf_op jit(solution)/shard_map/ppermute | solution.py:227
  31.2 2.3 %collective-permute-start.11 = (bf16[96,1792]{1,0:T(8,128)(2,1)S(1)}, bf16[96,1792]{1,0:T(8,128)(2,1)S(1)}, u32[]{:S(2)}, u32[]{:S(2)}) collective-permute-start(bf16[96,1792]{1,0:T(8,128)(2,1)S(1)} %pack_kernel.7.refs_0_.refs_5_), channel_id=1, source_target_pairs={{0,1},{1,0},{2,3},{3,2},{4,5},{5,4},{6,7},{7,6},{8,9},{9,8},{10,11... | collective-permute-start | bytes 1032200 | tf_op jit(solution)/shard_map/ppermute | solution.py:227
  31.8 12.7 %collective-permute-start.4 = (bf16[96,1792]{1,0:T(8,128)(2,1)S(1)}, bf16[96,1792]{1,0:T(8,128)(2,1)S(1)}, u32[]{:S(2)}, u32[]{:S(2)}) collective-permute-start(bf16[96,1792]{1,0:T(8,128)(2,1)S(1)} %get-tuple-element.28), channel_id=1, source_target_pairs={{0,1},{1,0},{2,3},{3,2},{4,5},{5,4},{6,7},{7,6},{8,9},{9,8},{10,11... | collective-permute-start | bytes 1032200 | tf_op jit(solution)/shard_map/ppermute | solution.py:227
  31.8 4.3 %collective-permute-start.15 = (bf16[96,1792]{1,0:T(8,128)(2,1)S(1)}, bf16[96,1792]{1,0:T(8,128)(2,1)S(1)}, u32[]{:S(2)}, u32[]{:S(2)}) collective-permute-start(bf16[96,1792]{1,0:T(8,128)(2,1)S(1)} %get-tuple-element.36), channel_id=1, source_target_pairs={{0,1},{1,0},{2,3},{3,2},{4,5},{5,4},{6,7},{7,6},{8,9},{9,8},{10,11... | collective-permute-start | bytes 1032200 | tf_op jit(solution)/shard_map/ppermute | solution.py:227
  32.3 6.4 %collective-permute-start.14 = (bf16[96,896]{1,0:T(8,128)(2,1)S(1)}, bf16[96,896]{1,0:T(8,128)(2,1)S(1)}, u32[]{:S(2)}, u32[]{:S(2)}) collective-permute-start(bf16[96,896]{1,0:T(8,128)(2,1)S(1)} %get-tuple-element.35), channel_id=1, source_target_pairs={{0,2},{1,3},{2,0},{3,1},{4,6},{5,7},{6,4},{7,5},{8,10},{9,11},{10,... | collective-permute-start | bytes 516104 | tf_op jit(solution)/shard_map/ppermute | solution.py:227
  36.1 4.8 %collective-permute-start.13 = (bf16[96,1792]{1,0:T(8,128)(2,1)S(1)}, bf16[96,1792]{1,0:T(8,128)(2,1)S(1)}, u32[]{:S(2)}, u32[]{:S(2)}) collective-permute-start(bf16[96,1792]{1,0:T(8,128)(2,1)S(1)} %get-tuple-element.34), channel_id=1, source_target_pairs={{0,1},{1,0},{2,3},{3,2},{4,5},{5,4},{6,7},{7,6},{8,9},{9,8},{10,11... | collective-permute-start | bytes 1032200 | tf_op jit(solution)/shard_map/ppermute | solution.py:227
  36.3 7.2 %collective-permute-start.19 = (bf16[96,896]{1,0:T(8,128)(2,1)S(1)}, bf16[96,896]{1,0:T(8,128)(2,1)S(1)}, u32[]{:S(2)}, u32[]{:S(2)}) collective-permute-start(bf16[96,896]{1,0:T(8,128)(2,1)S(1)} %get-tuple-element.42), channel_id=1, source_target_pairs={{0,2},{1,3},{2,0},{3,1},{4,6},{5,7},{6,4},{7,5},{8,10},{9,11},{10,... | collective-permute-start | bytes 516104 | tf_op jit(solution)/shard_map/ppermute | solution.py:227
  38.8 9.1 %collective-permute-start.17 = (bf16[96,896]{1,0:T(8,128)(2,1)S(1)}, bf16[96,896]{1,0:T(8,128)(2,1)S(1)}, u32[]{:S(2)}, u32[]{:S(2)}) collective-permute-start(bf16[96,896]{1,0:T(8,128)(2,1)S(1)} %chip_sum_kernel.3.refs_2_), channel_id=1, source_target_pairs={{0,12},{4,0},{8,4},{12,8},{1,13},{5,1},{9,5},{13,9},{2,14},{6,2},{... | collective-permute-start | bytes 516104 | tf_op jit(solution)/shard_map/ppermute | solution.py:234
  41.0 6.3 %collective-permute-start.18 = (bf16[96,896]{1,0:T(8,128)(2,1)S(1)}, bf16[96,896]{1,0:T(8,128)(2,1)S(1)}, u32[]{:S(2)}, u32[]{:S(2)}) collective-permute-start(bf16[96,896]{1,0:T(8,128)(2,1)S(1)} %get-tuple-element.41), channel_id=1, source_target_pairs={{0,2},{1,3},{2,0},{3,1},{4,6},{5,7},{6,4},{7,5},{8,10},{9,11},{10,... | collective-permute-start | bytes 516104 | tf_op jit(solution)/shard_map/ppermute | solution.py:227
  43.5 8.4 %collective-permute-start.21 = (bf16[96,896]{1,0:T(8,128)(2,1)S(1)}, bf16[96,896]{1,0:T(8,128)(2,1)S(1)}, u32[]{:S(2)}, u32[]{:S(2)}) collective-permute-start(bf16[96,896]{1,0:T(8,128)(2,1)S(1)} %chip_sum_kernel.4.refs_2_), channel_id=1, source_target_pairs={{0,4},{4,8},{8,12},{12,0},{1,5},{5,9},{9,13},{13,1},{2,6},{6,10},{... | collective-permute-start | bytes 516104 | tf_op jit(solution)/shard_map/ppermute | solution.py:234
  44.5 7.4 %collective-permute-start.16 = (bf16[96,896]{1,0:T(8,128)(2,1)S(1)}, bf16[96,896]{1,0:T(8,128)(2,1)S(1)}, u32[]{:S(2)}, u32[]{:S(2)}) collective-permute-start(bf16[96,896]{1,0:T(8,128)(2,1)S(1)} %get-tuple-element.40), channel_id=1, source_target_pairs={{0,2},{1,3},{2,0},{3,1},{4,6},{5,7},{6,4},{7,5},{8,10},{9,11},{10,... | collective-permute-start | bytes 516104 | tf_op jit(solution)/shard_map/ppermute | solution.py:227
  47.3 11.0 %collective-permute-start.20 = (bf16[96,896]{1,0:T(8,128)(2,1)S(1)}, bf16[96,896]{1,0:T(8,128)(2,1)S(1)}, u32[]{:S(2)}, u32[]{:S(2)}) collective-permute-start(bf16[96,896]{1,0:T(8,128)(2,1)S(1)} %chip_sum_kernel.5), channel_id=1, source_target_pairs={{0,8},{4,12},{8,0},{12,4},{1,9},{5,13},{9,1},{13,5},{2,10},{6,14},... | collective-permute-start | bytes 516104 | tf_op jit(solution)/shard_map/ppermute | solution.py:234

commit v8 on v7

--- a/solution.py
+++ b/solution.py
@@ -120,13 +120,14 @@
         packed[at : at + rows, column : column + width] = ref[...]
 
 
-def pack(pairs, others):
+def pack(pairs, others, cost):
     rows, width = pairs[0][0].shape
     return local_call(
         pack_kernel,
         jax.ShapeDtypeStruct((len(pairs) * rows, 2 * width), pairs[0][0].dtype),
         [array for pair in pairs for array in pair],
         others,
+        cost=cost,
     )
 
 
@@ -206,20 +207,35 @@
     )
 
 
-def combine_kernel(columns, own, got, *rest):
-    parts, mixed = rest[:-1], rest[-1]
-    total = columns[0, :, 0:1] * (own[...] + got[...].astype(jnp.float32))
-    for step, part in enumerate(parts, 1):
-        total += columns[step, :, 0:1] * part[...].astype(jnp.float32)
-    mixed[...] = total.astype(mixed.dtype)
-
-
-def combine(columns, own, got, parts, others):
-    return local_call(
-        combine_kernel,
-        jax.ShapeDtypeStruct(own.shape, jnp.bfloat16),
+def weigh_kernel(steps, columns, own, got, *rest):
+    parts, out = rest[:-1], rest[-1]
+    for at in range(0, out.shape[1], 128):
+        here = slice(at, at + 128)
+        total = own[:, here]
+        if got is not None:
+            total = columns[0] * (total + got[:, here].astype(jnp.float32))
+        for step, part in zip(steps, parts):
+            total = total + columns[step] * part[:, here].astype(jnp.float32)
+        out[:, here] = total.astype(out.dtype)
+
+
+def weigh(columns, own, got, steps, parts):
+    return local_call(
+        functools.partial(weigh_kernel, steps),
+        jax.ShapeDtypeStruct(own.shape, jnp.float32),
         (columns, own, got, *parts),
-        others,
+    )
+
+
+def finish_kernel(steps, columns, total, *rest):
+    weigh_kernel(steps, columns, total, None, *rest)
+
+
+def finish(columns, total, steps, parts):
+    return local_call(
+        functools.partial(finish_kernel, steps),
+        jax.ShapeDtypeStruct(total.shape, jnp.bfloat16),
+        (columns, total, *parts),
     )
 
 
@@ -246,41 +262,41 @@
             blocks[step] = after(blocks[step], wait)
         others[step] = swap(blocks[step], 2)
 
-    def lay(step, waits):
-        chips[step] = pack([(blocks[step], others[step])], waits)
-
-    def run(step, waits):
-        kept[step] = expert_rows(chips[step], swap(chips[step], 1), up_t, down, waits)
-
-    def leave(step, waits):
-        keep, send = kept[step]
-        own, away = core_sum(keep, swap(send, 1), 1, waits)
-        sums[step] = own, swap(away, 2)
+    def lay(steps, waits, cost=0.5):
+        chips[steps] = pack([(blocks[step], others[step]) for step in steps], waits, cost)
+
+    def run(steps, waits):
+        chip = chips[steps]
+        kept[steps] = expert_rows(chip, swap(chip, 1), up_t, down, waits)
+
+    def leave(steps, waits):
+        keep, send = kept[steps]
+        own, *aways = core_sum(keep, swap(send, 1), len(steps), waits)
+        for index, step in enumerate(steps):
+            sums[step] = own, swap(aways[index], 2), index
 
     def give(step, waits):
-        added[step] = chip_sum(*sums[step], 0, waits)
+        added[step] = chip_sum(*sums[step], waits)
         parts[step] = shift(added[step], -step)
 
     arrive(0, tokens, 0, [])
     arrive(1, tokens, 1, [columns])
     arrive(3, tokens, -1, [columns])
-    lay(0, [blocks[1], blocks[3]])
-    run(0, [])
-    arrive(2, blocks[1], 1, [kept[0][0]])
-    lay(1, [kept[0][0], blocks[2], others[3]])
-    run(1, [])
-    lay(3, [chips[1]])
-    run(3, [kept[1][0]])
-    lay(2, [kept[3][0]])
-    leave(1, [])
-    run(2, [sums[1][0], chips[2]])
-    leave(3, [kept[2][0]])
-    give(1, [sums[3][0]])
-    leave(2, [added[1]])
-    leave(0, [sums[2][0]])
+    lay((0,), [blocks[1], blocks[3]])
+    run((0,), [])
+    arrive(2, blocks[1], 1, [kept[0,][0]])
+    lay((1, 3), [kept[0,][0], blocks[2]])
+    run((1, 3), [])
+    lay((2,), [kept[1, 3][0]], cost=4)
+    leave((1, 3), [chips[2,]])
+    run((2,), [sums[1][0]])
+    give(1, [kept[2,][0]])
+    leave((2,), [added[1]])
+    leave((0,), [sums[2][0]])
     give(3, [sums[2][0]])
     give(2, [added[3]])
-    return combine(columns, *sums[0], [parts[step] for step in range(1, experts_n)], ())
+    total = weigh(columns, *sums[0][:2], (1,), [parts[1]])
+    return finish(columns, total, (3, 2), [parts[3], parts[2]])
 
 
 def slotted(tokens, expert_ids, weight_codes, up_local, down_local, capacity):

time: 59.4 us -> 59.3 us (level)
  Pallas kernels: 16.2 us -> 14.6 us
  starting transfers between devices: 20.6 us -> 21.8 us
    ppermute x16 -> x14, waiting for transfers between devices: 4.9 us -> 11 us  [swap(): return lax.ppermute(array, 'tensor', [(i, i ^ bit) for i in range(4)])]
    ppermute x6, waiting for transfers between devices: 17.4 us -> 11.7 us  [shift(): lax.ppermute(array, 'expert', [(i, (i + by) % experts_n) for i in range(e...]
    ppermute x6, starting transfers between devices: 9.51 us -> 11.6 us  [shift(): lax.ppermute(array, 'expert', [(i, (i + by) % experts_n) for i in range(e...]
    pallas_call x17 -> x15, Pallas kernels: 16.2 us -> 14.6 us  [local_call(): pl.pallas_call(body_of, name=name, out_shape=out_shape, in_specs=list(in_...]
    ppermute x16 -> x14, starting transfers between devices: 11.1 us -> 10.2 us  [swap(): return lax.ppermute(array, 'tensor', [(i, i ^ bit) for i in range(4)])]
  transfers between devices with their start and end apart: 22 -> 20, of which waited for: 8 -> 12; matrix products, arithmetic and copies ran while one was open for 0% -> 0% of each run, Pallas kernels for 26% -> 23%
where the time goes in v8:
time: 59.3 us; the launch traced here: 59.1 us
  waiting for transfers between devices  22.7 us (38%)
  starting transfers between devices  21.8 us (37%)
  Pallas kernels  14.6 us (25%)
    pallas_call x15, Pallas kernels, local_call(): pl.pallas_call(body_of, name=name, out_shape=out_shape, in_specs=list(in_...  14.6 us
    ppermute x6, waiting for transfers between devices, shift(): lax.ppermute(array, 'expert', [(i, (i + by) % experts_n) for i in range(e...  11.7 us
    ppermute x6, starting transfers between devices, shift(): lax.ppermute(array, 'expert', [(i, (i + by) % experts_n) for i in range(e...  11.6 us
    ppermute x14, waiting for transfers between devices, swap(): return lax.ppermute(array, 'tensor', [(i, i ^ bit) for i in range(4)])  11 us
    ppermute x14, starting transfers between devices, swap(): return lax.ppermute(array, 'tensor', [(i, i ^ bit) for i in range(4)])  10.2 us
  transfers between devices with their start and end apart: 20, of which 12 were waited for; matrix products, arithmetic and copies ran while one was open for 0% of the time, Pallas kernels for 23%

profile of v8, /device:TPU:0, one launch (start us, length us, event | category | flops | bytes accessed | tf_op | source)
XLA Modules:
  0.0 59.1 jit_solution(7562658010135844215)
XLA Ops:
  0.0 3.0 %collective-permute-start.1 = (bf16[96,896]{1,0:T(8,128)(2,1)}, bf16[96,896]{1,0:T(8,128)(2,1)S(1)}, u32[]{:S(2)}, u32[]{:S(2)}) collective-permute-start(bf16[96,896]{1,0:T(8,128)(2,1)} %refs_0_.1), channel_id=1, source_target_pairs={{0,4},{4,8},{8,12},{12,0},{1,5},{5,9},{9,13},{13,1},{2,6},{6,10},{... | collective-permute-start | bytes 516104 | tf_op jit(solution)/shard_map/ppermute | solution.py:250
  3.0 2.0 %collective-permute-start.2 = (bf16[96,896]{1,0:T(8,128)(2,1)}, bf16[96,896]{1,0:T(8,128)(2,1)S(1)}, u32[]{:S(2)}, u32[]{:S(2)}) collective-permute-start(bf16[96,896]{1,0:T(8,128)(2,1)} %refs_0_.1), channel_id=1, source_target_pairs={{0,12},{4,0},{8,4},{12,8},{1,13},{5,1},{9,5},{13,9},{2,14},{6,2},{... | collective-permute-start | bytes 516104 | tf_op jit(solution)/shard_map/ppermute | solution.py:250
  5.1 1.7 %collective-permute-start = (bf16[96,896]{1,0:T(8,128)(2,1)}, bf16[96,896]{1,0:T(8,128)(2,1)S(1)}, u32[]{:S(2)}, u32[]{:S(2)}) collective-permute-start(bf16[96,896]{1,0:T(8,128)(2,1)} %refs_0_.1), channel_id=1, source_target_pairs={{0,2},{1,3},{2,0},{3,1},{4,6},{5,7},{6,4},{7,5},{8,10},{9,11},{10,... | collective-permute-start | bytes 516104 | tf_op jit(solution)/shard_map/ppermute | solution.py:243
  6.8 4.3 %prepare_kernel.1 = (f32[4,96,128]{2,1,0:T(8,128)S(1)}, bf16[608,3584]{1,0:T(8,128)(2,1)S(1)}, bf16[608,3584]{1,0:T(8,128)(2,1)S(1)}) custom-call(s32[2,96]{1,0:T(2,128)} %bitcast.8, s32[2,96]{1,0:T(2,128)} %bitcast.9, bf16[608,3584]{1,0:T(8,128)(2,1)} %bitcast.6, bf16[608,3584]{1,0:T(8,128)(2,1)} %bitcast.7), custom_call_target="tpu_custom_call" | custom-call | flops 4600000000 | tf_op jit(solution)/shard_map/prepare_kernel/pallas_call | solution.py:72
  11.1 1.6 %collective-permute-done.2.refs_0_ = bf16[96,896]{1,0:T(8,128)(2,1)S(1)} collective-permute-done((bf16[96,896]{1,0:T(8,128)(2,1)}, bf16[96,896]{1,0:T(8,128)(2,1)S(1)}, u32[]{:S(2)}, u32[]{:S(2)}) %collective-permute-start.2) | collective-permute-done | bytes 172064 | tf_op jit(solution)/shard_map/ppermute | solution.py:250
  12.9 1.2 %collective-permute-start.5 = (bf16[96,896]{1,0:T(8,128)(2,1)S(1)}, bf16[96,896]{1,0:T(8,128)(2,1)S(1)}, u32[]{:S(2)}, u32[]{:S(2)}) collective-permute-start(bf16[96,896]{1,0:T(8,128)(2,1)S(1)} %shard_map.55.refs_2_.refs_0_), channel_id=1, source_target_pairs={{0,4},{4,8},{8,12},{12,0},{1,5},{5,9},{9,13},{13,1},{2,6},{6,10},{... | collective-permute-start | bytes 516104 | tf_op jit(solution)/shard_map/ppermute | solution.py:250
  14.1 1.5 %collective-permute-start.7 = (bf16[96,896]{1,0:T(8,128)(2,1)S(1)}, bf16[96,896]{1,0:T(8,128)(2,1)S(1)}, u32[]{:S(2)}, u32[]{:S(2)}) collective-permute-start(bf16[96,896]{1,0:T(8,128)(2,1)S(1)} %shard_map.55.refs_2_.refs_0_), channel_id=1, source_target_pairs={{0,2},{1,3},{2,0},{3,1},{4,6},{5,7},{6,4},{7,5},{8,10},{9,11},{10,... | collective-permute-start | bytes 516104 | tf_op jit(solution)/shard_map/ppermute | solution.py:243
  16.1 2.6 %expert_kernel.3 = (f32[96,1792]{1,0:T(8,128)S(1)}, bf16[96,1792]{1,0:T(8,128)(2,1)S(1)}) custom-call(bf16[96,1792]{1,0:T(8,128)(2,1)S(1)} %pack_kernel.3.refs_0_, bf16[96,1792]{1,0:T(8,128)(2,1)S(1)} %collective-permute-done.3.refs_1_, bf16[608,3584]{1,0:T(8,128)(2,1)S(1)} %get-tuple-element.22.refs_2_, bf16[608,3584]{1,0:T(8,128)(2,1)S(1)} %get-tuple-element.23.refs_3_), custom_call_target="tpu_custom_call" | custom-call | flops 2990000128 | tf_op jit(solution)/shard_map/expert_kernel/pallas_call | solution.py:72
  18.7 2.7 %collective-permute-done.5.refs_0_ = bf16[96,896]{1,0:T(8,128)(2,1)S(1)} collective-permute-done((bf16[96,896]{1,0:T(8,128)(2,1)S(1)}, bf16[96,896]{1,0:T(8,128)(2,1)S(1)}, u32[]{:S(2)}, u32[]{:S(2)}) %collective-permute-start.5) | collective-permute-done | bytes 172064 | tf_op jit(solution)/shard_map/ppermute | solution.py:250
  21.5 2.7 %collective-permute-done.8.refs_3_ = bf16[96,896]{1,0:T(8,128)(2,1)S(1)} collective-permute-done((bf16[96,896]{1,0:T(8,128)(2,1)S(1)}, bf16[96,896]{1,0:T(8,128)(2,1)S(1)}, u32[]{:S(2)}, u32[]{:S(2)}) %collective-permute-start.8) | collective-permute-done | bytes 172064 | tf_op jit(solution)/shard_map/ppermute | solution.py:243
  24.3 1.6 %collective-permute-start.6 = (bf16[96,896]{1,0:T(8,128)(2,1)S(1)}, bf16[96,896]{1,0:T(8,128)(2,1)S(1)}, u32[]{:S(2)}, u32[]{:S(2)}) collective-permute-start(bf16[96,896]{1,0:T(8,128)(2,1)S(1)} %shard_map.57.refs_5_.refs_0_), channel_id=1, source_target_pairs={{0,2},{1,3},{2,0},{3,1},{4,6},{5,7},{6,4},{7,5},{8,10},{9,11},{10,... | collective-permute-start | bytes 516104 | tf_op jit(solution)/shard_map/ppermute | solution.py:243
  26.5 3.6 %expert_kernel.4 = (f32[192,1792]{1,0:T(8,128)S(1)}, bf16[192,1792]{1,0:T(8,128)(2,1)S(1)}) custom-call(bf16[192,1792]{1,0:T(8,128)(2,1)S(1)} %pack_kernel.4.refs_0_, bf16[192,1792]{1,0:T(8,128)(2,1)S(1)} %collective-permute-done.9.refs_1_, bf16[608,3584]{1,0:T(8,128)(2,1)S(1)} %get-tuple-element.22.refs_2_, bf16[608,3584]{1,0:T(8,128)(2,1)S(1)} %get-tuple-element.23.refs_3_), custom_call_target="tpu_custom_call" | custom-call | flops 2990000128 | tf_op jit(solution)/shard_map/expert_kernel/pallas_call | solution.py:72
  30.3 0.8 %collective-permute-done.6.refs_1_ = bf16[96,896]{1,0:T(8,128)(2,1)S(1)} collective-permute-done((bf16[96,896]{1,0:T(8,128)(2,1)S(1)}, bf16[96,896]{1,0:T(8,128)(2,1)S(1)}, u32[]{:S(2)}, u32[]{:S(2)}) %collective-permute-start.6) | collective-permute-done | bytes 172064 | tf_op jit(solution)/shard_map/ppermute | solution.py:243
  31.2 1.1 %collective-permute-done.11.refs_1_ = bf16[192,1792]{1,0:T(8,128)(2,1)S(1)} collective-permute-done((bf16[192,1792]{1,0:T(8,128)(2,1)S(1)}, bf16[192,1792]{1,0:T(8,128)(2,1)S(1)}, u32[]{:S(2)}, u32[]{:S(2)}) %collective-permute-start.11) | collective-permute-done | bytes 688160 | tf_op jit(solution)/shard_map/ppermute | solution.py:243
  32.4 1.6 %collective-permute-start.13 = (bf16[96,896]{1,0:T(8,128)(2,1)S(1)}, bf16[96,896]{1,0:T(8,128)(2,1)S(1)}, u32[]{:S(2)}, u32[]{:S(2)}) collective-permute-start(bf16[96,896]{1,0:T(8,128)(2,1)S(1)} %get-tuple-element.31), channel_id=1, source_target_pairs={{0,2},{1,3},{2,0},{3,1},{4,6},{5,7},{6,4},{7,5},{8,10},{9,11},{10,... | collective-permute-start | bytes 516104 | tf_op jit(solution)/shard_map/ppermute | solution.py:243
  34.0 2.6 %expert_kernel.5 = (f32[96,1792]{1,0:T(8,128)S(1)}, bf16[96,1792]{1,0:T(8,128)(2,1)S(1)}) custom-call(bf16[96,1792]{1,0:T(8,128)(2,1)S(1)} %pack_kernel.5.refs_2_.refs_0_, bf16[96,1792]{1,0:T(8,128)(2,1)S(1)} %collective-permute-done.10.refs_1_, bf16[608,3584]{1,0:T(8,128)(2,1)S(1)} %get-tuple-element.22.refs_2_, ...), custom_call_target="tpu_custom_call" | custom-call | flops 2990000128 | tf_op jit(solution)/shard_map/expert_kernel/pallas_call | solution.py:72
  37.7 1.2 %collective-permute-done.13.refs_1_ = bf16[96,896]{1,0:T(8,128)(2,1)S(1)} collective-permute-done((bf16[96,896]{1,0:T(8,128)(2,1)S(1)}, bf16[96,896]{1,0:T(8,128)(2,1)S(1)}, u32[]{:S(2)}, u32[]{:S(2)}) %collective-permute-start.13) | collective-permute-done | bytes 172064 | tf_op jit(solution)/shard_map/ppermute | solution.py:243
  39.0 2.8 %collective-permute-start.15 = (bf16[96,896]{1,0:T(8,128)(2,1)S(1)}, bf16[96,896]{1,0:T(8,128)(2,1)S(1)}, u32[]{:S(2)}, u32[]{:S(2)}) collective-permute-start(bf16[96,896]{1,0:T(8,128)(2,1)S(1)} %chip_sum_kernel.3.refs_2_), channel_id=1, source_target_pairs={{0,12},{4,0},{8,4},{12,8},{1,13},{5,1},{9,5},{13,9},{2,14},{6,2},{... | collective-permute-start | bytes 516104 | tf_op jit(solution)/shard_map/ppermute | solution.py:250
  41.8 1.6 %collective-permute-start.18 = (bf16[96,896]{1,0:T(8,128)(2,1)S(1)}, bf16[96,896]{1,0:T(8,128)(2,1)S(1)}, u32[]{:S(2)}, u32[]{:S(2)}) collective-permute-start(bf16[96,896]{1,0:T(8,128)(2,1)S(1)} %get-tuple-element.36), channel_id=1, source_target_pairs={{0,2},{1,3},{2,0},{3,1},{4,6},{5,7},{6,4},{7,5},{8,10},{9,11},{10,... | collective-permute-start | bytes 516104 | tf_op jit(solution)/shard_map/ppermute | solution.py:243
  43.6 1.7 %collective-permute-start.17 = (bf16[96,896]{1,0:T(8,128)(2,1)S(1)}, bf16[96,896]{1,0:T(8,128)(2,1)S(1)}, u32[]{:S(2)}, u32[]{:S(2)}) collective-permute-start(bf16[96,896]{1,0:T(8,128)(2,1)S(1)} %chip_sum_kernel.4.refs_2_), channel_id=1, source_target_pairs={{0,4},{4,8},{8,12},{12,0},{1,5},{5,9},{9,13},{13,1},{2,6},{6,10},{... | collective-permute-start | bytes 516104 | tf_op jit(solution)/shard_map/ppermute | solution.py:250
  45.6 2.9 %collective-permute-done.18.refs_1_ = bf16[96,896]{1,0:T(8,128)(2,1)S(1)} collective-permute-done((bf16[96,896]{1,0:T(8,128)(2,1)S(1)}, bf16[96,896]{1,0:T(8,128)(2,1)S(1)}, u32[]{:S(2)}, u32[]{:S(2)}) %collective-permute-start.18) | collective-permute-done | bytes 172064 | tf_op jit(solution)/shard_map/ppermute | solution.py:243
  48.5 1.0 %collective-permute-start.19 = (bf16[96,896]{1,0:T(8,128)(2,1)S(1)}, bf16[96,896]{1,0:T(8,128)(2,1)S(1)}, u32[]{:S(2)}, u32[]{:S(2)}) collective-permute-start(bf16[96,896]{1,0:T(8,128)(2,1)S(1)} %chip_sum_kernel.5), channel_id=1, source_target_pairs={{0,8},{4,12},{8,0},{12,4},{1,9},{5,13},{9,1},{13,5},{2,10},{6,14},... | collective-permute-start | bytes 516104 | tf_op jit(solution)/shard_map/ppermute | solution.py:250
  49.5 1.5 %collective-permute-done.14.refs_2_ = bf16[96,896]{1,0:T(8,128)(2,1)S(1)} collective-permute-done((bf16[96,896]{1,0:T(8,128)(2,1)S(1)}, bf16[96,896]{1,0:T(8,128)(2,1)S(1)}, u32[]{:S(2)}, u32[]{:S(2)}) %collective-permute-start.14) | collective-permute-done | bytes 172064 | tf_op jit(solution)/shard_map/ppermute | solution.py:243
  51.7 6.6 %collective-permute-done.19.refs_3_ = bf16[96,896]{1,0:T(8,128)(2,1)S(1)} collective-permute-done((bf16[96,896]{1,0:T(8,128)(2,1)S(1)}, bf16[96,896]{1,0:T(8,128)(2,1)S(1)}, u32[]{:S(2)}, u32[]{:S(2)}) %collective-permute-start.19) | collective-permute-done | bytes 172064 | tf_op jit(solution)/shard_map/ppermute | solution.py:250
  (36 shorter events, 5.1 us)
Async XLA Ops:
  0.0 11.1 %collective-permute-start.1 = (bf16[96,896]{1,0:T(8,128)(2,1)}, bf16[96,896]{1,0:T(8,128)(2,1)S(1)}, u32[]{:S(2)}, u32[]{:S(2)}) collective-permute-start(bf16[96,896]{1,0:T(8,128)(2,1)} %refs_0_.1), channel_id=1, source_target_pairs={{0,4},{4,8},{8,12},{12,0},{1,5},{5,9},{9,13},{13,1},{2,6},{6,10},{... | collective-permute-start | bytes 516104 | tf_op jit(solution)/shard_map/ppermute | solution.py:250
  3.0 9.7 %collective-permute-start.2 = (bf16[96,896]{1,0:T(8,128)(2,1)}, bf16[96,896]{1,0:T(8,128)(2,1)S(1)}, u32[]{:S(2)}, u32[]{:S(2)}) collective-permute-start(bf16[96,896]{1,0:T(8,128)(2,1)} %refs_0_.1), channel_id=1, source_target_pairs={{0,12},{4,0},{8,4},{12,8},{1,13},{5,1},{9,5},{13,9},{2,14},{6,2},{... | collective-permute-start | bytes 516104 | tf_op jit(solution)/shard_map/ppermute | solution.py:250
  5.1 7.7 %collective-permute-start = (bf16[96,896]{1,0:T(8,128)(2,1)}, bf16[96,896]{1,0:T(8,128)(2,1)S(1)}, u32[]{:S(2)}, u32[]{:S(2)}) collective-permute-start(bf16[96,896]{1,0:T(8,128)(2,1)} %refs_0_.1), channel_id=1, source_target_pairs={{0,2},{1,3},{2,0},{3,1},{4,6},{5,7},{6,4},{7,5},{8,10},{9,11},{10,... | collective-permute-start | bytes 516104 | tf_op jit(solution)/shard_map/ppermute | solution.py:243
  6.8 6.0 %copy-start = (bf16[96,896]{1,0:T(8,128)(2,1)S(1)}, bf16[96,896]{1,0:T(8,128)(2,1)}, u32[]{:S(2)}) copy-start(bf16[96,896]{1,0:T(8,128)(2,1)} %refs_0_.1) | copy-start | bytes 516100
  12.8 3.3 %collective-permute-start.3 = (bf16[96,1792]{1,0:T(8,128)(2,1)S(1)}, bf16[96,1792]{1,0:T(8,128)(2,1)S(1)}, u32[]{:S(2)}, u32[]{:S(2)}) collective-permute-start(bf16[96,1792]{1,0:T(8,128)(2,1)S(1)} %pack_kernel.3.refs_0_), channel_id=1, source_target_pairs={{0,1},{1,0},{2,3},{3,2},{4,5},{5,4},{6,7},{7,6},{8,9},{9,8},{10,11... | collective-permute-start | bytes 1032200 | tf_op jit(solution)/shard_map/ppermute | solution.py:243
  12.9 8.6 %collective-permute-start.5 = (bf16[96,896]{1,0:T(8,128)(2,1)S(1)}, bf16[96,896]{1,0:T(8,128)(2,1)S(1)}, u32[]{:S(2)}, u32[]{:S(2)}) collective-permute-start(bf16[96,896]{1,0:T(8,128)(2,1)S(1)} %shard_map.55.refs_2_.refs_0_), channel_id=1, source_target_pairs={{0,4},{4,8},{8,12},{12,0},{1,5},{5,9},{9,13},{13,1},{2,6},{6,10},{... | collective-permute-start | bytes 516104 | tf_op jit(solution)/shard_map/ppermute | solution.py:250
  14.1 7.4 %collective-permute-start.7 = (bf16[96,896]{1,0:T(8,128)(2,1)S(1)}, bf16[96,896]{1,0:T(8,128)(2,1)S(1)}, u32[]{:S(2)}, u32[]{:S(2)}) collective-permute-start(bf16[96,896]{1,0:T(8,128)(2,1)S(1)} %shard_map.55.refs_2_.refs_0_), channel_id=1, source_target_pairs={{0,2},{1,3},{2,0},{3,1},{4,6},{5,7},{6,4},{7,5},{8,10},{9,11},{10,... | collective-permute-start | bytes 516104 | tf_op jit(solution)/shard_map/ppermute | solution.py:243
  15.5 8.6 %collective-permute-start.8 = (bf16[96,896]{1,0:T(8,128)(2,1)S(1)}, bf16[96,896]{1,0:T(8,128)(2,1)S(1)}, u32[]{:S(2)}, u32[]{:S(2)}) collective-permute-start(bf16[96,896]{1,0:T(8,128)(2,1)S(1)} %shard_map.56.refs_3_.refs_2_), channel_id=1, source_target_pairs={{0,2},{1,3},{2,0},{3,1},{4,6},{5,7},{6,4},{7,5},{8,10},{9,11},{10,... | collective-permute-start | bytes 516104 | tf_op jit(solution)/shard_map/ppermute | solution.py:243
  24.2 2.2 %collective-permute-start.9 = (bf16[192,1792]{1,0:T(8,128)(2,1)S(1)}, bf16[192,1792]{1,0:T(8,128)(2,1)S(1)}, u32[]{:S(2)}, u32[]{:S(2)}) collective-permute-start(bf16[192,1792]{1,0:T(8,128)(2,1)S(1)} %pack_kernel.4.refs_0_), channel_id=1, source_target_pairs={{0,1},{1,0},{2,3},{3,2},{4,5},{5,4},{6,7},{7,6},{8,9},{9,8},{10,11... | collective-permute-start | bytes 2064392 | tf_op jit(solution)/shard_map/ppermute | solution.py:243
  24.3 6.8 %collective-permute-start.6 = (bf16[96,896]{1,0:T(8,128)(2,1)S(1)}, bf16[96,896]{1,0:T(8,128)(2,1)S(1)}, u32[]{:S(2)}, u32[]{:S(2)}) collective-permute-start(bf16[96,896]{1,0:T(8,128)(2,1)S(1)} %shard_map.57.refs_5_.refs_0_), channel_id=1, source_target_pairs={{0,2},{1,3},{2,0},{3,1},{4,6},{5,7},{6,4},{7,5},{8,10},{9,11},{10,... | collective-permute-start | bytes 516104 | tf_op jit(solution)/shard_map/ppermute | solution.py:243
  30.1 2.2 %collective-permute-start.11 = (bf16[192,1792]{1,0:T(8,128)(2,1)S(1)}, bf16[192,1792]{1,0:T(8,128)(2,1)S(1)}, u32[]{:S(2)}, u32[]{:S(2)}) collective-permute-start(bf16[192,1792]{1,0:T(8,128)(2,1)S(1)} %get-tuple-element.27), channel_id=1, source_target_pairs={{0,1},{1,0},{2,3},{3,2},{4,5},{5,4},{6,7},{7,6},{8,9},{9,8},{10,11... | collective-permute-start | bytes 2064392 | tf_op jit(solution)/shard_map/ppermute | solution.py:243
  31.1 2.9 %collective-permute-start.10 = (bf16[96,1792]{1,0:T(8,128)(2,1)S(1)}, bf16[96,1792]{1,0:T(8,128)(2,1)S(1)}, u32[]{:S(2)}, u32[]{:S(2)}) collective-permute-start(bf16[96,1792]{1,0:T(8,128)(2,1)S(1)} %pack_kernel.5.refs_2_.refs_0_), channel_id=1, source_target_pairs={{0,1},{1,0},{2,3},{3,2},{4,5},{5,4},{6,7},{7,6},{8,9},{9,8},{10,11... | collective-permute-start | bytes 1032200 | tf_op jit(solution)/shard_map/ppermute | solution.py:243
  32.4 6.5 %collective-permute-start.13 = (bf16[96,896]{1,0:T(8,128)(2,1)S(1)}, bf16[96,896]{1,0:T(8,128)(2,1)S(1)}, u32[]{:S(2)}, u32[]{:S(2)}) collective-permute-start(bf16[96,896]{1,0:T(8,128)(2,1)S(1)} %get-tuple-element.31), channel_id=1, source_target_pairs={{0,2},{1,3},{2,0},{3,1},{4,6},{5,7},{6,4},{7,5},{8,10},{9,11},{10,... | collective-permute-start | bytes 516104 | tf_op jit(solution)/shard_map/ppermute | solution.py:243
  36.6 5.1 %collective-permute-start.12 = (bf16[96,1792]{1,0:T(8,128)(2,1)S(1)}, bf16[96,1792]{1,0:T(8,128)(2,1)S(1)}, u32[]{:S(2)}, u32[]{:S(2)}) collective-permute-start(bf16[96,1792]{1,0:T(8,128)(2,1)S(1)} %get-tuple-element.30), channel_id=1, source_target_pairs={{0,1},{1,0},{2,3},{3,2},{4,5},{5,4},{6,7},{7,6},{8,9},{9,8},{10,11... | collective-permute-start | bytes 1032200 | tf_op jit(solution)/shard_map/ppermute | solution.py:243
  36.7 8.6 %collective-permute-start.4 = (bf16[96,1792]{1,0:T(8,128)(2,1)S(1)}, bf16[96,1792]{1,0:T(8,128)(2,1)S(1)}, u32[]{:S(2)}, u32[]{:S(2)}) collective-permute-start(bf16[96,1792]{1,0:T(8,128)(2,1)S(1)} %get-tuple-element.25), channel_id=1, source_target_pairs={{0,1},{1,0},{2,3},{3,2},{4,5},{5,4},{6,7},{7,6},{8,9},{9,8},{10,11... | collective-permute-start | bytes 1032200 | tf_op jit(solution)/shard_map/ppermute | solution.py:243
  37.2 6.4 %collective-permute-start.16 = (bf16[96,896]{1,0:T(8,128)(2,1)S(1)}, bf16[96,896]{1,0:T(8,128)(2,1)S(1)}, u32[]{:S(2)}, u32[]{:S(2)}) collective-permute-start(bf16[96,896]{1,0:T(8,128)(2,1)S(1)} %get-tuple-element.35), channel_id=1, source_target_pairs={{0,2},{1,3},{2,0},{3,1},{4,6},{5,7},{6,4},{7,5},{8,10},{9,11},{10,... | collective-permute-start | bytes 516104 | tf_op jit(solution)/shard_map/ppermute | solution.py:243
  39.0 10.5 %collective-permute-start.15 = (bf16[96,896]{1,0:T(8,128)(2,1)S(1)}, bf16[96,896]{1,0:T(8,128)(2,1)S(1)}, u32[]{:S(2)}, u32[]{:S(2)}) collective-permute-start(bf16[96,896]{1,0:T(8,128)(2,1)S(1)} %chip_sum_kernel.3.refs_2_), channel_id=1, source_target_pairs={{0,12},{4,0},{8,4},{12,8},{1,13},{5,1},{9,5},{13,9},{2,14},{6,2},{... | collective-permute-start | bytes 516104 | tf_op jit(solution)/shard_map/ppermute | solution.py:250
  41.8 6.7 %collective-permute-start.18 = (bf16[96,896]{1,0:T(8,128)(2,1)S(1)}, bf16[96,896]{1,0:T(8,128)(2,1)S(1)}, u32[]{:S(2)}, u32[]{:S(2)}) collective-permute-start(bf16[96,896]{1,0:T(8,128)(2,1)S(1)} %get-tuple-element.36), channel_id=1, source_target_pairs={{0,2},{1,3},{2,0},{3,1},{4,6},{5,7},{6,4},{7,5},{8,10},{9,11},{10,... | collective-permute-start | bytes 516104 | tf_op jit(solution)/shard_map/ppermute | solution.py:243
  43.6 8.1 %collective-permute-start.17 = (bf16[96,896]{1,0:T(8,128)(2,1)S(1)}, bf16[96,896]{1,0:T(8,128)(2,1)S(1)}, u32[]{:S(2)}, u32[]{:S(2)}) collective-permute-start(bf16[96,896]{1,0:T(8,128)(2,1)S(1)} %chip_sum_kernel.4.refs_2_), channel_id=1, source_target_pairs={{0,4},{4,8},{8,12},{12,0},{1,5},{5,9},{9,13},{13,1},{2,6},{6,10},{... | collective-permute-start | bytes 516104 | tf_op jit(solution)/shard_map/ppermute | solution.py:250
  45.4 5.6 %collective-permute-start.14 = (bf16[96,896]{1,0:T(8,128)(2,1)S(1)}, bf16[96,896]{1,0:T(8,128)(2,1)S(1)}, u32[]{:S(2)}, u32[]{:S(2)}) collective-permute-start(bf16[96,896]{1,0:T(8,128)(2,1)S(1)} %get-tuple-element.34), channel_id=1, source_target_pairs={{0,2},{1,3},{2,0},{3,1},{4,6},{5,7},{6,4},{7,5},{8,10},{9,11},{10,... | collective-permute-start | bytes 516104 | tf_op jit(solution)/shard_map/ppermute | solution.py:243
  48.5 9.9 %collective-permute-start.19 = (bf16[96,896]{1,0:T(8,128)(2,1)S(1)}, bf16[96,896]{1,0:T(8,128)(2,1)S(1)}, u32[]{:S(2)}, u32[]{:S(2)}) collective-permute-start(bf16[96,896]{1,0:T(8,128)(2,1)S(1)} %chip_sum_kernel.5), channel_id=1, source_target_pairs={{0,8},{4,12},{8,0},{12,4},{1,9},{5,13},{9,1},{13,5},{2,10},{6,14},... | collective-permute-start | bytes 516104 | tf_op jit(solution)/shard_map/ppermute | solution.py:250

commit v9 on v8

--- a/solution.py
+++ b/solution.py
@@ -153,7 +153,7 @@
     send[:, width:] = out[:, columns(3)].astype(jnp.bfloat16)
 
 
-def expert_rows(chip, core, up_t, down, others):
+def expert_rows(chip, core, up_t, down, others, cost):
     rows, model = chip.shape[0], up_t.shape[1]
     return local_call(
         expert_kernel,
@@ -168,7 +168,7 @@
             pltpu.VMEM((rows, model), jnp.bfloat16),
             pltpu.VMEM((rows, model), jnp.float32),
         ],
-        cost=2.6,
+        cost=cost,
     )
 
 
@@ -180,7 +180,7 @@
         send[...] = (keep[rows, width:] + got[rows, width:].astype(jnp.float32)).astype(send.dtype)
 
 
-def core_sum(keep, got, count, others):
+def core_sum(keep, got, count, others, cost):
     rows, width = keep.shape[0], keep.shape[1] // 2
     return local_call(
         core_sum_kernel,
@@ -188,7 +188,7 @@
         + [jax.ShapeDtypeStruct((rows // count, width), jnp.bfloat16)] * count,
         (keep, got),
         others,
-        cost=2,
+        cost=cost,
     )
 
 
@@ -197,13 +197,13 @@
     part[...] = (own[rows, :] + got[...].astype(jnp.float32)).astype(part.dtype)
 
 
-def chip_sum(own, got, index, others):
+def chip_sum(own, got, index, others, cost):
     return local_call(
         functools.partial(chip_sum_kernel, index),
         jax.ShapeDtypeStruct(got.shape, jnp.bfloat16),
         (own, got),
         others,
-        cost=2,
+        cost=cost,
     )
 
 
@@ -224,6 +224,7 @@
         functools.partial(weigh_kernel, steps),
         jax.ShapeDtypeStruct(own.shape, jnp.float32),
         (columns, own, got, *parts),
+        cost=4,
     )
 
 
@@ -265,38 +266,41 @@
     def lay(steps, waits, cost=0.5):
         chips[steps] = pack([(blocks[step], others[step]) for step in steps], waits, cost)
 
-    def run(steps, waits):
+    def run(steps, waits, cost):
         chip = chips[steps]
-        kept[steps] = expert_rows(chip, swap(chip, 1), up_t, down, waits)
-
-    def leave(steps, waits):
+        kept[steps] = expert_rows(chip, swap(chip, 1), up_t, down, waits, cost)
+
+    def leave(steps, waits, cost=2):
         keep, send = kept[steps]
-        own, *aways = core_sum(keep, swap(send, 1), len(steps), waits)
+        own, *aways = core_sum(keep, swap(send, 1), len(steps), waits, cost)
         for index, step in enumerate(steps):
             sums[step] = own, swap(aways[index], 2), index
 
-    def give(step, waits):
-        added[step] = chip_sum(*sums[step], waits)
+    def give(step, waits, cost=2):
+        added[step] = chip_sum(*sums[step], waits, cost)
         parts[step] = shift(added[step], -step)
 
     arrive(0, tokens, 0, [])
     arrive(1, tokens, 1, [columns])
     arrive(3, tokens, -1, [columns])
     lay((0,), [blocks[1], blocks[3]])
-    run((0,), [])
+    run((0,), [], 2.6)
     arrive(2, blocks[1], 1, [kept[0,][0]])
-    lay((1, 3), [kept[0,][0], blocks[2]])
-    run((1, 3), [])
-    lay((2,), [kept[1, 3][0]], cost=4)
-    leave((1, 3), [chips[2,]])
-    run((2,), [sums[1][0]])
-    give(1, [kept[2,][0]])
-    leave((2,), [added[1]])
+    lay((1,), [kept[0,][0], blocks[2]])
+    run((1,), [], 4)
+    lay((3,), [kept[1,][0]], .5)
+    lay((2,), [chips[3,]], 4)
+    leave((1,), [chips[2,]], 2)
+    run((3,), [sums[1][0]], 4)
+    run((2,), [kept[3,][0]], .05)
+    give(1, [kept[2,][0]], 2)
+    leave((3,), [added[1]], 4)
+    leave((2,), [sums[3][0]], 2)
     leave((0,), [sums[2][0]])
-    give(3, [sums[2][0]])
-    give(2, [added[3]])
-    total = weigh(columns, *sums[0][:2], (1,), [parts[1]])
-    return finish(columns, total, (3, 2), [parts[3], parts[2]])
+    give(3, [sums[2][0]], 4)
+    give(2, [added[3]], 4)
+    total = weigh(columns, *sums[0][:2], (1, 3), [parts[1], parts[3]])
+    return finish(columns, total, (2,), [parts[2]])
 
 
 def slotted(tokens, expert_ids, weight_codes, up_local, down_local, capacity):

time: 59.3 us -> 67.6 us (1.14)
  waiting for transfers between devices: 22.7 us -> 33.2 us
  starting transfers between devices: 21.8 us -> 17.9 us
  Pallas kernels: 14.6 us -> 16.1 us
    ppermute x6, waiting for transfers between devices: 11.7 us -> 17.4 us  [shift(): lax.ppermute(array, 'expert', [(i, (i + by) % experts_n) for i in range(e...]
    ppermute x14 -> x16, waiting for transfers between devices: 11 us -> 15.9 us  [swap(): return lax.ppermute(array, 'tensor', [(i, i ^ bit) for i in range(4)])]
    ppermute x6, starting transfers between devices: 11.6 us -> 7.19 us  [shift(): lax.ppermute(array, 'expert', [(i, (i + by) % experts_n) for i in range(e...]
    pallas_call x15 -> x18, Pallas kernels: 14.6 us -> 16.1 us  [local_call(): pl.pallas_call(body_of, name=name, out_shape=out_shape, in_specs=list(in_...]
    ppermute x14 -> x16, starting transfers between devices: 10.2 us -> 10.7 us  [swap(): return lax.ppermute(array, 'tensor', [(i, i ^ bit) for i in range(4)])]
  transfers between devices with their start and end apart: 20 -> 22, of which waited for: 12 -> 9; matrix products, arithmetic and copies ran while one was open for 0% -> 0% of each run, Pallas kernels for 23% -> 23%
where the time goes in v9:
time: 67.6 us; the launch traced here: 67.4 us
  waiting for transfers between devices  33.2 us (49%)
  starting transfers between devices  17.9 us (26%)
  Pallas kernels  16.1 us (24%)
    ppermute x6, waiting for transfers between devices, shift(): lax.ppermute(array, 'expert', [(i, (i + by) % experts_n) for i in range(e...  17.4 us
    pallas_call x18, Pallas kernels, local_call(): pl.pallas_call(body_of, name=name, out_shape=out_shape, in_specs=list(in_...  16.1 us
    ppermute x16, waiting for transfers between devices, swap(): return lax.ppermute(array, 'tensor', [(i, i ^ bit) for i in range(4)])  15.9 us
    ppermute x16, starting transfers between devices, swap(): return lax.ppermute(array, 'tensor', [(i, i ^ bit) for i in range(4)])  10.7 us
    ppermute x6, starting transfers between devices, shift(): lax.ppermute(array, 'expert', [(i, (i + by) % experts_n) for i in range(e...  7.19 us
  transfers between devices with their start and end apart: 22, of which 9 were waited for; matrix products, arithmetic and copies ran while one was open for 0% of the time, Pallas kernels for 23%

profile of v9, /device:TPU:0, one launch (start us, length us, event | category | flops | bytes accessed | tf_op | source)
XLA Modules:
  0.0 67.4 jit_solution(12703011392502103023)
XLA Ops:
  0.0 3.0 %collective-permute-start.1 = (bf16[96,896]{1,0:T(8,128)(2,1)}, bf16[96,896]{1,0:T(8,128)(2,1)S(1)}, u32[]{:S(2)}, u32[]{:S(2)}) collective-permute-start(bf16[96,896]{1,0:T(8,128)(2,1)} %refs_0_.1), channel_id=1, source_target_pairs={{0,4},{4,8},{8,12},{12,0},{1,5},{5,9},{9,13},{13,1},{2,6},{6,10},{... | collective-permute-start | bytes 516104 | tf_op jit(solution)/shard_map/ppermute | solution.py:251
  3.0 1.5 %collective-permute-start = (bf16[96,896]{1,0:T(8,128)(2,1)}, bf16[96,896]{1,0:T(8,128)(2,1)S(1)}, u32[]{:S(2)}, u32[]{:S(2)}) collective-permute-start(bf16[96,896]{1,0:T(8,128)(2,1)} %refs_0_.1), channel_id=1, source_target_pairs={{0,2},{1,3},{2,0},{3,1},{4,6},{5,7},{6,4},{7,5},{8,10},{9,11},{10,... | collective-permute-start | bytes 516104 | tf_op jit(solution)/shard_map/ppermute | solution.py:244
  4.5 2.2 %collective-permute-start.2 = (bf16[96,896]{1,0:T(8,128)(2,1)}, bf16[96,896]{1,0:T(8,128)(2,1)S(1)}, u32[]{:S(2)}, u32[]{:S(2)}) collective-permute-start(bf16[96,896]{1,0:T(8,128)(2,1)} %refs_0_.1), channel_id=1, source_target_pairs={{0,12},{4,0},{8,4},{12,8},{1,13},{5,1},{9,5},{13,9},{2,14},{6,2},{... | collective-permute-start | bytes 516104 | tf_op jit(solution)/shard_map/ppermute | solution.py:251
  6.8 4.3 %prepare_kernel.1 = (f32[4,96,128]{2,1,0:T(8,128)S(1)}, bf16[608,3584]{1,0:T(8,128)(2,1)S(1)}, bf16[608,3584]{1,0:T(8,128)(2,1)S(1)}) custom-call(s32[2,96]{1,0:T(2,128)} %bitcast.8, s32[2,96]{1,0:T(2,128)} %bitcast.9, bf16[608,3584]{1,0:T(8,128)(2,1)} %bitcast.6, bf16[608,3584]{1,0:T(8,128)(2,1)} %bitcast.7), custom_call_target="tpu_custom_call" | custom-call | flops 4600000000 | tf_op jit(solution)/shard_map/prepare_kernel/pallas_call | solution.py:72
  11.1 2.2 %collective-permute-done.2.refs_0_ = bf16[96,896]{1,0:T(8,128)(2,1)S(1)} collective-permute-done((bf16[96,896]{1,0:T(8,128)(2,1)}, bf16[96,896]{1,0:T(8,128)(2,1)S(1)}, u32[]{:S(2)}, u32[]{:S(2)}) %collective-permute-start.2) | collective-permute-done | bytes 172064 | tf_op jit(solution)/shard_map/ppermute | solution.py:251
  13.4 1.2 %collective-permute-start.8 = (bf16[96,896]{1,0:T(8,128)(2,1)S(1)}, bf16[96,896]{1,0:T(8,128)(2,1)S(1)}, u32[]{:S(2)}, u32[]{:S(2)}) collective-permute-start(bf16[96,896]{1,0:T(8,128)(2,1)S(1)} %shard_map.55.refs_2_.refs_0_), channel_id=1, source_target_pairs={{0,2},{1,3},{2,0},{3,1},{4,6},{5,7},{6,4},{7,5},{8,10},{9,11},{10,... | collective-permute-start | bytes 516104 | tf_op jit(solution)/shard_map/ppermute | solution.py:244
  14.7 0.9 %collective-permute-start.5 = (bf16[96,896]{1,0:T(8,128)(2,1)S(1)}, bf16[96,896]{1,0:T(8,128)(2,1)S(1)}, u32[]{:S(2)}, u32[]{:S(2)}) collective-permute-start(bf16[96,896]{1,0:T(8,128)(2,1)S(1)} %shard_map.55.refs_2_.refs_0_), channel_id=1, source_target_pairs={{0,4},{4,8},{8,12},{12,0},{1,5},{5,9},{9,13},{13,1},{2,6},{6,10},{... | collective-permute-start | bytes 516104 | tf_op jit(solution)/shard_map/ppermute | solution.py:251
  15.6 2.6 %expert_kernel.4 = (f32[96,1792]{1,0:T(8,128)S(1)}, bf16[96,1792]{1,0:T(8,128)(2,1)S(1)}) custom-call(bf16[96,1792]{1,0:T(8,128)(2,1)S(1)} %pack_kernel.4.refs_0_, bf16[96,1792]{1,0:T(8,128)(2,1)S(1)} %collective-permute-done.3.refs_1_, bf16[608,3584]{1,0:T(8,128)(2,1)S(1)} %get-tuple-element.25.refs_2_, bf16[608,3584]{1,0:T(8,128)(2,1)S(1)} %get-tuple-element.26.refs_3_), custom_call_target="tpu_custom_call" | custom-call | flops 2990000128 | tf_op jit(solution)/shard_map/expert_kernel/pallas_call | solution.py:72
  18.2 4.7 %collective-permute-done.5.refs_0_ = bf16[96,896]{1,0:T(8,128)(2,1)S(1)} collective-permute-done((bf16[96,896]{1,0:T(8,128)(2,1)S(1)}, bf16[96,896]{1,0:T(8,128)(2,1)S(1)}, u32[]{:S(2)}, u32[]{:S(2)}) %collective-permute-start.5) | collective-permute-done | bytes 172064 | tf_op jit(solution)/shard_map/ppermute | solution.py:251
  23.0 0.9 %collective-permute-start.7 = (bf16[96,896]{1,0:T(8,128)(2,1)S(1)}, bf16[96,896]{1,0:T(8,128)(2,1)S(1)}, u32[]{:S(2)}, u32[]{:S(2)}) collective-permute-start(bf16[96,896]{1,0:T(8,128)(2,1)S(1)} %shard_map.56.refs_3_.refs_0_), channel_id=1, source_target_pairs={{0,2},{1,3},{2,0},{3,1},{4,6},{5,7},{6,4},{7,5},{8,10},{9,11},{10,... | collective-permute-start | bytes 516104 | tf_op jit(solution)/shard_map/ppermute | solution.py:244
  24.0 1.2 %collective-permute-start.6 = (bf16[96,896]{1,0:T(8,128)(2,1)S(1)}, bf16[96,896]{1,0:T(8,128)(2,1)S(1)}, u32[]{:S(2)}, u32[]{:S(2)}) collective-permute-start(bf16[96,896]{1,0:T(8,128)(2,1)S(1)} %shard_map.57.refs_3_.refs_0_), channel_id=1, source_target_pairs={{0,2},{1,3},{2,0},{3,1},{4,6},{5,7},{6,4},{7,5},{8,10},{9,11},{10,... | collective-permute-start | bytes 516104 | tf_op jit(solution)/shard_map/ppermute | solution.py:244
  25.1 2.6 %expert_kernel.5 = (f32[96,1792]{1,0:T(8,128)S(1)}, bf16[96,1792]{1,0:T(8,128)(2,1)S(1)}) custom-call(bf16[96,1792]{1,0:T(8,128)(2,1)S(1)} %pack_kernel.5.refs_0_, bf16[96,1792]{1,0:T(8,128)(2,1)S(1)} %collective-permute-done.9.refs_1_, bf16[608,3584]{1,0:T(8,128)(2,1)S(1)} %get-tuple-element.25.refs_2_, bf16[608,3584]{1,0:T(8,128)(2,1)S(1)} %get-tuple-element.26.refs_3_), custom_call_target="tpu_custom_call" | custom-call | flops 4600000000 | tf_op jit(solution)/shard_map/expert_kernel/pallas_call | solution.py:72
  27.8 2.5 %collective-permute-done.7.refs_1_ = bf16[96,896]{1,0:T(8,128)(2,1)S(1)} collective-permute-done((bf16[96,896]{1,0:T(8,128)(2,1)S(1)}, bf16[96,896]{1,0:T(8,128)(2,1)S(1)}, u32[]{:S(2)}, u32[]{:S(2)}) %collective-permute-start.7) | collective-permute-done | bytes 172064 | tf_op jit(solution)/shard_map/ppermute | solution.py:244
  30.9 2.6 %collective-permute-done.6.refs_1_ = bf16[96,896]{1,0:T(8,128)(2,1)S(1)} collective-permute-done((bf16[96,896]{1,0:T(8,128)(2,1)S(1)}, bf16[96,896]{1,0:T(8,128)(2,1)S(1)}, u32[]{:S(2)}, u32[]{:S(2)}) %collective-permute-start.6) | collective-permute-done | bytes 172064 | tf_op jit(solution)/shard_map/ppermute | solution.py:244
  33.7 0.9 %collective-permute-start.15 = (bf16[96,896]{1,0:T(8,128)(2,1)S(1)}, bf16[96,896]{1,0:T(8,128)(2,1)S(1)}, u32[]{:S(2)}, u32[]{:S(2)}) collective-permute-start(bf16[96,896]{1,0:T(8,128)(2,1)S(1)} %get-tuple-element.36), channel_id=1, source_target_pairs={{0,2},{1,3},{2,0},{3,1},{4,6},{5,7},{6,4},{7,5},{8,10},{9,11},{10,... | collective-permute-start | bytes 516104 | tf_op jit(solution)/shard_map/ppermute | solution.py:244
  34.6 2.6 %expert_kernel.6 = (f32[96,1792]{1,0:T(8,128)S(1)}, bf16[96,1792]{1,0:T(8,128)(2,1)S(1)}) custom-call(bf16[96,1792]{1,0:T(8,128)(2,1)S(1)} %pack_kernel.6.refs_2_.refs_0_, bf16[96,1792]{1,0:T(8,128)(2,1)S(1)} %collective-permute-done.11.refs_1_, bf16[608,3584]{1,0:T(8,128)(2,1)S(1)} %get-tuple-element.25.refs_2_, ...), custom_call_target="tpu_custom_call" | custom-call | flops 4600000000 | tf_op jit(solution)/shard_map/expert_kernel/pallas_call | solution.py:72
  37.8 2.6 %expert_kernel.7 = (f32[96,1792]{1,0:T(8,128)S(1)}, bf16[96,1792]{1,0:T(8,128)(2,1)S(1)}) custom-call(bf16[96,1792]{1,0:T(8,128)(2,1)S(1)} %pack_kernel.7.refs_2_.refs_0_, bf16[96,1792]{1,0:T(8,128)(2,1)S(1)} %collective-permute-done.10.refs_1_, bf16[608,3584]{1,0:T(8,128)(2,1)S(1)} %get-tuple-element.25.refs_2_, ...), custom_call_target="tpu_custom_call" | custom-call | flops 57500000 | tf_op jit(solution)/shard_map/expert_kernel/pallas_call | solution.py:72
  41.0 1.2 %collective-permute-done.13.refs_1_ = bf16[96,1792]{1,0:T(8,128)(2,1)S(1)} collective-permute-done((bf16[96,1792]{1,0:T(8,128)(2,1)S(1)}, bf16[96,1792]{1,0:T(8,128)(2,1)S(1)}, u32[]{:S(2)}, u32[]{:S(2)}) %collective-permute-start.13) | collective-permute-done | bytes 344096 | tf_op jit(solution)/shard_map/ppermute | solution.py:244
  42.2 1.3 %collective-permute-start.20 = (bf16[96,896]{1,0:T(8,128)(2,1)S(1)}, bf16[96,896]{1,0:T(8,128)(2,1)S(1)}, u32[]{:S(2)}, u32[]{:S(2)}) collective-permute-start(bf16[96,896]{1,0:T(8,128)(2,1)S(1)} %get-tuple-element.42), channel_id=1, source_target_pairs={{0,2},{1,3},{2,0},{3,1},{4,6},{5,7},{6,4},{7,5},{8,10},{9,11},{10,... | collective-permute-start | bytes 516104 | tf_op jit(solution)/shard_map/ppermute | solution.py:244
  44.4 1.3 %collective-permute-start.16 = (bf16[96,896]{1,0:T(8,128)(2,1)S(1)}, bf16[96,896]{1,0:T(8,128)(2,1)S(1)}, u32[]{:S(2)}, u32[]{:S(2)}) collective-permute-start(bf16[96,896]{1,0:T(8,128)(2,1)S(1)} %get-tuple-element.40), channel_id=1, source_target_pairs={{0,2},{1,3},{2,0},{3,1},{4,6},{5,7},{6,4},{7,5},{8,10},{9,11},{10,... | collective-permute-start | bytes 516104 | tf_op jit(solution)/shard_map/ppermute | solution.py:244
  45.6 7.5 %collective-permute-done.18.refs_1_ = bf16[96,896]{1,0:T(8,128)(2,1)S(1)} collective-permute-done((bf16[96,896]{1,0:T(8,128)(2,1)S(1)}, bf16[96,896]{1,0:T(8,128)(2,1)S(1)}, u32[]{:S(2)}, u32[]{:S(2)}) %collective-permute-start.18) | collective-permute-done | bytes 172064 | tf_op jit(solution)/shard_map/ppermute | solution.py:244
  54.2 1.9 %collective-permute-done.16.refs_2_ = bf16[96,896]{1,0:T(8,128)(2,1)S(1)} collective-permute-done((bf16[96,896]{1,0:T(8,128)(2,1)S(1)}, bf16[96,896]{1,0:T(8,128)(2,1)S(1)}, u32[]{:S(2)}, u32[]{:S(2)}) %collective-permute-start.16) | collective-permute-done | bytes 172064 | tf_op jit(solution)/shard_map/ppermute | solution.py:244
  56.2 5.8 %collective-permute-done.19.refs_4_ = bf16[96,896]{1,0:T(8,128)(2,1)S(1)} collective-permute-done((bf16[96,896]{1,0:T(8,128)(2,1)S(1)}, bf16[96,896]{1,0:T(8,128)(2,1)S(1)}, u32[]{:S(2)}, u32[]{:S(2)}) %collective-permute-start.19) | collective-permute-done | bytes 172064 | tf_op jit(solution)/shard_map/ppermute | solution.py:251
  62.1 4.6 %collective-permute-done.21.refs_2_ = bf16[96,896]{1,0:T(8,128)(2,1)S(1)} collective-permute-done((bf16[96,896]{1,0:T(8,128)(2,1)S(1)}, bf16[96,896]{1,0:T(8,128)(2,1)S(1)}, u32[]{:S(2)}, u32[]{:S(2)}) %collective-permute-start.21) | collective-permute-done | bytes 172064 | tf_op jit(solution)/shard_map/ppermute | solution.py:251
  (43 shorter events, 4.9 us)
Async XLA Ops:
  0.0 11.1 %collective-permute-start.1 = (bf16[96,896]{1,0:T(8,128)(2,1)}, bf16[96,896]{1,0:T(8,128)(2,1)S(1)}, u32[]{:S(2)}, u32[]{:S(2)}) collective-permute-start(bf16[96,896]{1,0:T(8,128)(2,1)} %refs_0_.1), channel_id=1, source_target_pairs={{0,4},{4,8},{8,12},{12,0},{1,5},{5,9},{9,13},{13,1},{2,6},{6,10},{... | collective-permute-start | bytes 516104 | tf_op jit(solution)/shard_map/ppermute | solution.py:251
  3.0 10.3 %collective-permute-start = (bf16[96,896]{1,0:T(8,128)(2,1)}, bf16[96,896]{1,0:T(8,128)(2,1)S(1)}, u32[]{:S(2)}, u32[]{:S(2)}) collective-permute-start(bf16[96,896]{1,0:T(8,128)(2,1)} %refs_0_.1), channel_id=1, source_target_pairs={{0,2},{1,3},{2,0},{3,1},{4,6},{5,7},{6,4},{7,5},{8,10},{9,11},{10,... | collective-permute-start | bytes 516104 | tf_op jit(solution)/shard_map/ppermute | solution.py:244
  4.5 8.8 %collective-permute-start.2 = (bf16[96,896]{1,0:T(8,128)(2,1)}, bf16[96,896]{1,0:T(8,128)(2,1)S(1)}, u32[]{:S(2)}, u32[]{:S(2)}) collective-permute-start(bf16[96,896]{1,0:T(8,128)(2,1)} %refs_0_.1), channel_id=1, source_target_pairs={{0,12},{4,0},{8,4},{12,8},{1,13},{5,1},{9,5},{13,9},{2,14},{6,2},{... | collective-permute-start | bytes 516104 | tf_op jit(solution)/shard_map/ppermute | solution.py:251
  6.8 6.6 %copy-start = (bf16[96,896]{1,0:T(8,128)(2,1)S(1)}, bf16[96,896]{1,0:T(8,128)(2,1)}, u32[]{:S(2)}) copy-start(bf16[96,896]{1,0:T(8,128)(2,1)} %refs_0_.1) | copy-start | bytes 516100
  13.4 2.2 %collective-permute-start.3 = (bf16[96,1792]{1,0:T(8,128)(2,1)S(1)}, bf16[96,1792]{1,0:T(8,128)(2,1)S(1)}, u32[]{:S(2)}, u32[]{:S(2)}) collective-permute-start(bf16[96,1792]{1,0:T(8,128)(2,1)S(1)} %pack_kernel.4.refs_0_), channel_id=1, source_target_pairs={{0,1},{1,0},{2,3},{3,2},{4,5},{5,4},{6,7},{7,6},{8,9},{9,8},{10,11... | collective-permute-start | bytes 1032200 | tf_op jit(solution)/shard_map/ppermute | solution.py:244
  13.4 9.5 %collective-permute-start.8 = (bf16[96,896]{1,0:T(8,128)(2,1)S(1)}, bf16[96,896]{1,0:T(8,128)(2,1)S(1)}, u32[]{:S(2)}, u32[]{:S(2)}) collective-permute-start(bf16[96,896]{1,0:T(8,128)(2,1)S(1)} %shard_map.55.refs_2_.refs_0_), channel_id=1, source_target_pairs={{0,2},{1,3},{2,0},{3,1},{4,6},{5,7},{6,4},{7,5},{8,10},{9,11},{10,... | collective-permute-start | bytes 516104 | tf_op jit(solution)/shard_map/ppermute | solution.py:244
  14.7 8.2 %collective-permute-start.5 = (bf16[96,896]{1,0:T(8,128)(2,1)S(1)}, bf16[96,896]{1,0:T(8,128)(2,1)S(1)}, u32[]{:S(2)}, u32[]{:S(2)}) collective-permute-start(bf16[96,896]{1,0:T(8,128)(2,1)S(1)} %shard_map.55.refs_2_.refs_0_), channel_id=1, source_target_pairs={{0,4},{4,8},{8,12},{12,0},{1,5},{5,9},{9,13},{13,1},{2,6},{6,10},{... | collective-permute-start | bytes 516104 | tf_op jit(solution)/shard_map/ppermute | solution.py:251
  23.0 2.2 %collective-permute-start.9 = (bf16[96,1792]{1,0:T(8,128)(2,1)S(1)}, bf16[96,1792]{1,0:T(8,128)(2,1)S(1)}, u32[]{:S(2)}, u32[]{:S(2)}) collective-permute-start(bf16[96,1792]{1,0:T(8,128)(2,1)S(1)} %pack_kernel.5.refs_0_), channel_id=1, source_target_pairs={{0,1},{1,0},{2,3},{3,2},{4,5},{5,4},{6,7},{7,6},{8,9},{9,8},{10,11... | collective-permute-start | bytes 1032200 | tf_op jit(solution)/shard_map/ppermute | solution.py:244
  23.0 7.2 %collective-permute-start.7 = (bf16[96,896]{1,0:T(8,128)(2,1)S(1)}, bf16[96,896]{1,0:T(8,128)(2,1)S(1)}, u32[]{:S(2)}, u32[]{:S(2)}) collective-permute-start(bf16[96,896]{1,0:T(8,128)(2,1)S(1)} %shard_map.56.refs_3_.refs_0_), channel_id=1, source_target_pairs={{0,2},{1,3},{2,0},{3,1},{4,6},{5,7},{6,4},{7,5},{8,10},{9,11},{10,... | collective-permute-start | bytes 516104 | tf_op jit(solution)/shard_map/ppermute | solution.py:244
  24.0 9.6 %collective-permute-start.6 = (bf16[96,896]{1,0:T(8,128)(2,1)S(1)}, bf16[96,896]{1,0:T(8,128)(2,1)S(1)}, u32[]{:S(2)}, u32[]{:S(2)}) collective-permute-start(bf16[96,896]{1,0:T(8,128)(2,1)S(1)} %shard_map.57.refs_3_.refs_0_), channel_id=1, source_target_pairs={{0,2},{1,3},{2,0},{3,1},{4,6},{5,7},{6,4},{7,5},{8,10},{9,11},{10,... | collective-permute-start | bytes 516104 | tf_op jit(solution)/shard_map/ppermute | solution.py:244
  30.3 4.3 %collective-permute-start.11 = (bf16[96,1792]{1,0:T(8,128)(2,1)S(1)}, bf16[96,1792]{1,0:T(8,128)(2,1)S(1)}, u32[]{:S(2)}, u32[]{:S(2)}) collective-permute-start(bf16[96,1792]{1,0:T(8,128)(2,1)S(1)} %pack_kernel.6.refs_2_.refs_0_), channel_id=1, source_target_pairs={{0,1},{1,0},{2,3},{3,2},{4,5},{5,4},{6,7},{7,6},{8,9},{9,8},{10,11... | collective-permute-start | bytes 1032200 | tf_op jit(solution)/shard_map/ppermute | solution.py:244
  30.4 3.2 %collective-permute-start.12 = (bf16[96,1792]{1,0:T(8,128)(2,1)S(1)}, bf16[96,1792]{1,0:T(8,128)(2,1)S(1)}, u32[]{:S(2)}, u32[]{:S(2)}) collective-permute-start(bf16[96,1792]{1,0:T(8,128)(2,1)S(1)} %get-tuple-element.30), channel_id=1, source_target_pairs={{0,1},{1,0},{2,3},{3,2},{4,5},{5,4},{6,7},{7,6},{8,9},{9,8},{10,11... | collective-permute-start | bytes 1032200 | tf_op jit(solution)/shard_map/ppermute | solution.py:244
  33.6 4.3 %collective-permute-start.10 = (bf16[96,1792]{1,0:T(8,128)(2,1)S(1)}, bf16[96,1792]{1,0:T(8,128)(2,1)S(1)}, u32[]{:S(2)}, u32[]{:S(2)}) collective-permute-start(bf16[96,1792]{1,0:T(8,128)(2,1)S(1)} %pack_kernel.7.refs_2_.refs_0_), channel_id=1, source_target_pairs={{0,1},{1,0},{2,3},{3,2},{4,5},{5,4},{6,7},{7,6},{8,9},{9,8},{10,11... | collective-permute-start | bytes 1032200 | tf_op jit(solution)/shard_map/ppermute | solution.py:244
  33.7 7.0 %collective-permute-start.15 = (bf16[96,896]{1,0:T(8,128)(2,1)S(1)}, bf16[96,896]{1,0:T(8,128)(2,1)S(1)}, u32[]{:S(2)}, u32[]{:S(2)}) collective-permute-start(bf16[96,896]{1,0:T(8,128)(2,1)S(1)} %get-tuple-element.36), channel_id=1, source_target_pairs={{0,2},{1,3},{2,0},{3,1},{4,6},{5,7},{6,4},{7,5},{8,10},{9,11},{10,... | collective-permute-start | bytes 516104 | tf_op jit(solution)/shard_map/ppermute | solution.py:244
  37.2 3.7 %collective-permute-start.14 = (bf16[96,1792]{1,0:T(8,128)(2,1)S(1)}, bf16[96,1792]{1,0:T(8,128)(2,1)S(1)}, u32[]{:S(2)}, u32[]{:S(2)}) collective-permute-start(bf16[96,1792]{1,0:T(8,128)(2,1)S(1)} %get-tuple-element.35), channel_id=1, source_target_pairs={{0,1},{1,0},{2,3},{3,2},{4,5},{5,4},{6,7},{7,6},{8,9},{9,8},{10,11... | collective-permute-start | bytes 1032200 | tf_op jit(solution)/shard_map/ppermute | solution.py:244
  37.5 6.8 %collective-permute-start.4 = (bf16[96,1792]{1,0:T(8,128)(2,1)S(1)}, bf16[96,1792]{1,0:T(8,128)(2,1)S(1)}, u32[]{:S(2)}, u32[]{:S(2)}) collective-permute-start(bf16[96,1792]{1,0:T(8,128)(2,1)S(1)} %get-tuple-element.28), channel_id=1, source_target_pairs={{0,1},{1,0},{2,3},{3,2},{4,5},{5,4},{6,7},{7,6},{8,9},{9,8},{10,11... | collective-permute-start | bytes 1032200 | tf_op jit(solution)/shard_map/ppermute | solution.py:244
  40.5 1.7 %collective-permute-start.13 = (bf16[96,1792]{1,0:T(8,128)(2,1)S(1)}, bf16[96,1792]{1,0:T(8,128)(2,1)S(1)}, u32[]{:S(2)}, u32[]{:S(2)}) collective-permute-start(bf16[96,1792]{1,0:T(8,128)(2,1)S(1)} %get-tuple-element.34), channel_id=1, source_target_pairs={{0,1},{1,0},{2,3},{3,2},{4,5},{5,4},{6,7},{7,6},{8,9},{9,8},{10,11... | collective-permute-start | bytes 1032200 | tf_op jit(solution)/shard_map/ppermute | solution.py:244
  40.8 13.4 %collective-permute-start.17 = (bf16[96,896]{1,0:T(8,128)(2,1)S(1)}, bf16[96,896]{1,0:T(8,128)(2,1)S(1)}, u32[]{:S(2)}, u32[]{:S(2)}) collective-permute-start(bf16[96,896]{1,0:T(8,128)(2,1)S(1)} %chip_sum_kernel.3.refs_2_), channel_id=1, source_target_pairs={{0,12},{4,0},{8,4},{12,8},{1,13},{5,1},{9,5},{13,9},{2,14},{6,2},{... | collective-permute-start | bytes 516104 | tf_op jit(solution)/shard_map/ppermute | solution.py:251
  42.2 11.9 %collective-permute-start.20 = (bf16[96,896]{1,0:T(8,128)(2,1)S(1)}, bf16[96,896]{1,0:T(8,128)(2,1)S(1)}, u32[]{:S(2)}, u32[]{:S(2)}) collective-permute-start(bf16[96,896]{1,0:T(8,128)(2,1)S(1)} %get-tuple-element.42), channel_id=1, source_target_pairs={{0,2},{1,3},{2,0},{3,1},{4,6},{5,7},{6,4},{7,5},{8,10},{9,11},{10,... | collective-permute-start | bytes 516104 | tf_op jit(solution)/shard_map/ppermute | solution.py:244
  43.5 9.7 %collective-permute-start.18 = (bf16[96,896]{1,0:T(8,128)(2,1)S(1)}, bf16[96,896]{1,0:T(8,128)(2,1)S(1)}, u32[]{:S(2)}, u32[]{:S(2)}) collective-permute-start(bf16[96,896]{1,0:T(8,128)(2,1)S(1)} %get-tuple-element.41), channel_id=1, source_target_pairs={{0,2},{1,3},{2,0},{3,1},{4,6},{5,7},{6,4},{7,5},{8,10},{9,11},{10,... | collective-permute-start | bytes 516104 | tf_op jit(solution)/shard_map/ppermute | solution.py:244
  44.4 11.8 %collective-permute-start.16 = (bf16[96,896]{1,0:T(8,128)(2,1)S(1)}, bf16[96,896]{1,0:T(8,128)(2,1)S(1)}, u32[]{:S(2)}, u32[]{:S(2)}) collective-permute-start(bf16[96,896]{1,0:T(8,128)(2,1)S(1)} %get-tuple-element.40), channel_id=1, source_target_pairs={{0,2},{1,3},{2,0},{3,1},{4,6},{5,7},{6,4},{7,5},{8,10},{9,11},{10,... | collective-permute-start | bytes 516104 | tf_op jit(solution)/shard_map/ppermute | solution.py:244
  53.2 8.7 %collective-permute-start.19 = (bf16[96,896]{1,0:T(8,128)(2,1)S(1)}, bf16[96,896]{1,0:T(8,128)(2,1)S(1)}, u32[]{:S(2)}, u32[]{:S(2)}) collective-permute-start(bf16[96,896]{1,0:T(8,128)(2,1)S(1)} %chip_sum_kernel.4.refs_2_), channel_id=1, source_target_pairs={{0,4},{4,8},{8,12},{12,0},{1,5},{5,9},{9,13},{13,1},{2,6},{6,10},{... | collective-permute-start | bytes 516104 | tf_op jit(solution)/shard_map/ppermute | solution.py:251
  54.1 12.6 %collective-permute-start.21 = (bf16[96,896]{1,0:T(8,128)(2,1)S(1)}, bf16[96,896]{1,0:T(8,128)(2,1)S(1)}, u32[]{:S(2)}, u32[]{:S(2)}) collective-permute-start(bf16[96,896]{1,0:T(8,128)(2,1)S(1)} %chip_sum_kernel.5), channel_id=1, source_target_pairs={{0,8},{4,12},{8,0},{12,4},{1,9},{5,13},{9,1},{13,5},{2,10},{6,14},... | collective-permute-start | bytes 516104 | tf_op jit(solution)/shard_map/ppermute | solution.py:251

commit v10 on v9

--- a/solution.py
+++ b/solution.py
@@ -131,7 +131,7 @@
     )
 
 
-def expert_kernel(chip, core, up_t, down, keep, send, features, out):
+def expert_kernel(chip, core, up_t, down, keep, near, away, features, out):
     width = chip.shape[1] // 2
     place = lax.axis_index("tensor")
 
@@ -149,17 +149,18 @@
     out[...] = jnp.dot(hidden, down[...], preferred_element_type=jnp.float32)
     keep[:, :width] = out[:, columns(0)]
     keep[:, width:] = out[:, columns(2)]
-    send[:, :width] = out[:, columns(1)].astype(jnp.bfloat16)
-    send[:, width:] = out[:, columns(3)].astype(jnp.bfloat16)
+    near[...] = out[:, columns(1)].astype(jnp.bfloat16)
+    away[...] = out[:, columns(3)].astype(jnp.bfloat16)
 
 
 def expert_rows(chip, core, up_t, down, others, cost):
-    rows, model = chip.shape[0], up_t.shape[1]
+    rows, width, model = chip.shape[0], chip.shape[1] // 2, up_t.shape[1]
     return local_call(
         expert_kernel,
         [
             jax.ShapeDtypeStruct(chip.shape, jnp.float32),
-            jax.ShapeDtypeStruct(chip.shape, jnp.bfloat16),
+            jax.ShapeDtypeStruct((rows, width), jnp.bfloat16),
+            jax.ShapeDtypeStruct((rows, width), jnp.bfloat16),
         ],
         (chip, core, up_t, down),
         others,
@@ -172,71 +173,56 @@
     )
 
 
-def core_sum_kernel(keep, got, own, *sends):
-    width = own.shape[1]
-    own[...] = keep[:, :width] + got[:, :width].astype(jnp.float32)
-    for index, send in enumerate(sends):
-        rows = slice(index * send.shape[0], (index + 1) * send.shape[0])
-        send[...] = (keep[rows, width:] + got[rows, width:].astype(jnp.float32)).astype(send.dtype)
-
-
-def core_sum(keep, got, count, others, cost):
-    rows, width = keep.shape[0], keep.shape[1] // 2
-    return local_call(
-        core_sum_kernel,
-        [jax.ShapeDtypeStruct((rows, width), jnp.float32)]
-        + [jax.ShapeDtypeStruct((rows // count, width), jnp.bfloat16)] * count,
-        (keep, got),
+def core_sum_kernel(keep, got, away):
+    width = away.shape[1]
+    away[...] = (keep[:, width:] + got[...].astype(jnp.float32)).astype(away.dtype)
+
+
+def core_sum(keep, got, others, cost):
+    return local_call(
+        core_sum_kernel, jax.ShapeDtypeStruct(got.shape, jnp.bfloat16), (keep, got), others, cost=cost
+    )
+
+
+def chip_sum_kernel(keep, near, far, *parts):
+    rows, width = parts[0].shape
+    for index, part in enumerate(parts):
+        here = slice(index * rows, (index + 1) * rows)
+        total = keep[here, :width] + near[here, :].astype(jnp.float32)
+        part[...] = (total + far[here, :].astype(jnp.float32)).astype(part.dtype)
+
+
+def chip_sum(keep, near, far, count, others, cost):
+    shape = near.shape[0] // count, near.shape[1]
+    return local_call(
+        chip_sum_kernel,
+        [jax.ShapeDtypeStruct(shape, jnp.bfloat16)] * count,
+        (keep, near, far),
         others,
         cost=cost,
     )
 
 
-def chip_sum_kernel(index, own, got, part):
-    rows = slice(index * got.shape[0], (index + 1) * got.shape[0])
-    part[...] = (own[rows, :] + got[...].astype(jnp.float32)).astype(part.dtype)
-
-
-def chip_sum(own, got, index, others, cost):
-    return local_call(
-        functools.partial(chip_sum_kernel, index),
-        jax.ShapeDtypeStruct(got.shape, jnp.bfloat16),
-        (own, got),
-        others,
-        cost=cost,
-    )
-
-
-def weigh_kernel(steps, columns, own, got, *rest):
-    parts, out = rest[:-1], rest[-1]
+def weigh_kernel(steps, counts, columns, *refs):
+    refs, out = list(refs[:-1]), refs[-1]
     for at in range(0, out.shape[1], 128):
         here = slice(at, at + 128)
-        total = own[:, here]
-        if got is not None:
-            total = columns[0] * (total + got[:, here].astype(jnp.float32))
-        for step, part in zip(steps, parts):
-            total = total + columns[step] * part[:, here].astype(jnp.float32)
+        left = list(refs)
+        total = left.pop(0)[:, here] if len(left) > sum(counts) else None
+        for step, count in zip(steps, counts):
+            rows = sum(left.pop(0)[:, here].astype(jnp.float32) for _ in range(count))
+            rows = columns[step] * rows
+            total = rows if total is None else total + rows
         out[:, here] = total.astype(out.dtype)
 
 
-def weigh(columns, own, got, steps, parts):
-    return local_call(
-        functools.partial(weigh_kernel, steps),
-        jax.ShapeDtypeStruct(own.shape, jnp.float32),
-        (columns, own, got, *parts),
-        cost=4,
-    )
-
-
-def finish_kernel(steps, columns, total, *rest):
-    weigh_kernel(steps, columns, total, None, *rest)
-
-
-def finish(columns, total, steps, parts):
-    return local_call(
-        functools.partial(finish_kernel, steps),
-        jax.ShapeDtypeStruct(total.shape, jnp.bfloat16),
-        (columns, total, *parts),
+def weigh(columns, totals, steps, terms, dtype, cost):
+    arrays = [*totals, *[array for term in terms for array in term]]
+    return local_call(
+        functools.partial(weigh_kernel, steps, [len(term) for term in terms]),
+        jax.ShapeDtypeStruct(arrays[-1].shape, dtype),
+        (columns, *arrays),
+        cost=cost,
     )
 
 
@@ -255,7 +241,7 @@
     columns, up_t, down = prepare(
         expert_ids.T, weight_codes.T, up_local.T, down_local, experts_n, capacity
     )
-    blocks, others, chips, kept, sums, added, parts = {}, {}, {}, {}, {}, {}, {}
+    blocks, others, chips, kept, left, sums, added, parts = {}, {}, {}, {}, {}, {}, {}, {}
 
     def arrive(step, source, by, waits):
         blocks[step] = shift(source, by) if step else tokens
@@ -270,15 +256,15 @@
         chip = chips[steps]
         kept[steps] = expert_rows(chip, swap(chip, 1), up_t, down, waits, cost)
 
-    def leave(steps, waits, cost=2):
-        keep, send = kept[steps]
-        own, *aways = core_sum(keep, swap(send, 1), len(steps), waits, cost)
-        for index, step in enumerate(steps):
-            sums[step] = own, swap(aways[index], 2), index
-
-    def give(step, waits, cost=2):
-        added[step] = chip_sum(*sums[step], waits, cost)
-        parts[step] = shift(added[step], -step)
+    def leave(steps, waits, cost):
+        keep, near, away = kept[steps]
+        left[steps] = core_sum(keep, swap(away, 1), waits, cost)
+        sums[steps] = keep, swap(near, 1), swap(left[steps], 2)
+
+    def give(steps, waits, cost):
+        added[steps] = chip_sum(*sums[steps], len(steps), waits, cost)
+        for step, part in zip(steps, added[steps]):
+            parts[step] = shift(part, -step)
 
     arrive(0, tokens, 0, [])
     arrive(1, tokens, 1, [columns])
@@ -286,21 +272,22 @@
     lay((0,), [blocks[1], blocks[3]])
     run((0,), [], 2.6)
     arrive(2, blocks[1], 1, [kept[0,][0]])
-    lay((1,), [kept[0,][0], blocks[2]])
-    run((1,), [], 4)
-    lay((3,), [kept[1,][0]], .5)
-    lay((2,), [chips[3,]], 4)
-    leave((1,), [chips[2,]], 2)
-    run((3,), [sums[1][0]], 4)
-    run((2,), [kept[3,][0]], .05)
-    give(1, [kept[2,][0]], 2)
-    leave((3,), [added[1]], 4)
-    leave((2,), [sums[3][0]], 2)
-    leave((0,), [sums[2][0]])
-    give(3, [sums[2][0]], 4)
-    give(2, [added[3]], 4)
-    total = weigh(columns, *sums[0][:2], (1, 3), [parts[1], parts[3]])
-    return finish(columns, total, (2,), [parts[2]])
+    lay((1, 3), [kept[0,][0], blocks[2]])
+    run((1, 3), [], 2.6)
+    lay((2,), [kept[1, 3][0]], cost=4)
+    leave((1, 3), [chips[2,]], 2)
+    run((2,), [left[1, 3]], .05)
+    leave((2,), [kept[2,][0]], .05)
+    give((1, 3), [left[2,]], 2)
+    if False:
+        leave((0,), [added[1, 3][0]], 2)
+        give((2,), [left[0,]], 2)
+    else:
+        give((2,), [added[1, 3][0]], 2)
+        leave((0,), [added[2,][0]], 2)
+    total = weigh(columns, [], (1, 3), [[parts[1]], [parts[3]]], jnp.float32, 4)
+    total = weigh(columns, [total], (0,), [sums[0,]], jnp.float32, 4)
+    return weigh(columns, [total], (2,), [[parts[2]]], jnp.bfloat16, 0.5)
 
 
 def slotted(tokens, expert_ids, weight_codes, up_local, down_local, capacity):

time: 67.6 us -> 60.5 us (0.89)
  waiting for transfers between devices: 33.2 us -> 23.8 us
  starting transfers between devices: 17.9 us -> 22 us
  Pallas kernels: 16.1 us -> 14.5 us
    ppermute x16, waiting for transfers between devices: 15.9 us -> 9.16 us  [swap(): return lax.ppermute(array, 'tensor', [(i, i ^ bit) for i in range(4)])]
    ppermute x6, starting transfers between devices: 7.19 us -> 10.8 us  [shift(): lax.ppermute(array, 'expert', [(i, (i + by) % experts_n) for i in range(e...]
    ppermute x6, waiting for transfers between devices: 17.4 us -> 14.6 us  [shift(): lax.ppermute(array, 'expert', [(i, (i + by) % experts_n) for i in range(e...]
    pallas_call x18 -> x15, Pallas kernels: 16.1 us -> 14.5 us  [local_call(): pl.pallas_call(body_of, name=name, out_shape=out_shape, in_specs=list(in_...]
  transfers between devices with their start and end apart: 22 -> 22, of which waited for: 9 -> 11; matrix products, arithmetic and copies ran while one was open for 0% -> 0% of each run, Pallas kernels for 23% -> 23%
where the time goes in v10:
time: 60.5 us; the launch traced here: 60.3 us
  waiting for transfers between devices  23.8 us (39%)
  starting transfers between devices  22 us (36%)
  Pallas kernels  14.5 us (24%)
    ppermute x6, waiting for transfers between devices, shift(): lax.ppermute(array, 'expert', [(i, (i + by) % experts_n) for i in range(e...  14.6 us
    pallas_call x15, Pallas kernels, local_call(): pl.pallas_call(body_of, name=name, out_shape=out_shape, in_specs=list(in_...  14.5 us
    ppermute x16, starting transfers between devices, swap(): return lax.ppermute(array, 'tensor', [(i, i ^ bit) for i in range(4)])  11.2 us
    ppermute x6, starting transfers between devices, shift(): lax.ppermute(array, 'expert', [(i, (i + by) % experts_n) for i in range(e...  10.8 us
    ppermute x16, waiting for transfers between devices, swap(): return lax.ppermute(array, 'tensor', [(i, i ^ bit) for i in range(4)])  9.16 us
  transfers between devices with their start and end apart: 22, of which 11 were waited for; matrix products, arithmetic and copies ran while one was open for 0% of the time, Pallas kernels for 23%

profile of v10, /device:TPU:0, one launch (start us, length us, event | category | flops | bytes accessed | tf_op | source)
XLA Modules:
  0.0 60.3 jit_solution(16212253883131132988)
XLA Ops:
  0.0 3.0 %collective-permute-start = (bf16[96,896]{1,0:T(8,128)(2,1)}, bf16[96,896]{1,0:T(8,128)(2,1)S(1)}, u32[]{:S(2)}, u32[]{:S(2)}) collective-permute-start(bf16[96,896]{1,0:T(8,128)(2,1)} %refs_0_.1), channel_id=1, source_target_pairs={{0,4},{4,8},{8,12},{12,0},{1,5},{5,9},{9,13},{13,1},{2,6},{6,10},{... | collective-permute-start | bytes 516104 | tf_op jit(solution)/shard_map/ppermute | solution.py:237
  3.0 2.0 %collective-permute-start.2 = (bf16[96,896]{1,0:T(8,128)(2,1)}, bf16[96,896]{1,0:T(8,128)(2,1)S(1)}, u32[]{:S(2)}, u32[]{:S(2)}) collective-permute-start(bf16[96,896]{1,0:T(8,128)(2,1)} %refs_0_.1), channel_id=1, source_target_pairs={{0,12},{4,0},{8,4},{12,8},{1,13},{5,1},{9,5},{13,9},{2,14},{6,2},{... | collective-permute-start | bytes 516104 | tf_op jit(solution)/shard_map/ppermute | solution.py:237
  5.1 1.7 %collective-permute-start.4 = (bf16[96,896]{1,0:T(8,128)(2,1)}, bf16[96,896]{1,0:T(8,128)(2,1)S(1)}, u32[]{:S(2)}, u32[]{:S(2)}) collective-permute-start(bf16[96,896]{1,0:T(8,128)(2,1)} %refs_0_.1), channel_id=1, source_target_pairs={{0,2},{1,3},{2,0},{3,1},{4,6},{5,7},{6,4},{7,5},{8,10},{9,11},{10,... | collective-permute-start | bytes 516104 | tf_op jit(solution)/shard_map/ppermute | solution.py:230
  6.8 4.3 %prepare_kernel.1 = (f32[4,96,128]{2,1,0:T(8,128)S(1)}, bf16[608,3584]{1,0:T(8,128)(2,1)S(1)}, bf16[608,3584]{1,0:T(8,128)(2,1)S(1)}) custom-call(s32[2,96]{1,0:T(2,128)} %bitcast.8, s32[2,96]{1,0:T(2,128)} %bitcast.9, bf16[608,3584]{1,0:T(8,128)(2,1)} %bitcast.6, bf16[608,3584]{1,0:T(8,128)(2,1)} %bitcast.7), custom_call_target="tpu_custom_call" | custom-call | flops 4600000000 | tf_op jit(solution)/shard_map/prepare_kernel/pallas_call | solution.py:72
  11.1 1.6 %collective-permute-done.2.refs_0_ = bf16[96,896]{1,0:T(8,128)(2,1)S(1)} collective-permute-done((bf16[96,896]{1,0:T(8,128)(2,1)}, bf16[96,896]{1,0:T(8,128)(2,1)S(1)}, u32[]{:S(2)}, u32[]{:S(2)}) %collective-permute-start.2) | collective-permute-done | bytes 172064 | tf_op jit(solution)/shard_map/ppermute | solution.py:237
  12.9 1.2 %collective-permute-start.6 = (bf16[96,896]{1,0:T(8,128)(2,1)S(1)}, bf16[96,896]{1,0:T(8,128)(2,1)S(1)}, u32[]{:S(2)}, u32[]{:S(2)}) collective-permute-start(bf16[96,896]{1,0:T(8,128)(2,1)S(1)} %shard_map.55.refs_2_.refs_0_), channel_id=1, source_target_pairs={{0,4},{4,8},{8,12},{12,0},{1,5},{5,9},{9,13},{13,1},{2,6},{6,10},{... | collective-permute-start | bytes 516104 | tf_op jit(solution)/shard_map/ppermute | solution.py:237
  14.1 1.5 %collective-permute-start.1 = (bf16[96,896]{1,0:T(8,128)(2,1)S(1)}, bf16[96,896]{1,0:T(8,128)(2,1)S(1)}, u32[]{:S(2)}, u32[]{:S(2)}) collective-permute-start(bf16[96,896]{1,0:T(8,128)(2,1)S(1)} %shard_map.55.refs_2_.refs_0_), channel_id=1, source_target_pairs={{0,2},{1,3},{2,0},{3,1},{4,6},{5,7},{6,4},{7,5},{8,10},{9,11},{10,... | collective-permute-start | bytes 516104 | tf_op jit(solution)/shard_map/ppermute | solution.py:230
  16.1 2.6 %expert_kernel.3 = (f32[96,1792]{1,0:T(8,128)S(1)}, bf16[96,896]{1,0:T(8,128)(2,1)S(1)}, bf16[96,896]{1,0:T(8,128)(2,1)S(1)}) custom-call(bf16[96,1792]{1,0:T(8,128)(2,1)S(1)} %pack_kernel.3.refs_0_, bf16[96,1792]{1,0:T(8,128)(2,1)S(1)} %collective-permute-done.5.refs_1_, bf16[608,3584]{1,0:T(8,128)(2,1)S(1)} %get-tuple-element.20.refs_2_, ...), custom_call_target="tpu_custom_call" | custom-call | flops 2990000128 | tf_op jit(solution)/shard_map/expert_kernel/pallas_call | solution.py:72
  18.7 2.7 %collective-permute-done.6.refs_0_ = bf16[96,896]{1,0:T(8,128)(2,1)S(1)} collective-permute-done((bf16[96,896]{1,0:T(8,128)(2,1)S(1)}, bf16[96,896]{1,0:T(8,128)(2,1)S(1)}, u32[]{:S(2)}, u32[]{:S(2)}) %collective-permute-start.6) | collective-permute-done | bytes 172064 | tf_op jit(solution)/shard_map/ppermute | solution.py:237
  21.5 2.7 %collective-permute-done.3.refs_3_ = bf16[96,896]{1,0:T(8,128)(2,1)S(1)} collective-permute-done((bf16[96,896]{1,0:T(8,128)(2,1)S(1)}, bf16[96,896]{1,0:T(8,128)(2,1)S(1)}, u32[]{:S(2)}, u32[]{:S(2)}) %collective-permute-start.3) | collective-permute-done | bytes 172064 | tf_op jit(solution)/shard_map/ppermute | solution.py:230
  24.3 1.6 %collective-permute-start.10 = (bf16[96,896]{1,0:T(8,128)(2,1)S(1)}, bf16[96,896]{1,0:T(8,128)(2,1)S(1)}, u32[]{:S(2)}, u32[]{:S(2)}) collective-permute-start(bf16[96,896]{1,0:T(8,128)(2,1)S(1)} %shard_map.57.refs_5_.refs_0_), channel_id=1, source_target_pairs={{0,2},{1,3},{2,0},{3,1},{4,6},{5,7},{6,4},{7,5},{8,10},{9,11},{10,... | collective-permute-start | bytes 516104 | tf_op jit(solution)/shard_map/ppermute | solution.py:230
  26.5 3.6 %expert_kernel.4 = (f32[192,1792]{1,0:T(8,128)S(1)}, bf16[192,896]{1,0:T(8,128)(2,1)S(1)}, bf16[192,896]{1,0:T(8,128)(2,1)S(1)}) custom-call(bf16[192,1792]{1,0:T(8,128)(2,1)S(1)} %pack_kernel.4.refs_0_, bf16[192,1792]{1,0:T(8,128)(2,1)S(1)} %collective-permute-done.7.refs_1_, bf16[608,3584]{1,0:T(8,128)(2,1)S(1)} %get-tuple-element.20.refs_2_, ...), custom_call_target="tpu_custom_call" | custom-call | flops 2990000128 | tf_op jit(solution)/shard_map/expert_kernel/pallas_call | solution.py:72
  30.3 0.8 %collective-permute-done.10.refs_1_ = bf16[96,896]{1,0:T(8,128)(2,1)S(1)} collective-permute-done((bf16[96,896]{1,0:T(8,128)(2,1)S(1)}, bf16[96,896]{1,0:T(8,128)(2,1)S(1)}, u32[]{:S(2)}, u32[]{:S(2)}) %collective-permute-start.10) | collective-permute-done | bytes 172064 | tf_op jit(solution)/shard_map/ppermute | solution.py:230
  31.8 1.6 %collective-permute-start.11 = (bf16[192,896]{1,0:T(8,128)(2,1)S(1)}, bf16[192,896]{1,0:T(8,128)(2,1)S(1)}, u32[]{:S(2)}, u32[]{:S(2)}) collective-permute-start(bf16[192,896]{1,0:T(8,128)(2,1)S(1)} %core_sum_kernel.3.refs_4_), channel_id=1, source_target_pairs={{0,2},{1,3},{2,0},{3,1},{4,6},{5,7},{6,4},{7,5},{8,10},{9,11},{10,... | collective-permute-start | bytes 1032200 | tf_op jit(solution)/shard_map/ppermute | solution.py:230
  33.4 2.6 %expert_kernel.5 = (f32[96,1792]{1,0:T(8,128)S(1)}, bf16[96,896]{1,0:T(8,128)(2,1)S(1)}, bf16[96,896]{1,0:T(8,128)(2,1)S(1)}) custom-call(bf16[96,1792]{1,0:T(8,128)(2,1)S(1)} %pack_kernel.5.refs_2_.refs_0_, bf16[96,1792]{1,0:T(8,128)(2,1)S(1)} %collective-permute-done.12.refs_1_, bf16[608,3584]{1,0:T(8,128)(2,1)S(1)} %get-tuple-element.20.refs_2_, ...), custom_call_target="tpu_custom_call" | custom-call | flops 57500000 | tf_op jit(solution)/shard_map/expert_kernel/pallas_call | solution.py:72
  36.7 0.8 %collective-permute-done.13.refs_1_ = bf16[96,896]{1,0:T(8,128)(2,1)S(1)} collective-permute-done((bf16[96,896]{1,0:T(8,128)(2,1)S(1)}, bf16[96,896]{1,0:T(8,128)(2,1)S(1)}, u32[]{:S(2)}, u32[]{:S(2)}) %collective-permute-start.13) | collective-permute-done | bytes 172064 | tf_op jit(solution)/shard_map/ppermute | solution.py:230
  37.7 1.0 %collective-permute-start.19 = (bf16[96,896]{1,0:T(8,128)(2,1)S(1)}, bf16[96,896]{1,0:T(8,128)(2,1)S(1)}, u32[]{:S(2)}, u32[]{:S(2)}) collective-permute-start(bf16[96,896]{1,0:T(8,128)(2,1)S(1)} %core_sum_kernel.4.refs_3_), channel_id=1, source_target_pairs={{0,2},{1,3},{2,0},{3,1},{4,6},{5,7},{6,4},{7,5},{8,10},{9,11},{10,... | collective-permute-start | bytes 516104 | tf_op jit(solution)/shard_map/ppermute | solution.py:230
  38.7 4.1 %collective-permute-done.11.refs_2_ = bf16[192,896]{1,0:T(8,128)(2,1)S(1)} collective-permute-done((bf16[192,896]{1,0:T(8,128)(2,1)S(1)}, bf16[192,896]{1,0:T(8,128)(2,1)S(1)}, u32[]{:S(2)}, u32[]{:S(2)}) %collective-permute-start.11) | collective-permute-done | bytes 344096 | tf_op jit(solution)/shard_map/ppermute | solution.py:230
  42.9 2.8 %collective-permute-start.14 = (bf16[96,896]{1,0:T(8,128)(2,1)S(1)}, bf16[96,896]{1,0:T(8,128)(2,1)S(1)}, u32[]{:S(2)}, u32[]{:S(2)}) collective-permute-start(bf16[96,896]{1,0:T(8,128)(2,1)S(1)} %get-tuple-element.28.refs_3_), channel_id=1, source_target_pairs={{0,12},{4,0},{8,4},{12,8},{1,13},{5,1},{9,5},{13,9},{2,14},{6,2},{... | collective-permute-start | bytes 516104 | tf_op jit(solution)/shard_map/ppermute | solution.py:237
  45.8 1.8 %collective-permute-start.21 = (bf16[96,896]{1,0:T(8,128)(2,1)S(1)}, bf16[96,896]{1,0:T(8,128)(2,1)S(1)}, u32[]{:S(2)}, u32[]{:S(2)}) collective-permute-start(bf16[96,896]{1,0:T(8,128)(2,1)S(1)} %chip_sum_kernel.3.refs_2_), channel_id=1, source_target_pairs={{0,8},{4,12},{8,0},{12,4},{1,9},{5,13},{9,1},{13,5},{2,10},{6,14},... | collective-permute-start | bytes 516104 | tf_op jit(solution)/shard_map/ppermute | solution.py:237
  47.6 1.6 %collective-permute-start.20 = (bf16[96,896]{1,0:T(8,128)(2,1)S(1)}, bf16[96,896]{1,0:T(8,128)(2,1)S(1)}, u32[]{:S(2)}, u32[]{:S(2)}) collective-permute-start(bf16[96,896]{1,0:T(8,128)(2,1)S(1)} %core_sum_kernel.5), channel_id=1, source_target_pairs={{0,2},{1,3},{2,0},{3,1},{4,6},{5,7},{6,4},{7,5},{8,10},{9,11},{10,... | collective-permute-start | bytes 516104 | tf_op jit(solution)/shard_map/ppermute | solution.py:230
  49.2 1.3 %collective-permute-done.14.refs_1_ = bf16[96,896]{1,0:T(8,128)(2,1)S(1)} collective-permute-done((bf16[96,896]{1,0:T(8,128)(2,1)S(1)}, bf16[96,896]{1,0:T(8,128)(2,1)S(1)}, u32[]{:S(2)}, u32[]{:S(2)}) %collective-permute-start.14) | collective-permute-done | bytes 172064 | tf_op jit(solution)/shard_map/ppermute | solution.py:237
  50.6 4.2 %collective-permute-done.15.refs_2_ = bf16[96,896]{1,0:T(8,128)(2,1)S(1)} collective-permute-done((bf16[96,896]{1,0:T(8,128)(2,1)S(1)}, bf16[96,896]{1,0:T(8,128)(2,1)S(1)}, u32[]{:S(2)}, u32[]{:S(2)}) %collective-permute-start.15) | collective-permute-done | bytes 172064 | tf_op jit(solution)/shard_map/ppermute | solution.py:237
  55.0 4.6 %collective-permute-done.21.refs_2_ = bf16[96,896]{1,0:T(8,128)(2,1)S(1)} collective-permute-done((bf16[96,896]{1,0:T(8,128)(2,1)S(1)}, bf16[96,896]{1,0:T(8,128)(2,1)S(1)}, u32[]{:S(2)}, u32[]{:S(2)}) %collective-permute-start.21) | collective-permute-done | bytes 172064 | tf_op jit(solution)/shard_map/ppermute | solution.py:237
  (40 shorter events, 4.2 us)
Async XLA Ops:
  0.0 11.1 %collective-permute-start = (bf16[96,896]{1,0:T(8,128)(2,1)}, bf16[96,896]{1,0:T(8,128)(2,1)S(1)}, u32[]{:S(2)}, u32[]{:S(2)}) collective-permute-start(bf16[96,896]{1,0:T(8,128)(2,1)} %refs_0_.1), channel_id=1, source_target_pairs={{0,4},{4,8},{8,12},{12,0},{1,5},{5,9},{9,13},{13,1},{2,6},{6,10},{... | collective-permute-start | bytes 516104 | tf_op jit(solution)/shard_map/ppermute | solution.py:237
  3.0 9.7 %collective-permute-start.2 = (bf16[96,896]{1,0:T(8,128)(2,1)}, bf16[96,896]{1,0:T(8,128)(2,1)S(1)}, u32[]{:S(2)}, u32[]{:S(2)}) collective-permute-start(bf16[96,896]{1,0:T(8,128)(2,1)} %refs_0_.1), channel_id=1, source_target_pairs={{0,12},{4,0},{8,4},{12,8},{1,13},{5,1},{9,5},{13,9},{2,14},{6,2},{... | collective-permute-start | bytes 516104 | tf_op jit(solution)/shard_map/ppermute | solution.py:237
  5.1 7.7 %collective-permute-start.4 = (bf16[96,896]{1,0:T(8,128)(2,1)}, bf16[96,896]{1,0:T(8,128)(2,1)S(1)}, u32[]{:S(2)}, u32[]{:S(2)}) collective-permute-start(bf16[96,896]{1,0:T(8,128)(2,1)} %refs_0_.1), channel_id=1, source_target_pairs={{0,2},{1,3},{2,0},{3,1},{4,6},{5,7},{6,4},{7,5},{8,10},{9,11},{10,... | collective-permute-start | bytes 516104 | tf_op jit(solution)/shard_map/ppermute | solution.py:230
  6.8 6.0 %copy-start = (bf16[96,896]{1,0:T(8,128)(2,1)S(1)}, bf16[96,896]{1,0:T(8,128)(2,1)}, u32[]{:S(2)}) copy-start(bf16[96,896]{1,0:T(8,128)(2,1)} %refs_0_.1) | copy-start | bytes 516100
  12.8 3.3 %collective-permute-start.5 = (bf16[96,1792]{1,0:T(8,128)(2,1)S(1)}, bf16[96,1792]{1,0:T(8,128)(2,1)S(1)}, u32[]{:S(2)}, u32[]{:S(2)}) collective-permute-start(bf16[96,1792]{1,0:T(8,128)(2,1)S(1)} %pack_kernel.3.refs_0_), channel_id=1, source_target_pairs={{0,1},{1,0},{2,3},{3,2},{4,5},{5,4},{6,7},{7,6},{8,9},{9,8},{10,11... | collective-permute-start | bytes 1032200 | tf_op jit(solution)/shard_map/ppermute | solution.py:230
  12.9 8.6 %collective-permute-start.6 = (bf16[96,896]{1,0:T(8,128)(2,1)S(1)}, bf16[96,896]{1,0:T(8,128)(2,1)S(1)}, u32[]{:S(2)}, u32[]{:S(2)}) collective-permute-start(bf16[96,896]{1,0:T(8,128)(2,1)S(1)} %shard_map.55.refs_2_.refs_0_), channel_id=1, source_target_pairs={{0,4},{4,8},{8,12},{12,0},{1,5},{5,9},{9,13},{13,1},{2,6},{6,10},{... | collective-permute-start | bytes 516104 | tf_op jit(solution)/shard_map/ppermute | solution.py:237
  14.1 7.4 %collective-permute-start.1 = (bf16[96,896]{1,0:T(8,128)(2,1)S(1)}, bf16[96,896]{1,0:T(8,128)(2,1)S(1)}, u32[]{:S(2)}, u32[]{:S(2)}) collective-permute-start(bf16[96,896]{1,0:T(8,128)(2,1)S(1)} %shard_map.55.refs_2_.refs_0_), channel_id=1, source_target_pairs={{0,2},{1,3},{2,0},{3,1},{4,6},{5,7},{6,4},{7,5},{8,10},{9,11},{10,... | collective-permute-start | bytes 516104 | tf_op jit(solution)/shard_map/ppermute | solution.py:230
  15.5 8.6 %collective-permute-start.3 = (bf16[96,896]{1,0:T(8,128)(2,1)S(1)}, bf16[96,896]{1,0:T(8,128)(2,1)S(1)}, u32[]{:S(2)}, u32[]{:S(2)}) collective-permute-start(bf16[96,896]{1,0:T(8,128)(2,1)S(1)} %shard_map.56.refs_3_.refs_2_), channel_id=1, source_target_pairs={{0,2},{1,3},{2,0},{3,1},{4,6},{5,7},{6,4},{7,5},{8,10},{9,11},{10,... | collective-permute-start | bytes 516104 | tf_op jit(solution)/shard_map/ppermute | solution.py:230
  24.2 2.2 %collective-permute-start.7 = (bf16[192,1792]{1,0:T(8,128)(2,1)S(1)}, bf16[192,1792]{1,0:T(8,128)(2,1)S(1)}, u32[]{:S(2)}, u32[]{:S(2)}) collective-permute-start(bf16[192,1792]{1,0:T(8,128)(2,1)S(1)} %pack_kernel.4.refs_0_), channel_id=1, source_target_pairs={{0,1},{1,0},{2,3},{3,2},{4,5},{5,4},{6,7},{7,6},{8,9},{9,8},{10,11... | collective-permute-start | bytes 2064392 | tf_op jit(solution)/shard_map/ppermute | solution.py:230
  24.3 6.8 %collective-permute-start.10 = (bf16[96,896]{1,0:T(8,128)(2,1)S(1)}, bf16[96,896]{1,0:T(8,128)(2,1)S(1)}, u32[]{:S(2)}, u32[]{:S(2)}) collective-permute-start(bf16[96,896]{1,0:T(8,128)(2,1)S(1)} %shard_map.57.refs_5_.refs_0_), channel_id=1, source_target_pairs={{0,2},{1,3},{2,0},{3,1},{4,6},{5,7},{6,4},{7,5},{8,10},{9,11},{10,... | collective-permute-start | bytes 516104 | tf_op jit(solution)/shard_map/ppermute | solution.py:230
  30.1 1.7 %collective-permute-start.9 = (bf16[192,896]{1,0:T(8,128)(2,1)S(1)}, bf16[192,896]{1,0:T(8,128)(2,1)S(1)}, u32[]{:S(2)}, u32[]{:S(2)}) collective-permute-start(bf16[192,896]{1,0:T(8,128)(2,1)S(1)} %get-tuple-element.25), channel_id=1, source_target_pairs={{0,1},{1,0},{2,3},{3,2},{4,5},{5,4},{6,7},{7,6},{8,9},{9,8},{10,11... | collective-permute-start | bytes 1032200 | tf_op jit(solution)/shard_map/ppermute | solution.py:230
  31.1 2.3 %collective-permute-start.12 = (bf16[96,1792]{1,0:T(8,128)(2,1)S(1)}, bf16[96,1792]{1,0:T(8,128)(2,1)S(1)}, u32[]{:S(2)}, u32[]{:S(2)}) collective-permute-start(bf16[96,1792]{1,0:T(8,128)(2,1)S(1)} %pack_kernel.5.refs_2_.refs_0_), channel_id=1, source_target_pairs={{0,1},{1,0},{2,3},{3,2},{4,5},{5,4},{6,7},{7,6},{8,9},{9,8},{10,11... | collective-permute-start | bytes 1032200 | tf_op jit(solution)/shard_map/ppermute | solution.py:230
  31.2 6.5 %collective-permute-start.8 = (bf16[192,896]{1,0:T(8,128)(2,1)S(1)}, bf16[192,896]{1,0:T(8,128)(2,1)S(1)}, u32[]{:S(2)}, u32[]{:S(2)}) collective-permute-start(bf16[192,896]{1,0:T(8,128)(2,1)S(1)} %get-tuple-element.24), channel_id=1, source_target_pairs={{0,1},{1,0},{2,3},{3,2},{4,5},{5,4},{6,7},{7,6},{8,9},{9,8},{10,11... | collective-permute-start | bytes 1032200 | tf_op jit(solution)/shard_map/ppermute | solution.py:230
  31.8 11.0 %collective-permute-start.11 = (bf16[192,896]{1,0:T(8,128)(2,1)S(1)}, bf16[192,896]{1,0:T(8,128)(2,1)S(1)}, u32[]{:S(2)}, u32[]{:S(2)}) collective-permute-start(bf16[192,896]{1,0:T(8,128)(2,1)S(1)} %core_sum_kernel.3.refs_4_), channel_id=1, source_target_pairs={{0,2},{1,3},{2,0},{3,1},{4,6},{5,7},{6,4},{7,5},{8,10},{9,11},{10,... | collective-permute-start | bytes 1032200 | tf_op jit(solution)/shard_map/ppermute | solution.py:230
  36.0 1.5 %collective-permute-start.13 = (bf16[96,896]{1,0:T(8,128)(2,1)S(1)}, bf16[96,896]{1,0:T(8,128)(2,1)S(1)}, u32[]{:S(2)}, u32[]{:S(2)}) collective-permute-start(bf16[96,896]{1,0:T(8,128)(2,1)S(1)} %get-tuple-element.27), channel_id=1, source_target_pairs={{0,1},{1,0},{2,3},{3,2},{4,5},{5,4},{6,7},{7,6},{8,9},{9,8},{10,11... | collective-permute-start | bytes 516104 | tf_op jit(solution)/shard_map/ppermute | solution.py:230
  36.1 11.5 %collective-permute-start.17 = (bf16[96,896]{1,0:T(8,128)(2,1)S(1)}, bf16[96,896]{1,0:T(8,128)(2,1)S(1)}, u32[]{:S(2)}, u32[]{:S(2)}) collective-permute-start(bf16[96,896]{1,0:T(8,128)(2,1)S(1)} %get-tuple-element.31), channel_id=1, source_target_pairs={{0,1},{1,0},{2,3},{3,2},{4,5},{5,4},{6,7},{7,6},{8,9},{9,8},{10,11... | collective-permute-start | bytes 516104 | tf_op jit(solution)/shard_map/ppermute | solution.py:230
  36.6 18.2 %collective-permute-start.16 = (bf16[96,896]{1,0:T(8,128)(2,1)S(1)}, bf16[96,896]{1,0:T(8,128)(2,1)S(1)}, u32[]{:S(2)}, u32[]{:S(2)}) collective-permute-start(bf16[96,896]{1,0:T(8,128)(2,1)S(1)} %get-tuple-element.30), channel_id=1, source_target_pairs={{0,1},{1,0},{2,3},{3,2},{4,5},{5,4},{6,7},{7,6},{8,9},{9,8},{10,11... | collective-permute-start | bytes 516104 | tf_op jit(solution)/shard_map/ppermute | solution.py:230
  37.5 8.2 %collective-permute-start.18 = (bf16[96,896]{1,0:T(8,128)(2,1)S(1)}, bf16[96,896]{1,0:T(8,128)(2,1)S(1)}, u32[]{:S(2)}, u32[]{:S(2)}) collective-permute-start(bf16[96,896]{1,0:T(8,128)(2,1)S(1)} %get-tuple-element.32), channel_id=1, source_target_pairs={{0,1},{1,0},{2,3},{3,2},{4,5},{5,4},{6,7},{7,6},{8,9},{9,8},{10,11... | collective-permute-start | bytes 516104 | tf_op jit(solution)/shard_map/ppermute | solution.py:230
  37.7 8.0 %collective-permute-start.19 = (bf16[96,896]{1,0:T(8,128)(2,1)S(1)}, bf16[96,896]{1,0:T(8,128)(2,1)S(1)}, u32[]{:S(2)}, u32[]{:S(2)}) collective-permute-start(bf16[96,896]{1,0:T(8,128)(2,1)S(1)} %core_sum_kernel.4.refs_3_), channel_id=1, source_target_pairs={{0,2},{1,3},{2,0},{3,1},{4,6},{5,7},{6,4},{7,5},{8,10},{9,11},{10,... | collective-permute-start | bytes 516104 | tf_op jit(solution)/shard_map/ppermute | solution.py:230
  42.9 7.6 %collective-permute-start.14 = (bf16[96,896]{1,0:T(8,128)(2,1)S(1)}, bf16[96,896]{1,0:T(8,128)(2,1)S(1)}, u32[]{:S(2)}, u32[]{:S(2)}) collective-permute-start(bf16[96,896]{1,0:T(8,128)(2,1)S(1)} %get-tuple-element.28.refs_3_), channel_id=1, source_target_pairs={{0,12},{4,0},{8,4},{12,8},{1,13},{5,1},{9,5},{13,9},{2,14},{6,2},{... | collective-permute-start | bytes 516104 | tf_op jit(solution)/shard_map/ppermute | solution.py:237
  45.7 9.1 %collective-permute-start.15 = (bf16[96,896]{1,0:T(8,128)(2,1)S(1)}, bf16[96,896]{1,0:T(8,128)(2,1)S(1)}, u32[]{:S(2)}, u32[]{:S(2)}) collective-permute-start(bf16[96,896]{1,0:T(8,128)(2,1)S(1)} %get-tuple-element.29), channel_id=1, source_target_pairs={{0,4},{4,8},{8,12},{12,0},{1,5},{5,9},{9,13},{13,1},{2,6},{6,10},{... | collective-permute-start | bytes 516104 | tf_op jit(solution)/shard_map/ppermute | solution.py:237
  45.8 13.9 %collective-permute-start.21 = (bf16[96,896]{1,0:T(8,128)(2,1)S(1)}, bf16[96,896]{1,0:T(8,128)(2,1)S(1)}, u32[]{:S(2)}, u32[]{:S(2)}) collective-permute-start(bf16[96,896]{1,0:T(8,128)(2,1)S(1)} %chip_sum_kernel.3.refs_2_), channel_id=1, source_target_pairs={{0,8},{4,12},{8,0},{12,4},{1,9},{5,13},{9,1},{13,5},{2,10},{6,14},... | collective-permute-start | bytes 516104 | tf_op jit(solution)/shard_map/ppermute | solution.py:237
  47.6 7.2 %collective-permute-start.20 = (bf16[96,896]{1,0:T(8,128)(2,1)S(1)}, bf16[96,896]{1,0:T(8,128)(2,1)S(1)}, u32[]{:S(2)}, u32[]{:S(2)}) collective-permute-start(bf16[96,896]{1,0:T(8,128)(2,1)S(1)} %core_sum_kernel.5), channel_id=1, source_target_pairs={{0,2},{1,3},{2,0},{3,1},{4,6},{5,7},{6,4},{7,5},{8,10},{9,11},{10,... | collective-permute-start | bytes 516104 | tf_op jit(solution)/shard_map/ppermute | solution.py:230

commit v11 on v9

--- a/solution.py
+++ b/solution.py
@@ -36,13 +36,16 @@
     )
 
 
-def prepare_kernel(capacity, experts_n, ids, codes, up, down, columns, up_out, down_out, sems):
+def prepare_kernel(
+    capacity, experts_n, ids, codes, tokens, up, down, columns, copy_out, up_out, down_out, sems
+):
     copies = [
         pltpu.make_async_copy(up, up_out, sems.at[0]),
         pltpu.make_async_copy(down, down_out, sems.at[1]),
     ]
     for copy in copies:
         copy.start()
+    copy_out[...] = tokens[...]
     me = lax.axis_index("expert")
     weight = kept_weights(ids[...], codes[...], experts_n, capacity)
     rows = weight.shape[1]
@@ -95,17 +98,18 @@
     )(array, other)
 
 
-def prepare(ids, codes, up_t, down, experts_n, capacity):
+def prepare(ids, codes, tokens, up_t, down, experts_n, capacity):
     rows = ids.shape[1]
     return local_call(
         functools.partial(prepare_kernel, capacity, experts_n),
         [
             pltpu.VMEM((experts_n, rows, 128), jnp.float32),
+            pltpu.VMEM(tokens.shape, tokens.dtype),
             pltpu.VMEM(up_t.shape, up_t.dtype),
             pltpu.VMEM(down.shape, down.dtype),
         ],
-        (ids, codes, up_t, down),
-        in_specs=[VMEM, VMEM, HBM, HBM],
+        (ids, codes, tokens, up_t, down),
+        in_specs=[VMEM, VMEM, VMEM, HBM, HBM],
         scratch_shapes=[pltpu.SemaphoreType.DMA((2,))],
         limit=50 * MIB,
         cost=4,
@@ -252,8 +256,8 @@
             array, "expert", [(i, (i + by) % experts_n) for i in range(experts_n)]
         )
 
-    columns, up_t, down = prepare(
-        expert_ids.T, weight_codes.T, up_local.T, down_local, experts_n, capacity
+    columns, copied, up_t, down = prepare(
+        expert_ids.T, weight_codes.T, tokens, up_local.T, down_local, experts_n, capacity
     )
     blocks, others, chips, kept, sums, added, parts = {}, {}, {}, {}, {}, {}, {}
 
@@ -282,25 +286,25 @@
 
     arrive(0, tokens, 0, [])
     arrive(1, tokens, 1, [columns])
-    arrive(3, tokens, -1, [columns])
-    lay((0,), [blocks[1], blocks[3]])
+    lay((0,), [blocks[1]])
     run((0,), [], 2.6)
     arrive(2, blocks[1], 1, [kept[0,][0]])
-    lay((1,), [kept[0,][0], blocks[2]])
+    arrive(3, after(copied, chips[0,]), -1, [kept[0,][0]])
+    lay((1,), [blocks[2], blocks[3]], .5)
     run((1,), [], 4)
-    lay((3,), [kept[1,][0]], .5)
-    lay((2,), [chips[3,]], 4)
+    lay((2,), [kept[1,][0]], 4)
     leave((1,), [chips[2,]], 2)
-    run((3,), [sums[1][0]], 4)
-    run((2,), [kept[3,][0]], .05)
-    give(1, [kept[2,][0]], 2)
+    run((2,), [sums[1][0]], 4)
+    lay((3,), [kept[2,][0]], 4)
+    leave((2,), [chips[3,]], 4)
+    run((3,), [sums[2][0]], 4)
+    give(1, [kept[3,][0]], 4)
     leave((3,), [added[1]], 4)
-    leave((2,), [sums[3][0]], 2)
-    leave((0,), [sums[2][0]])
-    give(3, [sums[2][0]], 4)
-    give(2, [added[3]], 4)
-    total = weigh(columns, *sums[0][:2], (1, 3), [parts[1], parts[3]])
-    return finish(columns, total, (2,), [parts[2]])
+    give(2, [sums[3][0]], 2)
+    give(3, [added[2]], 2)
+    leave((0,), [added[3]], 2)
+    total = weigh(columns, *sums[0][:2], (1, 2), [parts[1], parts[2]])
+    return finish(columns, total, (3,), [parts[3]])
 
 
 def slotted(tokens, expert_ids, weight_codes, up_local, down_local, capacity):

time: 67.6 us -> 63.4 us (0.938)
  waiting for transfers between devices: 33.2 us -> 26.5 us
  starting transfers between devices: 17.9 us -> 20.1 us
    ppermute x6, waiting for transfers between devices: 17.4 us -> 13.3 us  [shift(): lax.ppermute(array, 'expert', [(i, (i + by) % experts_n) for i in range(e...]
    ppermute x16, waiting for transfers between devices: 15.9 us -> 13.3 us  [swap(): return lax.ppermute(array, 'tensor', [(i, i ^ bit) for i in range(4)])]
    ppermute x16, starting transfers between devices: 10.7 us -> 11.9 us  [swap(): return lax.ppermute(array, 'tensor', [(i, i ^ bit) for i in range(4)])]
    ppermute x6, starting transfers between devices: 7.19 us -> 8.17 us  [shift(): lax.ppermute(array, 'expert', [(i, (i + by) % experts_n) for i in range(e...]
  transfers between devices with their start and end apart: 22 -> 22, of which waited for: 9 -> 10; matrix products, arithmetic and copies ran while one was open for 0% -> 0% of each run, Pallas kernels for 23% -> 25%
where the time goes in v11:
time: 63.4 us; the launch traced here: 63.2 us
  waiting for transfers between devices  26.5 us (42%)
  starting transfers between devices  20.1 us (32%)
  Pallas kernels  16.5 us (26%)
    pallas_call x18, Pallas kernels, local_call(): pl.pallas_call(body_of, name=name, out_shape=out_shape, in_specs=list(in_...  16.5 us
    ppermute x6, waiting for transfers between devices, shift(): lax.ppermute(array, 'expert', [(i, (i + by) % experts_n) for i in range(e...  13.3 us
    ppermute x16, waiting for transfers between devices, swap(): return lax.ppermute(array, 'tensor', [(i, i ^ bit) for i in range(4)])  13.3 us
    ppermute x16, starting transfers between devices, swap(): return lax.ppermute(array, 'tensor', [(i, i ^ bit) for i in range(4)])  11.9 us
    ppermute x6, starting transfers between devices, shift(): lax.ppermute(array, 'expert', [(i, (i + by) % experts_n) for i in range(e...  8.17 us
  transfers between devices with their start and end apart: 22, of which 10 were waited for; matrix products, arithmetic and copies ran while one was open for 0% of the time, Pallas kernels for 25%

profile of v11, /device:TPU:0, one launch (start us, length us, event | category | flops | bytes accessed | tf_op | source)
XLA Modules:
  0.0 63.2 jit_solution(5008657649583430190)
XLA Ops:
  0.0 2.9 %collective-permute-start = (bf16[96,896]{1,0:T(8,128)(2,1)}, bf16[96,896]{1,0:T(8,128)(2,1)S(1)}, u32[]{:S(2)}, u32[]{:S(2)}) collective-permute-start(bf16[96,896]{1,0:T(8,128)(2,1)} %refs_0_.1), channel_id=1, source_target_pairs={{0,2},{1,3},{2,0},{3,1},{4,6},{5,7},{6,4},{7,5},{8,10},{9,11},{10,... | collective-permute-start | bytes 516104 | tf_op jit(solution)/shard_map/ppermute | solution.py:248
  2.9 1.6 %collective-permute-start.1 = (bf16[96,896]{1,0:T(8,128)(2,1)}, bf16[96,896]{1,0:T(8,128)(2,1)S(1)}, u32[]{:S(2)}, u32[]{:S(2)}) collective-permute-start(bf16[96,896]{1,0:T(8,128)(2,1)} %refs_0_.1), channel_id=1, source_target_pairs={{0,4},{4,8},{8,12},{12,0},{1,5},{5,9},{9,13},{13,1},{2,6},{6,10},{... | collective-permute-start | bytes 516104 | tf_op jit(solution)/shard_map/ppermute | solution.py:255
  4.5 4.6 %prepare_kernel.1 = (f32[4,96,128]{2,1,0:T(8,128)S(1)}, bf16[96,896]{1,0:T(8,128)(2,1)S(1)}, bf16[608,3584]{1,0:T(8,128)(2,1)S(1)}, bf16[608,3584]{1,0:T(8,128)(2,1)S(1)}) custom-call(s32[2,96]{1,0:T(2,128)} %bitcast.8, s32[2,96]{1,0:T(2,128)} %bitcast.9, bf16[96,896]{1,0:T(8,128)(2,1)} %refs_0_.1, bf16[608,3584]{1,0:T(8,128)(2,1)} %bitcast.6, ...), custom_call_target="tpu_custom_call" | custom-call | flops 4600000000 | tf_op jit(solution)/shard_map/prepare_kernel/pallas_call | solution.py:75
  9.2 1.7 %collective-permute-done.1.refs_0_ = bf16[96,896]{1,0:T(8,128)(2,1)S(1)} collective-permute-done((bf16[96,896]{1,0:T(8,128)(2,1)}, bf16[96,896]{1,0:T(8,128)(2,1)S(1)}, u32[]{:S(2)}, u32[]{:S(2)}) %collective-permute-start.1) | collective-permute-done | bytes 172064 | tf_op jit(solution)/shard_map/ppermute | solution.py:255
  11.6 3.8 %collective-permute-start.4 = (bf16[96,896]{1,0:T(8,128)(2,1)S(1)}, bf16[96,896]{1,0:T(8,128)(2,1)S(1)}, u32[]{:S(2)}, u32[]{:S(2)}) collective-permute-start(bf16[96,896]{1,0:T(8,128)(2,1)S(1)} %shard_map.56), channel_id=1, source_target_pairs={{0,12},{4,0},{8,4},{12,8},{1,13},{5,1},{9,5},{13,9},{2,14},{6,2},{... | collective-permute-start | bytes 516104 | tf_op jit(solution)/shard_map/ppermute | solution.py:255
  15.4 2.6 %expert_kernel.4 = (f32[96,1792]{1,0:T(8,128)S(1)}, bf16[96,1792]{1,0:T(8,128)(2,1)S(1)}) custom-call(bf16[96,1792]{1,0:T(8,128)(2,1)S(1)} %pack_kernel.4.refs_0_.refs_1_, bf16[96,1792]{1,0:T(8,128)(2,1)S(1)} %collective-permute-done.2.refs_1_, bf16[608,3584]{1,0:T(8,128)(2,1)S(1)} %get-tuple-element.26.refs_2_, bf16[608,3584]{1,0:T(8,128)(2,1)S(1)} %get-tuple-element.27.refs_3_), custom_call_target="tpu_custom_call" | custom-call | flops 2990000128 | tf_op jit(solution)/shard_map/expert_kernel/pallas_call | solution.py:75
  18.0 2.6 %collective-permute-done.6.refs_0_ = bf16[96,896]{1,0:T(8,128)(2,1)S(1)} collective-permute-done((bf16[96,896]{1,0:T(8,128)(2,1)S(1)}, bf16[96,896]{1,0:T(8,128)(2,1)S(1)}, u32[]{:S(2)}, u32[]{:S(2)}) %collective-permute-start.6) | collective-permute-done | bytes 172064 | tf_op jit(solution)/shard_map/ppermute | solution.py:255
  20.7 1.1 %collective-permute-done.4.refs_0_ = bf16[96,896]{1,0:T(8,128)(2,1)S(1)} collective-permute-done((bf16[96,896]{1,0:T(8,128)(2,1)S(1)}, bf16[96,896]{1,0:T(8,128)(2,1)S(1)}, u32[]{:S(2)}, u32[]{:S(2)}) %collective-permute-start.4) | collective-permute-done | bytes 172064 | tf_op jit(solution)/shard_map/ppermute | solution.py:255
  21.8 1.6 %collective-permute-start.7 = (bf16[96,896]{1,0:T(8,128)(2,1)S(1)}, bf16[96,896]{1,0:T(8,128)(2,1)S(1)}, u32[]{:S(2)}, u32[]{:S(2)}) collective-permute-start(bf16[96,896]{1,0:T(8,128)(2,1)S(1)} %shard_map.58.refs_2_.refs_0_), channel_id=1, source_target_pairs={{0,2},{1,3},{2,0},{3,1},{4,6},{5,7},{6,4},{7,5},{8,10},{9,11},{10,... | collective-permute-start | bytes 516104 | tf_op jit(solution)/shard_map/ppermute | solution.py:248
  23.5 2.6 %expert_kernel.5 = (f32[96,1792]{1,0:T(8,128)S(1)}, bf16[96,1792]{1,0:T(8,128)(2,1)S(1)}) custom-call(bf16[96,1792]{1,0:T(8,128)(2,1)S(1)} %pack_kernel.5.refs_0_, bf16[96,1792]{1,0:T(8,128)(2,1)S(1)} %collective-permute-done.9.refs_1_, bf16[608,3584]{1,0:T(8,128)(2,1)S(1)} %get-tuple-element.26.refs_2_, bf16[608,3584]{1,0:T(8,128)(2,1)S(1)} %get-tuple-element.27.refs_3_), custom_call_target="tpu_custom_call" | custom-call | flops 4600000000 | tf_op jit(solution)/shard_map/expert_kernel/pallas_call | solution.py:75
  26.3 2.3 %collective-permute-done.7.refs_1_ = bf16[96,896]{1,0:T(8,128)(2,1)S(1)} collective-permute-done((bf16[96,896]{1,0:T(8,128)(2,1)S(1)}, bf16[96,896]{1,0:T(8,128)(2,1)S(1)}, u32[]{:S(2)}, u32[]{:S(2)}) %collective-permute-start.7) | collective-permute-done | bytes 172064 | tf_op jit(solution)/shard_map/ppermute | solution.py:248
  28.7 1.6 %collective-permute-start.5 = (bf16[96,896]{1,0:T(8,128)(2,1)S(1)}, bf16[96,896]{1,0:T(8,128)(2,1)S(1)}, u32[]{:S(2)}, u32[]{:S(2)}) collective-permute-start(bf16[96,896]{1,0:T(8,128)(2,1)S(1)} %shard_map.57.refs_3_.refs_0_), channel_id=1, source_target_pairs={{0,2},{1,3},{2,0},{3,1},{4,6},{5,7},{6,4},{7,5},{8,10},{9,11},{10,... | collective-permute-start | bytes 516104 | tf_op jit(solution)/shard_map/ppermute | solution.py:248
  31.1 2.6 %expert_kernel.6 = (f32[96,1792]{1,0:T(8,128)S(1)}, bf16[96,1792]{1,0:T(8,128)(2,1)S(1)}) custom-call(bf16[96,1792]{1,0:T(8,128)(2,1)S(1)} %pack_kernel.6.refs_2_.refs_0_, bf16[96,1792]{1,0:T(8,128)(2,1)S(1)} %collective-permute-done.10.refs_1_, bf16[608,3584]{1,0:T(8,128)(2,1)S(1)} %get-tuple-element.26.refs_2_, ...), custom_call_target="tpu_custom_call" | custom-call | flops 4600000000 | tf_op jit(solution)/shard_map/expert_kernel/pallas_call | solution.py:75
  33.9 2.1 %collective-permute-done.5.refs_1_ = bf16[96,896]{1,0:T(8,128)(2,1)S(1)} collective-permute-done((bf16[96,896]{1,0:T(8,128)(2,1)S(1)}, bf16[96,896]{1,0:T(8,128)(2,1)S(1)}, u32[]{:S(2)}, u32[]{:S(2)}) %collective-permute-start.5) | collective-permute-done | bytes 172064 | tf_op jit(solution)/shard_map/ppermute | solution.py:248
  36.2 1.5 %collective-permute-done.12.refs_1_ = bf16[96,1792]{1,0:T(8,128)(2,1)S(1)} collective-permute-done((bf16[96,1792]{1,0:T(8,128)(2,1)S(1)}, bf16[96,1792]{1,0:T(8,128)(2,1)S(1)}, u32[]{:S(2)}, u32[]{:S(2)}) %collective-permute-start.12) | collective-permute-done | bytes 344096 | tf_op jit(solution)/shard_map/ppermute | solution.py:248
  37.7 2.6 %expert_kernel.7 = (f32[96,1792]{1,0:T(8,128)S(1)}, bf16[96,1792]{1,0:T(8,128)(2,1)S(1)}) custom-call(bf16[96,1792]{1,0:T(8,128)(2,1)S(1)} %pack_kernel.7.refs_2_.refs_0_, bf16[96,1792]{1,0:T(8,128)(2,1)S(1)} %collective-permute-done.12.refs_1_, bf16[608,3584]{1,0:T(8,128)(2,1)S(1)} %get-tuple-element.26.refs_2_, ...), custom_call_target="tpu_custom_call" | custom-call | flops 4600000000 | tf_op jit(solution)/shard_map/expert_kernel/pallas_call | solution.py:75
  40.6 2.1 %collective-permute-start.19 = (bf16[96,896]{1,0:T(8,128)(2,1)S(1)}, bf16[96,896]{1,0:T(8,128)(2,1)S(1)}, u32[]{:S(2)}, u32[]{:S(2)}) collective-permute-start(bf16[96,896]{1,0:T(8,128)(2,1)S(1)} %chip_sum_kernel.3.refs_2_), channel_id=1, source_target_pairs={{0,12},{4,0},{8,4},{12,8},{1,13},{5,1},{9,5},{13,9},{2,14},{6,2},{... | collective-permute-start | bytes 516104 | tf_op jit(solution)/shard_map/ppermute | solution.py:255
  42.8 1.5 %collective-permute-start.17 = (bf16[96,896]{1,0:T(8,128)(2,1)S(1)}, bf16[96,896]{1,0:T(8,128)(2,1)S(1)}, u32[]{:S(2)}, u32[]{:S(2)}) collective-permute-start(bf16[96,896]{1,0:T(8,128)(2,1)S(1)} %get-tuple-element.42), channel_id=1, source_target_pairs={{0,2},{1,3},{2,0},{3,1},{4,6},{5,7},{6,4},{7,5},{8,10},{9,11},{10,... | collective-permute-start | bytes 516104 | tf_op jit(solution)/shard_map/ppermute | solution.py:248
  44.9 5.0 %collective-permute-done.17.refs_1_ = bf16[96,896]{1,0:T(8,128)(2,1)S(1)} collective-permute-done((bf16[96,896]{1,0:T(8,128)(2,1)S(1)}, bf16[96,896]{1,0:T(8,128)(2,1)S(1)}, u32[]{:S(2)}, u32[]{:S(2)}) %collective-permute-start.17) | collective-permute-done | bytes 172064 | tf_op jit(solution)/shard_map/ppermute | solution.py:248
  50.0 0.6 collective-permute-start.20
  50.6 2.1 %collective-permute-done.16.refs_1_ = bf16[96,896]{1,0:T(8,128)(2,1)S(1)} collective-permute-done((bf16[96,896]{1,0:T(8,128)(2,1)S(1)}, bf16[96,896]{1,0:T(8,128)(2,1)S(1)}, u32[]{:S(2)}, u32[]{:S(2)}) %collective-permute-start.16) | collective-permute-done | bytes 172064 | tf_op jit(solution)/shard_map/ppermute | solution.py:248
  52.9 1.6 %collective-permute-start.18 = (bf16[96,896]{1,0:T(8,128)(2,1)S(1)}, bf16[96,896]{1,0:T(8,128)(2,1)S(1)}, u32[]{:S(2)}, u32[]{:S(2)}) collective-permute-start(bf16[96,896]{1,0:T(8,128)(2,1)S(1)} %get-tuple-element.44), channel_id=1, source_target_pairs={{0,2},{1,3},{2,0},{3,1},{4,6},{5,7},{6,4},{7,5},{8,10},{9,11},{10,... | collective-permute-start | bytes 516104 | tf_op jit(solution)/shard_map/ppermute | solution.py:248
  54.5 7.9 %collective-permute-done.20.refs_4_ = bf16[96,896]{1,0:T(8,128)(2,1)S(1)} collective-permute-done((bf16[96,896]{1,0:T(8,128)(2,1)S(1)}, bf16[96,896]{1,0:T(8,128)(2,1)S(1)}, u32[]{:S(2)}, u32[]{:S(2)}) %collective-permute-start.20) | collective-permute-done | bytes 172064 | tf_op jit(solution)/shard_map/ppermute | solution.py:255
  62.5 0.7 %finish_kernel.1 = bf16[96,896]{1,0:T(8,128)(2,1)} custom-call(f32[4,96,128]{2,1,0:T(8,128)S(1)} %get-tuple-element.25.refs_1_.refs_0_, f32[96,896]{1,0:T(8,128)S(1)} %weigh_kernel.1.refs_1_, bf16[96,896]{1,0:T(8,128)(2,1)S(1)} %collective-permute-done.21.refs_2_), custom_call_target="tpu_custom_call" | custom-call | flops 575000000 | tf_op jit(solution)/shard_map/finish_kernel/pallas_call | solution.py:75
  (44 shorter events, 3.5 us)
Async XLA Ops:
  0.0 10.9 %collective-permute-start = (bf16[96,896]{1,0:T(8,128)(2,1)}, bf16[96,896]{1,0:T(8,128)(2,1)S(1)}, u32[]{:S(2)}, u32[]{:S(2)}) collective-permute-start(bf16[96,896]{1,0:T(8,128)(2,1)} %refs_0_.1), channel_id=1, source_target_pairs={{0,2},{1,3},{2,0},{3,1},{4,6},{5,7},{6,4},{7,5},{8,10},{9,11},{10,... | collective-permute-start | bytes 516104 | tf_op jit(solution)/shard_map/ppermute | solution.py:248
  2.9 7.9 %collective-permute-start.1 = (bf16[96,896]{1,0:T(8,128)(2,1)}, bf16[96,896]{1,0:T(8,128)(2,1)S(1)}, u32[]{:S(2)}, u32[]{:S(2)}) collective-permute-start(bf16[96,896]{1,0:T(8,128)(2,1)} %refs_0_.1), channel_id=1, source_target_pairs={{0,4},{4,8},{8,12},{12,0},{1,5},{5,9},{9,13},{13,1},{2,6},{6,10},{... | collective-permute-start | bytes 516104 | tf_op jit(solution)/shard_map/ppermute | solution.py:255
  4.5 6.4 %copy-start = (bf16[96,896]{1,0:T(8,128)(2,1)S(1)}, bf16[96,896]{1,0:T(8,128)(2,1)}, u32[]{:S(2)}) copy-start(bf16[96,896]{1,0:T(8,128)(2,1)} %refs_0_.1) | copy-start | bytes 516100
  10.9 4.5 %collective-permute-start.2 = (bf16[96,1792]{1,0:T(8,128)(2,1)S(1)}, bf16[96,1792]{1,0:T(8,128)(2,1)S(1)}, u32[]{:S(2)}, u32[]{:S(2)}) collective-permute-start(bf16[96,1792]{1,0:T(8,128)(2,1)S(1)} %pack_kernel.4.refs_0_.refs_1_), channel_id=1, source_target_pairs={{0,1},{1,0},{2,3},{3,2},{4,5},{5,4},{6,7},{7,6},{8,9},{9,8},{10,11... | collective-permute-start | bytes 1032200 | tf_op jit(solution)/shard_map/ppermute | solution.py:248
  11.0 10.7 %collective-permute-start.8 = (bf16[96,896]{1,0:T(8,128)(2,1)S(1)}, bf16[96,896]{1,0:T(8,128)(2,1)S(1)}, u32[]{:S(2)}, u32[]{:S(2)}) collective-permute-start(bf16[96,896]{1,0:T(8,128)(2,1)S(1)} %shard_map.55.refs_2_.refs_0_), channel_id=1, source_target_pairs={{0,2},{1,3},{2,0},{3,1},{4,6},{5,7},{6,4},{7,5},{8,10},{9,11},{10,... | collective-permute-start | bytes 516104 | tf_op jit(solution)/shard_map/ppermute | solution.py:248
  11.6 9.1 %collective-permute-start.6 = (bf16[96,896]{1,0:T(8,128)(2,1)S(1)}, bf16[96,896]{1,0:T(8,128)(2,1)S(1)}, u32[]{:S(2)}, u32[]{:S(2)}) collective-permute-start(bf16[96,896]{1,0:T(8,128)(2,1)S(1)} %shard_map.55.refs_2_.refs_0_), channel_id=1, source_target_pairs={{0,4},{4,8},{8,12},{12,0},{1,5},{5,9},{9,13},{13,1},{2,6},{6,10},{... | collective-permute-start | bytes 516104 | tf_op jit(solution)/shard_map/ppermute | solution.py:255
  11.6 10.1 %collective-permute-start.4 = (bf16[96,896]{1,0:T(8,128)(2,1)S(1)}, bf16[96,896]{1,0:T(8,128)(2,1)S(1)}, u32[]{:S(2)}, u32[]{:S(2)}) collective-permute-start(bf16[96,896]{1,0:T(8,128)(2,1)S(1)} %shard_map.56), channel_id=1, source_target_pairs={{0,12},{4,0},{8,4},{12,8},{1,13},{5,1},{9,5},{13,9},{2,14},{6,2},{... | collective-permute-start | bytes 516104 | tf_op jit(solution)/shard_map/ppermute | solution.py:255
  21.8 1.7 %collective-permute-start.9 = (bf16[96,1792]{1,0:T(8,128)(2,1)S(1)}, bf16[96,1792]{1,0:T(8,128)(2,1)S(1)}, u32[]{:S(2)}, u32[]{:S(2)}) collective-permute-start(bf16[96,1792]{1,0:T(8,128)(2,1)S(1)} %pack_kernel.5.refs_0_), channel_id=1, source_target_pairs={{0,1},{1,0},{2,3},{3,2},{4,5},{5,4},{6,7},{7,6},{8,9},{9,8},{10,11... | collective-permute-start | bytes 1032200 | tf_op jit(solution)/shard_map/ppermute | solution.py:248
  21.8 6.8 %collective-permute-start.7 = (bf16[96,896]{1,0:T(8,128)(2,1)S(1)}, bf16[96,896]{1,0:T(8,128)(2,1)S(1)}, u32[]{:S(2)}, u32[]{:S(2)}) collective-permute-start(bf16[96,896]{1,0:T(8,128)(2,1)S(1)} %shard_map.58.refs_2_.refs_0_), channel_id=1, source_target_pairs={{0,2},{1,3},{2,0},{3,1},{4,6},{5,7},{6,4},{7,5},{8,10},{9,11},{10,... | collective-permute-start | bytes 516104 | tf_op jit(solution)/shard_map/ppermute | solution.py:248
  26.1 4.4 %collective-permute-start.11 = (bf16[96,1792]{1,0:T(8,128)(2,1)S(1)}, bf16[96,1792]{1,0:T(8,128)(2,1)S(1)}, u32[]{:S(2)}, u32[]{:S(2)}) collective-permute-start(bf16[96,1792]{1,0:T(8,128)(2,1)S(1)} %get-tuple-element.32), channel_id=1, source_target_pairs={{0,1},{1,0},{2,3},{3,2},{4,5},{5,4},{6,7},{7,6},{8,9},{9,8},{10,11... | collective-permute-start | bytes 1032200 | tf_op jit(solution)/shard_map/ppermute | solution.py:248
  28.7 2.5 %collective-permute-start.10 = (bf16[96,1792]{1,0:T(8,128)(2,1)S(1)}, bf16[96,1792]{1,0:T(8,128)(2,1)S(1)}, u32[]{:S(2)}, u32[]{:S(2)}) collective-permute-start(bf16[96,1792]{1,0:T(8,128)(2,1)S(1)} %pack_kernel.6.refs_2_.refs_0_), channel_id=1, source_target_pairs={{0,1},{1,0},{2,3},{3,2},{4,5},{5,4},{6,7},{7,6},{8,9},{9,8},{10,11... | collective-permute-start | bytes 1032200 | tf_op jit(solution)/shard_map/ppermute | solution.py:248
  28.7 7.2 %collective-permute-start.5 = (bf16[96,896]{1,0:T(8,128)(2,1)S(1)}, bf16[96,896]{1,0:T(8,128)(2,1)S(1)}, u32[]{:S(2)}, u32[]{:S(2)}) collective-permute-start(bf16[96,896]{1,0:T(8,128)(2,1)S(1)} %shard_map.57.refs_3_.refs_0_), channel_id=1, source_target_pairs={{0,2},{1,3},{2,0},{3,1},{4,6},{5,7},{6,4},{7,5},{8,10},{9,11},{10,... | collective-permute-start | bytes 516104 | tf_op jit(solution)/shard_map/ppermute | solution.py:248
  30.3 22.5 %collective-permute-start.3 = (bf16[96,1792]{1,0:T(8,128)(2,1)S(1)}, bf16[96,1792]{1,0:T(8,128)(2,1)S(1)}, u32[]{:S(2)}, u32[]{:S(2)}) collective-permute-start(bf16[96,1792]{1,0:T(8,128)(2,1)S(1)} %get-tuple-element.29), channel_id=1, source_target_pairs={{0,1},{1,0},{2,3},{3,2},{4,5},{5,4},{6,7},{7,6},{8,9},{9,8},{10,11... | collective-permute-start | bytes 1032200 | tf_op jit(solution)/shard_map/ppermute | solution.py:248
  30.5 10.0 %collective-permute-start.15 = (bf16[96,896]{1,0:T(8,128)(2,1)S(1)}, bf16[96,896]{1,0:T(8,128)(2,1)S(1)}, u32[]{:S(2)}, u32[]{:S(2)}) collective-permute-start(bf16[96,896]{1,0:T(8,128)(2,1)S(1)} %get-tuple-element.39), channel_id=1, source_target_pairs={{0,2},{1,3},{2,0},{3,1},{4,6},{5,7},{6,4},{7,5},{8,10},{9,11},{10,... | collective-permute-start | bytes 516104 | tf_op jit(solution)/shard_map/ppermute | solution.py:248
  33.8 2.3 %collective-permute-start.13 = (bf16[96,1792]{1,0:T(8,128)(2,1)S(1)}, bf16[96,1792]{1,0:T(8,128)(2,1)S(1)}, u32[]{:S(2)}, u32[]{:S(2)}) collective-permute-start(bf16[96,1792]{1,0:T(8,128)(2,1)S(1)} %get-tuple-element.35), channel_id=1, source_target_pairs={{0,1},{1,0},{2,3},{3,2},{4,5},{5,4},{6,7},{7,6},{8,9},{9,8},{10,11... | collective-permute-start | bytes 1032200 | tf_op jit(solution)/shard_map/ppermute | solution.py:248
  36.0 1.7 %collective-permute-start.12 = (bf16[96,1792]{1,0:T(8,128)(2,1)S(1)}, bf16[96,1792]{1,0:T(8,128)(2,1)S(1)}, u32[]{:S(2)}, u32[]{:S(2)}) collective-permute-start(bf16[96,1792]{1,0:T(8,128)(2,1)S(1)} %pack_kernel.7.refs_2_.refs_0_), channel_id=1, source_target_pairs={{0,1},{1,0},{2,3},{3,2},{4,5},{5,4},{6,7},{7,6},{8,9},{9,8},{10,11... | collective-permute-start | bytes 1032200 | tf_op jit(solution)/shard_map/ppermute | solution.py:248
  40.4 3.9 %collective-permute-start.14 = (bf16[96,1792]{1,0:T(8,128)(2,1)S(1)}, bf16[96,1792]{1,0:T(8,128)(2,1)S(1)}, u32[]{:S(2)}, u32[]{:S(2)}) collective-permute-start(bf16[96,1792]{1,0:T(8,128)(2,1)S(1)} %get-tuple-element.38), channel_id=1, source_target_pairs={{0,1},{1,0},{2,3},{3,2},{4,5},{5,4},{6,7},{7,6},{8,9},{9,8},{10,11... | collective-permute-start | bytes 1032200 | tf_op jit(solution)/shard_map/ppermute | solution.py:248
  40.6 13.9 %collective-permute-start.19 = (bf16[96,896]{1,0:T(8,128)(2,1)S(1)}, bf16[96,896]{1,0:T(8,128)(2,1)S(1)}, u32[]{:S(2)}, u32[]{:S(2)}) collective-permute-start(bf16[96,896]{1,0:T(8,128)(2,1)S(1)} %chip_sum_kernel.3.refs_2_), channel_id=1, source_target_pairs={{0,12},{4,0},{8,4},{12,8},{1,13},{5,1},{9,5},{13,9},{2,14},{6,2},{... | collective-permute-start | bytes 516104 | tf_op jit(solution)/shard_map/ppermute | solution.py:255
  42.8 7.2 %collective-permute-start.17 = (bf16[96,896]{1,0:T(8,128)(2,1)S(1)}, bf16[96,896]{1,0:T(8,128)(2,1)S(1)}, u32[]{:S(2)}, u32[]{:S(2)}) collective-permute-start(bf16[96,896]{1,0:T(8,128)(2,1)S(1)} %get-tuple-element.42), channel_id=1, source_target_pairs={{0,2},{1,3},{2,0},{3,1},{4,6},{5,7},{6,4},{7,5},{8,10},{9,11},{10,... | collective-permute-start | bytes 516104 | tf_op jit(solution)/shard_map/ppermute | solution.py:248
  44.3 8.5 %collective-permute-start.16 = (bf16[96,896]{1,0:T(8,128)(2,1)S(1)}, bf16[96,896]{1,0:T(8,128)(2,1)S(1)}, u32[]{:S(2)}, u32[]{:S(2)}) collective-permute-start(bf16[96,896]{1,0:T(8,128)(2,1)S(1)} %get-tuple-element.41), channel_id=1, source_target_pairs={{0,2},{1,3},{2,0},{3,1},{4,6},{5,7},{6,4},{7,5},{8,10},{9,11},{10,... | collective-permute-start | bytes 516104 | tf_op jit(solution)/shard_map/ppermute | solution.py:248
  50.0 12.4 %collective-permute-start.20 = (bf16[96,896]{1,0:T(8,128)(2,1)S(1)}, bf16[96,896]{1,0:T(8,128)(2,1)S(1)}, u32[]{:S(2)}, u32[]{:S(2)}) collective-permute-start(bf16[96,896]{1,0:T(8,128)(2,1)S(1)} %chip_sum_kernel.4.refs_2_), channel_id=1, source_target_pairs={{0,8},{4,12},{8,0},{12,4},{1,9},{5,13},{9,1},{13,5},{2,10},{6,14},... | collective-permute-start | bytes 516104 | tf_op jit(solution)/shard_map/ppermute | solution.py:255
  52.9 9.5 %collective-permute-start.18 = (bf16[96,896]{1,0:T(8,128)(2,1)S(1)}, bf16[96,896]{1,0:T(8,128)(2,1)S(1)}, u32[]{:S(2)}, u32[]{:S(2)}) collective-permute-start(bf16[96,896]{1,0:T(8,128)(2,1)S(1)} %get-tuple-element.44), channel_id=1, source_target_pairs={{0,2},{1,3},{2,0},{3,1},{4,6},{5,7},{6,4},{7,5},{8,10},{9,11},{10,... | collective-permute-start | bytes 516104 | tf_op jit(solution)/shard_map/ppermute | solution.py:248
  54.5 8.0 %collective-permute-start.21 = (bf16[96,896]{1,0:T(8,128)(2,1)S(1)}, bf16[96,896]{1,0:T(8,128)(2,1)S(1)}, u32[]{:S(2)}, u32[]{:S(2)}) collective-permute-start(bf16[96,896]{1,0:T(8,128)(2,1)S(1)} %chip_sum_kernel.5.refs_2_), channel_id=1, source_target_pairs={{0,4},{4,8},{8,12},{12,0},{1,5},{5,9},{9,13},{13,1},{2,6},{6,10},{... | collective-permute-start | bytes 516104 | tf_op jit(solution)/shard_map/ppermute | solution.py:255

commit v12 on v9

--- a/solution.py
+++ b/solution.py
@@ -282,23 +282,22 @@
 
     arrive(0, tokens, 0, [])
     arrive(1, tokens, 1, [columns])
-    arrive(3, tokens, -1, [columns])
-    lay((0,), [blocks[1], blocks[3]])
+    lay((0,), [blocks[1]])
+    chips[3,] = shift(chips[0,], -1)
     run((0,), [], 2.6)
     arrive(2, blocks[1], 1, [kept[0,][0]])
-    lay((1,), [kept[0,][0], blocks[2]])
-    run((1,), [], 4)
-    lay((3,), [kept[1,][0]], .5)
-    lay((2,), [chips[3,]], 4)
+    lay((1,), [blocks[2]], .5)
+    run((1,), [], 8)
+    run((3,), [kept[1,][0]], 8)
+    lay((2,), [kept[3,][0]], 8)
     leave((1,), [chips[2,]], 2)
-    run((3,), [sums[1][0]], 4)
-    run((2,), [kept[3,][0]], .05)
-    give(1, [kept[2,][0]], 2)
-    leave((3,), [added[1]], 4)
-    leave((2,), [sums[3][0]], 2)
-    leave((0,), [sums[2][0]])
-    give(3, [sums[2][0]], 4)
-    give(2, [added[3]], 4)
+    run((2,), [sums[1][0]], 2.6)
+    leave((3,), [kept[2,][0]], 2)
+    give(1, [sums[3][0]], 2)
+    leave((2,), [added[1]], 2)
+    leave((0,), [sums[2][0]], 2)
+    give(3, [sums[2][0]], 2)
+    give(2, [added[3]], 2)
     total = weigh(columns, *sums[0][:2], (1, 3), [parts[1], parts[3]])
     return finish(columns, total, (2,), [parts[2]])
 

time: 67.6 us -> 59.2 us (0.88)
  waiting for transfers between devices: 33.2 us -> 19.5 us
  starting transfers between devices: 17.9 us -> 23.3 us
    ppermute x16 -> x15, waiting for transfers between devices: 15.9 us -> 3.55 us  [swap(): return lax.ppermute(array, 'tensor', [(i, i ^ bit) for i in range(4)])]
    ppermute x6, starting transfers between devices: 7.19 us -> 11.5 us  [shift(): lax.ppermute(array, 'expert', [(i, (i + by) % experts_n) for i in range(e...]
    ppermute x6, waiting for transfers between devices: 17.4 us -> 15.9 us  [shift(): lax.ppermute(array, 'expert', [(i, (i + by) % experts_n) for i in range(e...]
    ppermute x16 -> x15, starting transfers between devices: 10.7 us -> 11.8 us  [swap(): return lax.ppermute(array, 'tensor', [(i, i ^ bit) for i in range(4)])]
    pallas_call x18 -> x17, Pallas kernels: 16.1 us -> 16.1 us  [local_call(): pl.pallas_call(body_of, name=name, out_shape=out_shape, in_specs=list(in_...]
  transfers between devices with their start and end apart: 22 -> 21, of which waited for: 9 -> 8; matrix products, arithmetic and copies ran while one was open for 0% -> 0% of each run, Pallas kernels for 23% -> 26%
where the time goes in v12:
time: 59.2 us; the launch traced here: 59 us
  starting transfers between devices  23.3 us (39%)
  waiting for transfers between devices  19.5 us (33%)
  Pallas kernels  16.1 us (27%)
    pallas_call x17, Pallas kernels, local_call(): pl.pallas_call(body_of, name=name, out_shape=out_shape, in_specs=list(in_...  16.1 us
    ppermute x6, waiting for transfers between devices, shift(): lax.ppermute(array, 'expert', [(i, (i + by) % experts_n) for i in range(e...  15.9 us
    ppermute x15, starting transfers between devices, swap(): return lax.ppermute(array, 'tensor', [(i, i ^ bit) for i in range(4)])  11.8 us
    ppermute x6, starting transfers between devices, shift(): lax.ppermute(array, 'expert', [(i, (i + by) % experts_n) for i in range(e...  11.5 us
    ppermute x15, waiting for transfers between devices, swap(): return lax.ppermute(array, 'tensor', [(i, i ^ bit) for i in range(4)])  3.55 us
  transfers between devices with their start and end apart: 21, of which 8 were waited for; matrix products, arithmetic and copies ran while one was open for 0% of the time, Pallas kernels for 26%

profile of v12, /device:TPU:0, one launch (start us, length us, event | category | flops | bytes accessed | tf_op | source)
XLA Modules:
  0.0 59.0 jit_solution(11614588787895732190)
XLA Ops:
  0.0 2.9 %collective-permute-start = (bf16[96,896]{1,0:T(8,128)(2,1)}, bf16[96,896]{1,0:T(8,128)(2,1)S(1)}, u32[]{:S(2)}, u32[]{:S(2)}) collective-permute-start(bf16[96,896]{1,0:T(8,128)(2,1)} %refs_0_.1), channel_id=1, source_target_pairs={{0,2},{1,3},{2,0},{3,1},{4,6},{5,7},{6,4},{7,5},{8,10},{9,11},{10,... | collective-permute-start | bytes 516104 | tf_op jit(solution)/shard_map/ppermute | solution.py:244
  2.9 1.6 %collective-permute-start.1 = (bf16[96,896]{1,0:T(8,128)(2,1)}, bf16[96,896]{1,0:T(8,128)(2,1)S(1)}, u32[]{:S(2)}, u32[]{:S(2)}) collective-permute-start(bf16[96,896]{1,0:T(8,128)(2,1)} %refs_0_.1), channel_id=1, source_target_pairs={{0,4},{4,8},{8,12},{12,0},{1,5},{5,9},{9,13},{13,1},{2,6},{6,10},{... | collective-permute-start | bytes 516104 | tf_op jit(solution)/shard_map/ppermute | solution.py:251
  4.5 4.3 %prepare_kernel.1 = (f32[4,96,128]{2,1,0:T(8,128)S(1)}, bf16[608,3584]{1,0:T(8,128)(2,1)S(1)}, bf16[608,3584]{1,0:T(8,128)(2,1)S(1)}) custom-call(s32[2,96]{1,0:T(2,128)} %bitcast.8, s32[2,96]{1,0:T(2,128)} %bitcast.9, bf16[608,3584]{1,0:T(8,128)(2,1)} %bitcast.6, bf16[608,3584]{1,0:T(8,128)(2,1)} %bitcast.7), custom_call_target="tpu_custom_call" | custom-call | flops 4600000000 | tf_op jit(solution)/shard_map/prepare_kernel/pallas_call | solution.py:72
  8.9 2.0 %collective-permute-done.1.refs_0_ = bf16[96,896]{1,0:T(8,128)(2,1)S(1)} collective-permute-done((bf16[96,896]{1,0:T(8,128)(2,1)}, bf16[96,896]{1,0:T(8,128)(2,1)S(1)}, u32[]{:S(2)}, u32[]{:S(2)}) %collective-permute-start.1) | collective-permute-done | bytes 172064 | tf_op jit(solution)/shard_map/ppermute | solution.py:251
  11.6 3.8 %collective-permute-start.6 = (bf16[96,1792]{1,0:T(8,128)(2,1)S(1)}, bf16[96,1792]{1,0:T(8,128)(2,1)S(1)}, u32[]{:S(2)}, u32[]{:S(2)}) collective-permute-start(bf16[96,1792]{1,0:T(8,128)(2,1)S(1)} %pack_kernel.3.refs_0_), channel_id=1, source_target_pairs={{0,12},{4,0},{8,4},{12,8},{1,13},{5,1},{9,5},{13,9},{2,14},{6,2},{... | collective-permute-start | bytes 1032200 | tf_op jit(solution)/shard_map/ppermute | solution.py:251
  15.4 2.6 %expert_kernel.4 = (f32[96,1792]{1,0:T(8,128)S(1)}, bf16[96,1792]{1,0:T(8,128)(2,1)S(1)}) custom-call(bf16[96,1792]{1,0:T(8,128)(2,1)S(1)} %pack_kernel.3.refs_0_, bf16[96,1792]{1,0:T(8,128)(2,1)S(1)} %collective-permute-done.2.refs_1_, bf16[608,3584]{1,0:T(8,128)(2,1)S(1)} %get-tuple-element.25.refs_2_, bf16[608,3584]{1,0:T(8,128)(2,1)S(1)} %get-tuple-element.26.refs_3_), custom_call_target="tpu_custom_call" | custom-call | flops 2990000128 | tf_op jit(solution)/shard_map/expert_kernel/pallas_call | solution.py:72
  18.0 2.6 %collective-permute-done.4.refs_0_ = bf16[96,896]{1,0:T(8,128)(2,1)S(1)} collective-permute-done((bf16[96,896]{1,0:T(8,128)(2,1)S(1)}, bf16[96,896]{1,0:T(8,128)(2,1)S(1)}, u32[]{:S(2)}, u32[]{:S(2)}) %collective-permute-start.4) | collective-permute-done | bytes 172064 | tf_op jit(solution)/shard_map/ppermute | solution.py:251
  20.8 1.6 %collective-permute-start.5 = (bf16[96,896]{1,0:T(8,128)(2,1)S(1)}, bf16[96,896]{1,0:T(8,128)(2,1)S(1)}, u32[]{:S(2)}, u32[]{:S(2)}) collective-permute-start(bf16[96,896]{1,0:T(8,128)(2,1)S(1)} %shard_map.56.refs_2_.refs_0_), channel_id=1, source_target_pairs={{0,2},{1,3},{2,0},{3,1},{4,6},{5,7},{6,4},{7,5},{8,10},{9,11},{10,... | collective-permute-start | bytes 516104 | tf_op jit(solution)/shard_map/ppermute | solution.py:244
  22.3 3.1 %collective-permute-done.6.refs_0_ = bf16[96,1792]{1,0:T(8,128)(2,1)S(1)} collective-permute-done((bf16[96,1792]{1,0:T(8,128)(2,1)S(1)}, bf16[96,1792]{1,0:T(8,128)(2,1)S(1)}, u32[]{:S(2)}, u32[]{:S(2)}) %collective-permute-start.6) | collective-permute-done | bytes 344096 | tf_op jit(solution)/shard_map/ppermute | solution.py:251
  25.4 2.6 %expert_kernel.5 = (f32[96,1792]{1,0:T(8,128)S(1)}, bf16[96,1792]{1,0:T(8,128)(2,1)S(1)}) custom-call(bf16[96,1792]{1,0:T(8,128)(2,1)S(1)} %pack_kernel.4.refs_0_, bf16[96,1792]{1,0:T(8,128)(2,1)S(1)} %collective-permute-done.9.refs_1_, bf16[608,3584]{1,0:T(8,128)(2,1)S(1)} %get-tuple-element.25.refs_2_, bf16[608,3584]{1,0:T(8,128)(2,1)S(1)} %get-tuple-element.26.refs_3_), custom_call_target="tpu_custom_call" | custom-call | flops 9200000000 | tf_op jit(solution)/shard_map/expert_kernel/pallas_call | solution.py:72
  28.6 2.6 %expert_kernel.6 = (f32[96,1792]{1,0:T(8,128)S(1)}, bf16[96,1792]{1,0:T(8,128)(2,1)S(1)}) custom-call(bf16[96,1792]{1,0:T(8,128)(2,1)S(1)} %collective-permute-done.6.refs_0_, bf16[96,1792]{1,0:T(8,128)(2,1)S(1)} %collective-permute-done.7.refs_1_, bf16[608,3584]{1,0:T(8,128)(2,1)S(1)} %get-tuple-element.25.refs_2_, ...), custom_call_target="tpu_custom_call" | custom-call | flops 9200000000 | tf_op jit(solution)/shard_map/expert_kernel/pallas_call | solution.py:72
  32.0 1.6 %collective-permute-start.13 = (bf16[96,896]{1,0:T(8,128)(2,1)S(1)}, bf16[96,896]{1,0:T(8,128)(2,1)S(1)}, u32[]{:S(2)}, u32[]{:S(2)}) collective-permute-start(bf16[96,896]{1,0:T(8,128)(2,1)S(1)} %get-tuple-element.35), channel_id=1, source_target_pairs={{0,2},{1,3},{2,0},{3,1},{4,6},{5,7},{6,4},{7,5},{8,10},{9,11},{10,... | collective-permute-start | bytes 516104 | tf_op jit(solution)/shard_map/ppermute | solution.py:244
  33.6 2.6 %expert_kernel.7 = (f32[96,1792]{1,0:T(8,128)S(1)}, bf16[96,1792]{1,0:T(8,128)(2,1)S(1)}) custom-call(bf16[96,1792]{1,0:T(8,128)(2,1)S(1)} %pack_kernel.5.refs_2_.refs_0_, bf16[96,1792]{1,0:T(8,128)(2,1)S(1)} %collective-permute-done.10.refs_1_, bf16[608,3584]{1,0:T(8,128)(2,1)S(1)} %get-tuple-element.25.refs_2_, ...), custom_call_target="tpu_custom_call" | custom-call | flops 2990000128 | tf_op jit(solution)/shard_map/expert_kernel/pallas_call | solution.py:72
  36.5 1.0 %collective-permute-start.17 = (bf16[96,896]{1,0:T(8,128)(2,1)S(1)}, bf16[96,896]{1,0:T(8,128)(2,1)S(1)}, u32[]{:S(2)}, u32[]{:S(2)}) collective-permute-start(bf16[96,896]{1,0:T(8,128)(2,1)S(1)} %get-tuple-element.41), channel_id=1, source_target_pairs={{0,2},{1,3},{2,0},{3,1},{4,6},{5,7},{6,4},{7,5},{8,10},{9,11},{10,... | collective-permute-start | bytes 516104 | tf_op jit(solution)/shard_map/ppermute | solution.py:244
  37.5 1.3 %collective-permute-done.13.refs_1_ = bf16[96,896]{1,0:T(8,128)(2,1)S(1)} collective-permute-done((bf16[96,896]{1,0:T(8,128)(2,1)S(1)}, bf16[96,896]{1,0:T(8,128)(2,1)S(1)}, u32[]{:S(2)}, u32[]{:S(2)}) %collective-permute-start.13) | collective-permute-done | bytes 172064 | tf_op jit(solution)/shard_map/ppermute | solution.py:244
  38.9 2.1 %collective-permute-start.16 = (bf16[96,896]{1,0:T(8,128)(2,1)S(1)}, bf16[96,896]{1,0:T(8,128)(2,1)S(1)}, u32[]{:S(2)}, u32[]{:S(2)}) collective-permute-start(bf16[96,896]{1,0:T(8,128)(2,1)S(1)} %chip_sum_kernel.3.refs_2_), channel_id=1, source_target_pairs={{0,12},{4,0},{8,4},{12,8},{1,13},{5,1},{9,5},{13,9},{2,14},{6,2},{... | collective-permute-start | bytes 516104 | tf_op jit(solution)/shard_map/ppermute | solution.py:251
  41.1 1.6 %collective-permute-start.19 = (bf16[96,896]{1,0:T(8,128)(2,1)S(1)}, bf16[96,896]{1,0:T(8,128)(2,1)S(1)}, u32[]{:S(2)}, u32[]{:S(2)}) collective-permute-start(bf16[96,896]{1,0:T(8,128)(2,1)S(1)} %get-tuple-element.42), channel_id=1, source_target_pairs={{0,2},{1,3},{2,0},{3,1},{4,6},{5,7},{6,4},{7,5},{8,10},{9,11},{10,... | collective-permute-start | bytes 516104 | tf_op jit(solution)/shard_map/ppermute | solution.py:244
  43.4 1.5 %collective-permute-start.18 = (bf16[96,896]{1,0:T(8,128)(2,1)S(1)}, bf16[96,896]{1,0:T(8,128)(2,1)S(1)}, u32[]{:S(2)}, u32[]{:S(2)}) collective-permute-start(bf16[96,896]{1,0:T(8,128)(2,1)S(1)} %chip_sum_kernel.4.refs_2_), channel_id=1, source_target_pairs={{0,4},{4,8},{8,12},{12,0},{1,5},{5,9},{9,13},{13,1},{2,6},{6,10},{... | collective-permute-start | bytes 516104 | tf_op jit(solution)/shard_map/ppermute | solution.py:251
  45.0 1.0 %collective-permute-start.15 = (bf16[96,896]{1,0:T(8,128)(2,1)S(1)}, bf16[96,896]{1,0:T(8,128)(2,1)S(1)}, u32[]{:S(2)}, u32[]{:S(2)}) collective-permute-start(bf16[96,896]{1,0:T(8,128)(2,1)S(1)} %get-tuple-element.40), channel_id=1, source_target_pairs={{0,2},{1,3},{2,0},{3,1},{4,6},{5,7},{6,4},{7,5},{8,10},{9,11},{10,... | collective-permute-start | bytes 516104 | tf_op jit(solution)/shard_map/ppermute | solution.py:244
  45.9 1.5 %collective-permute-done.19.refs_1_ = bf16[96,896]{1,0:T(8,128)(2,1)S(1)} collective-permute-done((bf16[96,896]{1,0:T(8,128)(2,1)S(1)}, bf16[96,896]{1,0:T(8,128)(2,1)S(1)}, u32[]{:S(2)}, u32[]{:S(2)}) %collective-permute-start.19) | collective-permute-done | bytes 172064 | tf_op jit(solution)/shard_map/ppermute | solution.py:244
  47.5 2.5 %collective-permute-start.20 = (bf16[96,896]{1,0:T(8,128)(2,1)S(1)}, bf16[96,896]{1,0:T(8,128)(2,1)S(1)}, u32[]{:S(2)}, u32[]{:S(2)}) collective-permute-start(bf16[96,896]{1,0:T(8,128)(2,1)S(1)} %chip_sum_kernel.5), channel_id=1, source_target_pairs={{0,8},{4,12},{8,0},{12,4},{1,9},{5,13},{9,1},{13,5},{2,10},{6,14},... | collective-permute-start | bytes 516104 | tf_op jit(solution)/shard_map/ppermute | solution.py:251
  50.0 1.5 %collective-permute-done.18.refs_4_ = bf16[96,896]{1,0:T(8,128)(2,1)S(1)} collective-permute-done((bf16[96,896]{1,0:T(8,128)(2,1)S(1)}, bf16[96,896]{1,0:T(8,128)(2,1)S(1)}, u32[]{:S(2)}, u32[]{:S(2)}) %collective-permute-start.18) | collective-permute-done | bytes 172064 | tf_op jit(solution)/shard_map/ppermute | solution.py:251
  51.6 6.7 %collective-permute-done.20.refs_2_ = bf16[96,896]{1,0:T(8,128)(2,1)S(1)} collective-permute-done((bf16[96,896]{1,0:T(8,128)(2,1)S(1)}, bf16[96,896]{1,0:T(8,128)(2,1)S(1)}, u32[]{:S(2)}, u32[]{:S(2)}) %collective-permute-start.20) | collective-permute-done | bytes 172064 | tf_op jit(solution)/shard_map/ppermute | solution.py:251
  58.3 0.7 %finish_kernel.1 = bf16[96,896]{1,0:T(8,128)(2,1)} custom-call(f32[4,96,128]{2,1,0:T(8,128)S(1)} %get-tuple-element.24.refs_1_.refs_0_, f32[96,896]{1,0:T(8,128)S(1)} %weigh_kernel.1.refs_1_, bf16[96,896]{1,0:T(8,128)(2,1)S(1)} %collective-permute-done.20.refs_2_), custom_call_target="tpu_custom_call" | custom-call | flops 575000000 | tf_op jit(solution)/shard_map/finish_kernel/pallas_call | solution.py:72
  (39 shorter events, 3.5 us)
Async XLA Ops:
  0.0 10.9 %collective-permute-start = (bf16[96,896]{1,0:T(8,128)(2,1)}, bf16[96,896]{1,0:T(8,128)(2,1)S(1)}, u32[]{:S(2)}, u32[]{:S(2)}) collective-permute-start(bf16[96,896]{1,0:T(8,128)(2,1)} %refs_0_.1), channel_id=1, source_target_pairs={{0,2},{1,3},{2,0},{3,1},{4,6},{5,7},{6,4},{7,5},{8,10},{9,11},{10,... | collective-permute-start | bytes 516104 | tf_op jit(solution)/shard_map/ppermute | solution.py:244
  2.9 7.9 %collective-permute-start.1 = (bf16[96,896]{1,0:T(8,128)(2,1)}, bf16[96,896]{1,0:T(8,128)(2,1)S(1)}, u32[]{:S(2)}, u32[]{:S(2)}) collective-permute-start(bf16[96,896]{1,0:T(8,128)(2,1)} %refs_0_.1), channel_id=1, source_target_pairs={{0,4},{4,8},{8,12},{12,0},{1,5},{5,9},{9,13},{13,1},{2,6},{6,10},{... | collective-permute-start | bytes 516104 | tf_op jit(solution)/shard_map/ppermute | solution.py:251
  4.5 6.4 %copy-start = (bf16[96,896]{1,0:T(8,128)(2,1)S(1)}, bf16[96,896]{1,0:T(8,128)(2,1)}, u32[]{:S(2)}) copy-start(bf16[96,896]{1,0:T(8,128)(2,1)} %refs_0_.1) | copy-start | bytes 516100
  10.9 4.5 %collective-permute-start.2 = (bf16[96,1792]{1,0:T(8,128)(2,1)S(1)}, bf16[96,1792]{1,0:T(8,128)(2,1)S(1)}, u32[]{:S(2)}, u32[]{:S(2)}) collective-permute-start(bf16[96,1792]{1,0:T(8,128)(2,1)S(1)} %pack_kernel.3.refs_0_), channel_id=1, source_target_pairs={{0,1},{1,0},{2,3},{3,2},{4,5},{5,4},{6,7},{7,6},{8,9},{9,8},{10,11... | collective-permute-start | bytes 1032200 | tf_op jit(solution)/shard_map/ppermute | solution.py:244
  11.0 9.7 %collective-permute-start.8 = (bf16[96,896]{1,0:T(8,128)(2,1)S(1)}, bf16[96,896]{1,0:T(8,128)(2,1)S(1)}, u32[]{:S(2)}, u32[]{:S(2)}) collective-permute-start(bf16[96,896]{1,0:T(8,128)(2,1)S(1)} %shard_map.55.refs_2_.refs_0_), channel_id=1, source_target_pairs={{0,2},{1,3},{2,0},{3,1},{4,6},{5,7},{6,4},{7,5},{8,10},{9,11},{10,... | collective-permute-start | bytes 516104 | tf_op jit(solution)/shard_map/ppermute | solution.py:244
  11.6 9.1 %collective-permute-start.4 = (bf16[96,896]{1,0:T(8,128)(2,1)S(1)}, bf16[96,896]{1,0:T(8,128)(2,1)S(1)}, u32[]{:S(2)}, u32[]{:S(2)}) collective-permute-start(bf16[96,896]{1,0:T(8,128)(2,1)S(1)} %shard_map.55.refs_2_.refs_0_), channel_id=1, source_target_pairs={{0,4},{4,8},{8,12},{12,0},{1,5},{5,9},{9,13},{13,1},{2,6},{6,10},{... | collective-permute-start | bytes 516104 | tf_op jit(solution)/shard_map/ppermute | solution.py:251
  11.6 13.8 %collective-permute-start.6 = (bf16[96,1792]{1,0:T(8,128)(2,1)S(1)}, bf16[96,1792]{1,0:T(8,128)(2,1)S(1)}, u32[]{:S(2)}, u32[]{:S(2)}) collective-permute-start(bf16[96,1792]{1,0:T(8,128)(2,1)S(1)} %pack_kernel.3.refs_0_), channel_id=1, source_target_pairs={{0,12},{4,0},{8,4},{12,8},{1,13},{5,1},{9,5},{13,9},{2,14},{6,2},{... | collective-permute-start | bytes 1032200 | tf_op jit(solution)/shard_map/ppermute | solution.py:251
  20.7 4.7 %collective-permute-start.9 = (bf16[96,1792]{1,0:T(8,128)(2,1)S(1)}, bf16[96,1792]{1,0:T(8,128)(2,1)S(1)}, u32[]{:S(2)}, u32[]{:S(2)}) collective-permute-start(bf16[96,1792]{1,0:T(8,128)(2,1)S(1)} %pack_kernel.4.refs_0_), channel_id=1, source_target_pairs={{0,1},{1,0},{2,3},{3,2},{4,5},{5,4},{6,7},{7,6},{8,9},{9,8},{10,11... | collective-permute-start | bytes 1032200 | tf_op jit(solution)/shard_map/ppermute | solution.py:244
  20.8 10.5 %collective-permute-start.5 = (bf16[96,896]{1,0:T(8,128)(2,1)S(1)}, bf16[96,896]{1,0:T(8,128)(2,1)S(1)}, u32[]{:S(2)}, u32[]{:S(2)}) collective-permute-start(bf16[96,896]{1,0:T(8,128)(2,1)S(1)} %shard_map.56.refs_2_.refs_0_), channel_id=1, source_target_pairs={{0,2},{1,3},{2,0},{3,1},{4,6},{5,7},{6,4},{7,5},{8,10},{9,11},{10,... | collective-permute-start | bytes 516104 | tf_op jit(solution)/shard_map/ppermute | solution.py:244
  25.4 3.2 %collective-permute-start.7 = (bf16[96,1792]{1,0:T(8,128)(2,1)S(1)}, bf16[96,1792]{1,0:T(8,128)(2,1)S(1)}, u32[]{:S(2)}, u32[]{:S(2)}) collective-permute-start(bf16[96,1792]{1,0:T(8,128)(2,1)S(1)} %collective-permute-done.6.refs_0_), channel_id=1, source_target_pairs={{0,1},{1,0},{2,3},{3,2},{4,5},{5,4},{6,7},{7,6},{8,9},{9,8},{10,11... | collective-permute-start | bytes 1032200 | tf_op jit(solution)/shard_map/ppermute | solution.py:244
  28.1 3.9 %collective-permute-start.11 = (bf16[96,1792]{1,0:T(8,128)(2,1)S(1)}, bf16[96,1792]{1,0:T(8,128)(2,1)S(1)}, u32[]{:S(2)}, u32[]{:S(2)}) collective-permute-start(bf16[96,1792]{1,0:T(8,128)(2,1)S(1)} %get-tuple-element.31), channel_id=1, source_target_pairs={{0,1},{1,0},{2,3},{3,2},{4,5},{5,4},{6,7},{7,6},{8,9},{9,8},{10,11... | collective-permute-start | bytes 1032200 | tf_op jit(solution)/shard_map/ppermute | solution.py:244
  31.3 2.3 %collective-permute-start.10 = (bf16[96,1792]{1,0:T(8,128)(2,1)S(1)}, bf16[96,1792]{1,0:T(8,128)(2,1)S(1)}, u32[]{:S(2)}, u32[]{:S(2)}) collective-permute-start(bf16[96,1792]{1,0:T(8,128)(2,1)S(1)} %pack_kernel.5.refs_2_.refs_0_), channel_id=1, source_target_pairs={{0,1},{1,0},{2,3},{3,2},{4,5},{5,4},{6,7},{7,6},{8,9},{9,8},{10,11... | collective-permute-start | bytes 1032200 | tf_op jit(solution)/shard_map/ppermute | solution.py:244
  31.4 13.5 %collective-permute-start.3 = (bf16[96,1792]{1,0:T(8,128)(2,1)S(1)}, bf16[96,1792]{1,0:T(8,128)(2,1)S(1)}, u32[]{:S(2)}, u32[]{:S(2)}) collective-permute-start(bf16[96,1792]{1,0:T(8,128)(2,1)S(1)} %get-tuple-element.28), channel_id=1, source_target_pairs={{0,1},{1,0},{2,3},{3,2},{4,5},{5,4},{6,7},{7,6},{8,9},{9,8},{10,11... | collective-permute-start | bytes 1032200 | tf_op jit(solution)/shard_map/ppermute | solution.py:244
  31.9 4.6 %collective-permute-start.14 = (bf16[96,1792]{1,0:T(8,128)(2,1)S(1)}, bf16[96,1792]{1,0:T(8,128)(2,1)S(1)}, u32[]{:S(2)}, u32[]{:S(2)}) collective-permute-start(bf16[96,1792]{1,0:T(8,128)(2,1)S(1)} %get-tuple-element.36), channel_id=1, source_target_pairs={{0,1},{1,0},{2,3},{3,2},{4,5},{5,4},{6,7},{7,6},{8,9},{9,8},{10,11... | collective-permute-start | bytes 1032200 | tf_op jit(solution)/shard_map/ppermute | solution.py:244
  32.0 6.8 %collective-permute-start.13 = (bf16[96,896]{1,0:T(8,128)(2,1)S(1)}, bf16[96,896]{1,0:T(8,128)(2,1)S(1)}, u32[]{:S(2)}, u32[]{:S(2)}) collective-permute-start(bf16[96,896]{1,0:T(8,128)(2,1)S(1)} %get-tuple-element.35), channel_id=1, source_target_pairs={{0,2},{1,3},{2,0},{3,1},{4,6},{5,7},{6,4},{7,5},{8,10},{9,11},{10,... | collective-permute-start | bytes 516104 | tf_op jit(solution)/shard_map/ppermute | solution.py:244
  36.2 4.8 %collective-permute-start.12 = (bf16[96,1792]{1,0:T(8,128)(2,1)S(1)}, bf16[96,1792]{1,0:T(8,128)(2,1)S(1)}, u32[]{:S(2)}, u32[]{:S(2)}) collective-permute-start(bf16[96,1792]{1,0:T(8,128)(2,1)S(1)} %get-tuple-element.34), channel_id=1, source_target_pairs={{0,1},{1,0},{2,3},{3,2},{4,5},{5,4},{6,7},{7,6},{8,9},{9,8},{10,11... | collective-permute-start | bytes 1032200 | tf_op jit(solution)/shard_map/ppermute | solution.py:244
  36.5 6.8 %collective-permute-start.17 = (bf16[96,896]{1,0:T(8,128)(2,1)S(1)}, bf16[96,896]{1,0:T(8,128)(2,1)S(1)}, u32[]{:S(2)}, u32[]{:S(2)}) collective-permute-start(bf16[96,896]{1,0:T(8,128)(2,1)S(1)} %get-tuple-element.41), channel_id=1, source_target_pairs={{0,2},{1,3},{2,0},{3,1},{4,6},{5,7},{6,4},{7,5},{8,10},{9,11},{10,... | collective-permute-start | bytes 516104 | tf_op jit(solution)/shard_map/ppermute | solution.py:244
  38.9 11.2 %collective-permute-start.16 = (bf16[96,896]{1,0:T(8,128)(2,1)S(1)}, bf16[96,896]{1,0:T(8,128)(2,1)S(1)}, u32[]{:S(2)}, u32[]{:S(2)}) collective-permute-start(bf16[96,896]{1,0:T(8,128)(2,1)S(1)} %chip_sum_kernel.3.refs_2_), channel_id=1, source_target_pairs={{0,12},{4,0},{8,4},{12,8},{1,13},{5,1},{9,5},{13,9},{2,14},{6,2},{... | collective-permute-start | bytes 516104 | tf_op jit(solution)/shard_map/ppermute | solution.py:251
  41.1 6.4 %collective-permute-start.19 = (bf16[96,896]{1,0:T(8,128)(2,1)S(1)}, bf16[96,896]{1,0:T(8,128)(2,1)S(1)}, u32[]{:S(2)}, u32[]{:S(2)}) collective-permute-start(bf16[96,896]{1,0:T(8,128)(2,1)S(1)} %get-tuple-element.42), channel_id=1, source_target_pairs={{0,2},{1,3},{2,0},{3,1},{4,6},{5,7},{6,4},{7,5},{8,10},{9,11},{10,... | collective-permute-start | bytes 516104 | tf_op jit(solution)/shard_map/ppermute | solution.py:244
  43.4 8.1 %collective-permute-start.18 = (bf16[96,896]{1,0:T(8,128)(2,1)S(1)}, bf16[96,896]{1,0:T(8,128)(2,1)S(1)}, u32[]{:S(2)}, u32[]{:S(2)}) collective-permute-start(bf16[96,896]{1,0:T(8,128)(2,1)S(1)} %chip_sum_kernel.4.refs_2_), channel_id=1, source_target_pairs={{0,4},{4,8},{8,12},{12,0},{1,5},{5,9},{9,13},{13,1},{2,6},{6,10},{... | collective-permute-start | bytes 516104 | tf_op jit(solution)/shard_map/ppermute | solution.py:251
  45.0 6.5 %collective-permute-start.15 = (bf16[96,896]{1,0:T(8,128)(2,1)S(1)}, bf16[96,896]{1,0:T(8,128)(2,1)S(1)}, u32[]{:S(2)}, u32[]{:S(2)}) collective-permute-start(bf16[96,896]{1,0:T(8,128)(2,1)S(1)} %get-tuple-element.40), channel_id=1, source_target_pairs={{0,2},{1,3},{2,0},{3,1},{4,6},{5,7},{6,4},{7,5},{8,10},{9,11},{10,... | collective-permute-start | bytes 516104 | tf_op jit(solution)/shard_map/ppermute | solution.py:244
  47.5 10.8 %collective-permute-start.20 = (bf16[96,896]{1,0:T(8,128)(2,1)S(1)}, bf16[96,896]{1,0:T(8,128)(2,1)S(1)}, u32[]{:S(2)}, u32[]{:S(2)}) collective-permute-start(bf16[96,896]{1,0:T(8,128)(2,1)S(1)} %chip_sum_kernel.5), channel_id=1, source_target_pairs={{0,8},{4,12},{8,0},{12,4},{1,9},{5,13},{9,1},{13,5},{2,10},{6,14},... | collective-permute-start | bytes 516104 | tf_op jit(solution)/shard_map/ppermute | solution.py:251

commit v13 on v9

--- a/solution.py
+++ b/solution.py
@@ -131,17 +131,18 @@
     )
 
 
-def expert_kernel(chip, core, up_t, down, keep, send, features, out):
-    width = chip.shape[1] // 2
+def expert_kernel(count, *refs):
+    pieces, (up_t, down, keep, send, features, out) = refs[:count], refs[count:]
+    width = send.shape[1] // 2
     place = lax.axis_index("tensor")
 
     def columns(bits):
         return pl.ds(pl.multiple_of((place ^ bits) * width, width), width)
 
-    features[:, columns(0)] = chip[:, :width]
-    features[:, columns(2)] = chip[:, width:]
-    features[:, columns(1)] = core[:, :width]
-    features[:, columns(3)] = core[:, width:]
+    order = [0, 2, 1, 3]
+    for piece in pieces:
+        for at in range(0, piece.shape[1], width):
+            features[:, columns(order.pop(0))] = piece[:, at : at + width]
     lifted = lax.dot_general(
         features[...], up_t[...], (((1,), (1,)), ((), ())), preferred_element_type=jnp.float32
     )
@@ -153,15 +154,15 @@
     send[:, width:] = out[:, columns(3)].astype(jnp.bfloat16)
 
 
-def expert_rows(chip, core, up_t, down, others, cost):
-    rows, model = chip.shape[0], up_t.shape[1]
-    return local_call(
-        expert_kernel,
+def expert_rows(pieces, up_t, down, others, cost):
+    rows, model = pieces[0].shape[0], up_t.shape[1]
+    return local_call(
+        functools.partial(expert_kernel, len(pieces)),
         [
-            jax.ShapeDtypeStruct(chip.shape, jnp.float32),
-            jax.ShapeDtypeStruct(chip.shape, jnp.bfloat16),
+            jax.ShapeDtypeStruct((rows, model // 2), jnp.float32),
+            jax.ShapeDtypeStruct((rows, model // 2), jnp.bfloat16),
         ],
-        (chip, core, up_t, down),
+        (*pieces, up_t, down),
         others,
         limit=10 * MIB,
         scratch_shapes=[
@@ -267,8 +268,9 @@
         chips[steps] = pack([(blocks[step], others[step]) for step in steps], waits, cost)
 
     def run(steps, waits, cost):
-        chip = chips[steps]
-        kept[steps] = expert_rows(chip, swap(chip, 1), up_t, down, waits, cost)
+        mine = [chips[steps]] if steps in chips else [blocks[steps[0]], others[steps[0]]]
+        pieces = mine + [swap(piece, 1) for piece in mine]
+        kept[steps] = expert_rows(pieces, up_t, down, waits, cost)
 
     def leave(steps, waits, cost=2):
         keep, send = kept[steps]
@@ -282,23 +284,22 @@
 
     arrive(0, tokens, 0, [])
     arrive(1, tokens, 1, [columns])
-    arrive(3, tokens, -1, [columns])
-    lay((0,), [blocks[1], blocks[3]])
-    run((0,), [], 2.6)
+    lay((0,), [blocks[1]])
+    chips[3,] = shift(chips[0,], -1)
+    run((0,), [], 8)
     arrive(2, blocks[1], 1, [kept[0,][0]])
-    lay((1,), [kept[0,][0], blocks[2]])
-    run((1,), [], 4)
-    lay((3,), [kept[1,][0]], .5)
-    lay((2,), [chips[3,]], 4)
+    run((1,), [blocks[2]], .05)
+    chips[3,] = after(chips[3,], kept[1,][0])
+    lay((2,), [chips[3,]], 8)
     leave((1,), [chips[2,]], 2)
     run((3,), [sums[1][0]], 4)
     run((2,), [kept[3,][0]], .05)
     give(1, [kept[2,][0]], 2)
     leave((3,), [added[1]], 4)
     leave((2,), [sums[3][0]], 2)
-    leave((0,), [sums[2][0]])
     give(3, [sums[2][0]], 4)
     give(2, [added[3]], 4)
+    leave((0,), [added[2]], 2)
     total = weigh(columns, *sums[0][:2], (1, 3), [parts[1], parts[3]])
     return finish(columns, total, (2,), [parts[2]])
 

time: 67.6 us -> 60.7 us (0.90)
  waiting for transfers between devices: 33.2 us -> 26.4 us
    ppermute x6, waiting for transfers between devices: 17.4 us -> 12.8 us  [shift(): lax.ppermute(array, 'expert', [(i, (i + by) % experts_n) for i in range(e...]
    ppermute x16, waiting for transfers between devices: 15.9 us -> 13.6 us  [swap(): return lax.ppermute(array, 'tensor', [(i, i ^ bit) for i in range(4)])]
    ppermute x16, starting transfers between devices: 10.7 us -> 9.88 us  [swap(): return lax.ppermute(array, 'tensor', [(i, i ^ bit) for i in range(4)])]
    ppermute x6, starting transfers between devices: 7.19 us -> 7.99 us  [shift(): lax.ppermute(array, 'expert', [(i, (i + by) % experts_n) for i in range(e...]
    pallas_call x18 -> x16, Pallas kernels: 16.1 us -> 16.1 us  [local_call(): pl.pallas_call(body_of, name=name, out_shape=out_shape, in_specs=list(in_...]
  transfers between devices with their start and end apart: 22 -> 22, of which waited for: 9 -> 12; matrix products, arithmetic and copies ran while one was open for 0% -> 0% of each run, Pallas kernels for 23% -> 25%
where the time goes in v13:
time: 60.7 us; the launch traced here: 60.5 us
  waiting for transfers between devices  26.4 us (43%)
  starting transfers between devices  17.9 us (29%)
  Pallas kernels  16.1 us (27%)
    pallas_call x16, Pallas kernels, local_call(): pl.pallas_call(body_of, name=name, out_shape=out_shape, in_specs=list(in_...  16.1 us
    ppermute x16, waiting for transfers between devices, swap(): return lax.ppermute(array, 'tensor', [(i, i ^ bit) for i in range(4)])  13.6 us
    ppermute x6, waiting for transfers between devices, shift(): lax.ppermute(array, 'expert', [(i, (i + by) % experts_n) for i in range(e...  12.8 us
    ppermute x16, starting transfers between devices, swap(): return lax.ppermute(array, 'tensor', [(i, i ^ bit) for i in range(4)])  9.88 us
    ppermute x6, starting transfers between devices, shift(): lax.ppermute(array, 'expert', [(i, (i + by) % experts_n) for i in range(e...  7.99 us
  transfers between devices with their start and end apart: 22, of which 12 were waited for; matrix products, arithmetic and copies ran while one was open for 0% of the time, Pallas kernels for 25%

profile of v13, /device:TPU:0, one launch (start us, length us, event | category | flops | bytes accessed | tf_op | source)
XLA Modules:
  0.0 60.5 jit_solution(14748426564735223422)
XLA Ops:
  0.0 2.9 %collective-permute-start = (bf16[96,896]{1,0:T(8,128)(2,1)}, bf16[96,896]{1,0:T(8,128)(2,1)S(1)}, u32[]{:S(2)}, u32[]{:S(2)}) collective-permute-start(bf16[96,896]{1,0:T(8,128)(2,1)} %refs_0_.1), channel_id=1, source_target_pairs={{0,2},{1,3},{2,0},{3,1},{4,6},{5,7},{6,4},{7,5},{8,10},{9,11},{10,... | collective-permute-start | bytes 516104 | tf_op jit(solution)/shard_map/ppermute | solution.py:245
  2.9 1.6 %collective-permute-start.1 = (bf16[96,896]{1,0:T(8,128)(2,1)}, bf16[96,896]{1,0:T(8,128)(2,1)S(1)}, u32[]{:S(2)}, u32[]{:S(2)}) collective-permute-start(bf16[96,896]{1,0:T(8,128)(2,1)} %refs_0_.1), channel_id=1, source_target_pairs={{0,4},{4,8},{8,12},{12,0},{1,5},{5,9},{9,13},{13,1},{2,6},{6,10},{... | collective-permute-start | bytes 516104 | tf_op jit(solution)/shard_map/ppermute | solution.py:252
  4.5 4.3 %prepare_kernel.1 = (f32[4,96,128]{2,1,0:T(8,128)S(1)}, bf16[608,3584]{1,0:T(8,128)(2,1)S(1)}, bf16[608,3584]{1,0:T(8,128)(2,1)S(1)}) custom-call(s32[2,96]{1,0:T(2,128)} %bitcast.8, s32[2,96]{1,0:T(2,128)} %bitcast.9, bf16[608,3584]{1,0:T(8,128)(2,1)} %bitcast.6, bf16[608,3584]{1,0:T(8,128)(2,1)} %bitcast.7), custom_call_target="tpu_custom_call" | custom-call | flops 4600000000 | tf_op jit(solution)/shard_map/prepare_kernel/pallas_call | solution.py:72
  8.9 2.0 %collective-permute-done.1.refs_0_ = bf16[96,896]{1,0:T(8,128)(2,1)S(1)} collective-permute-done((bf16[96,896]{1,0:T(8,128)(2,1)}, bf16[96,896]{1,0:T(8,128)(2,1)S(1)}, u32[]{:S(2)}, u32[]{:S(2)}) %collective-permute-start.1) | collective-permute-done | bytes 172064 | tf_op jit(solution)/shard_map/ppermute | solution.py:252
  11.8 3.8 %collective-permute-start.6 = (bf16[96,1792]{1,0:T(8,128)(2,1)S(1)}, bf16[96,1792]{1,0:T(8,128)(2,1)S(1)}, u32[]{:S(2)}, u32[]{:S(2)}) collective-permute-start(bf16[96,1792]{1,0:T(8,128)(2,1)S(1)} %pack_kernel.2.refs_0_), channel_id=1, source_target_pairs={{0,12},{4,0},{8,4},{12,8},{1,13},{5,1},{9,5},{13,9},{2,14},{6,2},{... | collective-permute-start | bytes 1032200 | tf_op jit(solution)/shard_map/ppermute | solution.py:252
  15.6 2.2 %collective-permute-done.7.refs_1_ = bf16[96,896]{1,0:T(8,128)(2,1)S(1)} collective-permute-done((bf16[96,896]{1,0:T(8,128)(2,1)S(1)}, bf16[96,896]{1,0:T(8,128)(2,1)S(1)}, u32[]{:S(2)}, u32[]{:S(2)}) %collective-permute-start.7) | collective-permute-done | bytes 172064 | tf_op jit(solution)/shard_map/ppermute | solution.py:245
  17.8 2.6 %expert_kernel.4 = (f32[96,1792]{1,0:T(8,128)S(1)}, bf16[96,1792]{1,0:T(8,128)(2,1)S(1)}) custom-call(bf16[96,1792]{1,0:T(8,128)(2,1)S(1)} %pack_kernel.2.refs_0_, bf16[96,1792]{1,0:T(8,128)(2,1)S(1)} %collective-permute-done.2.refs_1_, bf16[608,3584]{1,0:T(8,128)(2,1)S(1)} %get-tuple-element.25.refs_2_.refs_4_, ...), custom_call_target="tpu_custom_call" | custom-call | flops 9200000000 | tf_op jit(solution)/shard_map/expert_kernel/pallas_call | solution.py:72
  20.8 1.5 %collective-permute-start.5 = (bf16[96,896]{1,0:T(8,128)(2,1)S(1)}, bf16[96,896]{1,0:T(8,128)(2,1)S(1)}, u32[]{:S(2)}, u32[]{:S(2)}) collective-permute-start(bf16[96,896]{1,0:T(8,128)(2,1)S(1)} %shard_map.56.refs_6_.refs_0_), channel_id=1, source_target_pairs={{0,2},{1,3},{2,0},{3,1},{4,6},{5,7},{6,4},{7,5},{8,10},{9,11},{10,... | collective-permute-start | bytes 516104 | tf_op jit(solution)/shard_map/ppermute | solution.py:245
  22.3 2.6 %expert_kernel.5 = (f32[96,1792]{1,0:T(8,128)S(1)}, bf16[96,1792]{1,0:T(8,128)(2,1)S(1)}) custom-call(bf16[96,896]{1,0:T(8,128)(2,1)S(1)} %shard_map.55.refs_2_.refs_0_, bf16[96,896]{1,0:T(8,128)(2,1)S(1)} %collective-permute-done.7.refs_1_, bf16[96,896]{1,0:T(8,128)(2,1)S(1)} %collective-permute-done.8.refs_2_, ...), custom_call_target="tpu_custom_call" | custom-call | flops 57500000 | tf_op jit(solution)/shard_map/expert_kernel/pallas_call | solution.py:72
  24.9 0.8 %collective-permute-done.6.refs_0_ = bf16[96,1792]{1,0:T(8,128)(2,1)S(1)} collective-permute-done((bf16[96,1792]{1,0:T(8,128)(2,1)S(1)}, bf16[96,1792]{1,0:T(8,128)(2,1)S(1)}, u32[]{:S(2)}, u32[]{:S(2)}) %collective-permute-start.6) | collective-permute-done | bytes 344096 | tf_op jit(solution)/shard_map/ppermute | solution.py:252
  26.3 1.0 %collective-permute-done.5.refs_1_ = bf16[96,896]{1,0:T(8,128)(2,1)S(1)} collective-permute-done((bf16[96,896]{1,0:T(8,128)(2,1)S(1)}, bf16[96,896]{1,0:T(8,128)(2,1)S(1)}, u32[]{:S(2)}, u32[]{:S(2)}) %collective-permute-start.5) | collective-permute-done | bytes 172064 | tf_op jit(solution)/shard_map/ppermute | solution.py:245
  28.0 1.6 %collective-permute-start.15 = (bf16[96,896]{1,0:T(8,128)(2,1)S(1)}, bf16[96,896]{1,0:T(8,128)(2,1)S(1)}, u32[]{:S(2)}, u32[]{:S(2)}) collective-permute-start(bf16[96,896]{1,0:T(8,128)(2,1)S(1)} %get-tuple-element.36), channel_id=1, source_target_pairs={{0,2},{1,3},{2,0},{3,1},{4,6},{5,7},{6,4},{7,5},{8,10},{9,11},{10,... | collective-permute-start | bytes 516104 | tf_op jit(solution)/shard_map/ppermute | solution.py:245
  29.6 2.6 %expert_kernel.6 = (f32[96,1792]{1,0:T(8,128)S(1)}, bf16[96,1792]{1,0:T(8,128)(2,1)S(1)}) custom-call(bf16[96,1792]{1,0:T(8,128)(2,1)S(1)} %shard_map.57.refs_2_.refs_0_, bf16[96,1792]{1,0:T(8,128)(2,1)S(1)} %collective-permute-done.11.refs_1_, bf16[608,3584]{1,0:T(8,128)(2,1)S(1)} %get-tuple-element.25.refs_2_.refs_4_, ...), custom_call_target="tpu_custom_call" | custom-call | flops 4600000000 | tf_op jit(solution)/shard_map/expert_kernel/pallas_call | solution.py:72
  32.8 2.6 %expert_kernel.7 = (f32[96,1792]{1,0:T(8,128)S(1)}, bf16[96,1792]{1,0:T(8,128)(2,1)S(1)}) custom-call(bf16[96,1792]{1,0:T(8,128)(2,1)S(1)} %pack_kernel.3.refs_2_.refs_0_, bf16[96,1792]{1,0:T(8,128)(2,1)S(1)} %collective-permute-done.10.refs_1_, bf16[608,3584]{1,0:T(8,128)(2,1)S(1)} %get-tuple-element.25.refs_2_.refs_4_, ...), custom_call_target="tpu_custom_call" | custom-call | flops 57500000 | tf_op jit(solution)/shard_map/expert_kernel/pallas_call | solution.py:72
  35.5 2.1 %collective-permute-start.19 = (bf16[96,896]{1,0:T(8,128)(2,1)S(1)}, bf16[96,896]{1,0:T(8,128)(2,1)S(1)}, u32[]{:S(2)}, u32[]{:S(2)}) collective-permute-start(bf16[96,896]{1,0:T(8,128)(2,1)S(1)} %chip_sum_kernel.3.refs_2_), channel_id=1, source_target_pairs={{0,12},{4,0},{8,4},{12,8},{1,13},{5,1},{9,5},{13,9},{2,14},{6,2},{... | collective-permute-start | bytes 516104 | tf_op jit(solution)/shard_map/ppermute | solution.py:252
  37.6 0.6 %collective-permute-start.17 = (bf16[96,896]{1,0:T(8,128)(2,1)S(1)}, bf16[96,896]{1,0:T(8,128)(2,1)S(1)}, u32[]{:S(2)}, u32[]{:S(2)}) collective-permute-start(bf16[96,896]{1,0:T(8,128)(2,1)S(1)} %get-tuple-element.40), channel_id=1, source_target_pairs={{0,2},{1,3},{2,0},{3,1},{4,6},{5,7},{6,4},{7,5},{8,10},{9,11},{10,... | collective-permute-start | bytes 516104 | tf_op jit(solution)/shard_map/ppermute | solution.py:245
  38.3 0.9 %collective-permute-done.13.refs_1_ = bf16[96,1792]{1,0:T(8,128)(2,1)S(1)} collective-permute-done((bf16[96,1792]{1,0:T(8,128)(2,1)S(1)}, bf16[96,1792]{1,0:T(8,128)(2,1)S(1)}, u32[]{:S(2)}, u32[]{:S(2)}) %collective-permute-start.13) | collective-permute-done | bytes 344096 | tf_op jit(solution)/shard_map/ppermute | solution.py:245
  39.9 5.0 %collective-permute-done.17.refs_1_ = bf16[96,896]{1,0:T(8,128)(2,1)S(1)} collective-permute-done((bf16[96,896]{1,0:T(8,128)(2,1)S(1)}, bf16[96,896]{1,0:T(8,128)(2,1)S(1)}, u32[]{:S(2)}, u32[]{:S(2)}) %collective-permute-start.17) | collective-permute-done | bytes 172064 | tf_op jit(solution)/shard_map/ppermute | solution.py:245
  45.0 3.2 %collective-permute-done.16.refs_1_ = bf16[96,896]{1,0:T(8,128)(2,1)S(1)} collective-permute-done((bf16[96,896]{1,0:T(8,128)(2,1)S(1)}, bf16[96,896]{1,0:T(8,128)(2,1)S(1)}, u32[]{:S(2)}, u32[]{:S(2)}) %collective-permute-start.16) | collective-permute-done | bytes 172064 | tf_op jit(solution)/shard_map/ppermute | solution.py:245
  48.3 0.6 %collective-permute-start.18 = (bf16[96,896]{1,0:T(8,128)(2,1)S(1)}, bf16[96,896]{1,0:T(8,128)(2,1)S(1)}, u32[]{:S(2)}, u32[]{:S(2)}) collective-permute-start(bf16[96,896]{1,0:T(8,128)(2,1)S(1)} %get-tuple-element.42), channel_id=1, source_target_pairs={{0,2},{1,3},{2,0},{3,1},{4,6},{5,7},{6,4},{7,5},{8,10},{9,11},{10,... | collective-permute-start | bytes 516104 | tf_op jit(solution)/shard_map/ppermute | solution.py:245
  49.4 4.3 %collective-permute-done.20.refs_4_ = bf16[96,896]{1,0:T(8,128)(2,1)S(1)} collective-permute-done((bf16[96,896]{1,0:T(8,128)(2,1)S(1)}, bf16[96,896]{1,0:T(8,128)(2,1)S(1)}, u32[]{:S(2)}, u32[]{:S(2)}) %collective-permute-start.20) | collective-permute-done | bytes 172064 | tf_op jit(solution)/shard_map/ppermute | solution.py:252
  53.6 0.7 %collective-permute-done.18.refs_2_ = bf16[96,896]{1,0:T(8,128)(2,1)S(1)} collective-permute-done((bf16[96,896]{1,0:T(8,128)(2,1)S(1)}, bf16[96,896]{1,0:T(8,128)(2,1)S(1)}, u32[]{:S(2)}, u32[]{:S(2)}) %collective-permute-start.18) | collective-permute-done | bytes 172064 | tf_op jit(solution)/shard_map/ppermute | solution.py:245
  54.5 5.3 %collective-permute-done.21.refs_2_ = bf16[96,896]{1,0:T(8,128)(2,1)S(1)} collective-permute-done((bf16[96,896]{1,0:T(8,128)(2,1)S(1)}, bf16[96,896]{1,0:T(8,128)(2,1)S(1)}, u32[]{:S(2)}, u32[]{:S(2)}) %collective-permute-start.21) | collective-permute-done | bytes 172064 | tf_op jit(solution)/shard_map/ppermute | solution.py:252
  59.8 0.7 %finish_kernel.1 = bf16[96,896]{1,0:T(8,128)(2,1)} custom-call(f32[4,96,128]{2,1,0:T(8,128)S(1)} %get-tuple-element.24.refs_1_.refs_0_, f32[96,896]{1,0:T(8,128)S(1)} %weigh_kernel.1.refs_1_, bf16[96,896]{1,0:T(8,128)(2,1)S(1)} %collective-permute-done.21.refs_2_), custom_call_target="tpu_custom_call" | custom-call | flops 575000000 | tf_op jit(solution)/shard_map/finish_kernel/pallas_call | solution.py:72
  (41 shorter events, 4.6 us)
Async XLA Ops:
  0.0 10.9 %collective-permute-start = (bf16[96,896]{1,0:T(8,128)(2,1)}, bf16[96,896]{1,0:T(8,128)(2,1)S(1)}, u32[]{:S(2)}, u32[]{:S(2)}) collective-permute-start(bf16[96,896]{1,0:T(8,128)(2,1)} %refs_0_.1), channel_id=1, source_target_pairs={{0,2},{1,3},{2,0},{3,1},{4,6},{5,7},{6,4},{7,5},{8,10},{9,11},{10,... | collective-permute-start | bytes 516104 | tf_op jit(solution)/shard_map/ppermute | solution.py:245
  2.9 7.9 %collective-permute-start.1 = (bf16[96,896]{1,0:T(8,128)(2,1)}, bf16[96,896]{1,0:T(8,128)(2,1)S(1)}, u32[]{:S(2)}, u32[]{:S(2)}) collective-permute-start(bf16[96,896]{1,0:T(8,128)(2,1)} %refs_0_.1), channel_id=1, source_target_pairs={{0,4},{4,8},{8,12},{12,0},{1,5},{5,9},{9,13},{13,1},{2,6},{6,10},{... | collective-permute-start | bytes 516104 | tf_op jit(solution)/shard_map/ppermute | solution.py:252
  4.5 6.4 %copy-start = (bf16[96,896]{1,0:T(8,128)(2,1)S(1)}, bf16[96,896]{1,0:T(8,128)(2,1)}, u32[]{:S(2)}) copy-start(bf16[96,896]{1,0:T(8,128)(2,1)} %refs_0_.1) | copy-start | bytes 516100
  10.9 6.9 %collective-permute-start.2 = (bf16[96,1792]{1,0:T(8,128)(2,1)S(1)}, bf16[96,1792]{1,0:T(8,128)(2,1)S(1)}, u32[]{:S(2)}, u32[]{:S(2)}) collective-permute-start(bf16[96,1792]{1,0:T(8,128)(2,1)S(1)} %pack_kernel.2.refs_0_), channel_id=1, source_target_pairs={{0,1},{1,0},{2,3},{3,2},{4,5},{5,4},{6,7},{7,6},{8,9},{9,8},{10,11... | collective-permute-start | bytes 1032200 | tf_op jit(solution)/shard_map/ppermute | solution.py:245
  11.0 6.8 %collective-permute-start.7 = (bf16[96,896]{1,0:T(8,128)(2,1)S(1)}, bf16[96,896]{1,0:T(8,128)(2,1)S(1)}, u32[]{:S(2)}, u32[]{:S(2)}) collective-permute-start(bf16[96,896]{1,0:T(8,128)(2,1)S(1)} %shard_map.55.refs_2_.refs_0_), channel_id=1, source_target_pairs={{0,2},{1,3},{2,0},{3,1},{4,6},{5,7},{6,4},{7,5},{8,10},{9,11},{10,... | collective-permute-start | bytes 516104 | tf_op jit(solution)/shard_map/ppermute | solution.py:245
  11.6 10.7 %collective-permute-start.8 = (bf16[96,896]{1,0:T(8,128)(2,1)S(1)}, bf16[96,896]{1,0:T(8,128)(2,1)S(1)}, u32[]{:S(2)}, u32[]{:S(2)}) collective-permute-start(bf16[96,896]{1,0:T(8,128)(2,1)S(1)} %shard_map.55.refs_2_.refs_0_), channel_id=1, source_target_pairs={{0,1},{1,0},{2,3},{3,2},{4,5},{5,4},{6,7},{7,6},{8,9},{9,8},{10,11... | collective-permute-start | bytes 516104 | tf_op jit(solution)/shard_map/ppermute | solution.py:245
  11.8 9.0 %collective-permute-start.4 = (bf16[96,896]{1,0:T(8,128)(2,1)S(1)}, bf16[96,896]{1,0:T(8,128)(2,1)S(1)}, u32[]{:S(2)}, u32[]{:S(2)}) collective-permute-start(bf16[96,896]{1,0:T(8,128)(2,1)S(1)} %shard_map.55.refs_2_.refs_0_), channel_id=1, source_target_pairs={{0,4},{4,8},{8,12},{12,0},{1,5},{5,9},{9,13},{13,1},{2,6},{6,10},{... | collective-permute-start | bytes 516104 | tf_op jit(solution)/shard_map/ppermute | solution.py:252
  11.8 14.0 %collective-permute-start.6 = (bf16[96,1792]{1,0:T(8,128)(2,1)S(1)}, bf16[96,1792]{1,0:T(8,128)(2,1)S(1)}, u32[]{:S(2)}, u32[]{:S(2)}) collective-permute-start(bf16[96,1792]{1,0:T(8,128)(2,1)S(1)} %pack_kernel.2.refs_0_), channel_id=1, source_target_pairs={{0,12},{4,0},{8,4},{12,8},{1,13},{5,1},{9,5},{13,9},{2,14},{6,2},{... | collective-permute-start | bytes 1032200 | tf_op jit(solution)/shard_map/ppermute | solution.py:252
  17.8 4.5 %collective-permute-start.9 = (bf16[96,896]{1,0:T(8,128)(2,1)S(1)}, bf16[96,896]{1,0:T(8,128)(2,1)S(1)}, u32[]{:S(2)}, u32[]{:S(2)}) collective-permute-start(bf16[96,896]{1,0:T(8,128)(2,1)S(1)} %collective-permute-done.7.refs_1_), channel_id=1, source_target_pairs={{0,1},{1,0},{2,3},{3,2},{4,5},{5,4},{6,7},{7,6},{8,9},{9,8},{10,11... | collective-permute-start | bytes 516104 | tf_op jit(solution)/shard_map/ppermute | solution.py:245
  20.8 6.5 %collective-permute-start.5 = (bf16[96,896]{1,0:T(8,128)(2,1)S(1)}, bf16[96,896]{1,0:T(8,128)(2,1)S(1)}, u32[]{:S(2)}, u32[]{:S(2)}) collective-permute-start(bf16[96,896]{1,0:T(8,128)(2,1)S(1)} %shard_map.56.refs_6_.refs_0_), channel_id=1, source_target_pairs={{0,2},{1,3},{2,0},{3,1},{4,6},{5,7},{6,4},{7,5},{8,10},{9,11},{10,... | collective-permute-start | bytes 516104 | tf_op jit(solution)/shard_map/ppermute | solution.py:245
  25.8 3.8 %collective-permute-start.11 = (bf16[96,1792]{1,0:T(8,128)(2,1)S(1)}, bf16[96,1792]{1,0:T(8,128)(2,1)S(1)}, u32[]{:S(2)}, u32[]{:S(2)}) collective-permute-start(bf16[96,1792]{1,0:T(8,128)(2,1)S(1)} %shard_map.57.refs_2_.refs_0_), channel_id=1, source_target_pairs={{0,1},{1,0},{2,3},{3,2},{4,5},{5,4},{6,7},{7,6},{8,9},{9,8},{10,11... | collective-permute-start | bytes 1032200 | tf_op jit(solution)/shard_map/ppermute | solution.py:245
  25.8 2.1 %collective-permute-start.12 = (bf16[96,1792]{1,0:T(8,128)(2,1)S(1)}, bf16[96,1792]{1,0:T(8,128)(2,1)S(1)}, u32[]{:S(2)}, u32[]{:S(2)}) collective-permute-start(bf16[96,1792]{1,0:T(8,128)(2,1)S(1)} %get-tuple-element.30), channel_id=1, source_target_pairs={{0,1},{1,0},{2,3},{3,2},{4,5},{5,4},{6,7},{7,6},{8,9},{9,8},{10,11... | collective-permute-start | bytes 1032200 | tf_op jit(solution)/shard_map/ppermute | solution.py:245
  27.3 5.4 %collective-permute-start.10 = (bf16[96,1792]{1,0:T(8,128)(2,1)S(1)}, bf16[96,1792]{1,0:T(8,128)(2,1)S(1)}, u32[]{:S(2)}, u32[]{:S(2)}) collective-permute-start(bf16[96,1792]{1,0:T(8,128)(2,1)S(1)} %pack_kernel.3.refs_2_.refs_0_), channel_id=1, source_target_pairs={{0,1},{1,0},{2,3},{3,2},{4,5},{5,4},{6,7},{7,6},{8,9},{9,8},{10,11... | collective-permute-start | bytes 1032200 | tf_op jit(solution)/shard_map/ppermute | solution.py:245
  28.0 7.4 %collective-permute-start.15 = (bf16[96,896]{1,0:T(8,128)(2,1)S(1)}, bf16[96,896]{1,0:T(8,128)(2,1)S(1)}, u32[]{:S(2)}, u32[]{:S(2)}) collective-permute-start(bf16[96,896]{1,0:T(8,128)(2,1)S(1)} %get-tuple-element.36), channel_id=1, source_target_pairs={{0,2},{1,3},{2,0},{3,1},{4,6},{5,7},{6,4},{7,5},{8,10},{9,11},{10,... | collective-permute-start | bytes 516104 | tf_op jit(solution)/shard_map/ppermute | solution.py:245
  32.2 5.4 %collective-permute-start.14 = (bf16[96,1792]{1,0:T(8,128)(2,1)S(1)}, bf16[96,1792]{1,0:T(8,128)(2,1)S(1)}, u32[]{:S(2)}, u32[]{:S(2)}) collective-permute-start(bf16[96,1792]{1,0:T(8,128)(2,1)S(1)} %get-tuple-element.35), channel_id=1, source_target_pairs={{0,1},{1,0},{2,3},{3,2},{4,5},{5,4},{6,7},{7,6},{8,9},{9,8},{10,11... | collective-permute-start | bytes 1032200 | tf_op jit(solution)/shard_map/ppermute | solution.py:245
  32.3 16.0 %collective-permute-start.3 = (bf16[96,1792]{1,0:T(8,128)(2,1)S(1)}, bf16[96,1792]{1,0:T(8,128)(2,1)S(1)}, u32[]{:S(2)}, u32[]{:S(2)}) collective-permute-start(bf16[96,1792]{1,0:T(8,128)(2,1)S(1)} %get-tuple-element.28), channel_id=1, source_target_pairs={{0,1},{1,0},{2,3},{3,2},{4,5},{5,4},{6,7},{7,6},{8,9},{9,8},{10,11... | collective-permute-start | bytes 1032200 | tf_op jit(solution)/shard_map/ppermute | solution.py:245
  35.5 13.9 %collective-permute-start.19 = (bf16[96,896]{1,0:T(8,128)(2,1)S(1)}, bf16[96,896]{1,0:T(8,128)(2,1)S(1)}, u32[]{:S(2)}, u32[]{:S(2)}) collective-permute-start(bf16[96,896]{1,0:T(8,128)(2,1)S(1)} %chip_sum_kernel.3.refs_2_), channel_id=1, source_target_pairs={{0,12},{4,0},{8,4},{12,8},{1,13},{5,1},{9,5},{13,9},{2,14},{6,2},{... | collective-permute-start | bytes 516104 | tf_op jit(solution)/shard_map/ppermute | solution.py:252
  37.6 1.7 %collective-permute-start.13 = (bf16[96,1792]{1,0:T(8,128)(2,1)S(1)}, bf16[96,1792]{1,0:T(8,128)(2,1)S(1)}, u32[]{:S(2)}, u32[]{:S(2)}) collective-permute-start(bf16[96,1792]{1,0:T(8,128)(2,1)S(1)} %get-tuple-element.34), channel_id=1, source_target_pairs={{0,1},{1,0},{2,3},{3,2},{4,5},{5,4},{6,7},{7,6},{8,9},{9,8},{10,11... | collective-permute-start | bytes 1032200 | tf_op jit(solution)/shard_map/ppermute | solution.py:245
  37.6 7.2 %collective-permute-start.17 = (bf16[96,896]{1,0:T(8,128)(2,1)S(1)}, bf16[96,896]{1,0:T(8,128)(2,1)S(1)}, u32[]{:S(2)}, u32[]{:S(2)}) collective-permute-start(bf16[96,896]{1,0:T(8,128)(2,1)S(1)} %get-tuple-element.40), channel_id=1, source_target_pairs={{0,2},{1,3},{2,0},{3,1},{4,6},{5,7},{6,4},{7,5},{8,10},{9,11},{10,... | collective-permute-start | bytes 516104 | tf_op jit(solution)/shard_map/ppermute | solution.py:245
  39.3 8.9 %collective-permute-start.16 = (bf16[96,896]{1,0:T(8,128)(2,1)S(1)}, bf16[96,896]{1,0:T(8,128)(2,1)S(1)}, u32[]{:S(2)}, u32[]{:S(2)}) collective-permute-start(bf16[96,896]{1,0:T(8,128)(2,1)S(1)} %get-tuple-element.39), channel_id=1, source_target_pairs={{0,2},{1,3},{2,0},{3,1},{4,6},{5,7},{6,4},{7,5},{8,10},{9,11},{10,... | collective-permute-start | bytes 516104 | tf_op jit(solution)/shard_map/ppermute | solution.py:245
  44.9 8.7 %collective-permute-start.20 = (bf16[96,896]{1,0:T(8,128)(2,1)S(1)}, bf16[96,896]{1,0:T(8,128)(2,1)S(1)}, u32[]{:S(2)}, u32[]{:S(2)}) collective-permute-start(bf16[96,896]{1,0:T(8,128)(2,1)S(1)} %chip_sum_kernel.4.refs_2_), channel_id=1, source_target_pairs={{0,4},{4,8},{8,12},{12,0},{1,5},{5,9},{9,13},{13,1},{2,6},{6,10},{... | collective-permute-start | bytes 516104 | tf_op jit(solution)/shard_map/ppermute | solution.py:252
  48.3 6.1 %collective-permute-start.18 = (bf16[96,896]{1,0:T(8,128)(2,1)S(1)}, bf16[96,896]{1,0:T(8,128)(2,1)S(1)}, u32[]{:S(2)}, u32[]{:S(2)}) collective-permute-start(bf16[96,896]{1,0:T(8,128)(2,1)S(1)} %get-tuple-element.42), channel_id=1, source_target_pairs={{0,2},{1,3},{2,0},{3,1},{4,6},{5,7},{6,4},{7,5},{8,10},{9,11},{10,... | collective-permute-start | bytes 516104 | tf_op jit(solution)/shard_map/ppermute | solution.py:245
  49.0 10.8 %collective-permute-start.21 = (bf16[96,896]{1,0:T(8,128)(2,1)S(1)}, bf16[96,896]{1,0:T(8,128)(2,1)S(1)}, u32[]{:S(2)}, u32[]{:S(2)}) collective-permute-start(bf16[96,896]{1,0:T(8,128)(2,1)S(1)} %chip_sum_kernel.5.refs_2_), channel_id=1, source_target_pairs={{0,8},{4,12},{8,0},{12,4},{1,9},{5,13},{9,1},{13,5},{2,10},{6,14},... | collective-permute-start | bytes 516104 | tf_op jit(solution)/shard_map/ppermute | solution.py:252

commit v14 on v13

--- a/solution.py
+++ b/solution.py
@@ -289,19 +289,18 @@
     run((0,), [], 8)
     arrive(2, blocks[1], 1, [kept[0,][0]])
     run((1,), [blocks[2]], .05)
-    chips[3,] = after(chips[3,], kept[1,][0])
-    lay((2,), [chips[3,]], 8)
-    leave((1,), [chips[2,]], 2)
-    run((3,), [sums[1][0]], 4)
-    run((2,), [kept[3,][0]], .05)
-    give(1, [kept[2,][0]], 2)
-    leave((3,), [added[1]], 4)
-    leave((2,), [sums[3][0]], 2)
-    give(3, [sums[2][0]], 4)
-    give(2, [added[3]], 4)
-    leave((0,), [added[2]], 2)
-    total = weigh(columns, *sums[0][:2], (1, 3), [parts[1], parts[3]])
-    return finish(columns, total, (2,), [parts[2]])
+    run((2,), [kept[1,][0]], .05)
+    chips[3,] = after(chips[3,], kept[2,][0])
+    leave((1,), [kept[2,][0]], 2)
+    leave((2,), [sums[1][0]], 2)
+    run((3,), [sums[2][0]], 4)
+    give(1, [kept[3,][0]], 4)
+    leave((3,), [added[1]], 2)
+    give(2, [sums[3][0]], 4)
+    give(3, [added[2]], 4)
+    leave((0,), [added[3]], 2)
+    total = weigh(columns, *sums[0][:2], (1, 2), [parts[1], parts[2]])
+    return finish(columns, total, (3,), [parts[3]])
 
 
 def slotted(tokens, expert_ids, weight_codes, up_local, down_local, capacity):

time: 60.7 us -> 57.5 us (0.947)
  waiting for transfers between devices: 26.4 us -> 18.8 us
  starting transfers between devices: 17.9 us -> 22.4 us
    ppermute x6, starting transfers between devices: 7.99 us -> 12.5 us  [shift(): lax.ppermute(array, 'expert', [(i, (i + by) % experts_n) for i in range(e...]
    ppermute x16 -> x17, waiting for transfers between devices: 13.6 us -> 9.49 us  [swap(): return lax.ppermute(array, 'tensor', [(i, i ^ bit) for i in range(4)])]
    ppermute x6, waiting for transfers between devices: 12.8 us -> 9.27 us  [shift(): lax.ppermute(array, 'expert', [(i, (i + by) % experts_n) for i in range(e...]
    ppermute x16 -> x17, starting transfers between devices: 9.88 us -> 9.82 us  [swap(): return lax.ppermute(array, 'tensor', [(i, i ^ bit) for i in range(4)])]
    pallas_call x16 -> x15, Pallas kernels: 16.1 us -> 16.1 us  [local_call(): pl.pallas_call(body_of, name=name, out_shape=out_shape, in_specs=list(in_...]
  transfers between devices with their start and end apart: 22 -> 23, of which waited for: 12 -> 11; matrix products, arithmetic and copies ran while one was open for 0% -> 0% of each run, Pallas kernels for 25% -> 27%
where the time goes in v14:
time: 57.5 us; the launch traced here: 57.3 us
  starting transfers between devices  22.4 us (39%)
  waiting for transfers between devices  18.8 us (33%)
  Pallas kernels  16.1 us (28%)
    pallas_call x15, Pallas kernels, local_call(): pl.pallas_call(body_of, name=name, out_shape=out_shape, in_specs=list(in_...  16.1 us
    ppermute x6, starting transfers between devices, shift(): lax.ppermute(array, 'expert', [(i, (i + by) % experts_n) for i in range(e...  12.5 us
    ppermute x17, starting transfers between devices, swap(): return lax.ppermute(array, 'tensor', [(i, i ^ bit) for i in range(4)])  9.82 us
    ppermute x17, waiting for transfers between devices, swap(): return lax.ppermute(array, 'tensor', [(i, i ^ bit) for i in range(4)])  9.49 us
    ppermute x6, waiting for transfers between devices, shift(): lax.ppermute(array, 'expert', [(i, (i + by) % experts_n) for i in range(e...  9.27 us
  transfers between devices with their start and end apart: 23, of which 11 were waited for; matrix products, arithmetic and copies ran while one was open for 0% of the time, Pallas kernels for 27%

profile of v14, /device:TPU:0, one launch (start us, length us, event | category | flops | bytes accessed | tf_op | source)
XLA Modules:
  0.0 57.3 jit_solution(11376691853243446566)
XLA Ops:
  0.0 3.0 %collective-permute-start.1 = (bf16[96,896]{1,0:T(8,128)(2,1)}, bf16[96,896]{1,0:T(8,128)(2,1)S(1)}, u32[]{:S(2)}, u32[]{:S(2)}) collective-permute-start(bf16[96,896]{1,0:T(8,128)(2,1)} %refs_0_.1), channel_id=1, source_target_pairs={{0,4},{4,8},{8,12},{12,0},{1,5},{5,9},{9,13},{13,1},{2,6},{6,10},{... | collective-permute-start | bytes 516104 | tf_op jit(solution)/shard_map/ppermute | solution.py:252
  3.0 1.5 %collective-permute-start = (bf16[96,896]{1,0:T(8,128)(2,1)}, bf16[96,896]{1,0:T(8,128)(2,1)S(1)}, u32[]{:S(2)}, u32[]{:S(2)}) collective-permute-start(bf16[96,896]{1,0:T(8,128)(2,1)} %refs_0_.1), channel_id=1, source_target_pairs={{0,2},{1,3},{2,0},{3,1},{4,6},{5,7},{6,4},{7,5},{8,10},{9,11},{10,... | collective-permute-start | bytes 516104 | tf_op jit(solution)/shard_map/ppermute | solution.py:245
  4.5 4.3 %prepare_kernel.1 = (f32[4,96,128]{2,1,0:T(8,128)S(1)}, bf16[608,3584]{1,0:T(8,128)(2,1)S(1)}, bf16[608,3584]{1,0:T(8,128)(2,1)S(1)}) custom-call(s32[2,96]{1,0:T(2,128)} %bitcast.8, s32[2,96]{1,0:T(2,128)} %bitcast.9, bf16[608,3584]{1,0:T(8,128)(2,1)} %bitcast.6, bf16[608,3584]{1,0:T(8,128)(2,1)} %bitcast.7), custom_call_target="tpu_custom_call" | custom-call | flops 4600000000 | tf_op jit(solution)/shard_map/prepare_kernel/pallas_call | solution.py:72
  8.9 0.8 %collective-permute-done.1.refs_0_ = bf16[96,896]{1,0:T(8,128)(2,1)S(1)} collective-permute-done((bf16[96,896]{1,0:T(8,128)(2,1)}, bf16[96,896]{1,0:T(8,128)(2,1)S(1)}, u32[]{:S(2)}, u32[]{:S(2)}) %collective-permute-start.1) | collective-permute-done | bytes 172064 | tf_op jit(solution)/shard_map/ppermute | solution.py:252
  9.7 1.6 %collective-permute-start.9 = (bf16[96,896]{1,0:T(8,128)(2,1)S(1)}, bf16[96,896]{1,0:T(8,128)(2,1)S(1)}, u32[]{:S(2)}, u32[]{:S(2)}) collective-permute-start(bf16[96,896]{1,0:T(8,128)(2,1)S(1)} %shard_map.55.refs_2_.refs_0_), channel_id=1, source_target_pairs={{0,2},{1,3},{2,0},{3,1},{4,6},{5,7},{6,4},{7,5},{8,10},{9,11},{10,... | collective-permute-start | bytes 516104 | tf_op jit(solution)/shard_map/ppermute | solution.py:245
  11.3 1.0 %collective-permute-start.5 = (bf16[96,896]{1,0:T(8,128)(2,1)S(1)}, bf16[96,896]{1,0:T(8,128)(2,1)S(1)}, u32[]{:S(2)}, u32[]{:S(2)}) collective-permute-start(bf16[96,896]{1,0:T(8,128)(2,1)S(1)} %shard_map.55.refs_2_.refs_0_), channel_id=1, source_target_pairs={{0,4},{4,8},{8,12},{12,0},{1,5},{5,9},{9,13},{13,1},{2,6},{6,10},{... | collective-permute-start | bytes 516104 | tf_op jit(solution)/shard_map/ppermute | solution.py:252
  12.3 4.2 %collective-permute-done.9.refs_1_ = bf16[96,896]{1,0:T(8,128)(2,1)S(1)} collective-permute-done((bf16[96,896]{1,0:T(8,128)(2,1)S(1)}, bf16[96,896]{1,0:T(8,128)(2,1)S(1)}, u32[]{:S(2)}, u32[]{:S(2)}) %collective-permute-start.9) | collective-permute-done | bytes 172064 | tf_op jit(solution)/shard_map/ppermute | solution.py:245
  16.5 2.6 %expert_kernel.4 = (f32[96,1792]{1,0:T(8,128)S(1)}, bf16[96,1792]{1,0:T(8,128)(2,1)S(1)}) custom-call(bf16[96,1792]{1,0:T(8,128)(2,1)S(1)} %pack_kernel.1.refs_0_, bf16[96,1792]{1,0:T(8,128)(2,1)S(1)} %collective-permute-done.2.refs_1_, bf16[608,3584]{1,0:T(8,128)(2,1)S(1)} %get-tuple-element.25.refs_2_.refs_4_, ...), custom_call_target="tpu_custom_call" | custom-call | flops 9200000000 | tf_op jit(solution)/shard_map/expert_kernel/pallas_call | solution.py:72
  19.6 1.2 %collective-permute-start.6 = (bf16[96,896]{1,0:T(8,128)(2,1)S(1)}, bf16[96,896]{1,0:T(8,128)(2,1)S(1)}, u32[]{:S(2)}, u32[]{:S(2)}) collective-permute-start(bf16[96,896]{1,0:T(8,128)(2,1)S(1)} %shard_map.56.refs_6_.refs_0_), channel_id=1, source_target_pairs={{0,2},{1,3},{2,0},{3,1},{4,6},{5,7},{6,4},{7,5},{8,10},{9,11},{10,... | collective-permute-start | bytes 516104 | tf_op jit(solution)/shard_map/ppermute | solution.py:245
  20.8 1.7 %collective-permute-start.4 = (bf16[96,1792]{1,0:T(8,128)(2,1)S(1)}, bf16[96,1792]{1,0:T(8,128)(2,1)S(1)}, u32[]{:S(2)}, u32[]{:S(2)}) collective-permute-start(bf16[96,1792]{1,0:T(8,128)(2,1)S(1)} %pack_kernel.1.refs_0_), channel_id=1, source_target_pairs={{0,12},{4,0},{8,4},{12,8},{1,13},{5,1},{9,5},{13,9},{2,14},{6,2},{... | collective-permute-start | bytes 1032200 | tf_op jit(solution)/shard_map/ppermute | solution.py:252
  22.5 2.6 %expert_kernel.5 = (f32[96,1792]{1,0:T(8,128)S(1)}, bf16[96,1792]{1,0:T(8,128)(2,1)S(1)}) custom-call(bf16[96,896]{1,0:T(8,128)(2,1)S(1)} %shard_map.55.refs_2_.refs_0_, bf16[96,896]{1,0:T(8,128)(2,1)S(1)} %collective-permute-done.9.refs_1_, bf16[96,896]{1,0:T(8,128)(2,1)S(1)} %collective-permute-done.10.refs_2_, ...), custom_call_target="tpu_custom_call" | custom-call | flops 57500000 | tf_op jit(solution)/shard_map/expert_kernel/pallas_call | solution.py:72
  26.1 1.0 %collective-permute-done.7.refs_2_ = bf16[96,896]{1,0:T(8,128)(2,1)S(1)} collective-permute-done((bf16[96,896]{1,0:T(8,128)(2,1)S(1)}, bf16[96,896]{1,0:T(8,128)(2,1)S(1)}, u32[]{:S(2)}, u32[]{:S(2)}) %collective-permute-start.7) | collective-permute-done | bytes 172064 | tf_op jit(solution)/shard_map/ppermute | solution.py:245
  27.5 2.6 %expert_kernel.6 = (f32[96,1792]{1,0:T(8,128)S(1)}, bf16[96,1792]{1,0:T(8,128)(2,1)S(1)}) custom-call(bf16[96,896]{1,0:T(8,128)(2,1)S(1)} %shard_map.56.refs_6_.refs_0_, bf16[96,896]{1,0:T(8,128)(2,1)S(1)} %collective-permute-done.6.refs_1_, bf16[96,896]{1,0:T(8,128)(2,1)S(1)} %collective-permute-done.7.refs_2_, ...), custom_call_target="tpu_custom_call" | custom-call | flops 57500000 | tf_op jit(solution)/shard_map/expert_kernel/pallas_call | solution.py:72
  31.1 1.4 %collective-permute-start.16 = (bf16[96,896]{1,0:T(8,128)(2,1)S(1)}, bf16[96,896]{1,0:T(8,128)(2,1)S(1)}, u32[]{:S(2)}, u32[]{:S(2)}) collective-permute-start(bf16[96,896]{1,0:T(8,128)(2,1)S(1)} %get-tuple-element.37), channel_id=1, source_target_pairs={{0,2},{1,3},{2,0},{3,1},{4,6},{5,7},{6,4},{7,5},{8,10},{9,11},{10,... | collective-permute-start | bytes 516104 | tf_op jit(solution)/shard_map/ppermute | solution.py:245
  32.8 2.6 %expert_kernel.7 = (f32[96,1792]{1,0:T(8,128)S(1)}, bf16[96,1792]{1,0:T(8,128)(2,1)S(1)}) custom-call(bf16[96,1792]{1,0:T(8,128)(2,1)S(1)} %shard_map.57.refs_0_, bf16[96,1792]{1,0:T(8,128)(2,1)S(1)} %collective-permute-done.12.refs_1_, bf16[608,3584]{1,0:T(8,128)(2,1)S(1)} %get-tuple-element.25.refs_2_.refs_4_, ...), custom_call_target="tpu_custom_call" | custom-call | flops 4600000000 | tf_op jit(solution)/shard_map/expert_kernel/pallas_call | solution.py:72
  35.6 1.5 %collective-permute-start.18 = (bf16[96,896]{1,0:T(8,128)(2,1)S(1)}, bf16[96,896]{1,0:T(8,128)(2,1)S(1)}, u32[]{:S(2)}, u32[]{:S(2)}) collective-permute-start(bf16[96,896]{1,0:T(8,128)(2,1)S(1)} %get-tuple-element.40), channel_id=1, source_target_pairs={{0,2},{1,3},{2,0},{3,1},{4,6},{5,7},{6,4},{7,5},{8,10},{9,11},{10,... | collective-permute-start | bytes 516104 | tf_op jit(solution)/shard_map/ppermute | solution.py:245
  37.1 0.8 %collective-permute-done.16.refs_1_ = bf16[96,896]{1,0:T(8,128)(2,1)S(1)} collective-permute-done((bf16[96,896]{1,0:T(8,128)(2,1)S(1)}, bf16[96,896]{1,0:T(8,128)(2,1)S(1)}, u32[]{:S(2)}, u32[]{:S(2)}) %collective-permute-start.16) | collective-permute-done | bytes 172064 | tf_op jit(solution)/shard_map/ppermute | solution.py:245
  37.9 3.6 %collective-permute-start.20 = (bf16[96,896]{1,0:T(8,128)(2,1)S(1)}, bf16[96,896]{1,0:T(8,128)(2,1)S(1)}, u32[]{:S(2)}, u32[]{:S(2)}) collective-permute-start(bf16[96,896]{1,0:T(8,128)(2,1)S(1)} %chip_sum_kernel.3.refs_2_), channel_id=1, source_target_pairs={{0,12},{4,0},{8,4},{12,8},{1,13},{5,1},{9,5},{13,9},{2,14},{6,2},{... | collective-permute-start | bytes 516104 | tf_op jit(solution)/shard_map/ppermute | solution.py:252
  41.6 0.6 %collective-permute-start.17 = (bf16[96,896]{1,0:T(8,128)(2,1)S(1)}, bf16[96,896]{1,0:T(8,128)(2,1)S(1)}, u32[]{:S(2)}, u32[]{:S(2)}) collective-permute-start(bf16[96,896]{1,0:T(8,128)(2,1)S(1)} %get-tuple-element.39), channel_id=1, source_target_pairs={{0,2},{1,3},{2,0},{3,1},{4,6},{5,7},{6,4},{7,5},{8,10},{9,11},{10,... | collective-permute-start | bytes 516104 | tf_op jit(solution)/shard_map/ppermute | solution.py:245
  42.3 2.7 %collective-permute-start.21 = (bf16[96,896]{1,0:T(8,128)(2,1)S(1)}, bf16[96,896]{1,0:T(8,128)(2,1)S(1)}, u32[]{:S(2)}, u32[]{:S(2)}) collective-permute-start(bf16[96,896]{1,0:T(8,128)(2,1)S(1)} %chip_sum_kernel.4.refs_2_), channel_id=1, source_target_pairs={{0,8},{4,12},{8,0},{12,4},{1,9},{5,13},{9,1},{13,5},{2,10},{6,14},... | collective-permute-start | bytes 516104 | tf_op jit(solution)/shard_map/ppermute | solution.py:252
  45.0 2.5 %collective-permute-done.17.refs_1_ = bf16[96,896]{1,0:T(8,128)(2,1)S(1)} collective-permute-done((bf16[96,896]{1,0:T(8,128)(2,1)S(1)}, bf16[96,896]{1,0:T(8,128)(2,1)S(1)}, u32[]{:S(2)}, u32[]{:S(2)}) %collective-permute-start.17) | collective-permute-done | bytes 172064 | tf_op jit(solution)/shard_map/ppermute | solution.py:245
  47.5 0.6 %collective-permute-start.19 = (bf16[96,896]{1,0:T(8,128)(2,1)S(1)}, bf16[96,896]{1,0:T(8,128)(2,1)S(1)}, u32[]{:S(2)}, u32[]{:S(2)}) collective-permute-start(bf16[96,896]{1,0:T(8,128)(2,1)S(1)} %get-tuple-element.42), channel_id=1, source_target_pairs={{0,2},{1,3},{2,0},{3,1},{4,6},{5,7},{6,4},{7,5},{8,10},{9,11},{10,... | collective-permute-start | bytes 516104 | tf_op jit(solution)/shard_map/ppermute | solution.py:245
  48.7 7.8 %collective-permute-done.21.refs_4_ = bf16[96,896]{1,0:T(8,128)(2,1)S(1)} collective-permute-done((bf16[96,896]{1,0:T(8,128)(2,1)S(1)}, bf16[96,896]{1,0:T(8,128)(2,1)S(1)}, u32[]{:S(2)}, u32[]{:S(2)}) %collective-permute-start.21) | collective-permute-done | bytes 172064 | tf_op jit(solution)/shard_map/ppermute | solution.py:252
  56.6 0.7 %finish_kernel.1 = bf16[96,896]{1,0:T(8,128)(2,1)} custom-call(f32[4,96,128]{2,1,0:T(8,128)S(1)} %get-tuple-element.24.refs_1_.refs_0_, f32[96,896]{1,0:T(8,128)S(1)} %weigh_kernel.1.refs_1_, bf16[96,896]{1,0:T(8,128)(2,1)S(1)} %collective-permute-done.22.refs_2_), custom_call_target="tpu_custom_call" | custom-call | flops 575000000 | tf_op jit(solution)/shard_map/finish_kernel/pallas_call | solution.py:72
  (42 shorter events, 4.2 us)
Async XLA Ops:
  0.0 9.6 %collective-permute-start.1 = (bf16[96,896]{1,0:T(8,128)(2,1)}, bf16[96,896]{1,0:T(8,128)(2,1)S(1)}, u32[]{:S(2)}, u32[]{:S(2)}) collective-permute-start(bf16[96,896]{1,0:T(8,128)(2,1)} %refs_0_.1), channel_id=1, source_target_pairs={{0,4},{4,8},{8,12},{12,0},{1,5},{5,9},{9,13},{13,1},{2,6},{6,10},{... | collective-permute-start | bytes 516104 | tf_op jit(solution)/shard_map/ppermute | solution.py:252
  3.0 6.6 %collective-permute-start = (bf16[96,896]{1,0:T(8,128)(2,1)}, bf16[96,896]{1,0:T(8,128)(2,1)S(1)}, u32[]{:S(2)}, u32[]{:S(2)}) collective-permute-start(bf16[96,896]{1,0:T(8,128)(2,1)} %refs_0_.1), channel_id=1, source_target_pairs={{0,2},{1,3},{2,0},{3,1},{4,6},{5,7},{6,4},{7,5},{8,10},{9,11},{10,... | collective-permute-start | bytes 516104 | tf_op jit(solution)/shard_map/ppermute | solution.py:245
  4.5 5.1 %copy-start = (bf16[96,896]{1,0:T(8,128)(2,1)S(1)}, bf16[96,896]{1,0:T(8,128)(2,1)}, u32[]{:S(2)}) copy-start(bf16[96,896]{1,0:T(8,128)(2,1)} %refs_0_.1) | copy-start | bytes 516100
  9.7 6.9 %collective-permute-start.2 = (bf16[96,1792]{1,0:T(8,128)(2,1)S(1)}, bf16[96,1792]{1,0:T(8,128)(2,1)S(1)}, u32[]{:S(2)}, u32[]{:S(2)}) collective-permute-start(bf16[96,1792]{1,0:T(8,128)(2,1)S(1)} %pack_kernel.1.refs_0_), channel_id=1, source_target_pairs={{0,1},{1,0},{2,3},{3,2},{4,5},{5,4},{6,7},{7,6},{8,9},{9,8},{10,11... | collective-permute-start | bytes 1032200 | tf_op jit(solution)/shard_map/ppermute | solution.py:245
  9.7 6.8 %collective-permute-start.9 = (bf16[96,896]{1,0:T(8,128)(2,1)S(1)}, bf16[96,896]{1,0:T(8,128)(2,1)S(1)}, u32[]{:S(2)}, u32[]{:S(2)}) collective-permute-start(bf16[96,896]{1,0:T(8,128)(2,1)S(1)} %shard_map.55.refs_2_.refs_0_), channel_id=1, source_target_pairs={{0,2},{1,3},{2,0},{3,1},{4,6},{5,7},{6,4},{7,5},{8,10},{9,11},{10,... | collective-permute-start | bytes 516104 | tf_op jit(solution)/shard_map/ppermute | solution.py:245
  11.3 8.2 %collective-permute-start.5 = (bf16[96,896]{1,0:T(8,128)(2,1)S(1)}, bf16[96,896]{1,0:T(8,128)(2,1)S(1)}, u32[]{:S(2)}, u32[]{:S(2)}) collective-permute-start(bf16[96,896]{1,0:T(8,128)(2,1)S(1)} %shard_map.55.refs_2_.refs_0_), channel_id=1, source_target_pairs={{0,4},{4,8},{8,12},{12,0},{1,5},{5,9},{9,13},{13,1},{2,6},{6,10},{... | collective-permute-start | bytes 516104 | tf_op jit(solution)/shard_map/ppermute | solution.py:252
  12.3 10.2 %collective-permute-start.10 = (bf16[96,896]{1,0:T(8,128)(2,1)S(1)}, bf16[96,896]{1,0:T(8,128)(2,1)S(1)}, u32[]{:S(2)}, u32[]{:S(2)}) collective-permute-start(bf16[96,896]{1,0:T(8,128)(2,1)S(1)} %shard_map.55.refs_2_.refs_0_), channel_id=1, source_target_pairs={{0,1},{1,0},{2,3},{3,2},{4,5},{5,4},{6,7},{7,6},{8,9},{9,8},{10,11... | collective-permute-start | bytes 516104 | tf_op jit(solution)/shard_map/ppermute | solution.py:245
  16.5 6.0 %collective-permute-start.11 = (bf16[96,896]{1,0:T(8,128)(2,1)S(1)}, bf16[96,896]{1,0:T(8,128)(2,1)S(1)}, u32[]{:S(2)}, u32[]{:S(2)}) collective-permute-start(bf16[96,896]{1,0:T(8,128)(2,1)S(1)} %collective-permute-done.9.refs_1_), channel_id=1, source_target_pairs={{0,1},{1,0},{2,3},{3,2},{4,5},{5,4},{6,7},{7,6},{8,9},{9,8},{10,11... | collective-permute-start | bytes 516104 | tf_op jit(solution)/shard_map/ppermute | solution.py:245
  19.6 6.5 %collective-permute-start.6 = (bf16[96,896]{1,0:T(8,128)(2,1)S(1)}, bf16[96,896]{1,0:T(8,128)(2,1)S(1)}, u32[]{:S(2)}, u32[]{:S(2)}) collective-permute-start(bf16[96,896]{1,0:T(8,128)(2,1)S(1)} %shard_map.56.refs_6_.refs_0_), channel_id=1, source_target_pairs={{0,2},{1,3},{2,0},{3,1},{4,6},{5,7},{6,4},{7,5},{8,10},{9,11},{10,... | collective-permute-start | bytes 516104 | tf_op jit(solution)/shard_map/ppermute | solution.py:245
  20.8 10.2 %collective-permute-start.4 = (bf16[96,1792]{1,0:T(8,128)(2,1)S(1)}, bf16[96,1792]{1,0:T(8,128)(2,1)S(1)}, u32[]{:S(2)}, u32[]{:S(2)}) collective-permute-start(bf16[96,1792]{1,0:T(8,128)(2,1)S(1)} %pack_kernel.1.refs_0_), channel_id=1, source_target_pairs={{0,12},{4,0},{8,4},{12,8},{1,13},{5,1},{9,5},{13,9},{2,14},{6,2},{... | collective-permute-start | bytes 1032200 | tf_op jit(solution)/shard_map/ppermute | solution.py:252
  25.1 5.8 %collective-permute-start.14 = (bf16[96,1792]{1,0:T(8,128)(2,1)S(1)}, bf16[96,1792]{1,0:T(8,128)(2,1)S(1)}, u32[]{:S(2)}, u32[]{:S(2)}) collective-permute-start(bf16[96,1792]{1,0:T(8,128)(2,1)S(1)} %get-tuple-element.32), channel_id=1, source_target_pairs={{0,1},{1,0},{2,3},{3,2},{4,5},{5,4},{6,7},{7,6},{8,9},{9,8},{10,11... | collective-permute-start | bytes 1032200 | tf_op jit(solution)/shard_map/ppermute | solution.py:245
  25.2 1.9 %collective-permute-start.7 = (bf16[96,896]{1,0:T(8,128)(2,1)S(1)}, bf16[96,896]{1,0:T(8,128)(2,1)S(1)}, u32[]{:S(2)}, u32[]{:S(2)}) collective-permute-start(bf16[96,896]{1,0:T(8,128)(2,1)S(1)} %shard_map.56.refs_6_.refs_0_), channel_id=1, source_target_pairs={{0,1},{1,0},{2,3},{3,2},{4,5},{5,4},{6,7},{7,6},{8,9},{9,8},{10,11... | collective-permute-start | bytes 516104 | tf_op jit(solution)/shard_map/ppermute | solution.py:245
  26.0 1.4 %collective-permute-start.8 = (bf16[96,896]{1,0:T(8,128)(2,1)S(1)}, bf16[96,896]{1,0:T(8,128)(2,1)S(1)}, u32[]{:S(2)}, u32[]{:S(2)}) collective-permute-start(bf16[96,896]{1,0:T(8,128)(2,1)S(1)} %collective-permute-done.6.refs_1_), channel_id=1, source_target_pairs={{0,1},{1,0},{2,3},{3,2},{4,5},{5,4},{6,7},{7,6},{8,9},{9,8},{10,11... | collective-permute-start | bytes 516104 | tf_op jit(solution)/shard_map/ppermute | solution.py:245
  30.1 2.4 %collective-permute-start.13 = (bf16[96,1792]{1,0:T(8,128)(2,1)S(1)}, bf16[96,1792]{1,0:T(8,128)(2,1)S(1)}, u32[]{:S(2)}, u32[]{:S(2)}) collective-permute-start(bf16[96,1792]{1,0:T(8,128)(2,1)S(1)} %get-tuple-element.31), channel_id=1, source_target_pairs={{0,1},{1,0},{2,3},{3,2},{4,5},{5,4},{6,7},{7,6},{8,9},{9,8},{10,11... | collective-permute-start | bytes 1032200 | tf_op jit(solution)/shard_map/ppermute | solution.py:245
  30.3 17.2 %collective-permute-start.3 = (bf16[96,1792]{1,0:T(8,128)(2,1)S(1)}, bf16[96,1792]{1,0:T(8,128)(2,1)S(1)}, u32[]{:S(2)}, u32[]{:S(2)}) collective-permute-start(bf16[96,1792]{1,0:T(8,128)(2,1)S(1)} %get-tuple-element.28), channel_id=1, source_target_pairs={{0,1},{1,0},{2,3},{3,2},{4,5},{5,4},{6,7},{7,6},{8,9},{9,8},{10,11... | collective-permute-start | bytes 1032200 | tf_op jit(solution)/shard_map/ppermute | solution.py:245
  31.0 1.8 %collective-permute-start.12 = (bf16[96,1792]{1,0:T(8,128)(2,1)S(1)}, bf16[96,1792]{1,0:T(8,128)(2,1)S(1)}, u32[]{:S(2)}, u32[]{:S(2)}) collective-permute-start(bf16[96,1792]{1,0:T(8,128)(2,1)S(1)} %shard_map.57.refs_0_), channel_id=1, source_target_pairs={{0,1},{1,0},{2,3},{3,2},{4,5},{5,4},{6,7},{7,6},{8,9},{9,8},{10,11... | collective-permute-start | bytes 1032200 | tf_op jit(solution)/shard_map/ppermute | solution.py:245
  31.1 6.9 %collective-permute-start.16 = (bf16[96,896]{1,0:T(8,128)(2,1)S(1)}, bf16[96,896]{1,0:T(8,128)(2,1)S(1)}, u32[]{:S(2)}, u32[]{:S(2)}) collective-permute-start(bf16[96,896]{1,0:T(8,128)(2,1)S(1)} %get-tuple-element.37), channel_id=1, source_target_pairs={{0,2},{1,3},{2,0},{3,1},{4,6},{5,7},{6,4},{7,5},{8,10},{9,11},{10,... | collective-permute-start | bytes 516104 | tf_op jit(solution)/shard_map/ppermute | solution.py:245
  35.4 6.1 %collective-permute-start.15 = (bf16[96,1792]{1,0:T(8,128)(2,1)S(1)}, bf16[96,1792]{1,0:T(8,128)(2,1)S(1)}, u32[]{:S(2)}, u32[]{:S(2)}) collective-permute-start(bf16[96,1792]{1,0:T(8,128)(2,1)S(1)} %get-tuple-element.36), channel_id=1, source_target_pairs={{0,1},{1,0},{2,3},{3,2},{4,5},{5,4},{6,7},{7,6},{8,9},{9,8},{10,11... | collective-permute-start | bytes 1032200 | tf_op jit(solution)/shard_map/ppermute | solution.py:245
  35.6 6.6 %collective-permute-start.18 = (bf16[96,896]{1,0:T(8,128)(2,1)S(1)}, bf16[96,896]{1,0:T(8,128)(2,1)S(1)}, u32[]{:S(2)}, u32[]{:S(2)}) collective-permute-start(bf16[96,896]{1,0:T(8,128)(2,1)S(1)} %get-tuple-element.40), channel_id=1, source_target_pairs={{0,2},{1,3},{2,0},{3,1},{4,6},{5,7},{6,4},{7,5},{8,10},{9,11},{10,... | collective-permute-start | bytes 516104 | tf_op jit(solution)/shard_map/ppermute | solution.py:245
  37.9 10.7 %collective-permute-start.20 = (bf16[96,896]{1,0:T(8,128)(2,1)S(1)}, bf16[96,896]{1,0:T(8,128)(2,1)S(1)}, u32[]{:S(2)}, u32[]{:S(2)}) collective-permute-start(bf16[96,896]{1,0:T(8,128)(2,1)S(1)} %chip_sum_kernel.3.refs_2_), channel_id=1, source_target_pairs={{0,12},{4,0},{8,4},{12,8},{1,13},{5,1},{9,5},{13,9},{2,14},{6,2},{... | collective-permute-start | bytes 516104 | tf_op jit(solution)/shard_map/ppermute | solution.py:252
  41.6 5.8 %collective-permute-start.17 = (bf16[96,896]{1,0:T(8,128)(2,1)S(1)}, bf16[96,896]{1,0:T(8,128)(2,1)S(1)}, u32[]{:S(2)}, u32[]{:S(2)}) collective-permute-start(bf16[96,896]{1,0:T(8,128)(2,1)S(1)} %get-tuple-element.39), channel_id=1, source_target_pairs={{0,2},{1,3},{2,0},{3,1},{4,6},{5,7},{6,4},{7,5},{8,10},{9,11},{10,... | collective-permute-start | bytes 516104 | tf_op jit(solution)/shard_map/ppermute | solution.py:245
  42.3 14.2 %collective-permute-start.21 = (bf16[96,896]{1,0:T(8,128)(2,1)S(1)}, bf16[96,896]{1,0:T(8,128)(2,1)S(1)}, u32[]{:S(2)}, u32[]{:S(2)}) collective-permute-start(bf16[96,896]{1,0:T(8,128)(2,1)S(1)} %chip_sum_kernel.4.refs_2_), channel_id=1, source_target_pairs={{0,8},{4,12},{8,0},{12,4},{1,9},{5,13},{9,1},{13,5},{2,10},{6,14},... | collective-permute-start | bytes 516104 | tf_op jit(solution)/shard_map/ppermute | solution.py:252
  47.5 8.9 %collective-permute-start.19 = (bf16[96,896]{1,0:T(8,128)(2,1)S(1)}, bf16[96,896]{1,0:T(8,128)(2,1)S(1)}, u32[]{:S(2)}, u32[]{:S(2)}) collective-permute-start(bf16[96,896]{1,0:T(8,128)(2,1)S(1)} %get-tuple-element.42), channel_id=1, source_target_pairs={{0,2},{1,3},{2,0},{3,1},{4,6},{5,7},{6,4},{7,5},{8,10},{9,11},{10,... | collective-permute-start | bytes 516104 | tf_op jit(solution)/shard_map/ppermute | solution.py:245
  48.1 8.5 %collective-permute-start.22 = (bf16[96,896]{1,0:T(8,128)(2,1)S(1)}, bf16[96,896]{1,0:T(8,128)(2,1)S(1)}, u32[]{:S(2)}, u32[]{:S(2)}) collective-permute-start(bf16[96,896]{1,0:T(8,128)(2,1)S(1)} %chip_sum_kernel.5.refs_2_), channel_id=1, source_target_pairs={{0,4},{4,8},{8,12},{12,0},{1,5},{5,9},{9,13},{13,1},{2,6},{6,10},{... | collective-permute-start | bytes 516104 | tf_op jit(solution)/shard_map/ppermute | solution.py:252

commit v15 on v14

--- a/solution.py
+++ b/solution.py
@@ -208,36 +208,26 @@
     )
 
 
-def weigh_kernel(steps, columns, own, got, *rest):
-    parts, out = rest[:-1], rest[-1]
+def weigh_kernel(steps, counts, columns, *refs):
+    refs, out = list(refs[:-1]), refs[-1]
     for at in range(0, out.shape[1], 128):
         here = slice(at, at + 128)
-        total = own[:, here]
-        if got is not None:
-            total = columns[0] * (total + got[:, here].astype(jnp.float32))
-        for step, part in zip(steps, parts):
-            total = total + columns[step] * part[:, here].astype(jnp.float32)
+        left = list(refs)
+        total = left.pop(0)[:, here] if len(left) > sum(counts) else None
+        for step, count in zip(steps, counts):
+            rows = sum(left.pop(0)[:, here].astype(jnp.float32) for _ in range(count))
+            rows = columns[step] * rows
+            total = rows if total is None else total + rows
         out[:, here] = total.astype(out.dtype)
 
 
-def weigh(columns, own, got, steps, parts):
-    return local_call(
-        functools.partial(weigh_kernel, steps),
-        jax.ShapeDtypeStruct(own.shape, jnp.float32),
-        (columns, own, got, *parts),
-        cost=4,
-    )
-
-
-def finish_kernel(steps, columns, total, *rest):
-    weigh_kernel(steps, columns, total, None, *rest)
-
-
-def finish(columns, total, steps, parts):
-    return local_call(
-        functools.partial(finish_kernel, steps),
-        jax.ShapeDtypeStruct(total.shape, jnp.bfloat16),
-        (columns, total, *parts),
+def weigh(columns, totals, steps, terms, dtype, cost):
+    arrays = [*totals, *[array for term in terms for array in term]]
+    return local_call(
+        functools.partial(weigh_kernel, steps, [len(term) for term in terms]),
+        jax.ShapeDtypeStruct(arrays[-1].shape, dtype),
+        (columns, *arrays),
+        cost=cost,
     )
 
 
@@ -288,6 +278,7 @@
     chips[3,] = shift(chips[0,], -1)
     run((0,), [], 8)
     arrive(2, blocks[1], 1, [kept[0,][0]])
+    others[1] = after(others[1], kept[0,][0])
     run((1,), [blocks[2]], .05)
     run((2,), [kept[1,][0]], .05)
     chips[3,] = after(chips[3,], kept[2,][0])
@@ -295,12 +286,13 @@
     leave((2,), [sums[1][0]], 2)
     run((3,), [sums[2][0]], 4)
     give(1, [kept[3,][0]], 4)
-    leave((3,), [added[1]], 2)
+    leave((3,), [added[1]], .05)
     give(2, [sums[3][0]], 4)
     give(3, [added[2]], 4)
     leave((0,), [added[3]], 2)
-    total = weigh(columns, *sums[0][:2], (1, 2), [parts[1], parts[2]])
-    return finish(columns, total, (3,), [parts[3]])
+    total = weigh(columns, [], (1, 2), [[parts[1]], [parts[2]]], jnp.float32, 4)
+    total = weigh(columns, [total], (0,), [sums[0][:2]], jnp.float32, 4)
+    return weigh(columns, [total], (3,), [[parts[3]]], jnp.bfloat16, 0.5)
 
 
 def slotted(tokens, expert_ids, weight_codes, up_local, down_local, capacity):

time: 57.5 us -> 55.8 us (0.970)
  starting transfers between devices: 22.4 us -> 16.2 us
  waiting for transfers between devices: 18.8 us -> 23.3 us
    ppermute x6, starting transfers between devices: 12.5 us -> 6.57 us  [shift(): lax.ppermute(array, 'expert', [(i, (i + by) % experts_n) for i in range(e...]
    ppermute x6, waiting for transfers between devices: 9.27 us -> 12.4 us  [shift(): lax.ppermute(array, 'expert', [(i, (i + by) % experts_n) for i in range(e...]
    ppermute x17, waiting for transfers between devices: 9.49 us -> 10.9 us  [swap(): return lax.ppermute(array, 'tensor', [(i, i ^ bit) for i in range(4)])]
    pallas_call x15 -> x16, Pallas kernels: 16.1 us -> 16.1 us  [local_call(): pl.pallas_call(body_of, name=name, out_shape=out_shape, in_specs=list(in_...]
  transfers between devices with their start and end apart: 23 -> 23, of which waited for: 11 -> 10; matrix products, arithmetic and copies ran while one was open for 0% -> 0% of each run, Pallas kernels for 27% -> 28%
where the time goes in v15:
time: 55.8 us; the launch traced here: 55.7 us
  waiting for transfers between devices  23.3 us (42%)
  starting transfers between devices  16.2 us (29%)
  Pallas kernels  16.1 us (29%)
    pallas_call x16, Pallas kernels, local_call(): pl.pallas_call(body_of, name=name, out_shape=out_shape, in_specs=list(in_...  16.1 us
    ppermute x6, waiting for transfers between devices, shift(): lax.ppermute(array, 'expert', [(i, (i + by) % experts_n) for i in range(e...  12.4 us
    ppermute x17, waiting for transfers between devices, swap(): return lax.ppermute(array, 'tensor', [(i, i ^ bit) for i in range(4)])  10.9 us
    ppermute x17, starting transfers between devices, swap(): return lax.ppermute(array, 'tensor', [(i, i ^ bit) for i in range(4)])  9.61 us
    ppermute x6, starting transfers between devices, shift(): lax.ppermute(array, 'expert', [(i, (i + by) % experts_n) for i in range(e...  6.57 us
  transfers between devices with their start and end apart: 23, of which 10 were waited for; matrix products, arithmetic and copies ran while one was open for 0% of the time, Pallas kernels for 28%

profile of v15, /device:TPU:0, one launch (start us, length us, event | category | flops | bytes accessed | tf_op | source)
XLA Modules:
  0.0 55.7 jit_solution(7472348707739348762)
XLA Ops:
  0.0 3.0 %collective-permute-start = (bf16[96,896]{1,0:T(8,128)(2,1)}, bf16[96,896]{1,0:T(8,128)(2,1)S(1)}, u32[]{:S(2)}, u32[]{:S(2)}) collective-permute-start(bf16[96,896]{1,0:T(8,128)(2,1)} %refs_0_.1), channel_id=1, source_target_pairs={{0,4},{4,8},{8,12},{12,0},{1,5},{5,9},{9,13},{13,1},{2,6},{6,10},{... | collective-permute-start | bytes 516104 | tf_op jit(solution)/shard_map/ppermute | solution.py:242
  3.0 1.5 %collective-permute-start.2 = (bf16[96,896]{1,0:T(8,128)(2,1)}, bf16[96,896]{1,0:T(8,128)(2,1)S(1)}, u32[]{:S(2)}, u32[]{:S(2)}) collective-permute-start(bf16[96,896]{1,0:T(8,128)(2,1)} %refs_0_.1), channel_id=1, source_target_pairs={{0,2},{1,3},{2,0},{3,1},{4,6},{5,7},{6,4},{7,5},{8,10},{9,11},{10,... | collective-permute-start | bytes 516104 | tf_op jit(solution)/shard_map/ppermute | solution.py:235
  4.5 4.3 %prepare_kernel.1 = (f32[4,96,128]{2,1,0:T(8,128)S(1)}, bf16[608,3584]{1,0:T(8,128)(2,1)S(1)}, bf16[608,3584]{1,0:T(8,128)(2,1)S(1)}) custom-call(s32[2,96]{1,0:T(2,128)} %bitcast.8, s32[2,96]{1,0:T(2,128)} %bitcast.9, bf16[608,3584]{1,0:T(8,128)(2,1)} %bitcast.6, bf16[608,3584]{1,0:T(8,128)(2,1)} %bitcast.7), custom_call_target="tpu_custom_call" | custom-call | flops 4600000000 | tf_op jit(solution)/shard_map/prepare_kernel/pallas_call | solution.py:72
  8.9 0.8 %collective-permute-done.refs_0_ = bf16[96,896]{1,0:T(8,128)(2,1)S(1)} collective-permute-done((bf16[96,896]{1,0:T(8,128)(2,1)}, bf16[96,896]{1,0:T(8,128)(2,1)S(1)}, u32[]{:S(2)}, u32[]{:S(2)}) %collective-permute-start) | collective-permute-done | bytes 172064 | tf_op jit(solution)/shard_map/ppermute | solution.py:242
  9.7 1.6 %collective-permute-start.1 = (bf16[96,896]{1,0:T(8,128)(2,1)S(1)}, bf16[96,896]{1,0:T(8,128)(2,1)S(1)}, u32[]{:S(2)}, u32[]{:S(2)}) collective-permute-start(bf16[96,896]{1,0:T(8,128)(2,1)S(1)} %shard_map.55.refs_2_.refs_0_), channel_id=1, source_target_pairs={{0,2},{1,3},{2,0},{3,1},{4,6},{5,7},{6,4},{7,5},{8,10},{9,11},{10,... | collective-permute-start | bytes 516104 | tf_op jit(solution)/shard_map/ppermute | solution.py:235
  11.5 1.0 %collective-permute-start.6 = (bf16[96,896]{1,0:T(8,128)(2,1)S(1)}, bf16[96,896]{1,0:T(8,128)(2,1)S(1)}, u32[]{:S(2)}, u32[]{:S(2)}) collective-permute-start(bf16[96,896]{1,0:T(8,128)(2,1)S(1)} %shard_map.55.refs_2_.refs_0_), channel_id=1, source_target_pairs={{0,4},{4,8},{8,12},{12,0},{1,5},{5,9},{9,13},{13,1},{2,6},{6,10},{... | collective-permute-start | bytes 516104 | tf_op jit(solution)/shard_map/ppermute | solution.py:242
  12.5 2.6 %expert_kernel.4 = (f32[96,1792]{1,0:T(8,128)S(1)}, bf16[96,1792]{1,0:T(8,128)(2,1)S(1)}) custom-call(bf16[96,1792]{1,0:T(8,128)(2,1)S(1)} %pack_kernel.1.refs_0_, bf16[96,1792]{1,0:T(8,128)(2,1)S(1)} %collective-permute-done.3.refs_1_, bf16[608,3584]{1,0:T(8,128)(2,1)S(1)} %get-tuple-element.25.refs_2_.refs_4_, ...), custom_call_target="tpu_custom_call" | custom-call | flops 9200000000 | tf_op jit(solution)/shard_map/expert_kernel/pallas_call | solution.py:72
  15.1 1.4 %collective-permute-done.1.refs_0_ = bf16[96,896]{1,0:T(8,128)(2,1)S(1)} collective-permute-done((bf16[96,896]{1,0:T(8,128)(2,1)S(1)}, bf16[96,896]{1,0:T(8,128)(2,1)S(1)}, u32[]{:S(2)}, u32[]{:S(2)}) %collective-permute-start.1) | collective-permute-done | bytes 172064 | tf_op jit(solution)/shard_map/ppermute | solution.py:235
  16.5 3.3 %collective-permute-done.6.refs_0_ = bf16[96,896]{1,0:T(8,128)(2,1)S(1)} collective-permute-done((bf16[96,896]{1,0:T(8,128)(2,1)S(1)}, bf16[96,896]{1,0:T(8,128)(2,1)S(1)}, u32[]{:S(2)}, u32[]{:S(2)}) %collective-permute-start.6) | collective-permute-done | bytes 172064 | tf_op jit(solution)/shard_map/ppermute | solution.py:242
  20.4 2.6 %expert_kernel.5 = (f32[96,1792]{1,0:T(8,128)S(1)}, bf16[96,1792]{1,0:T(8,128)(2,1)S(1)}) custom-call(bf16[96,896]{1,0:T(8,128)(2,1)S(1)} %shard_map.55.refs_2_.refs_0_, bf16[96,896]{1,0:T(8,128)(2,1)S(1)} %shard_map.56.refs_1_, bf16[96,896]{1,0:T(8,128)(2,1)S(1)} %collective-permute-done.4.refs_2_, bf16[96,896]{1,0:T(8,128)(2,1)S(1)} %collective-permute-done.5.refs_3_, ...), custom_call_target="tpu_custom_call" | custom-call | flops 57500000 | tf_op jit(solution)/shard_map/expert_kernel/pallas_call | solution.py:72
  23.6 2.1 %collective-permute-done.8.refs_1_ = bf16[96,896]{1,0:T(8,128)(2,1)S(1)} collective-permute-done((bf16[96,896]{1,0:T(8,128)(2,1)S(1)}, bf16[96,896]{1,0:T(8,128)(2,1)S(1)}, u32[]{:S(2)}, u32[]{:S(2)}) %collective-permute-start.8) | collective-permute-done | bytes 172064 | tf_op jit(solution)/shard_map/ppermute | solution.py:235
  25.7 1.4 %collective-permute-done.10.refs_3_ = bf16[96,896]{1,0:T(8,128)(2,1)S(1)} collective-permute-done((bf16[96,896]{1,0:T(8,128)(2,1)S(1)}, bf16[96,896]{1,0:T(8,128)(2,1)S(1)}, u32[]{:S(2)}, u32[]{:S(2)}) %collective-permute-start.10) | collective-permute-done | bytes 172064 | tf_op jit(solution)/shard_map/ppermute | solution.py:235
  27.1 2.6 %expert_kernel.6 = (f32[96,1792]{1,0:T(8,128)S(1)}, bf16[96,1792]{1,0:T(8,128)(2,1)S(1)}) custom-call(bf16[96,896]{1,0:T(8,128)(2,1)S(1)} %shard_map.57.refs_6_.refs_0_, bf16[96,896]{1,0:T(8,128)(2,1)S(1)} %collective-permute-done.8.refs_1_, bf16[96,896]{1,0:T(8,128)(2,1)S(1)} %collective-permute-done.9.refs_2_, ...), custom_call_target="tpu_custom_call" | custom-call | flops 57500000 | tf_op jit(solution)/shard_map/expert_kernel/pallas_call | solution.py:72
  30.6 0.7 %collective-permute-start.11 = (bf16[96,896]{1,0:T(8,128)(2,1)S(1)}, bf16[96,896]{1,0:T(8,128)(2,1)S(1)}, u32[]{:S(2)}, u32[]{:S(2)}) collective-permute-start(bf16[96,896]{1,0:T(8,128)(2,1)S(1)} %get-tuple-element.32), channel_id=1, source_target_pairs={{0,2},{1,3},{2,0},{3,1},{4,6},{5,7},{6,4},{7,5},{8,10},{9,11},{10,... | collective-permute-start | bytes 516104 | tf_op jit(solution)/shard_map/ppermute | solution.py:235
  31.5 1.3 %collective-permute-start.16 = (bf16[96,896]{1,0:T(8,128)(2,1)S(1)}, bf16[96,896]{1,0:T(8,128)(2,1)S(1)}, u32[]{:S(2)}, u32[]{:S(2)}) collective-permute-start(bf16[96,896]{1,0:T(8,128)(2,1)S(1)} %get-tuple-element.36), channel_id=1, source_target_pairs={{0,2},{1,3},{2,0},{3,1},{4,6},{5,7},{6,4},{7,5},{8,10},{9,11},{10,... | collective-permute-start | bytes 516104 | tf_op jit(solution)/shard_map/ppermute | solution.py:235
  32.8 2.6 %expert_kernel.7 = (f32[96,1792]{1,0:T(8,128)S(1)}, bf16[96,1792]{1,0:T(8,128)(2,1)S(1)}) custom-call(bf16[96,1792]{1,0:T(8,128)(2,1)S(1)} %shard_map.58.refs_0_, bf16[96,1792]{1,0:T(8,128)(2,1)S(1)} %collective-permute-done.13.refs_1_, bf16[608,3584]{1,0:T(8,128)(2,1)S(1)} %get-tuple-element.25.refs_2_.refs_4_, ...), custom_call_target="tpu_custom_call" | custom-call | flops 4600000000 | tf_op jit(solution)/shard_map/expert_kernel/pallas_call | solution.py:72
  35.5 2.3 %collective-permute-done.11.refs_1_ = bf16[96,896]{1,0:T(8,128)(2,1)S(1)} collective-permute-done((bf16[96,896]{1,0:T(8,128)(2,1)S(1)}, bf16[96,896]{1,0:T(8,128)(2,1)S(1)}, u32[]{:S(2)}, u32[]{:S(2)}) %collective-permute-start.11) | collective-permute-done | bytes 172064 | tf_op jit(solution)/shard_map/ppermute | solution.py:235
  37.9 1.3 %collective-permute-start.15 = (bf16[96,896]{1,0:T(8,128)(2,1)S(1)}, bf16[96,896]{1,0:T(8,128)(2,1)S(1)}, u32[]{:S(2)}, u32[]{:S(2)}) collective-permute-start(bf16[96,896]{1,0:T(8,128)(2,1)S(1)} %chip_sum_kernel.3.refs_2_), channel_id=1, source_target_pairs={{0,12},{4,0},{8,4},{12,8},{1,13},{5,1},{9,5},{13,9},{2,14},{6,2},{... | collective-permute-start | bytes 516104 | tf_op jit(solution)/shard_map/ppermute | solution.py:242
  39.3 1.5 %collective-permute-start.20 = (bf16[96,896]{1,0:T(8,128)(2,1)S(1)}, bf16[96,896]{1,0:T(8,128)(2,1)S(1)}, u32[]{:S(2)}, u32[]{:S(2)}) collective-permute-start(bf16[96,896]{1,0:T(8,128)(2,1)S(1)} %get-tuple-element.40), channel_id=1, source_target_pairs={{0,2},{1,3},{2,0},{3,1},{4,6},{5,7},{6,4},{7,5},{8,10},{9,11},{10,... | collective-permute-start | bytes 516104 | tf_op jit(solution)/shard_map/ppermute | solution.py:235
  41.4 3.3 %collective-permute-done.20.refs_1_ = bf16[96,896]{1,0:T(8,128)(2,1)S(1)} collective-permute-done((bf16[96,896]{1,0:T(8,128)(2,1)S(1)}, bf16[96,896]{1,0:T(8,128)(2,1)S(1)}, u32[]{:S(2)}, u32[]{:S(2)}) %collective-permute-start.20) | collective-permute-done | bytes 172064 | tf_op jit(solution)/shard_map/ppermute | solution.py:235
  44.8 0.8 %collective-permute-start.22 = (bf16[96,896]{1,0:T(8,128)(2,1)S(1)}, bf16[96,896]{1,0:T(8,128)(2,1)S(1)}, u32[]{:S(2)}, u32[]{:S(2)}) collective-permute-start(bf16[96,896]{1,0:T(8,128)(2,1)S(1)} %chip_sum_kernel.5.refs_2_), channel_id=1, source_target_pairs={{0,4},{4,8},{8,12},{12,0},{1,5},{5,9},{9,13},{13,1},{2,6},{6,10},{... | collective-permute-start | bytes 516104 | tf_op jit(solution)/shard_map/ppermute | solution.py:242
  45.7 0.9 %collective-permute-start.21 = (bf16[96,896]{1,0:T(8,128)(2,1)S(1)}, bf16[96,896]{1,0:T(8,128)(2,1)S(1)}, u32[]{:S(2)}, u32[]{:S(2)}) collective-permute-start(bf16[96,896]{1,0:T(8,128)(2,1)S(1)} %get-tuple-element.42), channel_id=1, source_target_pairs={{0,2},{1,3},{2,0},{3,1},{4,6},{5,7},{6,4},{7,5},{8,10},{9,11},{10,... | collective-permute-start | bytes 516104 | tf_op jit(solution)/shard_map/ppermute | solution.py:235
  46.6 8.2 %collective-permute-done.18.refs_2_ = bf16[96,896]{1,0:T(8,128)(2,1)S(1)} collective-permute-done((bf16[96,896]{1,0:T(8,128)(2,1)S(1)}, bf16[96,896]{1,0:T(8,128)(2,1)S(1)}, u32[]{:S(2)}, u32[]{:S(2)}) %collective-permute-start.18) | collective-permute-done | bytes 172064 | tf_op jit(solution)/shard_map/ppermute | solution.py:242
  55.0 0.7 %weigh_kernel.5 = bf16[96,896]{1,0:T(8,128)(2,1)} custom-call(f32[4,96,128]{2,1,0:T(8,128)S(1)} %get-tuple-element.24.refs_1_.refs_0_, f32[96,896]{1,0:T(8,128)S(1)} %weigh_kernel.4.refs_1_, bf16[96,896]{1,0:T(8,128)(2,1)S(1)} %collective-permute-done.22.refs_2_), custom_call_target="tpu_custom_call" | custom-call | flops 575000000 | tf_op jit(solution)/shard_map/weigh_kernel/pallas_call | solution.py:72
  (44 shorter events, 3.5 us)
Async XLA Ops:
  0.0 9.6 %collective-permute-start = (bf16[96,896]{1,0:T(8,128)(2,1)}, bf16[96,896]{1,0:T(8,128)(2,1)S(1)}, u32[]{:S(2)}, u32[]{:S(2)}) collective-permute-start(bf16[96,896]{1,0:T(8,128)(2,1)} %refs_0_.1), channel_id=1, source_target_pairs={{0,4},{4,8},{8,12},{12,0},{1,5},{5,9},{9,13},{13,1},{2,6},{6,10},{... | collective-permute-start | bytes 516104 | tf_op jit(solution)/shard_map/ppermute | solution.py:242
  3.0 6.6 %collective-permute-start.2 = (bf16[96,896]{1,0:T(8,128)(2,1)}, bf16[96,896]{1,0:T(8,128)(2,1)S(1)}, u32[]{:S(2)}, u32[]{:S(2)}) collective-permute-start(bf16[96,896]{1,0:T(8,128)(2,1)} %refs_0_.1), channel_id=1, source_target_pairs={{0,2},{1,3},{2,0},{3,1},{4,6},{5,7},{6,4},{7,5},{8,10},{9,11},{10,... | collective-permute-start | bytes 516104 | tf_op jit(solution)/shard_map/ppermute | solution.py:235
  4.5 5.1 %copy-start = (bf16[96,896]{1,0:T(8,128)(2,1)S(1)}, bf16[96,896]{1,0:T(8,128)(2,1)}, u32[]{:S(2)}) copy-start(bf16[96,896]{1,0:T(8,128)(2,1)} %refs_0_.1) | copy-start | bytes 516100
  9.7 2.8 %collective-permute-start.3 = (bf16[96,1792]{1,0:T(8,128)(2,1)S(1)}, bf16[96,1792]{1,0:T(8,128)(2,1)S(1)}, u32[]{:S(2)}, u32[]{:S(2)}) collective-permute-start(bf16[96,1792]{1,0:T(8,128)(2,1)S(1)} %pack_kernel.1.refs_0_), channel_id=1, source_target_pairs={{0,1},{1,0},{2,3},{3,2},{4,5},{5,4},{6,7},{7,6},{8,9},{9,8},{10,11... | collective-permute-start | bytes 1032200 | tf_op jit(solution)/shard_map/ppermute | solution.py:235
  9.7 6.8 %collective-permute-start.1 = (bf16[96,896]{1,0:T(8,128)(2,1)S(1)}, bf16[96,896]{1,0:T(8,128)(2,1)S(1)}, u32[]{:S(2)}, u32[]{:S(2)}) collective-permute-start(bf16[96,896]{1,0:T(8,128)(2,1)S(1)} %shard_map.55.refs_2_.refs_0_), channel_id=1, source_target_pairs={{0,2},{1,3},{2,0},{3,1},{4,6},{5,7},{6,4},{7,5},{8,10},{9,11},{10,... | collective-permute-start | bytes 516104 | tf_op jit(solution)/shard_map/ppermute | solution.py:235
  11.3 9.1 %collective-permute-start.4 = (bf16[96,896]{1,0:T(8,128)(2,1)S(1)}, bf16[96,896]{1,0:T(8,128)(2,1)S(1)}, u32[]{:S(2)}, u32[]{:S(2)}) collective-permute-start(bf16[96,896]{1,0:T(8,128)(2,1)S(1)} %shard_map.55.refs_2_.refs_0_), channel_id=1, source_target_pairs={{0,1},{1,0},{2,3},{3,2},{4,5},{5,4},{6,7},{7,6},{8,9},{9,8},{10,11... | collective-permute-start | bytes 516104 | tf_op jit(solution)/shard_map/ppermute | solution.py:235
  11.5 8.4 %collective-permute-start.6 = (bf16[96,896]{1,0:T(8,128)(2,1)S(1)}, bf16[96,896]{1,0:T(8,128)(2,1)S(1)}, u32[]{:S(2)}, u32[]{:S(2)}) collective-permute-start(bf16[96,896]{1,0:T(8,128)(2,1)S(1)} %shard_map.55.refs_2_.refs_0_), channel_id=1, source_target_pairs={{0,4},{4,8},{8,12},{12,0},{1,5},{5,9},{9,13},{13,1},{2,6},{6,10},{... | collective-permute-start | bytes 516104 | tf_op jit(solution)/shard_map/ppermute | solution.py:242
  16.5 3.9 %collective-permute-start.5 = (bf16[96,896]{1,0:T(8,128)(2,1)S(1)}, bf16[96,896]{1,0:T(8,128)(2,1)S(1)}, u32[]{:S(2)}, u32[]{:S(2)}) collective-permute-start(bf16[96,896]{1,0:T(8,128)(2,1)S(1)} %shard_map.56.refs_1_), channel_id=1, source_target_pairs={{0,1},{1,0},{2,3},{3,2},{4,5},{5,4},{6,7},{7,6},{8,9},{9,8},{10,11... | collective-permute-start | bytes 516104 | tf_op jit(solution)/shard_map/ppermute | solution.py:235
  19.9 5.8 %collective-permute-start.8 = (bf16[96,896]{1,0:T(8,128)(2,1)S(1)}, bf16[96,896]{1,0:T(8,128)(2,1)S(1)}, u32[]{:S(2)}, u32[]{:S(2)}) collective-permute-start(bf16[96,896]{1,0:T(8,128)(2,1)S(1)} %shard_map.57.refs_6_.refs_0_), channel_id=1, source_target_pairs={{0,2},{1,3},{2,0},{3,1},{4,6},{5,7},{6,4},{7,5},{8,10},{9,11},{10,... | collective-permute-start | bytes 516104 | tf_op jit(solution)/shard_map/ppermute | solution.py:235
  20.4 9.9 %collective-permute-start.12 = (bf16[96,1792]{1,0:T(8,128)(2,1)S(1)}, bf16[96,1792]{1,0:T(8,128)(2,1)S(1)}, u32[]{:S(2)}, u32[]{:S(2)}) collective-permute-start(bf16[96,1792]{1,0:T(8,128)(2,1)S(1)} %pack_kernel.1.refs_0_), channel_id=1, source_target_pairs={{0,12},{4,0},{8,4},{12,8},{1,13},{5,1},{9,5},{13,9},{2,14},{6,2},{... | collective-permute-start | bytes 1032200 | tf_op jit(solution)/shard_map/ppermute | solution.py:242
  23.1 7.4 %collective-permute-start.7 = (bf16[96,1792]{1,0:T(8,128)(2,1)S(1)}, bf16[96,1792]{1,0:T(8,128)(2,1)S(1)}, u32[]{:S(2)}, u32[]{:S(2)}) collective-permute-start(bf16[96,1792]{1,0:T(8,128)(2,1)S(1)} %get-tuple-element.29), channel_id=1, source_target_pairs={{0,1},{1,0},{2,3},{3,2},{4,5},{5,4},{6,7},{7,6},{8,9},{9,8},{10,11... | collective-permute-start | bytes 1032200 | tf_op jit(solution)/shard_map/ppermute | solution.py:235
  23.2 2.6 %collective-permute-start.9 = (bf16[96,896]{1,0:T(8,128)(2,1)S(1)}, bf16[96,896]{1,0:T(8,128)(2,1)S(1)}, u32[]{:S(2)}, u32[]{:S(2)}) collective-permute-start(bf16[96,896]{1,0:T(8,128)(2,1)S(1)} %shard_map.57.refs_6_.refs_0_), channel_id=1, source_target_pairs={{0,1},{1,0},{2,3},{3,2},{4,5},{5,4},{6,7},{7,6},{8,9},{9,8},{10,11... | collective-permute-start | bytes 516104 | tf_op jit(solution)/shard_map/ppermute | solution.py:235
  25.7 1.4 %collective-permute-start.10 = (bf16[96,896]{1,0:T(8,128)(2,1)S(1)}, bf16[96,896]{1,0:T(8,128)(2,1)S(1)}, u32[]{:S(2)}, u32[]{:S(2)}) collective-permute-start(bf16[96,896]{1,0:T(8,128)(2,1)S(1)} %collective-permute-done.8.refs_1_), channel_id=1, source_target_pairs={{0,1},{1,0},{2,3},{3,2},{4,5},{5,4},{6,7},{7,6},{8,9},{9,8},{10,11... | collective-permute-start | bytes 516104 | tf_op jit(solution)/shard_map/ppermute | solution.py:235
  29.8 1.7 %collective-permute-start.14 = (bf16[96,1792]{1,0:T(8,128)(2,1)S(1)}, bf16[96,1792]{1,0:T(8,128)(2,1)S(1)}, u32[]{:S(2)}, u32[]{:S(2)}) collective-permute-start(bf16[96,1792]{1,0:T(8,128)(2,1)S(1)} %get-tuple-element.33), channel_id=1, source_target_pairs={{0,1},{1,0},{2,3},{3,2},{4,5},{5,4},{6,7},{7,6},{8,9},{9,8},{10,11... | collective-permute-start | bytes 1032200 | tf_op jit(solution)/shard_map/ppermute | solution.py:235
  30.0 15.6 %collective-permute-start.19 = (bf16[96,1792]{1,0:T(8,128)(2,1)S(1)}, bf16[96,1792]{1,0:T(8,128)(2,1)S(1)}, u32[]{:S(2)}, u32[]{:S(2)}) collective-permute-start(bf16[96,1792]{1,0:T(8,128)(2,1)S(1)} %get-tuple-element.39), channel_id=1, source_target_pairs={{0,1},{1,0},{2,3},{3,2},{4,5},{5,4},{6,7},{7,6},{8,9},{9,8},{10,11... | collective-permute-start | bytes 1032200 | tf_op jit(solution)/shard_map/ppermute | solution.py:235
  30.3 2.5 %collective-permute-start.13 = (bf16[96,1792]{1,0:T(8,128)(2,1)S(1)}, bf16[96,1792]{1,0:T(8,128)(2,1)S(1)}, u32[]{:S(2)}, u32[]{:S(2)}) collective-permute-start(bf16[96,1792]{1,0:T(8,128)(2,1)S(1)} %shard_map.58.refs_0_), channel_id=1, source_target_pairs={{0,1},{1,0},{2,3},{3,2},{4,5},{5,4},{6,7},{7,6},{8,9},{9,8},{10,11... | collective-permute-start | bytes 1032200 | tf_op jit(solution)/shard_map/ppermute | solution.py:235
  30.6 7.3 %collective-permute-start.11 = (bf16[96,896]{1,0:T(8,128)(2,1)S(1)}, bf16[96,896]{1,0:T(8,128)(2,1)S(1)}, u32[]{:S(2)}, u32[]{:S(2)}) collective-permute-start(bf16[96,896]{1,0:T(8,128)(2,1)S(1)} %get-tuple-element.32), channel_id=1, source_target_pairs={{0,2},{1,3},{2,0},{3,1},{4,6},{5,7},{6,4},{7,5},{8,10},{9,11},{10,... | collective-permute-start | bytes 516104 | tf_op jit(solution)/shard_map/ppermute | solution.py:235
  31.5 9.4 %collective-permute-start.16 = (bf16[96,896]{1,0:T(8,128)(2,1)S(1)}, bf16[96,896]{1,0:T(8,128)(2,1)S(1)}, u32[]{:S(2)}, u32[]{:S(2)}) collective-permute-start(bf16[96,896]{1,0:T(8,128)(2,1)S(1)} %get-tuple-element.36), channel_id=1, source_target_pairs={{0,2},{1,3},{2,0},{3,1},{4,6},{5,7},{6,4},{7,5},{8,10},{9,11},{10,... | collective-permute-start | bytes 516104 | tf_op jit(solution)/shard_map/ppermute | solution.py:235
  35.4 3.8 %collective-permute-start.17 = (bf16[96,1792]{1,0:T(8,128)(2,1)S(1)}, bf16[96,1792]{1,0:T(8,128)(2,1)S(1)}, u32[]{:S(2)}, u32[]{:S(2)}) collective-permute-start(bf16[96,1792]{1,0:T(8,128)(2,1)S(1)} %get-tuple-element.37), channel_id=1, source_target_pairs={{0,1},{1,0},{2,3},{3,2},{4,5},{5,4},{6,7},{7,6},{8,9},{9,8},{10,11... | collective-permute-start | bytes 1032200 | tf_op jit(solution)/shard_map/ppermute | solution.py:235
  37.9 8.7 %collective-permute-start.15 = (bf16[96,896]{1,0:T(8,128)(2,1)S(1)}, bf16[96,896]{1,0:T(8,128)(2,1)S(1)}, u32[]{:S(2)}, u32[]{:S(2)}) collective-permute-start(bf16[96,896]{1,0:T(8,128)(2,1)S(1)} %chip_sum_kernel.3.refs_2_), channel_id=1, source_target_pairs={{0,12},{4,0},{8,4},{12,8},{1,13},{5,1},{9,5},{13,9},{2,14},{6,2},{... | collective-permute-start | bytes 516104 | tf_op jit(solution)/shard_map/ppermute | solution.py:242
  39.3 5.5 %collective-permute-start.20 = (bf16[96,896]{1,0:T(8,128)(2,1)S(1)}, bf16[96,896]{1,0:T(8,128)(2,1)S(1)}, u32[]{:S(2)}, u32[]{:S(2)}) collective-permute-start(bf16[96,896]{1,0:T(8,128)(2,1)S(1)} %get-tuple-element.40), channel_id=1, source_target_pairs={{0,2},{1,3},{2,0},{3,1},{4,6},{5,7},{6,4},{7,5},{8,10},{9,11},{10,... | collective-permute-start | bytes 516104 | tf_op jit(solution)/shard_map/ppermute | solution.py:235
  41.0 13.8 %collective-permute-start.18 = (bf16[96,896]{1,0:T(8,128)(2,1)S(1)}, bf16[96,896]{1,0:T(8,128)(2,1)S(1)}, u32[]{:S(2)}, u32[]{:S(2)}) collective-permute-start(bf16[96,896]{1,0:T(8,128)(2,1)S(1)} %chip_sum_kernel.4.refs_2_), channel_id=1, source_target_pairs={{0,8},{4,12},{8,0},{12,4},{1,9},{5,13},{9,1},{13,5},{2,10},{6,14},... | collective-permute-start | bytes 516104 | tf_op jit(solution)/shard_map/ppermute | solution.py:242
  44.8 10.2 %collective-permute-start.22 = (bf16[96,896]{1,0:T(8,128)(2,1)S(1)}, bf16[96,896]{1,0:T(8,128)(2,1)S(1)}, u32[]{:S(2)}, u32[]{:S(2)}) collective-permute-start(bf16[96,896]{1,0:T(8,128)(2,1)S(1)} %chip_sum_kernel.5.refs_2_), channel_id=1, source_target_pairs={{0,4},{4,8},{8,12},{12,0},{1,5},{5,9},{9,13},{13,1},{2,6},{6,10},{... | collective-permute-start | bytes 516104 | tf_op jit(solution)/shard_map/ppermute | solution.py:242
  45.7 9.2 %collective-permute-start.21 = (bf16[96,896]{1,0:T(8,128)(2,1)S(1)}, bf16[96,896]{1,0:T(8,128)(2,1)S(1)}, u32[]{:S(2)}, u32[]{:S(2)}) collective-permute-start(bf16[96,896]{1,0:T(8,128)(2,1)S(1)} %get-tuple-element.42), channel_id=1, source_target_pairs={{0,2},{1,3},{2,0},{3,1},{4,6},{5,7},{6,4},{7,5},{8,10},{9,11},{10,... | collective-permute-start | bytes 516104 | tf_op jit(solution)/shard_map/ppermute | solution.py:235

commit v16 on v15

--- a/solution.py
+++ b/solution.py
@@ -286,7 +286,7 @@
     leave((2,), [sums[1][0]], 2)
     run((3,), [sums[2][0]], 4)
     give(1, [kept[3,][0]], 4)
-    leave((3,), [added[1]], .05)
+    leave((3,), [added[1]], 2)
     give(2, [sums[3][0]], 4)
     give(3, [added[2]], 4)
     leave((0,), [added[3]], 2)

time: 55.8 us -> 59.1 us (1.059)
  waiting for transfers between devices: 23.3 us -> 27.2 us
  starting transfers between devices: 16.2 us -> 15.5 us
    ppermute x17, waiting for transfers between devices: 10.9 us -> 14.9 us  [swap(): return lax.ppermute(array, 'tensor', [(i, i ^ bit) for i in range(4)])]
  transfers between devices with their start and end apart: 23 -> 23, of which waited for: 10 -> 11; matrix products, arithmetic and copies ran while one was open for 0% -> 0% of each run, Pallas kernels for 28% -> 26%
where the time goes in v16:
time: 59.1 us; the launch traced here: 59 us
  waiting for transfers between devices  27.2 us (46%)
  Pallas kernels  16.1 us (27%)
  starting transfers between devices  15.5 us (26%)
    pallas_call x16, Pallas kernels, local_call(): pl.pallas_call(body_of, name=name, out_shape=out_shape, in_specs=list(in_...  16.1 us
    ppermute x17, waiting for transfers between devices, swap(): return lax.ppermute(array, 'tensor', [(i, i ^ bit) for i in range(4)])  14.9 us
    ppermute x6, waiting for transfers between devices, shift(): lax.ppermute(array, 'expert', [(i, (i + by) % experts_n) for i in range(e...  12.3 us
    ppermute x17, starting transfers between devices, swap(): return lax.ppermute(array, 'tensor', [(i, i ^ bit) for i in range(4)])  9.29 us
    ppermute x6, starting transfers between devices, shift(): lax.ppermute(array, 'expert', [(i, (i + by) % experts_n) for i in range(e...  6.25 us
  transfers between devices with their start and end apart: 23, of which 11 were waited for; matrix products, arithmetic and copies ran while one was open for 0% of the time, Pallas kernels for 26%

profile of v16, /device:TPU:0, one launch (start us, length us, event | category | flops | bytes accessed | tf_op | source)
XLA Modules:
  0.0 59.0 jit_solution(17400786546040740975)
XLA Ops:
  0.0 3.0 %collective-permute-start = (bf16[96,896]{1,0:T(8,128)(2,1)}, bf16[96,896]{1,0:T(8,128)(2,1)S(1)}, u32[]{:S(2)}, u32[]{:S(2)}) collective-permute-start(bf16[96,896]{1,0:T(8,128)(2,1)} %refs_0_.1), channel_id=1, source_target_pairs={{0,4},{4,8},{8,12},{12,0},{1,5},{5,9},{9,13},{13,1},{2,6},{6,10},{... | collective-permute-start | bytes 516104 | tf_op jit(solution)/shard_map/ppermute | solution.py:242
  3.0 1.5 %collective-permute-start.2 = (bf16[96,896]{1,0:T(8,128)(2,1)}, bf16[96,896]{1,0:T(8,128)(2,1)S(1)}, u32[]{:S(2)}, u32[]{:S(2)}) collective-permute-start(bf16[96,896]{1,0:T(8,128)(2,1)} %refs_0_.1), channel_id=1, source_target_pairs={{0,2},{1,3},{2,0},{3,1},{4,6},{5,7},{6,4},{7,5},{8,10},{9,11},{10,... | collective-permute-start | bytes 516104 | tf_op jit(solution)/shard_map/ppermute | solution.py:235
  4.5 4.3 %prepare_kernel.1 = (f32[4,96,128]{2,1,0:T(8,128)S(1)}, bf16[608,3584]{1,0:T(8,128)(2,1)S(1)}, bf16[608,3584]{1,0:T(8,128)(2,1)S(1)}) custom-call(s32[2,96]{1,0:T(2,128)} %bitcast.8, s32[2,96]{1,0:T(2,128)} %bitcast.9, bf16[608,3584]{1,0:T(8,128)(2,1)} %bitcast.6, bf16[608,3584]{1,0:T(8,128)(2,1)} %bitcast.7), custom_call_target="tpu_custom_call" | custom-call | flops 4600000000 | tf_op jit(solution)/shard_map/prepare_kernel/pallas_call | solution.py:72
  8.9 0.8 %collective-permute-done.refs_0_ = bf16[96,896]{1,0:T(8,128)(2,1)S(1)} collective-permute-done((bf16[96,896]{1,0:T(8,128)(2,1)}, bf16[96,896]{1,0:T(8,128)(2,1)S(1)}, u32[]{:S(2)}, u32[]{:S(2)}) %collective-permute-start) | collective-permute-done | bytes 172064 | tf_op jit(solution)/shard_map/ppermute | solution.py:242
  9.7 1.6 %collective-permute-start.1 = (bf16[96,896]{1,0:T(8,128)(2,1)S(1)}, bf16[96,896]{1,0:T(8,128)(2,1)S(1)}, u32[]{:S(2)}, u32[]{:S(2)}) collective-permute-start(bf16[96,896]{1,0:T(8,128)(2,1)S(1)} %shard_map.55.refs_2_.refs_0_), channel_id=1, source_target_pairs={{0,2},{1,3},{2,0},{3,1},{4,6},{5,7},{6,4},{7,5},{8,10},{9,11},{10,... | collective-permute-start | bytes 516104 | tf_op jit(solution)/shard_map/ppermute | solution.py:235
  11.5 1.0 %collective-permute-start.6 = (bf16[96,896]{1,0:T(8,128)(2,1)S(1)}, bf16[96,896]{1,0:T(8,128)(2,1)S(1)}, u32[]{:S(2)}, u32[]{:S(2)}) collective-permute-start(bf16[96,896]{1,0:T(8,128)(2,1)S(1)} %shard_map.55.refs_2_.refs_0_), channel_id=1, source_target_pairs={{0,4},{4,8},{8,12},{12,0},{1,5},{5,9},{9,13},{13,1},{2,6},{6,10},{... | collective-permute-start | bytes 516104 | tf_op jit(solution)/shard_map/ppermute | solution.py:242
  12.5 2.6 %expert_kernel.4 = (f32[96,1792]{1,0:T(8,128)S(1)}, bf16[96,1792]{1,0:T(8,128)(2,1)S(1)}) custom-call(bf16[96,1792]{1,0:T(8,128)(2,1)S(1)} %pack_kernel.1.refs_0_, bf16[96,1792]{1,0:T(8,128)(2,1)S(1)} %collective-permute-done.3.refs_1_, bf16[608,3584]{1,0:T(8,128)(2,1)S(1)} %get-tuple-element.25.refs_2_.refs_4_, ...), custom_call_target="tpu_custom_call" | custom-call | flops 9200000000 | tf_op jit(solution)/shard_map/expert_kernel/pallas_call | solution.py:72
  15.1 1.4 %collective-permute-done.1.refs_0_ = bf16[96,896]{1,0:T(8,128)(2,1)S(1)} collective-permute-done((bf16[96,896]{1,0:T(8,128)(2,1)S(1)}, bf16[96,896]{1,0:T(8,128)(2,1)S(1)}, u32[]{:S(2)}, u32[]{:S(2)}) %collective-permute-start.1) | collective-permute-done | bytes 172064 | tf_op jit(solution)/shard_map/ppermute | solution.py:235
  16.5 3.3 %collective-permute-done.6.refs_0_ = bf16[96,896]{1,0:T(8,128)(2,1)S(1)} collective-permute-done((bf16[96,896]{1,0:T(8,128)(2,1)S(1)}, bf16[96,896]{1,0:T(8,128)(2,1)S(1)}, u32[]{:S(2)}, u32[]{:S(2)}) %collective-permute-start.6) | collective-permute-done | bytes 172064 | tf_op jit(solution)/shard_map/ppermute | solution.py:242
  20.4 2.6 %expert_kernel.5 = (f32[96,1792]{1,0:T(8,128)S(1)}, bf16[96,1792]{1,0:T(8,128)(2,1)S(1)}) custom-call(bf16[96,896]{1,0:T(8,128)(2,1)S(1)} %shard_map.55.refs_2_.refs_0_, bf16[96,896]{1,0:T(8,128)(2,1)S(1)} %shard_map.56.refs_1_, bf16[96,896]{1,0:T(8,128)(2,1)S(1)} %collective-permute-done.4.refs_2_, bf16[96,896]{1,0:T(8,128)(2,1)S(1)} %collective-permute-done.5.refs_3_, ...), custom_call_target="tpu_custom_call" | custom-call | flops 57500000 | tf_op jit(solution)/shard_map/expert_kernel/pallas_call | solution.py:72
  23.6 2.1 %collective-permute-done.8.refs_1_ = bf16[96,896]{1,0:T(8,128)(2,1)S(1)} collective-permute-done((bf16[96,896]{1,0:T(8,128)(2,1)S(1)}, bf16[96,896]{1,0:T(8,128)(2,1)S(1)}, u32[]{:S(2)}, u32[]{:S(2)}) %collective-permute-start.8) | collective-permute-done | bytes 172064 | tf_op jit(solution)/shard_map/ppermute | solution.py:235
  25.7 1.4 %collective-permute-done.10.refs_3_ = bf16[96,896]{1,0:T(8,128)(2,1)S(1)} collective-permute-done((bf16[96,896]{1,0:T(8,128)(2,1)S(1)}, bf16[96,896]{1,0:T(8,128)(2,1)S(1)}, u32[]{:S(2)}, u32[]{:S(2)}) %collective-permute-start.10) | collective-permute-done | bytes 172064 | tf_op jit(solution)/shard_map/ppermute | solution.py:235
  27.1 2.6 %expert_kernel.6 = (f32[96,1792]{1,0:T(8,128)S(1)}, bf16[96,1792]{1,0:T(8,128)(2,1)S(1)}) custom-call(bf16[96,896]{1,0:T(8,128)(2,1)S(1)} %shard_map.57.refs_6_.refs_0_, bf16[96,896]{1,0:T(8,128)(2,1)S(1)} %collective-permute-done.8.refs_1_, bf16[96,896]{1,0:T(8,128)(2,1)S(1)} %collective-permute-done.9.refs_2_, ...), custom_call_target="tpu_custom_call" | custom-call | flops 57500000 | tf_op jit(solution)/shard_map/expert_kernel/pallas_call | solution.py:72
  30.6 0.7 %collective-permute-start.11 = (bf16[96,896]{1,0:T(8,128)(2,1)S(1)}, bf16[96,896]{1,0:T(8,128)(2,1)S(1)}, u32[]{:S(2)}, u32[]{:S(2)}) collective-permute-start(bf16[96,896]{1,0:T(8,128)(2,1)S(1)} %get-tuple-element.32), channel_id=1, source_target_pairs={{0,2},{1,3},{2,0},{3,1},{4,6},{5,7},{6,4},{7,5},{8,10},{9,11},{10,... | collective-permute-start | bytes 516104 | tf_op jit(solution)/shard_map/ppermute | solution.py:235
  31.5 0.9 %collective-permute-done.13.refs_1_ = bf16[96,1792]{1,0:T(8,128)(2,1)S(1)} collective-permute-done((bf16[96,1792]{1,0:T(8,128)(2,1)S(1)}, bf16[96,1792]{1,0:T(8,128)(2,1)S(1)}, u32[]{:S(2)}, u32[]{:S(2)}) %collective-permute-start.13) | collective-permute-done | bytes 344096 | tf_op jit(solution)/shard_map/ppermute | solution.py:235
  32.5 2.6 %expert_kernel.7 = (f32[96,1792]{1,0:T(8,128)S(1)}, bf16[96,1792]{1,0:T(8,128)(2,1)S(1)}) custom-call(bf16[96,1792]{1,0:T(8,128)(2,1)S(1)} %shard_map.58.refs_0_, bf16[96,1792]{1,0:T(8,128)(2,1)S(1)} %collective-permute-done.13.refs_1_, bf16[608,3584]{1,0:T(8,128)(2,1)S(1)} %get-tuple-element.25.refs_2_.refs_4_, ...), custom_call_target="tpu_custom_call" | custom-call | flops 4600000000 | tf_op jit(solution)/shard_map/expert_kernel/pallas_call | solution.py:72
  35.3 2.0 %collective-permute-done.11.refs_1_ = bf16[96,896]{1,0:T(8,128)(2,1)S(1)} collective-permute-done((bf16[96,896]{1,0:T(8,128)(2,1)S(1)}, bf16[96,896]{1,0:T(8,128)(2,1)S(1)}, u32[]{:S(2)}, u32[]{:S(2)}) %collective-permute-start.11) | collective-permute-done | bytes 172064 | tf_op jit(solution)/shard_map/ppermute | solution.py:235
  37.3 1.5 %collective-permute-start.15 = (bf16[96,896]{1,0:T(8,128)(2,1)S(1)}, bf16[96,896]{1,0:T(8,128)(2,1)S(1)}, u32[]{:S(2)}, u32[]{:S(2)}) collective-permute-start(bf16[96,896]{1,0:T(8,128)(2,1)S(1)} %chip_sum_kernel.3.refs_2_), channel_id=1, source_target_pairs={{0,12},{4,0},{8,4},{12,8},{1,13},{5,1},{9,5},{13,9},{2,14},{6,2},{... | collective-permute-start | bytes 516104 | tf_op jit(solution)/shard_map/ppermute | solution.py:242
  38.8 1.5 %collective-permute-start.16 = (bf16[96,896]{1,0:T(8,128)(2,1)S(1)}, bf16[96,896]{1,0:T(8,128)(2,1)S(1)}, u32[]{:S(2)}, u32[]{:S(2)}) collective-permute-start(bf16[96,896]{1,0:T(8,128)(2,1)S(1)} %get-tuple-element.36), channel_id=1, source_target_pairs={{0,2},{1,3},{2,0},{3,1},{4,6},{5,7},{6,4},{7,5},{8,10},{9,11},{10,... | collective-permute-start | bytes 516104 | tf_op jit(solution)/shard_map/ppermute | solution.py:235
  41.0 5.2 %collective-permute-done.16.refs_1_ = bf16[96,896]{1,0:T(8,128)(2,1)S(1)} collective-permute-done((bf16[96,896]{1,0:T(8,128)(2,1)S(1)}, bf16[96,896]{1,0:T(8,128)(2,1)S(1)}, u32[]{:S(2)}, u32[]{:S(2)}) %collective-permute-start.16) | collective-permute-done | bytes 172064 | tf_op jit(solution)/shard_map/ppermute | solution.py:235
  46.4 1.8 %collective-permute-done.20.refs_1_ = bf16[96,896]{1,0:T(8,128)(2,1)S(1)} collective-permute-done((bf16[96,896]{1,0:T(8,128)(2,1)S(1)}, bf16[96,896]{1,0:T(8,128)(2,1)S(1)}, u32[]{:S(2)}, u32[]{:S(2)}) %collective-permute-start.20) | collective-permute-done | bytes 172064 | tf_op jit(solution)/shard_map/ppermute | solution.py:235
  48.8 1.1 %collective-permute-start.21 = (bf16[96,896]{1,0:T(8,128)(2,1)S(1)}, bf16[96,896]{1,0:T(8,128)(2,1)S(1)}, u32[]{:S(2)}, u32[]{:S(2)}) collective-permute-start(bf16[96,896]{1,0:T(8,128)(2,1)S(1)} %get-tuple-element.42), channel_id=1, source_target_pairs={{0,2},{1,3},{2,0},{3,1},{4,6},{5,7},{6,4},{7,5},{8,10},{9,11},{10,... | collective-permute-start | bytes 516104 | tf_op jit(solution)/shard_map/ppermute | solution.py:235
  50.0 8.1 %collective-permute-done.18.refs_2_ = bf16[96,896]{1,0:T(8,128)(2,1)S(1)} collective-permute-done((bf16[96,896]{1,0:T(8,128)(2,1)S(1)}, bf16[96,896]{1,0:T(8,128)(2,1)S(1)}, u32[]{:S(2)}, u32[]{:S(2)}) %collective-permute-start.18) | collective-permute-done | bytes 172064 | tf_op jit(solution)/shard_map/ppermute | solution.py:242
  58.3 0.7 %weigh_kernel.5 = bf16[96,896]{1,0:T(8,128)(2,1)} custom-call(f32[4,96,128]{2,1,0:T(8,128)S(1)} %get-tuple-element.24.refs_1_.refs_0_, f32[96,896]{1,0:T(8,128)S(1)} %weigh_kernel.4.refs_1_, bf16[96,896]{1,0:T(8,128)(2,1)S(1)} %collective-permute-done.22.refs_2_), custom_call_target="tpu_custom_call" | custom-call | flops 575000000 | tf_op jit(solution)/shard_map/weigh_kernel/pallas_call | solution.py:72
  (44 shorter events, 4.4 us)
Async XLA Ops:
  0.0 9.6 %collective-permute-start = (bf16[96,896]{1,0:T(8,128)(2,1)}, bf16[96,896]{1,0:T(8,128)(2,1)S(1)}, u32[]{:S(2)}, u32[]{:S(2)}) collective-permute-start(bf16[96,896]{1,0:T(8,128)(2,1)} %refs_0_.1), channel_id=1, source_target_pairs={{0,4},{4,8},{8,12},{12,0},{1,5},{5,9},{9,13},{13,1},{2,6},{6,10},{... | collective-permute-start | bytes 516104 | tf_op jit(solution)/shard_map/ppermute | solution.py:242
  3.0 6.6 %collective-permute-start.2 = (bf16[96,896]{1,0:T(8,128)(2,1)}, bf16[96,896]{1,0:T(8,128)(2,1)S(1)}, u32[]{:S(2)}, u32[]{:S(2)}) collective-permute-start(bf16[96,896]{1,0:T(8,128)(2,1)} %refs_0_.1), channel_id=1, source_target_pairs={{0,2},{1,3},{2,0},{3,1},{4,6},{5,7},{6,4},{7,5},{8,10},{9,11},{10,... | collective-permute-start | bytes 516104 | tf_op jit(solution)/shard_map/ppermute | solution.py:235
  4.5 5.1 %copy-start = (bf16[96,896]{1,0:T(8,128)(2,1)S(1)}, bf16[96,896]{1,0:T(8,128)(2,1)}, u32[]{:S(2)}) copy-start(bf16[96,896]{1,0:T(8,128)(2,1)} %refs_0_.1) | copy-start | bytes 516100
  9.7 2.8 %collective-permute-start.3 = (bf16[96,1792]{1,0:T(8,128)(2,1)S(1)}, bf16[96,1792]{1,0:T(8,128)(2,1)S(1)}, u32[]{:S(2)}, u32[]{:S(2)}) collective-permute-start(bf16[96,1792]{1,0:T(8,128)(2,1)S(1)} %pack_kernel.1.refs_0_), channel_id=1, source_target_pairs={{0,1},{1,0},{2,3},{3,2},{4,5},{5,4},{6,7},{7,6},{8,9},{9,8},{10,11... | collective-permute-start | bytes 1032200 | tf_op jit(solution)/shard_map/ppermute | solution.py:235
  9.7 6.8 %collective-permute-start.1 = (bf16[96,896]{1,0:T(8,128)(2,1)S(1)}, bf16[96,896]{1,0:T(8,128)(2,1)S(1)}, u32[]{:S(2)}, u32[]{:S(2)}) collective-permute-start(bf16[96,896]{1,0:T(8,128)(2,1)S(1)} %shard_map.55.refs_2_.refs_0_), channel_id=1, source_target_pairs={{0,2},{1,3},{2,0},{3,1},{4,6},{5,7},{6,4},{7,5},{8,10},{9,11},{10,... | collective-permute-start | bytes 516104 | tf_op jit(solution)/shard_map/ppermute | solution.py:235
  11.3 9.1 %collective-permute-start.4 = (bf16[96,896]{1,0:T(8,128)(2,1)S(1)}, bf16[96,896]{1,0:T(8,128)(2,1)S(1)}, u32[]{:S(2)}, u32[]{:S(2)}) collective-permute-start(bf16[96,896]{1,0:T(8,128)(2,1)S(1)} %shard_map.55.refs_2_.refs_0_), channel_id=1, source_target_pairs={{0,1},{1,0},{2,3},{3,2},{4,5},{5,4},{6,7},{7,6},{8,9},{9,8},{10,11... | collective-permute-start | bytes 516104 | tf_op jit(solution)/shard_map/ppermute | solution.py:235
  11.5 8.4 %collective-permute-start.6 = (bf16[96,896]{1,0:T(8,128)(2,1)S(1)}, bf16[96,896]{1,0:T(8,128)(2,1)S(1)}, u32[]{:S(2)}, u32[]{:S(2)}) collective-permute-start(bf16[96,896]{1,0:T(8,128)(2,1)S(1)} %shard_map.55.refs_2_.refs_0_), channel_id=1, source_target_pairs={{0,4},{4,8},{8,12},{12,0},{1,5},{5,9},{9,13},{13,1},{2,6},{6,10},{... | collective-permute-start | bytes 516104 | tf_op jit(solution)/shard_map/ppermute | solution.py:242
  16.5 3.9 %collective-permute-start.5 = (bf16[96,896]{1,0:T(8,128)(2,1)S(1)}, bf16[96,896]{1,0:T(8,128)(2,1)S(1)}, u32[]{:S(2)}, u32[]{:S(2)}) collective-permute-start(bf16[96,896]{1,0:T(8,128)(2,1)S(1)} %shard_map.56.refs_1_), channel_id=1, source_target_pairs={{0,1},{1,0},{2,3},{3,2},{4,5},{5,4},{6,7},{7,6},{8,9},{9,8},{10,11... | collective-permute-start | bytes 516104 | tf_op jit(solution)/shard_map/ppermute | solution.py:235
  19.9 5.8 %collective-permute-start.8 = (bf16[96,896]{1,0:T(8,128)(2,1)S(1)}, bf16[96,896]{1,0:T(8,128)(2,1)S(1)}, u32[]{:S(2)}, u32[]{:S(2)}) collective-permute-start(bf16[96,896]{1,0:T(8,128)(2,1)S(1)} %shard_map.57.refs_6_.refs_0_), channel_id=1, source_target_pairs={{0,2},{1,3},{2,0},{3,1},{4,6},{5,7},{6,4},{7,5},{8,10},{9,11},{10,... | collective-permute-start | bytes 516104 | tf_op jit(solution)/shard_map/ppermute | solution.py:235
  20.4 9.9 %collective-permute-start.12 = (bf16[96,1792]{1,0:T(8,128)(2,1)S(1)}, bf16[96,1792]{1,0:T(8,128)(2,1)S(1)}, u32[]{:S(2)}, u32[]{:S(2)}) collective-permute-start(bf16[96,1792]{1,0:T(8,128)(2,1)S(1)} %pack_kernel.1.refs_0_), channel_id=1, source_target_pairs={{0,12},{4,0},{8,4},{12,8},{1,13},{5,1},{9,5},{13,9},{2,14},{6,2},{... | collective-permute-start | bytes 1032200 | tf_op jit(solution)/shard_map/ppermute | solution.py:242
  23.1 7.4 %collective-permute-start.7 = (bf16[96,1792]{1,0:T(8,128)(2,1)S(1)}, bf16[96,1792]{1,0:T(8,128)(2,1)S(1)}, u32[]{:S(2)}, u32[]{:S(2)}) collective-permute-start(bf16[96,1792]{1,0:T(8,128)(2,1)S(1)} %get-tuple-element.29), channel_id=1, source_target_pairs={{0,1},{1,0},{2,3},{3,2},{4,5},{5,4},{6,7},{7,6},{8,9},{9,8},{10,11... | collective-permute-start | bytes 1032200 | tf_op jit(solution)/shard_map/ppermute | solution.py:235
  23.2 2.6 %collective-permute-start.9 = (bf16[96,896]{1,0:T(8,128)(2,1)S(1)}, bf16[96,896]{1,0:T(8,128)(2,1)S(1)}, u32[]{:S(2)}, u32[]{:S(2)}) collective-permute-start(bf16[96,896]{1,0:T(8,128)(2,1)S(1)} %shard_map.57.refs_6_.refs_0_), channel_id=1, source_target_pairs={{0,1},{1,0},{2,3},{3,2},{4,5},{5,4},{6,7},{7,6},{8,9},{9,8},{10,11... | collective-permute-start | bytes 516104 | tf_op jit(solution)/shard_map/ppermute | solution.py:235
  25.7 1.4 %collective-permute-start.10 = (bf16[96,896]{1,0:T(8,128)(2,1)S(1)}, bf16[96,896]{1,0:T(8,128)(2,1)S(1)}, u32[]{:S(2)}, u32[]{:S(2)}) collective-permute-start(bf16[96,896]{1,0:T(8,128)(2,1)S(1)} %collective-permute-done.8.refs_1_), channel_id=1, source_target_pairs={{0,1},{1,0},{2,3},{3,2},{4,5},{5,4},{6,7},{7,6},{8,9},{9,8},{10,11... | collective-permute-start | bytes 516104 | tf_op jit(solution)/shard_map/ppermute | solution.py:235
  29.8 1.7 %collective-permute-start.14 = (bf16[96,1792]{1,0:T(8,128)(2,1)S(1)}, bf16[96,1792]{1,0:T(8,128)(2,1)S(1)}, u32[]{:S(2)}, u32[]{:S(2)}) collective-permute-start(bf16[96,1792]{1,0:T(8,128)(2,1)S(1)} %get-tuple-element.33), channel_id=1, source_target_pairs={{0,1},{1,0},{2,3},{3,2},{4,5},{5,4},{6,7},{7,6},{8,9},{9,8},{10,11... | collective-permute-start | bytes 1032200 | tf_op jit(solution)/shard_map/ppermute | solution.py:235
  30.0 18.8 %collective-permute-start.19 = (bf16[96,1792]{1,0:T(8,128)(2,1)S(1)}, bf16[96,1792]{1,0:T(8,128)(2,1)S(1)}, u32[]{:S(2)}, u32[]{:S(2)}) collective-permute-start(bf16[96,1792]{1,0:T(8,128)(2,1)S(1)} %get-tuple-element.39), channel_id=1, source_target_pairs={{0,1},{1,0},{2,3},{3,2},{4,5},{5,4},{6,7},{7,6},{8,9},{9,8},{10,11... | collective-permute-start | bytes 1032200 | tf_op jit(solution)/shard_map/ppermute | solution.py:235
  30.3 2.1 %collective-permute-start.13 = (bf16[96,1792]{1,0:T(8,128)(2,1)S(1)}, bf16[96,1792]{1,0:T(8,128)(2,1)S(1)}, u32[]{:S(2)}, u32[]{:S(2)}) collective-permute-start(bf16[96,1792]{1,0:T(8,128)(2,1)S(1)} %shard_map.58.refs_0_), channel_id=1, source_target_pairs={{0,1},{1,0},{2,3},{3,2},{4,5},{5,4},{6,7},{7,6},{8,9},{9,8},{10,11... | collective-permute-start | bytes 1032200 | tf_op jit(solution)/shard_map/ppermute | solution.py:235
  30.6 6.7 %collective-permute-start.11 = (bf16[96,896]{1,0:T(8,128)(2,1)S(1)}, bf16[96,896]{1,0:T(8,128)(2,1)S(1)}, u32[]{:S(2)}, u32[]{:S(2)}) collective-permute-start(bf16[96,896]{1,0:T(8,128)(2,1)S(1)} %get-tuple-element.32), channel_id=1, source_target_pairs={{0,2},{1,3},{2,0},{3,1},{4,6},{5,7},{6,4},{7,5},{8,10},{9,11},{10,... | collective-permute-start | bytes 516104 | tf_op jit(solution)/shard_map/ppermute | solution.py:235
  35.1 5.2 %collective-permute-start.17 = (bf16[96,1792]{1,0:T(8,128)(2,1)S(1)}, bf16[96,1792]{1,0:T(8,128)(2,1)S(1)}, u32[]{:S(2)}, u32[]{:S(2)}) collective-permute-start(bf16[96,1792]{1,0:T(8,128)(2,1)S(1)} %get-tuple-element.37), channel_id=1, source_target_pairs={{0,1},{1,0},{2,3},{3,2},{4,5},{5,4},{6,7},{7,6},{8,9},{9,8},{10,11... | collective-permute-start | bytes 1032200 | tf_op jit(solution)/shard_map/ppermute | solution.py:235
  37.3 12.6 %collective-permute-start.15 = (bf16[96,896]{1,0:T(8,128)(2,1)S(1)}, bf16[96,896]{1,0:T(8,128)(2,1)S(1)}, u32[]{:S(2)}, u32[]{:S(2)}) collective-permute-start(bf16[96,896]{1,0:T(8,128)(2,1)S(1)} %chip_sum_kernel.3.refs_2_), channel_id=1, source_target_pairs={{0,12},{4,0},{8,4},{12,8},{1,13},{5,1},{9,5},{13,9},{2,14},{6,2},{... | collective-permute-start | bytes 516104 | tf_op jit(solution)/shard_map/ppermute | solution.py:242
  38.8 7.3 %collective-permute-start.16 = (bf16[96,896]{1,0:T(8,128)(2,1)S(1)}, bf16[96,896]{1,0:T(8,128)(2,1)S(1)}, u32[]{:S(2)}, u32[]{:S(2)}) collective-permute-start(bf16[96,896]{1,0:T(8,128)(2,1)S(1)} %get-tuple-element.36), channel_id=1, source_target_pairs={{0,2},{1,3},{2,0},{3,1},{4,6},{5,7},{6,4},{7,5},{8,10},{9,11},{10,... | collective-permute-start | bytes 516104 | tf_op jit(solution)/shard_map/ppermute | solution.py:235
  40.3 7.9 %collective-permute-start.20 = (bf16[96,896]{1,0:T(8,128)(2,1)S(1)}, bf16[96,896]{1,0:T(8,128)(2,1)S(1)}, u32[]{:S(2)}, u32[]{:S(2)}) collective-permute-start(bf16[96,896]{1,0:T(8,128)(2,1)S(1)} %get-tuple-element.40), channel_id=1, source_target_pairs={{0,2},{1,3},{2,0},{3,1},{4,6},{5,7},{6,4},{7,5},{8,10},{9,11},{10,... | collective-permute-start | bytes 516104 | tf_op jit(solution)/shard_map/ppermute | solution.py:235
  46.2 11.9 %collective-permute-start.18 = (bf16[96,896]{1,0:T(8,128)(2,1)S(1)}, bf16[96,896]{1,0:T(8,128)(2,1)S(1)}, u32[]{:S(2)}, u32[]{:S(2)}) collective-permute-start(bf16[96,896]{1,0:T(8,128)(2,1)S(1)} %chip_sum_kernel.4.refs_2_), channel_id=1, source_target_pairs={{0,8},{4,12},{8,0},{12,4},{1,9},{5,13},{9,1},{13,5},{2,10},{6,14},... | collective-permute-start | bytes 516104 | tf_op jit(solution)/shard_map/ppermute | solution.py:242
  48.3 10.0 %collective-permute-start.22 = (bf16[96,896]{1,0:T(8,128)(2,1)S(1)}, bf16[96,896]{1,0:T(8,128)(2,1)S(1)}, u32[]{:S(2)}, u32[]{:S(2)}) collective-permute-start(bf16[96,896]{1,0:T(8,128)(2,1)S(1)} %chip_sum_kernel.5.refs_2_), channel_id=1, source_target_pairs={{0,4},{4,8},{8,12},{12,0},{1,5},{5,9},{9,13},{13,1},{2,6},{6,10},{... | collective-permute-start | bytes 516104 | tf_op jit(solution)/shard_map/ppermute | solution.py:242
  48.8 9.3 %collective-permute-start.21 = (bf16[96,896]{1,0:T(8,128)(2,1)S(1)}, bf16[96,896]{1,0:T(8,128)(2,1)S(1)}, u32[]{:S(2)}, u32[]{:S(2)}) collective-permute-start(bf16[96,896]{1,0:T(8,128)(2,1)S(1)} %get-tuple-element.42), channel_id=1, source_target_pairs={{0,2},{1,3},{2,0},{3,1},{4,6},{5,7},{6,4},{7,5},{8,10},{9,11},{10,... | collective-permute-start | bytes 516104 | tf_op jit(solution)/shard_map/ppermute | solution.py:235

commit v17 on v15

--- a/solution.py
+++ b/solution.py
@@ -276,7 +276,7 @@
     arrive(1, tokens, 1, [columns])
     lay((0,), [blocks[1]])
     chips[3,] = shift(chips[0,], -1)
-    run((0,), [], 8)
+    run((0,), [], .05)
     arrive(2, blocks[1], 1, [kept[0,][0]])
     others[1] = after(others[1], kept[0,][0])
     run((1,), [blocks[2]], .05)

time: 55.8 us -> 55.5 us (level)
  no operation moved by 1% of the time
where the time goes in v17:
time: 55.5 us; the launch traced here: 55.3 us
  waiting for transfers between devices  23.1 us (42%)
  Pallas kernels  16.1 us (29%)
  starting transfers between devices  16 us (29%)
    pallas_call x16, Pallas kernels, local_call(): pl.pallas_call(body_of, name=name, out_shape=out_shape, in_specs=list(in_...  16.1 us
    ppermute x6, waiting for transfers between devices, shift(): lax.ppermute(array, 'expert', [(i, (i + by) % experts_n) for i in range(e...  12 us
    ppermute x17, waiting for transfers between devices, swap(): return lax.ppermute(array, 'tensor', [(i, i ^ bit) for i in range(4)])  11.1 us
    ppermute x17, starting transfers between devices, swap(): return lax.ppermute(array, 'tensor', [(i, i ^ bit) for i in range(4)])  9.1 us
    ppermute x6, starting transfers between devices, shift(): lax.ppermute(array, 'expert', [(i, (i + by) % experts_n) for i in range(e...  6.87 us
  transfers between devices with their start and end apart: 23, of which 10 were waited for; matrix products, arithmetic and copies ran while one was open for 0% of the time, Pallas kernels for 28%

profile of v17, /device:TPU:0, one launch (start us, length us, event | category | flops | bytes accessed | tf_op | source)
XLA Modules:
  0.0 55.3 jit_solution(11450499091481438808)
XLA Ops:
  0.0 3.0 %collective-permute-start = (bf16[96,896]{1,0:T(8,128)(2,1)}, bf16[96,896]{1,0:T(8,128)(2,1)S(1)}, u32[]{:S(2)}, u32[]{:S(2)}) collective-permute-start(bf16[96,896]{1,0:T(8,128)(2,1)} %refs_0_.1), channel_id=1, source_target_pairs={{0,4},{4,8},{8,12},{12,0},{1,5},{5,9},{9,13},{13,1},{2,6},{6,10},{... | collective-permute-start | bytes 516104 | tf_op jit(solution)/shard_map/ppermute | solution.py:242
  3.0 1.5 %collective-permute-start.2 = (bf16[96,896]{1,0:T(8,128)(2,1)}, bf16[96,896]{1,0:T(8,128)(2,1)S(1)}, u32[]{:S(2)}, u32[]{:S(2)}) collective-permute-start(bf16[96,896]{1,0:T(8,128)(2,1)} %refs_0_.1), channel_id=1, source_target_pairs={{0,2},{1,3},{2,0},{3,1},{4,6},{5,7},{6,4},{7,5},{8,10},{9,11},{10,... | collective-permute-start | bytes 516104 | tf_op jit(solution)/shard_map/ppermute | solution.py:235
  4.5 4.3 %prepare_kernel.1 = (f32[4,96,128]{2,1,0:T(8,128)S(1)}, bf16[608,3584]{1,0:T(8,128)(2,1)S(1)}, bf16[608,3584]{1,0:T(8,128)(2,1)S(1)}) custom-call(s32[2,96]{1,0:T(2,128)} %bitcast.8, s32[2,96]{1,0:T(2,128)} %bitcast.9, bf16[608,3584]{1,0:T(8,128)(2,1)} %bitcast.6, bf16[608,3584]{1,0:T(8,128)(2,1)} %bitcast.7), custom_call_target="tpu_custom_call" | custom-call | flops 4600000000 | tf_op jit(solution)/shard_map/prepare_kernel/pallas_call | solution.py:72
  8.9 0.8 %collective-permute-done.refs_0_ = bf16[96,896]{1,0:T(8,128)(2,1)S(1)} collective-permute-done((bf16[96,896]{1,0:T(8,128)(2,1)}, bf16[96,896]{1,0:T(8,128)(2,1)S(1)}, u32[]{:S(2)}, u32[]{:S(2)}) %collective-permute-start) | collective-permute-done | bytes 172064 | tf_op jit(solution)/shard_map/ppermute | solution.py:242
  9.7 1.6 %collective-permute-start.1 = (bf16[96,896]{1,0:T(8,128)(2,1)S(1)}, bf16[96,896]{1,0:T(8,128)(2,1)S(1)}, u32[]{:S(2)}, u32[]{:S(2)}) collective-permute-start(bf16[96,896]{1,0:T(8,128)(2,1)S(1)} %shard_map.55.refs_2_.refs_0_), channel_id=1, source_target_pairs={{0,2},{1,3},{2,0},{3,1},{4,6},{5,7},{6,4},{7,5},{8,10},{9,11},{10,... | collective-permute-start | bytes 516104 | tf_op jit(solution)/shard_map/ppermute | solution.py:235
  11.3 1.0 %collective-permute-start.6 = (bf16[96,896]{1,0:T(8,128)(2,1)S(1)}, bf16[96,896]{1,0:T(8,128)(2,1)S(1)}, u32[]{:S(2)}, u32[]{:S(2)}) collective-permute-start(bf16[96,896]{1,0:T(8,128)(2,1)S(1)} %shard_map.55.refs_2_.refs_0_), channel_id=1, source_target_pairs={{0,4},{4,8},{8,12},{12,0},{1,5},{5,9},{9,13},{13,1},{2,6},{6,10},{... | collective-permute-start | bytes 516104 | tf_op jit(solution)/shard_map/ppermute | solution.py:242
  12.3 2.6 %expert_kernel.4 = (f32[96,1792]{1,0:T(8,128)S(1)}, bf16[96,1792]{1,0:T(8,128)(2,1)S(1)}) custom-call(bf16[96,1792]{1,0:T(8,128)(2,1)S(1)} %pack_kernel.1.refs_0_, bf16[96,1792]{1,0:T(8,128)(2,1)S(1)} %collective-permute-done.3.refs_1_, bf16[608,3584]{1,0:T(8,128)(2,1)S(1)} %get-tuple-element.25.refs_2_.refs_4_, ...), custom_call_target="tpu_custom_call" | custom-call | flops 57500000 | tf_op jit(solution)/shard_map/expert_kernel/pallas_call | solution.py:72
  14.9 1.6 %collective-permute-done.1.refs_0_ = bf16[96,896]{1,0:T(8,128)(2,1)S(1)} collective-permute-done((bf16[96,896]{1,0:T(8,128)(2,1)S(1)}, bf16[96,896]{1,0:T(8,128)(2,1)S(1)}, u32[]{:S(2)}, u32[]{:S(2)}) %collective-permute-start.1) | collective-permute-done | bytes 172064 | tf_op jit(solution)/shard_map/ppermute | solution.py:235
  16.5 3.0 %collective-permute-done.6.refs_0_ = bf16[96,896]{1,0:T(8,128)(2,1)S(1)} collective-permute-done((bf16[96,896]{1,0:T(8,128)(2,1)S(1)}, bf16[96,896]{1,0:T(8,128)(2,1)S(1)}, u32[]{:S(2)}, u32[]{:S(2)}) %collective-permute-start.6) | collective-permute-done | bytes 172064 | tf_op jit(solution)/shard_map/ppermute | solution.py:242
  20.1 2.6 %expert_kernel.5 = (f32[96,1792]{1,0:T(8,128)S(1)}, bf16[96,1792]{1,0:T(8,128)(2,1)S(1)}) custom-call(bf16[96,896]{1,0:T(8,128)(2,1)S(1)} %shard_map.55.refs_2_.refs_0_, bf16[96,896]{1,0:T(8,128)(2,1)S(1)} %shard_map.56.refs_1_, bf16[96,896]{1,0:T(8,128)(2,1)S(1)} %collective-permute-done.4.refs_2_, bf16[96,896]{1,0:T(8,128)(2,1)S(1)} %collective-permute-done.5.refs_3_, ...), custom_call_target="tpu_custom_call" | custom-call | flops 57500000 | tf_op jit(solution)/shard_map/expert_kernel/pallas_call | solution.py:72
  23.3 1.9 %collective-permute-done.8.refs_1_ = bf16[96,896]{1,0:T(8,128)(2,1)S(1)} collective-permute-done((bf16[96,896]{1,0:T(8,128)(2,1)S(1)}, bf16[96,896]{1,0:T(8,128)(2,1)S(1)}, u32[]{:S(2)}, u32[]{:S(2)}) %collective-permute-start.8) | collective-permute-done | bytes 172064 | tf_op jit(solution)/shard_map/ppermute | solution.py:235
  25.2 1.4 %collective-permute-done.10.refs_3_ = bf16[96,896]{1,0:T(8,128)(2,1)S(1)} collective-permute-done((bf16[96,896]{1,0:T(8,128)(2,1)S(1)}, bf16[96,896]{1,0:T(8,128)(2,1)S(1)}, u32[]{:S(2)}, u32[]{:S(2)}) %collective-permute-start.10) | collective-permute-done | bytes 172064 | tf_op jit(solution)/shard_map/ppermute | solution.py:235
  26.6 2.6 %expert_kernel.6 = (f32[96,1792]{1,0:T(8,128)S(1)}, bf16[96,1792]{1,0:T(8,128)(2,1)S(1)}) custom-call(bf16[96,896]{1,0:T(8,128)(2,1)S(1)} %shard_map.57.refs_6_.refs_0_, bf16[96,896]{1,0:T(8,128)(2,1)S(1)} %collective-permute-done.8.refs_1_, bf16[96,896]{1,0:T(8,128)(2,1)S(1)} %collective-permute-done.9.refs_2_, ...), custom_call_target="tpu_custom_call" | custom-call | flops 57500000 | tf_op jit(solution)/shard_map/expert_kernel/pallas_call | solution.py:72
  30.0 0.7 %collective-permute-start.11 = (bf16[96,896]{1,0:T(8,128)(2,1)S(1)}, bf16[96,896]{1,0:T(8,128)(2,1)S(1)}, u32[]{:S(2)}, u32[]{:S(2)}) collective-permute-start(bf16[96,896]{1,0:T(8,128)(2,1)S(1)} %get-tuple-element.32), channel_id=1, source_target_pairs={{0,2},{1,3},{2,0},{3,1},{4,6},{5,7},{6,4},{7,5},{8,10},{9,11},{10,... | collective-permute-start | bytes 516104 | tf_op jit(solution)/shard_map/ppermute | solution.py:235
  31.0 1.3 %collective-permute-start.16 = (bf16[96,896]{1,0:T(8,128)(2,1)S(1)}, bf16[96,896]{1,0:T(8,128)(2,1)S(1)}, u32[]{:S(2)}, u32[]{:S(2)}) collective-permute-start(bf16[96,896]{1,0:T(8,128)(2,1)S(1)} %get-tuple-element.36), channel_id=1, source_target_pairs={{0,2},{1,3},{2,0},{3,1},{4,6},{5,7},{6,4},{7,5},{8,10},{9,11},{10,... | collective-permute-start | bytes 516104 | tf_op jit(solution)/shard_map/ppermute | solution.py:235
  32.3 2.6 %expert_kernel.7 = (f32[96,1792]{1,0:T(8,128)S(1)}, bf16[96,1792]{1,0:T(8,128)(2,1)S(1)}) custom-call(bf16[96,1792]{1,0:T(8,128)(2,1)S(1)} %shard_map.58.refs_0_, bf16[96,1792]{1,0:T(8,128)(2,1)S(1)} %collective-permute-done.13.refs_1_, bf16[608,3584]{1,0:T(8,128)(2,1)S(1)} %get-tuple-element.25.refs_2_.refs_4_, ...), custom_call_target="tpu_custom_call" | custom-call | flops 4600000000 | tf_op jit(solution)/shard_map/expert_kernel/pallas_call | solution.py:72
  35.0 2.3 %collective-permute-done.11.refs_1_ = bf16[96,896]{1,0:T(8,128)(2,1)S(1)} collective-permute-done((bf16[96,896]{1,0:T(8,128)(2,1)S(1)}, bf16[96,896]{1,0:T(8,128)(2,1)S(1)}, u32[]{:S(2)}, u32[]{:S(2)}) %collective-permute-start.11) | collective-permute-done | bytes 172064 | tf_op jit(solution)/shard_map/ppermute | solution.py:235
  37.3 1.9 %collective-permute-start.15 = (bf16[96,896]{1,0:T(8,128)(2,1)S(1)}, bf16[96,896]{1,0:T(8,128)(2,1)S(1)}, u32[]{:S(2)}, u32[]{:S(2)}) collective-permute-start(bf16[96,896]{1,0:T(8,128)(2,1)S(1)} %chip_sum_kernel.3.refs_2_), channel_id=1, source_target_pairs={{0,12},{4,0},{8,4},{12,8},{1,13},{5,1},{9,5},{13,9},{2,14},{6,2},{... | collective-permute-start | bytes 516104 | tf_op jit(solution)/shard_map/ppermute | solution.py:242
  39.3 1.0 %collective-permute-start.20 = (bf16[96,896]{1,0:T(8,128)(2,1)S(1)}, bf16[96,896]{1,0:T(8,128)(2,1)S(1)}, u32[]{:S(2)}, u32[]{:S(2)}) collective-permute-start(bf16[96,896]{1,0:T(8,128)(2,1)S(1)} %get-tuple-element.40), channel_id=1, source_target_pairs={{0,2},{1,3},{2,0},{3,1},{4,6},{5,7},{6,4},{7,5},{8,10},{9,11},{10,... | collective-permute-start | bytes 516104 | tf_op jit(solution)/shard_map/ppermute | solution.py:235
  40.5 0.7 %collective-permute-start.18 = (bf16[96,896]{1,0:T(8,128)(2,1)S(1)}, bf16[96,896]{1,0:T(8,128)(2,1)S(1)}, u32[]{:S(2)}, u32[]{:S(2)}) collective-permute-start(bf16[96,896]{1,0:T(8,128)(2,1)S(1)} %chip_sum_kernel.4.refs_2_), channel_id=1, source_target_pairs={{0,8},{4,12},{8,0},{12,4},{1,9},{5,13},{9,1},{13,5},{2,10},{6,14},... | collective-permute-start | bytes 516104 | tf_op jit(solution)/shard_map/ppermute | solution.py:242
  41.2 3.6 %collective-permute-done.20.refs_1_ = bf16[96,896]{1,0:T(8,128)(2,1)S(1)} collective-permute-done((bf16[96,896]{1,0:T(8,128)(2,1)S(1)}, bf16[96,896]{1,0:T(8,128)(2,1)S(1)}, u32[]{:S(2)}, u32[]{:S(2)}) %collective-permute-start.20) | collective-permute-done | bytes 172064 | tf_op jit(solution)/shard_map/ppermute | solution.py:235
  45.1 1.1 %collective-permute-start.21 = (bf16[96,896]{1,0:T(8,128)(2,1)S(1)}, bf16[96,896]{1,0:T(8,128)(2,1)S(1)}, u32[]{:S(2)}, u32[]{:S(2)}) collective-permute-start(bf16[96,896]{1,0:T(8,128)(2,1)S(1)} %get-tuple-element.42), channel_id=1, source_target_pairs={{0,2},{1,3},{2,0},{3,1},{4,6},{5,7},{6,4},{7,5},{8,10},{9,11},{10,... | collective-permute-start | bytes 516104 | tf_op jit(solution)/shard_map/ppermute | solution.py:235
  46.2 8.2 %collective-permute-done.18.refs_2_ = bf16[96,896]{1,0:T(8,128)(2,1)S(1)} collective-permute-done((bf16[96,896]{1,0:T(8,128)(2,1)S(1)}, bf16[96,896]{1,0:T(8,128)(2,1)S(1)}, u32[]{:S(2)}, u32[]{:S(2)}) %collective-permute-start.18) | collective-permute-done | bytes 172064 | tf_op jit(solution)/shard_map/ppermute | solution.py:242
  54.6 0.7 %weigh_kernel.5 = bf16[96,896]{1,0:T(8,128)(2,1)} custom-call(f32[4,96,128]{2,1,0:T(8,128)S(1)} %get-tuple-element.24.refs_1_.refs_0_, f32[96,896]{1,0:T(8,128)S(1)} %weigh_kernel.4.refs_1_, bf16[96,896]{1,0:T(8,128)(2,1)S(1)} %collective-permute-done.22.refs_2_), custom_call_target="tpu_custom_call" | custom-call | flops 575000000 | tf_op jit(solution)/shard_map/weigh_kernel/pallas_call | solution.py:72
  (44 shorter events, 3.2 us)
Async XLA Ops:
  0.0 9.6 %collective-permute-start = (bf16[96,896]{1,0:T(8,128)(2,1)}, bf16[96,896]{1,0:T(8,128)(2,1)S(1)}, u32[]{:S(2)}, u32[]{:S(2)}) collective-permute-start(bf16[96,896]{1,0:T(8,128)(2,1)} %refs_0_.1), channel_id=1, source_target_pairs={{0,4},{4,8},{8,12},{12,0},{1,5},{5,9},{9,13},{13,1},{2,6},{6,10},{... | collective-permute-start | bytes 516104 | tf_op jit(solution)/shard_map/ppermute | solution.py:242
  3.0 6.6 %collective-permute-start.2 = (bf16[96,896]{1,0:T(8,128)(2,1)}, bf16[96,896]{1,0:T(8,128)(2,1)S(1)}, u32[]{:S(2)}, u32[]{:S(2)}) collective-permute-start(bf16[96,896]{1,0:T(8,128)(2,1)} %refs_0_.1), channel_id=1, source_target_pairs={{0,2},{1,3},{2,0},{3,1},{4,6},{5,7},{6,4},{7,5},{8,10},{9,11},{10,... | collective-permute-start | bytes 516104 | tf_op jit(solution)/shard_map/ppermute | solution.py:235
  4.5 5.1 %copy-start = (bf16[96,896]{1,0:T(8,128)(2,1)S(1)}, bf16[96,896]{1,0:T(8,128)(2,1)}, u32[]{:S(2)}) copy-start(bf16[96,896]{1,0:T(8,128)(2,1)} %refs_0_.1) | copy-start | bytes 516100
  9.7 2.7 %collective-permute-start.3 = (bf16[96,1792]{1,0:T(8,128)(2,1)S(1)}, bf16[96,1792]{1,0:T(8,128)(2,1)S(1)}, u32[]{:S(2)}, u32[]{:S(2)}) collective-permute-start(bf16[96,1792]{1,0:T(8,128)(2,1)S(1)} %pack_kernel.1.refs_0_), channel_id=1, source_target_pairs={{0,1},{1,0},{2,3},{3,2},{4,5},{5,4},{6,7},{7,6},{8,9},{9,8},{10,11... | collective-permute-start | bytes 1032200 | tf_op jit(solution)/shard_map/ppermute | solution.py:235
  9.7 6.8 %collective-permute-start.1 = (bf16[96,896]{1,0:T(8,128)(2,1)S(1)}, bf16[96,896]{1,0:T(8,128)(2,1)S(1)}, u32[]{:S(2)}, u32[]{:S(2)}) collective-permute-start(bf16[96,896]{1,0:T(8,128)(2,1)S(1)} %shard_map.55.refs_2_.refs_0_), channel_id=1, source_target_pairs={{0,2},{1,3},{2,0},{3,1},{4,6},{5,7},{6,4},{7,5},{8,10},{9,11},{10,... | collective-permute-start | bytes 516104 | tf_op jit(solution)/shard_map/ppermute | solution.py:235
  11.3 8.2 %collective-permute-start.6 = (bf16[96,896]{1,0:T(8,128)(2,1)S(1)}, bf16[96,896]{1,0:T(8,128)(2,1)S(1)}, u32[]{:S(2)}, u32[]{:S(2)}) collective-permute-start(bf16[96,896]{1,0:T(8,128)(2,1)S(1)} %shard_map.55.refs_2_.refs_0_), channel_id=1, source_target_pairs={{0,4},{4,8},{8,12},{12,0},{1,5},{5,9},{9,13},{13,1},{2,6},{6,10},{... | collective-permute-start | bytes 516104 | tf_op jit(solution)/shard_map/ppermute | solution.py:242
  12.3 7.8 %collective-permute-start.4 = (bf16[96,896]{1,0:T(8,128)(2,1)S(1)}, bf16[96,896]{1,0:T(8,128)(2,1)S(1)}, u32[]{:S(2)}, u32[]{:S(2)}) collective-permute-start(bf16[96,896]{1,0:T(8,128)(2,1)S(1)} %shard_map.55.refs_2_.refs_0_), channel_id=1, source_target_pairs={{0,1},{1,0},{2,3},{3,2},{4,5},{5,4},{6,7},{7,6},{8,9},{9,8},{10,11... | collective-permute-start | bytes 516104 | tf_op jit(solution)/shard_map/ppermute | solution.py:235
  16.5 3.6 %collective-permute-start.5 = (bf16[96,896]{1,0:T(8,128)(2,1)S(1)}, bf16[96,896]{1,0:T(8,128)(2,1)S(1)}, u32[]{:S(2)}, u32[]{:S(2)}) collective-permute-start(bf16[96,896]{1,0:T(8,128)(2,1)S(1)} %shard_map.56.refs_1_), channel_id=1, source_target_pairs={{0,1},{1,0},{2,3},{3,2},{4,5},{5,4},{6,7},{7,6},{8,9},{9,8},{10,11... | collective-permute-start | bytes 516104 | tf_op jit(solution)/shard_map/ppermute | solution.py:235
  19.6 5.6 %collective-permute-start.8 = (bf16[96,896]{1,0:T(8,128)(2,1)S(1)}, bf16[96,896]{1,0:T(8,128)(2,1)S(1)}, u32[]{:S(2)}, u32[]{:S(2)}) collective-permute-start(bf16[96,896]{1,0:T(8,128)(2,1)S(1)} %shard_map.57.refs_6_.refs_0_), channel_id=1, source_target_pairs={{0,2},{1,3},{2,0},{3,1},{4,6},{5,7},{6,4},{7,5},{8,10},{9,11},{10,... | collective-permute-start | bytes 516104 | tf_op jit(solution)/shard_map/ppermute | solution.py:235
  20.1 9.7 %collective-permute-start.12 = (bf16[96,1792]{1,0:T(8,128)(2,1)S(1)}, bf16[96,1792]{1,0:T(8,128)(2,1)S(1)}, u32[]{:S(2)}, u32[]{:S(2)}) collective-permute-start(bf16[96,1792]{1,0:T(8,128)(2,1)S(1)} %pack_kernel.1.refs_0_), channel_id=1, source_target_pairs={{0,12},{4,0},{8,4},{12,8},{1,13},{5,1},{9,5},{13,9},{2,14},{6,2},{... | collective-permute-start | bytes 1032200 | tf_op jit(solution)/shard_map/ppermute | solution.py:242
  22.7 7.2 %collective-permute-start.7 = (bf16[96,1792]{1,0:T(8,128)(2,1)S(1)}, bf16[96,1792]{1,0:T(8,128)(2,1)S(1)}, u32[]{:S(2)}, u32[]{:S(2)}) collective-permute-start(bf16[96,1792]{1,0:T(8,128)(2,1)S(1)} %get-tuple-element.29), channel_id=1, source_target_pairs={{0,1},{1,0},{2,3},{3,2},{4,5},{5,4},{6,7},{7,6},{8,9},{9,8},{10,11... | collective-permute-start | bytes 1032200 | tf_op jit(solution)/shard_map/ppermute | solution.py:235
  22.8 2.4 %collective-permute-start.9 = (bf16[96,896]{1,0:T(8,128)(2,1)S(1)}, bf16[96,896]{1,0:T(8,128)(2,1)S(1)}, u32[]{:S(2)}, u32[]{:S(2)}) collective-permute-start(bf16[96,896]{1,0:T(8,128)(2,1)S(1)} %shard_map.57.refs_6_.refs_0_), channel_id=1, source_target_pairs={{0,1},{1,0},{2,3},{3,2},{4,5},{5,4},{6,7},{7,6},{8,9},{9,8},{10,11... | collective-permute-start | bytes 516104 | tf_op jit(solution)/shard_map/ppermute | solution.py:235
  25.2 1.4 %collective-permute-start.10 = (bf16[96,896]{1,0:T(8,128)(2,1)S(1)}, bf16[96,896]{1,0:T(8,128)(2,1)S(1)}, u32[]{:S(2)}, u32[]{:S(2)}) collective-permute-start(bf16[96,896]{1,0:T(8,128)(2,1)S(1)} %collective-permute-done.8.refs_1_), channel_id=1, source_target_pairs={{0,1},{1,0},{2,3},{3,2},{4,5},{5,4},{6,7},{7,6},{8,9},{9,8},{10,11... | collective-permute-start | bytes 516104 | tf_op jit(solution)/shard_map/ppermute | solution.py:235
  29.2 1.7 %collective-permute-start.14 = (bf16[96,1792]{1,0:T(8,128)(2,1)S(1)}, bf16[96,1792]{1,0:T(8,128)(2,1)S(1)}, u32[]{:S(2)}, u32[]{:S(2)}) collective-permute-start(bf16[96,1792]{1,0:T(8,128)(2,1)S(1)} %get-tuple-element.33), channel_id=1, source_target_pairs={{0,1},{1,0},{2,3},{3,2},{4,5},{5,4},{6,7},{7,6},{8,9},{9,8},{10,11... | collective-permute-start | bytes 1032200 | tf_op jit(solution)/shard_map/ppermute | solution.py:235
  29.4 15.6 %collective-permute-start.19 = (bf16[96,1792]{1,0:T(8,128)(2,1)S(1)}, bf16[96,1792]{1,0:T(8,128)(2,1)S(1)}, u32[]{:S(2)}, u32[]{:S(2)}) collective-permute-start(bf16[96,1792]{1,0:T(8,128)(2,1)S(1)} %get-tuple-element.39), channel_id=1, source_target_pairs={{0,1},{1,0},{2,3},{3,2},{4,5},{5,4},{6,7},{7,6},{8,9},{9,8},{10,11... | collective-permute-start | bytes 1032200 | tf_op jit(solution)/shard_map/ppermute | solution.py:235
  29.8 2.5 %collective-permute-start.13 = (bf16[96,1792]{1,0:T(8,128)(2,1)S(1)}, bf16[96,1792]{1,0:T(8,128)(2,1)S(1)}, u32[]{:S(2)}, u32[]{:S(2)}) collective-permute-start(bf16[96,1792]{1,0:T(8,128)(2,1)S(1)} %shard_map.58.refs_0_), channel_id=1, source_target_pairs={{0,1},{1,0},{2,3},{3,2},{4,5},{5,4},{6,7},{7,6},{8,9},{9,8},{10,11... | collective-permute-start | bytes 1032200 | tf_op jit(solution)/shard_map/ppermute | solution.py:235
  30.0 7.3 %collective-permute-start.11 = (bf16[96,896]{1,0:T(8,128)(2,1)S(1)}, bf16[96,896]{1,0:T(8,128)(2,1)S(1)}, u32[]{:S(2)}, u32[]{:S(2)}) collective-permute-start(bf16[96,896]{1,0:T(8,128)(2,1)S(1)} %get-tuple-element.32), channel_id=1, source_target_pairs={{0,2},{1,3},{2,0},{3,1},{4,6},{5,7},{6,4},{7,5},{8,10},{9,11},{10,... | collective-permute-start | bytes 516104 | tf_op jit(solution)/shard_map/ppermute | solution.py:235
  31.0 9.4 %collective-permute-start.16 = (bf16[96,896]{1,0:T(8,128)(2,1)S(1)}, bf16[96,896]{1,0:T(8,128)(2,1)S(1)}, u32[]{:S(2)}, u32[]{:S(2)}) collective-permute-start(bf16[96,896]{1,0:T(8,128)(2,1)S(1)} %get-tuple-element.36), channel_id=1, source_target_pairs={{0,2},{1,3},{2,0},{3,1},{4,6},{5,7},{6,4},{7,5},{8,10},{9,11},{10,... | collective-permute-start | bytes 516104 | tf_op jit(solution)/shard_map/ppermute | solution.py:235
  34.9 4.3 %collective-permute-start.17 = (bf16[96,1792]{1,0:T(8,128)(2,1)S(1)}, bf16[96,1792]{1,0:T(8,128)(2,1)S(1)}, u32[]{:S(2)}, u32[]{:S(2)}) collective-permute-start(bf16[96,1792]{1,0:T(8,128)(2,1)S(1)} %get-tuple-element.37), channel_id=1, source_target_pairs={{0,1},{1,0},{2,3},{3,2},{4,5},{5,4},{6,7},{7,6},{8,9},{9,8},{10,11... | collective-permute-start | bytes 1032200 | tf_op jit(solution)/shard_map/ppermute | solution.py:235
  37.3 8.9 %collective-permute-start.15 = (bf16[96,896]{1,0:T(8,128)(2,1)S(1)}, bf16[96,896]{1,0:T(8,128)(2,1)S(1)}, u32[]{:S(2)}, u32[]{:S(2)}) collective-permute-start(bf16[96,896]{1,0:T(8,128)(2,1)S(1)} %chip_sum_kernel.3.refs_2_), channel_id=1, source_target_pairs={{0,12},{4,0},{8,4},{12,8},{1,13},{5,1},{9,5},{13,9},{2,14},{6,2},{... | collective-permute-start | bytes 516104 | tf_op jit(solution)/shard_map/ppermute | solution.py:242
  39.3 5.5 %collective-permute-start.20 = (bf16[96,896]{1,0:T(8,128)(2,1)S(1)}, bf16[96,896]{1,0:T(8,128)(2,1)S(1)}, u32[]{:S(2)}, u32[]{:S(2)}) collective-permute-start(bf16[96,896]{1,0:T(8,128)(2,1)S(1)} %get-tuple-element.40), channel_id=1, source_target_pairs={{0,2},{1,3},{2,0},{3,1},{4,6},{5,7},{6,4},{7,5},{8,10},{9,11},{10,... | collective-permute-start | bytes 516104 | tf_op jit(solution)/shard_map/ppermute | solution.py:235
  40.5 14.0 %collective-permute-start.18 = (bf16[96,896]{1,0:T(8,128)(2,1)S(1)}, bf16[96,896]{1,0:T(8,128)(2,1)S(1)}, u32[]{:S(2)}, u32[]{:S(2)}) collective-permute-start(bf16[96,896]{1,0:T(8,128)(2,1)S(1)} %chip_sum_kernel.4.refs_2_), channel_id=1, source_target_pairs={{0,8},{4,12},{8,0},{12,4},{1,9},{5,13},{9,1},{13,5},{2,10},{6,14},... | collective-permute-start | bytes 516104 | tf_op jit(solution)/shard_map/ppermute | solution.py:242
  44.8 9.8 %collective-permute-start.22 = (bf16[96,896]{1,0:T(8,128)(2,1)S(1)}, bf16[96,896]{1,0:T(8,128)(2,1)S(1)}, u32[]{:S(2)}, u32[]{:S(2)}) collective-permute-start(bf16[96,896]{1,0:T(8,128)(2,1)S(1)} %chip_sum_kernel.5.refs_2_), channel_id=1, source_target_pairs={{0,4},{4,8},{8,12},{12,0},{1,5},{5,9},{9,13},{13,1},{2,6},{6,10},{... | collective-permute-start | bytes 516104 | tf_op jit(solution)/shard_map/ppermute | solution.py:242
  45.1 9.4 %collective-permute-start.21 = (bf16[96,896]{1,0:T(8,128)(2,1)S(1)}, bf16[96,896]{1,0:T(8,128)(2,1)S(1)}, u32[]{:S(2)}, u32[]{:S(2)}) collective-permute-start(bf16[96,896]{1,0:T(8,128)(2,1)S(1)} %get-tuple-element.42), channel_id=1, source_target_pairs={{0,2},{1,3},{2,0},{3,1},{4,6},{5,7},{6,4},{7,5},{8,10},{9,11},{10,... | collective-permute-start | bytes 516104 | tf_op jit(solution)/shard_map/ppermute | solution.py:235
